TPU v7x, 32 devices: a whole 2x2x4 slice. The times are simulated.
32 devices in a mesh: box: 8 (over z, y), orb: 4 (over x, core).
Axes of the slice: x: 2, y: 2, z: 4, core: 2. Of those that a mesh axis runs over, the one named last changes fastest.
Arguments:
- orbitals: bfloat16 [16, 1000, 1536], P('box', None, 'orb'), may hold values from -0.0546875 to 0.0546875
- potential: float32 [16, 1000], P('box'), may hold values from -3 to 1
- deriv_blocks: bfloat16 [3, 10, 10], replicated, may hold values from -1 to 1
- levels: int32 [16], P('box'), may hold values from 0 to 2
- box_counts: int32 [8], P('box'), may hold values from 1 to 2, as said below
- neighbours: int32 [16, 3, 2], P('box'), may hold values from -1 to 15, as said below
Outputs:
- fock: float32 [1536, 1536], P('box', 'orb')
- correlation: float32 [1536, 1536], P('box', 'orb')
- inverse_root: float32 [1536, 1536], P('box', 'orb')
Inputs may be any that keep to these rules, and one draw needn't show every extreme that they name: Each index of box holds box_counts of live slots, which are its first slots; the counts sum to 12, and some index holds 2. `neighbours`: an entry is -1 or the global slot of a live slot, other than the slot itself, on the same index of box or on the index just before or just after it; every entry of a non-live slot is -1.
All inputs are finite; a program needn't handle non-finite values.
Results may differ from a plain program's by a relative error of at most 0.0012.
Values may be sent and summed in bfloat16 or wider, within the bound.
No kernel may reach another device: no remote copies, remote signals or barrier semaphores. Data moves between devices by JAX's collectives and lax.ppermute only.
A program may use at most 128 MiB of HBM per device.

v0:
```python
import functools

import jax
import jax.numpy as jnp
import numpy as np
from jax import lax
from jax.experimental import pallas as pl
from jax.experimental.pallas import tpu as pltpu
from jax.sharding import Mesh, PartitionSpec as P

PAIR = 2
ROWS = 16
BOX = ("lvl", "pair")
f32, bf16 = jnp.float32, jnp.bfloat16


def swap(value, axis, bit):
    count = lax.axis_size(axis)
    return lax.ppermute(value, axis, [(i, i ^ bit) for i in range(count)])


def trade(value, axis, start):
    pairs = [(i, i + 1) for i in range(start, lax.axis_size(axis) - 1, 2)]
    return lax.ppermute(value, axis, pairs + [(b, a) for a, b in pairs])


def matmul(left, right):
    return jnp.dot(left, right, preferred_element_type=f32)


def params(mebibytes):
    return pltpu.CompilerParams(vmem_limit_bytes=mebibytes * 1024 * 1024)


def pack_kernel(own, meta, orbitals, facts, packed, *active):
    slots, coefficients, width = orbitals.shape
    half, fold = width // PAIR, coefficients // 2
    low_half = (meta[0] == 0) == own
    for slot in range(slots):
        keep = slot < meta[1]
        for part in range(2):
            rows = slice(part * fold, (part + 1) * fold)
            here = orbitals[slot, rows, :]
            here = jnp.where(keep, here, jnp.zeros_like(here))
            if active:
                active[0][slot, rows, :] = here
            lanes = slice(part * half, (part + 1) * half)
            packed[slot, :fold, lanes] = jnp.where(low_half, here[:, :half], here[:, half:])
        rest = packed.shape[1] - fold
        packed[slot, fold:, :] = jnp.broadcast_to(facts[slot : slot + 1, :], (rest, width)).astype(bf16)


def pack(meta, orbitals, facts, own):
    slots, coefficients, width = orbitals.shape
    fold = coefficients // 2
    padded = (fold // ROWS + 1) * ROWS
    vmem = pl.BlockSpec(memory_space=pltpu.VMEM)
    shapes = [jax.ShapeDtypeStruct((slots, padded, width), bf16)]
    shapes += [jax.ShapeDtypeStruct(orbitals.shape, bf16)] * own
    return pl.pallas_call(
        functools.partial(pack_kernel, own),
        out_shape=shapes,
        in_specs=[pl.BlockSpec(memory_space=pltpu.SMEM), vmem, vmem],
        out_specs=[vmem] * len(shapes),
        compiler_params=params(24),
        name="pack",
    )(meta, orbitals, facts)


def unfold_kernel(fold, meta, beside, rest, whole, top):
    slots, _, width = beside.shape
    half = width // PAIR
    first = meta[0] == 0
    for slot in range(slots):
        for part in range(2):
            lanes = slice(part * half, (part + 1) * half)
            near, far = beside[slot, :fold, lanes], rest[slot, :fold, lanes]
            start = (2 * slot + part) * fold
            here = jnp.concatenate([jnp.where(first, near, far), jnp.where(first, far, near)], axis=1)
            whole[start : start + fold, :] = here
    top[...] = whole[: top.shape[0], :]


def unfold(meta, beside, rest, fold, cut):
    slots, _, width = beside.shape
    vmem = pl.BlockSpec(memory_space=pltpu.VMEM)
    return pl.pallas_call(
        functools.partial(unfold_kernel, fold),
        out_shape=[
            jax.ShapeDtypeStruct((2 * slots * fold, width), bf16),
            jax.ShapeDtypeStruct((cut, width), bf16),
        ],
        in_specs=[pl.BlockSpec(memory_space=pltpu.SMEM), vmem, vmem],
        out_specs=[vmem, vmem],
        compiler_params=params(24),
        name="unfold",
    )(meta, beside, rest)


def load_left(lefts, held, sems):
    copies = []
    for q, pieces in enumerate(lefts):
        row = 0
        for piece in pieces:
            rows, width = piece.shape
            here = held.at[row : row + rows, q * width : (q + 1) * width]
            copies.append(pltpu.make_async_copy(piece, here, sems.at[len(copies)]))
            row += rows
    for copy in copies:
        copy.start()
    return copies


def grouped(refs, counts):
    refs = list(refs)
    return [[refs.pop(0) for _ in range(count)] for count in counts]


def correlation_kernel(share, counts, meta, *refs):
    refs, (out, held, turned, sems) = refs[:-4], refs[-4:]
    groups, half, width = out.shape
    lefts, before = grouped(refs, counts), refs[sum(counts) :]
    copies = load_left(lefts, held, sems)
    first = meta[0] == 0
    for copy in copies[: counts[0]]:
        copy.wait()
    own = held[:, :width]
    turned[...] = jnp.where(first, own[:, :half], own[:, half:]).T
    for copy in copies[counts[0] :]:
        copy.wait()
    for base in range(0, groups, 2):
        wide = matmul(turned[...], held[:, base * width : (base + 2) * width])
        for q in (base, base + 1):
            total = wide[:, (q - base) * width : (q - base + 1) * width]
            if before:
                total = total + before[0][q]
                if q == 0:
                    rows = lax.broadcasted_iota(jnp.int32, (half, width), 0) + jnp.where(first, 0, half)
                    columns = lax.broadcasted_iota(jnp.int32, (half, width), 1)
                    total = total - jnp.where(rows == columns, share, 0.0)
            out[q] = total.astype(out.dtype)


def box_correlation(share, meta, lefts, before, half):
    depth, width = sum(piece.shape[0] for piece in lefts[0]), lefts[0][0].shape[1]
    counts = [len(pieces) for pieces in lefts]
    vmem = pl.BlockSpec(memory_space=pltpu.VMEM)
    extra = [] if before is None else [before]
    return pl.pallas_call(
        functools.partial(correlation_kernel, share, counts),
        out_shape=jax.ShapeDtypeStruct((len(lefts), half, width), f32 if before is None else bf16),
        in_specs=[pl.BlockSpec(memory_space=pltpu.SMEM)]
        + [pl.BlockSpec(memory_space=pl.ANY)] * sum(counts)
        + [vmem] * len(extra),
        out_specs=vmem,
        scratch_shapes=[
            pltpu.VMEM((depth, len(lefts) * width), bf16),
            pltpu.VMEM((half, depth), bf16),
            pltpu.SemaphoreType.DMA((sum(counts),)),
        ],
        compiler_params=params(32),
        cost_estimate=pl.CostEstimate(
            flops=2 * len(lefts) * depth * width * half, bytes_accessed=2 * len(lefts) * depth * width, transcendentals=0
        ),
        name="correlation",
    )(meta, *[piece for pieces in lefts for piece in pieces], *extra)


def fock_kernel(side, counts, right, *refs):
    refs, (out, held, raw, turned, sems, last_sem) = refs[:-6], refs[-6:]
    lefts, before = grouped(refs, counts), refs[sum(counts) :]
    last = pltpu.make_async_copy(right.at[side], raw, last_sem)
    last.start()
    copies = load_left(lefts, held, sems)
    half, width = out.shape[-2] // (1 if before else 3), out.shape[-1]
    last.wait()
    turned[...] = raw[...].T
    for copy in copies:
        copy.wait()
    for base in range(0, len(lefts), 2):
        wide = matmul(turned[...], held[:, base * width : (base + 2) * width])
        for q in (base, base + 1):
            total = wide[:, (q - base) * width : (q - base + 1) * width]
            if before:
                total = total + before[0][q]
                main = total[:half] + total[half : 2 * half]
                top = main.astype(bf16)
                out[q, 0], out[q, 1] = top, (main - top.astype(f32)).astype(bf16)
                out[q, 2] = total[2 * half :].astype(bf16)
            else:
                out[q] = total


def box_fock(side, lefts, right, before):
    depth, width = sum(piece.shape[0] for piece in lefts[0]), lefts[0][0].shape[1]
    counts = [len(pieces) for pieces in lefts]
    tall = right.shape[-1]
    anywhere, vmem = pl.BlockSpec(memory_space=pl.ANY), pl.BlockSpec(memory_space=pltpu.VMEM)
    extra = [] if before is None else [before]
    out = ((len(lefts), tall, width), f32) if before is None else ((len(lefts), 3, tall // 3, width), bf16)
    return pl.pallas_call(
        functools.partial(fock_kernel, side, counts),
        out_shape=jax.ShapeDtypeStruct(*out),
        in_specs=[anywhere] * (sum(counts) + 1) + [vmem] * len(extra),
        out_specs=vmem,
        scratch_shapes=[
            pltpu.VMEM((depth, len(lefts) * width), bf16),
            pltpu.VMEM(right.shape[1:], bf16),
            pltpu.VMEM((tall, depth), bf16),
            pltpu.SemaphoreType.DMA((sum(counts),)),
            pltpu.SemaphoreType.DMA(()),
        ],
        compiler_params=params(40),
        cost_estimate=pl.CostEstimate(
            flops=2 * len(lefts) * depth * width * tall, bytes_accessed=2 * len(lefts) * depth * width, transcendentals=0
        ),
        name="fock",
    )(right, *[piece for pieces in lefts for piece in pieces], *extra)


def root_kernel(levels, meta, *refs):
    pieces, (offset, root, whole, rows_f, cols_b, sems) = refs[:-6], refs[-6:]
    level, pair, orb = meta[0], meta[1], meta[2]
    coarse, width = offset.shape
    side = whole.shape[0]
    groups = side // width
    copies = []
    for piece, (z, y, q) in zip(pieces, piece_places(levels, groups)):
        for i in range(len(z)):
            start = ((orb ^ q[i]) * PAIR + (pair ^ y[i])) * coarse
            rows = pl.ds(pl.multiple_of(start, coarse), coarse)
            lanes = pl.ds(pl.multiple_of((level ^ z[i]) * width, width), width)
            copies.append(
                pltpu.make_async_copy(
                    piece.at[i * coarse : (i + 1) * coarse], whole.at[rows, lanes], sems.at[len(copies)]
                )
            )
    for copy in copies:
        copy.start()
    for copy in copies:
        copy.wait()
    row0 = pl.multiple_of((level * PAIR + pair) * coarse, coarse)
    own_lanes = pl.ds(pl.multiple_of(orb * width, width), width)
    rows = whole[pl.ds(row0, coarse), :]

    def across(j, carry):
        lanes = pl.ds(pl.multiple_of(j * width, width), width)
        rows_f[:, lanes] = matmul(rows, whole[:, lanes])
        return carry

    lax.fori_loop(0, groups, across, 0)
    columns = whole[:, own_lanes]

    def down(i, carry):
        here = pl.ds(pl.multiple_of(i * coarse, coarse), coarse)
        square = matmul(whole[here, :], columns)
        cols_b[here, :] = (0.25 * (whole[here, own_lanes].astype(f32) - square)).astype(bf16)
        return carry

    lax.fori_loop(0, side // coarse, down, 0)
    left = (rows.astype(f32) - 0.25 * rows_f[...]).astype(bf16)
    value = matmul(left, cols_b[...]) + 0.125 * rows_f[:, own_lanes] - 0.5 * offset[...]
    row_ids = lax.broadcasted_iota(jnp.int32, value.shape, 0) + row0
    col_ids = lax.broadcasted_iota(jnp.int32, value.shape, 1) + orb * width
    root[...] = value + jnp.where(row_ids == col_ids, 1.0, 0.0)


def piece_places(levels, groups):
    places = []
    for core in (0, 1):
        for half in range(2):
            low = [half * levels // 2 + z for z in range(levels // 2)]
            for second in (0, 1):
                z, y, q = [], [], []
                for inner in (0, 1):
                    z += low
                    y += [second if half else inner] * len(low)
                    q += [2 * (inner if half else second) + core] * len(low)
                places.append((z, y, q))
    return places


def root_of(meta, pieces, offset, side, levels):
    coarse, width = offset.shape
    vmem, anywhere = pl.BlockSpec(memory_space=pltpu.VMEM), pl.BlockSpec(memory_space=pl.ANY)
    return pl.pallas_call(
        functools.partial(root_kernel, levels),
        out_shape=jax.ShapeDtypeStruct(offset.shape, f32),
        in_specs=[pl.BlockSpec(memory_space=pltpu.SMEM)] + [anywhere] * len(pieces) + [vmem],
        out_specs=vmem,
        scratch_shapes=[
            pltpu.VMEM((side, side), bf16),
            pltpu.VMEM((coarse, side), f32),
            pltpu.VMEM((side, width), bf16),
            pltpu.SemaphoreType.DMA((side // coarse * (side // width),)),
        ],
        compiler_params=params(40),
        cost_estimate=pl.CostEstimate(flops=4 * side * side * width, bytes_accessed=4 * side * side, transcendentals=0),
        name="root",
    )(meta, *pieces, offset)


def kinetic_kernel(edge, slots, table, scale, *refs):
    parts, (pot, fwd_in, fwd_out, back_in, back_mid, back_out), out = refs[:6], refs[6:12], refs[12]
    raw, x, outer, inner, total, total_fix, columns, sems = refs[13:]
    square = edge * edge
    own = PAIR * slots
    padded, width = x.shape[2:]
    copies = [pltpu.make_async_copy(part, raw.at[place], sems.at[place]) for place, part in enumerate(parts)]
    for copy in copies:
        copy.start()
    x[...] = jnp.zeros_like(x)
    total[...] = jnp.zeros_like(total)
    total_fix[...] = jnp.zeros_like(total_fix)
    columns[...] = pot[...].T
    for copy in copies:
        copy.wait()

    def lay_out(place, carry):
        for slot in range(slots):
            for i in range(edge):
                part, row = i // (edge // 2), i % (edge // 2) * square
                x[place * slots + slot, i, :square, :] = raw[
                    place, slot, row : row + square, part * width : (part + 1) * width
                ]
        return carry

    lax.fori_loop(0, len(parts), lay_out, 0)
    chunks = -(-square // ROWS)

    def per_slot(s, carry):
        @pl.when(table[s, 0] >= 0)
        def _():
            own_scale = scale[s]
            half = 0.5 * own_scale
            sums = (total, total_fix)

            def split(exact):
                exact = own_scale * exact
                value = exact.astype(bf16).astype(f32)
                return (half * value).astype(bf16), (half * (value - exact)).astype(bf16)

            sources = [[table[s, 1 + 3 * a + k] for k in range(3)] for a in range(3)]
            for i in range(chunks):
                rows = slice(i * ROWS, (i + 1) * ROWS)
                block = [x[t, :, rows, :].reshape(edge * ROWS, width) for t in sources[0]]
                fields = split(matmul(fwd_out[...], jnp.concatenate(block, axis=0)))
                for field in range(2):
                    outer[field, :, rows, :] = fields[field].reshape(edge, ROWS, width)
            for i in range(edge):
                for a in (1, 2):
                    block = jnp.concatenate([x[t, i] for t in sources[a]], axis=0)
                    fields = split(matmul(fwd_in[a - 1], block))
                    for field in range(2):
                        inner[field, i, (a - 1) * padded : a * padded, :] = fields[field]

            def back_outer(k, target):
                for i in range(chunks):
                    rows = slice(i * ROWS, (i + 1) * ROWS)
                    for field in range(2):
                        term = matmul(back_out[k], outer[field, :, rows, :].reshape(edge * ROWS, width))
                        sums[field][target, :, rows, :] += term.reshape(edge, ROWS, width)

            for k in (0, 2):
                for a in range(3):
                    target = sources[a][k]

                    @pl.when(target < own)
                    def _():
                        if a == 0:
                            back_outer(k, target)
                        else:
                            for i in range(edge):
                                for field in range(2):
                                    here = inner[field, i, (a - 1) * padded : a * padded, :]
                                    sums[field][target, i] += matmul(back_in[a - 1, k], here)

            here = sources[0][1]

            @pl.when(here < own)
            def _():
                back_outer(1, here)
                for i in range(edge):
                    for field in range(2):
                        sums[field][here, i] += matmul(back_mid[...], inner[field, i])

        return carry

    lax.fori_loop(0, table.shape[0], per_slot, 0)

    for t in range(own):
        for i in range(edge):
            rows = slice(i * square, (i + 1) * square)
            weighted = (columns[rows, t : t + 1] * x[t, i, :square, :].astype(f32)).astype(bf16)
            whole = total[t, i, :square, :] + weighted.astype(f32)
            top = whole.astype(bf16)
            low = (whole - top.astype(f32)).astype(bf16)
            fix = total_fix[t, i, :square, :].astype(bf16)
            out[t, rows, :] = jnp.concatenate([top, low, fix], axis=1)


def block_matrices(deriv_blocks):
    edge = deriv_blocks.shape[1]
    square = edge * edge
    padded = -(-square // ROWS) * ROWS
    ids = np.arange(padded)
    slow = ((ids[:, None] // edge) == np.arange(edge)).astype(np.float32)
    fast = (((ids[:, None] % edge) == np.arange(edge)) & (ids[:, None] < square)).astype(np.float32)
    ids = np.arange(edge * ROWS)
    outer = ((ids[:, None] // ROWS) == np.arange(edge)).astype(np.float32)
    within = ((ids[:, None] % ROWS) == np.arange(ROWS)).astype(np.float32)
    stacked = jnp.moveaxis(deriv_blocks, 0, 1).reshape(edge, 3 * edge)
    forward, backward = [], []
    for spot, mask in ((slow, fast), (fast, slow), (outer, within)):
        same = mask @ mask.T
        spread_out = np.kron(np.eye(3, dtype=np.float32), spot.T)
        spot_b, same_b = jnp.asarray(spot, bf16), jnp.asarray(same, f32)
        wide = matmul(matmul(spot_b, stacked).astype(bf16), jnp.asarray(spread_out, bf16))
        forward.append((wide * jnp.tile(same_b, (1, 3))).astype(bf16))
        turned = jnp.einsum("ri,kji->krj", spot_b, deriv_blocks, preferred_element_type=f32).astype(bf16)
        turned = jnp.einsum("krj,cj->krc", turned, spot_b, preferred_element_type=f32)
        backward.append((turned * same_b).astype(bf16))
    middle = jnp.concatenate([backward[0][1], backward[1][1]], axis=1)
    return jnp.stack(forward[:2]), forward[2], jnp.stack(backward[:2]), middle, backward[2]


def kinetic(parts, pot, matrices, table, scale, edge, coefficients):
    slots, folded, lanes = parts[0].shape
    width = lanes // 2
    padded = matrices[0].shape[1]
    own = PAIR * slots
    vmem = pl.BlockSpec(memory_space=pltpu.VMEM)
    smem = pl.BlockSpec(memory_space=pltpu.SMEM)
    anywhere = pl.BlockSpec(memory_space=pl.ANY)
    return pl.pallas_call(
        functools.partial(kinetic_kernel, edge, slots),
        out_shape=jax.ShapeDtypeStruct((own, coefficients, 3 * width), bf16),
        in_specs=[smem, smem] + [anywhere] * 6 + [vmem] * 6,
        out_specs=vmem,
        scratch_shapes=[
            pltpu.VMEM((6, slots, folded, lanes), bf16),
            pltpu.VMEM((6 * slots + 1, edge, padded, width), bf16),
            pltpu.VMEM((2, edge, padded, width), bf16),
            pltpu.VMEM((2, edge, 2 * padded, width), bf16),
            pltpu.VMEM((own, edge, padded, width), f32),
            pltpu.VMEM((own, edge, padded, width), f32),
            pltpu.VMEM(pot.shape[::-1], f32),
            pltpu.SemaphoreType.DMA((6,)),
        ],
        compiler_params=params(48),
        cost_estimate=pl.CostEstimate(flops=2 * 10**10, bytes_accessed=40 * 10**6, transcendentals=0),
        name="kinetic",
    )(table, scale, *parts, pot, *matrices)


def body(orbitals, potential, deriv_blocks, levels, box_counts, neighbours):
    slots, coefficients, own_width = orbitals.shape
    edge = deriv_blocks.shape[1]
    level, pair, orb = lax.axis_index("lvl"), lax.axis_index("pair"), lax.axis_index("orb")
    level_count, orb_count = lax.axis_size("lvl"), lax.axis_size("orb")
    half, fold = own_width // PAIR, coefficients // 2
    all_width = own_width * orb_count
    box_rows = all_width // (level_count * PAIR)
    first = pair == 0
    groups = range(orb_count)
    square_grid = level_count == orb_count == 4 and box_rows == half
    row0, col0 = (level * PAIR + pair) * box_rows, orb * own_width

    slot_ids = jnp.arange(slots, dtype=jnp.int32)
    own_ids = (level * PAIR + pair) * slots + slot_ids
    none = 16 * slots
    apart_ids = jnp.where(neighbours >= 0, neighbours - own_ids[:, None, None], none).reshape(slots, 6)
    live = (slot_ids < box_counts[0]).astype(jnp.int32)
    facts = jnp.concatenate([apart_ids, levels[:, None], live[:, None]], axis=1)
    wide_facts = jnp.pad(facts.astype(f32), ((0, 0), (0, own_width - facts.shape[1])))
    pack_meta = jnp.stack([pair, box_counts[0]]).astype(jnp.int32)
    [theirs] = pack(pack_meta, orbitals, wide_facts, False)
    pack_meta, theirs = lax.optimization_barrier((pack_meta, theirs))
    mine, active = pack(pack_meta, orbitals, wide_facts, True)

    far = {q: swap(active, "orb", q) for q in groups if q and q % 2 == 0}
    beside = swap(theirs, "pair", 1)
    first_mine, second_mine = trade(mine, "lvl", 0), trade(mine, "lvl", 1)
    near_active = swap(active, "orb", 1)
    later_pot, later_mine, beside = lax.optimization_barrier((potential, mine, beside))
    beside_rest = swap(later_mine, "pair", 1)
    first_beside, second_beside = trade(beside, "lvl", 0), trade(beside, "lvl", 1)

    def facts_of(packed):
        return packed[:, fold, : facts.shape[1]].astype(f32).astype(jnp.int32)

    side_facts = jnp.stack([facts_of(first_mine), facts_of(second_mine)])
    across_facts = swap(side_facts, "pair", 1)
    other_pot = swap(later_pot, "pair", 1)
    matrices = block_matrices(deriv_blocks)

    even = level % 2 == 0
    box_of_level = level * PAIR
    ids = jnp.concatenate(
        [
            own_ids,
            (box_of_level + 1 - pair) * slots + slot_ids,
            (box_of_level - 1) * slots + slot_ids,
            (box_of_level + PAIR) * slots + slot_ids,
        ]
    ).astype(jnp.int32)
    lower_own, lower_across = (jnp.where(even, both[1], both[0]) for both in (side_facts, across_facts))
    upper_own, upper_across = (jnp.where(even, both[0], both[1]) for both in (side_facts, across_facts))
    chosen = jnp.concatenate(
        [
            facts,
            facts_of(beside),
            jnp.where(first, lower_across, lower_own),
            jnp.where(first, upper_own, upper_across),
        ]
    )
    there = (ids >= 0) & (ids < level_count * PAIR * slots)

    def place(slot_id):
        box = slot_id // slots
        apart = box // PAIR - level
        base = jnp.where(apart == 0, 0, jnp.where((apart < 0) == even, 4, 2))
        return (base + (box % PAIR != pair)) * slots + slot_id % slots

    distance = chosen[:, :6]
    near = jnp.where(distance < none, place(jnp.maximum(ids, 0)[:, None] + distance), 6 * slots)
    near = jnp.clip(near, 0, 6 * slots)
    self_place = place(jnp.maximum(ids, 0))
    table = [jnp.where(there & (chosen[:, 7] > 0), self_place, -1)]
    for a in range(3):
        table += [near[:, 2 * a], self_place, near[:, 2 * a + 1]]
    table = jnp.stack(table, axis=1).astype(jnp.int32)
    level_of = chosen[:, 6]
    scale = jnp.where(level_of == 0, 0.5, jnp.where(level_of == 1, 1.0, 2.0)).astype(f32)
    pot = jnp.concatenate([potential, other_pot])
    pot = jnp.pad(pot, ((0, -pot.shape[0] % 8), (0, -pot.shape[1] % 128)))

    (far, near_active, beside, beside_rest, first_mine, second_mine, first_beside, second_beside, active, matrices) = (
        lax.optimization_barrier(
            (far, near_active, beside, beside_rest, first_mine, second_mine, first_beside, second_beside, active, matrices)
        )
    )
    table, scale, pot = lax.optimization_barrier((table, scale, pot))

    flat = lambda block: block.reshape(-1, block.shape[-1])
    cut = -(-slots * coefficients // (2 * ROWS)) * ROWS
    beside_all, beside_top = unfold(pack_meta, beside, beside_rest, fold, cut)
    cross = {q: [swap(beside_top, "orb", q), swap(flat(far[q])[cut:], "pair", 1)] for q in far}
    left_own = {0: active, 1: near_active, **far}
    left_beside = {0: [beside_all], 1: [swap(beside_all, "orb", 1)]}
    for q in far:
        left_own[q + 1] = swap(far[q], "orb", 1)

    def natural(blocks):
        return jnp.concatenate([lax.dynamic_index_in_dim(blocks, orb ^ j, keepdims=False) for j in groups], axis=1)

    def along_levels(blocks):
        mine_block = lambda target: lax.dynamic_index_in_dim(blocks, orb ^ target, keepdims=False)
        steps = range(1, level_count)
        return mine_block(level), [swap(mine_block(level ^ step), "lvl", step) for step in steps]

    def add(parts):
        own, got = parts
        return own.astype(f32) + sum(block.astype(f32) for block in got)

    def turned_rows(strip):
        pieces = []
        for over in range(PAIR):
            to_first = (pair ^ over) == 0
            piece = jnp.where(to_first, strip[:, :half], strip[:, half:])
            pieces.append((swap(piece, "pair", over) if over else piece).T)
        own, other = pieces
        return jnp.concatenate([jnp.where(first, own, other), jnp.where(first, other, own)], axis=1)

    def own_block(strip):
        strip = lax.all_gather(lax.psum(strip, "lvl"), ("orb", "pair"), axis=0, tiled=True)
        strip = lax.dynamic_slice_in_dim(strip, row0, box_rows, axis=0)
        return lax.dynamic_slice_in_dim(strip, col0, own_width, axis=1)

    meta = jnp.stack([pair, level, orb]).astype(jnp.int32)

    parts = [mine, beside, first_mine, first_beside, second_mine, second_beside]
    right = kinetic(parts, pot, matrices, table, scale, edge, coefficients)

    cross, right, meta = lax.optimization_barrier((cross, right, meta))
    lefts_own = [[flat(left_own[q])] for q in groups]
    lefts_beside = dict(left_beside)
    for q in far:
        lefts_beside[q] = list(cross[q])
        lefts_beside[q + 1] = [swap(piece, "orb", 1) for piece in cross[q]]
    lefts_beside = [lefts_beside[q] for q in groups]

    share = 1.0 / level_count
    blocks = box_correlation(share, meta, lefts_own, None, half)
    blocks = box_correlation(share, meta, lefts_beside, blocks, half)
    right = right.reshape(2, slots * coefficients, 3 * half)
    fock_part = box_fock(0, lefts_own, right, None)
    if square_grid:
        sent = along_levels(blocks)
        sent, fock_part = lax.optimization_barrier((sent, fock_part))
        offset_turned = add(sent)
        small = offset_turned.astype(bf16)
        offset = turned_rows(offset_turned)
    else:
        offset = own_block(natural(blocks).astype(f32))
    row_ids = row0 + jnp.arange(box_rows, dtype=jnp.int32)
    col_ids = col0 + jnp.arange(own_width, dtype=jnp.int32)
    correlation = offset + (row_ids[:, None] == col_ids[None, :]).astype(f32)
    fock_blocks = box_fock(1, lefts_beside, right, fock_part)
    if square_grid:
        pieces = [small] + [swap(small, "lvl", z) for z in range(1, level_count)]
        pieces, fock_blocks, offset = lax.optimization_barrier((pieces, fock_blocks, offset))
        join = functools.partial(jnp.concatenate, axis=0)
        top, low = join(pieces[: level_count // 2]), join(pieces[level_count // 2 :])
        sent = along_levels(fock_blocks)
        top, low = join([top, swap(top, "pair", 1)]), join([low, swap(low, "orb", 2)])
        pieces = [top, swap(top, "orb", 2), low, swap(low, "pair", 1)]
        pieces += [swap(piece, "orb", 1) for piece in pieces]
        root_meta = jnp.stack([level, pair, orb]).astype(jnp.int32)
        inverse_root = root_of(root_meta, pieces, offset, all_width, level_count)
        inverse_root, sent = lax.optimization_barrier((inverse_root, sent))
        sums = add(sent)
        main = turned_rows(sums[0] + sums[1])
        to = [
            ((z * PAIR + y) * orb_count + o, (o * PAIR + y) * orb_count + z)
            for z in range(level_count)
            for y in range(PAIR)
            for o in groups
        ]
        fock = main + lax.ppermute(sums[2].astype(bf16), BOX + ("orb",), to).astype(f32)
    else:
        main = natural(fock_blocks[:, 0]).astype(f32) + natural(fock_blocks[:, 1]).astype(f32)
        main = lax.all_gather(lax.psum(main, "lvl"), "pair", axis=0, tiled=True)
        fock = lax.dynamic_slice_in_dim(main, row0, box_rows, axis=1).T + own_block(natural(fock_blocks[:, 2]).astype(f32))
        gathered = lax.all_gather(offset.astype(bf16), "orb", axis=1, tiled=True)
        whole = lax.all_gather(gathered, BOX, axis=0, tiled=True)
        rows_of = lax.dynamic_slice_in_dim(whole, row0, box_rows, axis=0)
        cols_of = lax.dynamic_slice_in_dim(whole, col0, own_width, axis=1)
        row_square, col_square = matmul(rows_of, whole), matmul(whole, cols_of)
        left = (rows_of.astype(f32) - 0.25 * row_square).astype(bf16)
        right_side = (0.25 * (cols_of.astype(f32) - col_square)).astype(bf16)
        own_square = lax.dynamic_slice_in_dim(row_square, col0, own_width, axis=1)
        inverse_root = correlation - 1.5 * offset + 0.125 * own_square + matmul(left, right_side)
    return fock, correlation, inverse_root


def solution(mesh):
    levels = mesh.shape["box"] // PAIR
    split = Mesh(mesh.devices.reshape(levels, PAIR, mesh.shape["orb"]), ("lvl", "pair", "orb"))
    in_specs = (P(BOX, None, "orb"), P(BOX, None), P(), P(BOX), P(BOX), P(BOX, None, None))
    out_specs = (P(BOX, "orb"),) * 3
    return jax.shard_map(body, mesh=split, in_specs=in_specs, out_specs=out_specs, check_vma=False)
```

profile of v0, /device:TPU:2, one launch (start us, length us, event | category | flops | bytes accessed | tf_op | source)
XLA Modules:
  0.0 238.9 jit_solution(17217930441296880768)
XLA Ops:
  5.6 2.2 pack.2
  7.8 2.2 pack.3
  10.0 1.6 collective-permute-start.4
  11.7 1.5 collective-permute-start.5
  13.7 1.5 collective-permute-start.2
  17.4 1.5 tile.12
  19.9 1.7 tile.31
  21.6 1.9 copy.89
  23.6 1.8 fusion.4
  27.3 1.8 fusion.6
  29.1 1.8 fusion.7
  31.9 1.6 pad_maximum_fusion.6.refs_9_
  36.1 2.1 fusion.1.refs_8_
  38.2 3.6 %collective-permute-start.6 = (bf16[2,512,384]{2,1,0:T(8,128)(2,1)}, bf16[2,512,384]{2,1,0:T(8,128)(2,1)}, u32[]{:S(2)}, u32[]{:S(2)}) collective-permute-start(bf16[2,512,384]{2,1,0:T(8,128)(2,1)} %collective-permute-done.2.beside.refs_1_), channel_id=1, source_target_pairs={{0,8},{16,24},{8,0},{24,16},{1,9},{17,25},{9,1},{25,17},{2,10},{18... | collective-permute-start | bytes 2359304 | tf_op jit(solution)/shard_map/ppermute | solution.py:24
  41.8 1.5 collective-permute-start.7
  46.6 1.7 collective-permute-done.10
  50.4 1.8 collective-permute-done.11
  55.4 1.5 stack.65.table
  58.5 1.6 collective-permute-done.6.refs_3_
  60.1 10.3 %collective-permute-done.3.rest = bf16[2,512,384]{2,1,0:T(8,128)(2,1)} collective-permute-done((bf16[2,512,384]{2,1,0:T(8,128)(2,1)}, bf16[2,512,384]{2,1,0:T(8,128)(2,1)}, u32[]{:S(2)}, u32[]{:S(2)}) %collective-permute-start.3) | collective-permute-done | bytes 786464 | tf_op jit(solution)/shard_map/ppermute | solution.py:19
  70.4 3.0 %unfold.1 = (bf16[2000,384]{1,0:T(8,128)(2,1)}, bf16[1008,384]{1,0:T(8,128)(2,1)S(1)}) custom-call(s32[2]{0:T(128)S(1)} %pad_add_fusion.2.meta, bf16[2,512,384]{2,1,0:T(8,128)(2,1)} %collective-permute-done.2.beside.refs_1_, bf16[2,512,384]{2,1,0:T(8,128)(2,1)} %collective-permute-done.3.rest), custom_call_target="tpu_custom_call" | custom-call | tf_op jit(solution)/shard_map/unfold/pallas_call | solution.py:87
  73.5 1.5 collective-permute-start.8
  75.8 21.5 %kinetic.1 = bf16[4,1000,576]{2,1,0:T(8,128)(2,1)} custom-call(s32[8,10]{1,0:T(8,128)S(1)} %copy-done.10, f32[8]{0:T(128)S(1)} %select_reduce_fusion.scale, bf16[2,512,384]{2,1,0:T(8,128)(2,1)} %get-tuple-element.54.refs_0_, bf16[2,512,384]{2,1,0:T(8,128)(2,1)} %collective-permute-done.2.beside.refs_1_, bf16[2,512,384]{2,1,0:T(8,128)(2,1)} %collective-permute-done.4.refs_2_, ...), custom_call_target="tpu_custom_call" | custom-call | flops 20000000000 | bytes 40000000 | tf_op jit(solution)/shard_map/kinetic/pallas_call | solution.py:435
  97.9 4.0 %correlation.2.refs_6_ = f32[4,192,384]{2,1,0:T(8,128)S(1)} custom-call(s32[3]{0:T(128)S(1)} %add_add_fusion.3.meta, bf16[2000,384]{1,0:T(8,128)(2,1)S(1)} %bitcast.99, bf16[2000,384]{1,0:T(8,128)(2,1)} %bitcast.34.refs_1_, bf16[2000,384]{1,0:T(8,128)(2,1)S(1)} %bitcast.97, bf16[2000,384]{1,0:T(8,128)(2,1)} %bitcast.35.refs_3_), custom_call_target="tpu_custom_call" | custom-call | flops 1179648000 | bytes 6144000 | tf_op jit(solution)/shard_map/correlation/pallas_call | solution.py:149
  102.0 4.7 %correlation.3 = bf16[4,192,384]{2,1,0:T(8,128)(2,1)S(1)} custom-call(s32[3]{0:T(128)S(1)} %add_add_fusion.3.meta, bf16[2000,384]{1,0:T(8,128)(2,1)} %get-tuple-element.73.refs_0_, bf16[2000,384]{1,0:T(8,128)(2,1)} %collective-permute-done.12.refs_1_, bf16[1008,384]{1,0:T(8,128)(2,1)} %collective-permute-done.8.refs_2_, ...), custom_call_target="tpu_custom_call" | custom-call | flops 1179648000 | bytes 6144000 | tf_op jit(solution)/shard_map/correlation/pallas_call | solution.py:149
  108.3 8.9 %collective-permute-start.16 = (bf16[192,384]{0,1:T(8,128)(2,1)}, bf16[192,384]{0,1:T(8,128)(2,1)}, u32[]{:S(2)}, u32[]{:S(2)}) collective-permute-start(bf16[192,384]{0,1:T(8,128)(2,1)} %bitcast.37), channel_id=1, source_target_pairs={{0,8},{8,0},{16,24},{24,16},{1,9},{9,1},{17,25},{25,17},{2,10},{10... | collective-permute-start | bytes 442376 | tf_op jit(solution)/shard_map/ppermute | solution.py:19
  120.1 1.5 collective-permute-start.18
  124.3 6.6 %fock.2.refs_6_ = f32[4,576,384]{2,1,0:T(8,128)S(1)} custom-call(bf16[2,2000,576]{2,1,0:T(8,128)(2,1)} %bitcast.101, bf16[2000,384]{1,0:T(8,128)(2,1)S(1)} %bitcast.100, bf16[2000,384]{1,0:T(8,128)(2,1)} %bitcast.34.refs_1_, bf16[2000,384]{1,0:T(8,128)(2,1)S(1)} %bitcast.98, bf16[2000,384]{1,0:T(8,128)(2,1)} %bitcast.35.refs_3_), custom_call_target="tpu_custom_call" | custom-call | flops 3538944000 | bytes 6144000 | tf_op jit(solution)/shard_map/fock/pallas_call | solution.py:201
  131.0 1.7 copy.98
  132.7 2.8 %collective-permute-done.17 = bf16[192,384]{0,1:T(8,128)(2,1)} collective-permute-done((bf16[192,384]{0,1:T(8,128)(2,1)}, bf16[192,384]{0,1:T(8,128)(2,1)}, u32[]{:S(2)}, u32[]{:S(2)}) %collective-permute-start.17) | collective-permute-done | bytes 147488 | tf_op jit(solution)/shard_map/ppermute | solution.py:19
  136.8 3.9 %collective-permute-start.19 = (bf16[192,384]{0,1:T(8,128)(2,1)S(1)}, bf16[192,384]{0,1:T(8,128)(2,1)S(1)}, u32[]{:S(2)}, u32[]{:S(2)}) collective-permute-start(bf16[192,384]{0,1:T(8,128)(2,1)S(1)} %get-tuple-element.84), channel_id=1, source_target_pairs={{0,8},{8,0},{16,24},{24,16},{1,9},{9,1},{17,25},{25,17},{2,10},{10... | collective-permute-start | bytes 442376 | tf_op jit(solution)/shard_map/ppermute | solution.py:19
  143.4 1.6 collective-permute-start.22
  145.0 8.0 %fock.3 = bf16[4,3,192,384]{3,2,1,0:T(8,128)(2,1)S(1)} custom-call(bf16[2,2000,576]{2,1,0:T(8,128)(2,1)} %bitcast.102, bf16[2000,384]{1,0:T(8,128)(2,1)} %get-tuple-element.73.refs_0_, bf16[2000,384]{1,0:T(8,128)(2,1)} %collective-permute-done.12.refs_1_, bf16[1008,384]{1,0:T(8,128)(2,1)} %collective-permute-done.8.refs_2_, ...), custom_call_target="tpu_custom_call" | custom-call | flops 3538944000 | bytes 6144000 | tf_op jit(solution)/shard_map/fock/pallas_call | solution.py:201
  154.1 3.8 %collective-permute-done.20 = bf16[192,384]{0,1:T(8,128)(2,1)S(1)} collective-permute-done((bf16[192,384]{0,1:T(8,128)(2,1)S(1)}, bf16[192,384]{0,1:T(8,128)(2,1)S(1)}, u32[]{:S(2)}, u32[]{:S(2)}) %collective-permute-start.20) | collective-permute-done | bytes 147488 | tf_op jit(solution)/shard_map/ppermute | solution.py:19
  158.7 1.6 collective-permute-start.23
  160.3 5.0 %collective-permute-done.25 = bf16[384,384]{0,1:T(8,128)(2,1)S(1)} collective-permute-done((bf16[384,384]{0,1:T(8,128)(2,1)S(1)}, bf16[384,384]{0,1:T(8,128)(2,1)S(1)}, u32[]{:S(2)}, u32[]{:S(2)}) %collective-permute-start.25) | collective-permute-done | bytes 294944 | tf_op jit(solution)/shard_map/ppermute | solution.py:19
  165.5 2.7 %collective-permute-start.26 = (bf16[768,384]{0,1:T(8,128)(2,1)S(1)}, bf16[768,384]{0,1:T(8,128)(2,1)}, u32[]{:S(2)}, u32[]{:S(2)}) collective-permute-start(bf16[768,384]{0,1:T(8,128)(2,1)S(1)} %pad_maximum_fusion.1), channel_id=1, source_target_pairs={{0,4},{4,0},{1,5},{5,1},{2,6},{6,2},{3,7},{7,3},{8,12},{12,8},{9,1... | collective-permute-start | bytes 1769480 | tf_op jit(solution)/shard_map/ppermute | solution.py:19
  168.6 1.8 collective-permute-start.24
  170.9 7.4 %collective-permute-done.26 = bf16[768,384]{0,1:T(8,128)(2,1)} collective-permute-done((bf16[768,384]{0,1:T(8,128)(2,1)S(1)}, bf16[768,384]{0,1:T(8,128)(2,1)}, u32[]{:S(2)}, u32[]{:S(2)}) %collective-permute-start.26) | collective-permute-done | bytes 589856 | tf_op jit(solution)/shard_map/ppermute | solution.py:19
  180.0 2.9 %collective-permute-start.31 = (bf16[3,192,384]{2,1,0:T(8,128)(2,1)}, bf16[3,192,384]{2,1,0:T(8,128)(2,1)}, u32[]{:S(2)}, u32[]{:S(2)}) collective-permute-start(bf16[3,192,384]{2,1,0:T(8,128)(2,1)} %get-tuple-element.105), channel_id=1, source_target_pairs={{0,8},{8,0},{16,24},{24,16},{1,9},{9,1},{17,25},{25,17},{2,10},{10... | collective-permute-start | bytes 1327112 | tf_op jit(solution)/shard_map/ppermute | solution.py:19
  182.9 2.6 %collective-permute-start.32 = (bf16[3,192,384]{2,1,0:T(8,128)(2,1)}, bf16[3,192,384]{2,1,0:T(8,128)(2,1)}, u32[]{:S(2)}, u32[]{:S(2)}) collective-permute-start(bf16[3,192,384]{2,1,0:T(8,128)(2,1)} %get-tuple-element.104), channel_id=1, source_target_pairs={{0,16},{8,24},{16,0},{24,8},{1,17},{9,25},{17,1},{25,9},{2,18},{10... | collective-permute-start | bytes 1327112 | tf_op jit(solution)/shard_map/ppermute | solution.py:19
  193.0 2.1 copy.112.refs_7_
  195.1 2.2 copy.110.refs_5_
  200.3 8.4 %root.1 = f32[192,384]{1,0:T(8,128)} custom-call(s32[3]{0:T(128)S(1)} %add_add_fusion.2.meta, bf16[768,384]{1,0:T(8,128)(2,1)S(1)} %copy.105.refs_0_, bf16[768,384]{1,0:T(8,128)(2,1)S(1)} %copy.106.refs_1_, bf16[768,384]{1,0:T(8,128)(2,1)S(1)} %copy.107.refs_2_, bf16[768,384]{1,0:T(8,128)(2,1)S(1)} %copy.108.refs_3_, bf16[768,384]{1,0:T(8,128)(2,1)S(1)} %copy.109.refs_4_, ...), custom_call_target="tpu_custom_call" | custom-call | flops 3623878656 | bytes 9437184 | tf_op jit(solution)/shard_map/root/pallas_call | solution.py:286
  208.7 8.2 %collective-permute-done.33 = bf16[3,192,384]{2,1,0:T(8,128)(2,1)} collective-permute-done((bf16[3,192,384]{2,1,0:T(8,128)(2,1)}, bf16[3,192,384]{2,1,0:T(8,128)(2,1)}, u32[]{:S(2)}, u32[]{:S(2)}) %collective-permute-start.33) | collective-permute-done | bytes 442400 | tf_op jit(solution)/shard_map/ppermute | solution.py:19
  216.9 1.5 add_add_fusion
  219.5 13.7 %collective-permute-start.35 = (bf16[192,384]{1,0:T(8,128)(2,1)S(1)}, bf16[192,384]{1,0:T(8,128)(2,1)S(1)}, u32[]{:S(2)}, u32[]{:S(2)}) collective-permute-start(bf16[192,384]{1,0:T(8,128)(2,1)S(1)} %fusion.12), channel_id=1, source_target_pairs={{0,0},{1,8},{2,16},{3,24},{4,4},{5,12},{6,20},{7,28},{8,1},{9,9},{... | collective-permute-start | bytes 442376 | tf_op jit(solution)/shard_map/ppermute | solution.py:630
  233.7 4.4 %collective-permute-done.35 = bf16[192,384]{1,0:T(8,128)(2,1)S(1)} collective-permute-done((bf16[192,384]{1,0:T(8,128)(2,1)S(1)}, bf16[192,384]{1,0:T(8,128)(2,1)S(1)}, u32[]{:S(2)}, u32[]{:S(2)}) %collective-permute-start.35) | collective-permute-done | bytes 147488 | tf_op jit(solution)/shard_map/ppermute | solution.py:630
  (172 shorter events, 53.7 us)
Async XLA Ops:
  5.6 11.6 %copy-start.17 = (f32[112,112]{0,1:T(8,128)S(1)}, f32[112,112]{0,1:T(8,128)}, u32[]{:S(2)}) copy-start(f32[112,112]{0,1:T(8,128)} %constant.180) | copy-start | bytes 150532
  10.0 87.9 %copy-start.3 = (bf16[2,1000,384]{2,1,0:T(8,128)(2,1)}, bf16[2,1000,384]{2,1,0:T(8,128)(2,1)S(1)}, u32[]{:S(2)}) copy-start(bf16[2,1000,384]{2,1,0:T(8,128)(2,1)S(1)} %get-tuple-element.76) | copy-start | bytes 4608004
  10.0 13.6 %copy-start.19 = (bf16[112,10,1]{0,1,2:T(8,128)(2,1)S(1)}, bf16[112,10,1]{0,1,2:T(8,128)(2,1)}, u32[]{:S(2)}) copy-start(bf16[112,10,1]{0,1,2:T(8,128)(2,1)} %constant.182) | copy-start | bytes 6724
  10.0 15.4 %copy-start.16 = (f32[112,112]{1,0:T(8,128)S(1)}, f32[112,112]{1,0:T(8,128)}, u32[]{:S(2)}) copy-start(f32[112,112]{1,0:T(8,128)} %constant.165.clone) | copy-start | bytes 150532
  10.0 15.4 %copy-start.18 = (bf16[112,10,1]{0,1,2:T(8,128)(2,1)S(1)}, bf16[112,10,1]{0,1,2:T(8,128)(2,1)}, u32[]{:S(2)}) copy-start(bf16[112,10,1]{0,1,2:T(8,128)(2,1)} %constant.183) | copy-start | bytes 6724
  10.0 31.8 %collective-permute-start.4 = (bf16[2,512,384]{2,1,0:T(8,128)(2,1)}, bf16[2,512,384]{2,1,0:T(8,128)(2,1)}, u32[]{:S(2)}, u32[]{:S(2)}) collective-permute-start(bf16[2,512,384]{2,1,0:T(8,128)(2,1)} %get-tuple-element.54.refs_0_), channel_id=1, source_target_pairs={{0,8},{16,24},{8,0},{24,16},{1,9},{17,25},{9,1},{25,17},{2,10},{18... | collective-permute-start | bytes 2359304 | tf_op jit(solution)/shard_map/ppermute | solution.py:24
  11.7 32.4 %collective-permute-start.5 = (bf16[2,512,384]{2,1,0:T(8,128)(2,1)}, bf16[2,512,384]{2,1,0:T(8,128)(2,1)}, u32[]{:S(2)}, u32[]{:S(2)}) collective-permute-start(bf16[2,512,384]{2,1,0:T(8,128)(2,1)} %get-tuple-element.54.refs_0_), channel_id=1, source_target_pairs={{8,16},{16,8},{9,17},{17,9},{10,18},{18,10},{11,19},{19,11},{12,20... | collective-permute-start | bytes 2359304 | tf_op jit(solution)/shard_map/ppermute | solution.py:24
  13.2 45.3 %collective-permute-start = (bf16[2,1000,384]{2,1,0:T(8,128)(2,1)S(1)}, bf16[2,1000,384]{2,1,0:T(8,128)(2,1)S(1)}, u32[]{:S(2)}, u32[]{:S(2)}) collective-permute-start(bf16[2,1000,384]{2,1,0:T(8,128)(2,1)S(1)} %get-tuple-element.76), channel_id=1, source_target_pairs={{0,2},{1,3},{2,0},{3,1},{4,6},{5,7},{6,4},{7,5},{8,10},{9,11},{10,... | collective-permute-start | bytes 4608008 | tf_op jit(solution)/shard_map/ppermute | solution.py:19
  13.7 44.8 %collective-permute-start.1 = (bf16[2,1000,384]{2,1,0:T(8,128)(2,1)S(1)}, bf16[2,1000,384]{2,1,0:T(8,128)(2,1)}, u32[]{:S(2)}, u32[]{:S(2)}) collective-permute-start(bf16[2,1000,384]{2,1,0:T(8,128)(2,1)S(1)} %get-tuple-element.76), channel_id=1, source_target_pairs={{0,1},{1,0},{2,3},{3,2},{4,5},{5,4},{6,7},{7,6},{8,9},{9,8},{10,11... | collective-permute-start | bytes 4608008 | tf_op jit(solution)/shard_map/ppermute | solution.py:19
  13.7 24.5 %collective-permute-start.2 = (bf16[2,512,384]{2,1,0:T(8,128)(2,1)}, bf16[2,512,384]{2,1,0:T(8,128)(2,1)}, u32[]{:S(2)}, u32[]{:S(2)}) collective-permute-start(bf16[2,512,384]{2,1,0:T(8,128)(2,1)} %pack.2), channel_id=1, source_target_pairs={{0,4},{4,0},{1,5},{5,1},{2,6},{6,2},{3,7},{7,3},{8,12},{12,8},{9,1... | collective-permute-start | bytes 2359304 | tf_op jit(solution)/shard_map/ppermute | solution.py:19
  17.2 11.9 %copy-start.14 = (bf16[10,30]{1,0:T(8,128)(2,1)}, bf16[10,30]{1,0:T(8,128)(2,1)S(1)}, u32[]{:S(2)}) copy-start(bf16[10,30]{1,0:T(8,128)(2,1)S(1)} %reshape.376) | copy-start | bytes 1804
  17.3 11.7 %copy-start.22 = (bf16[112,10]{0,1:T(8,128)(2,1)S(1)}, bf16[112,10]{0,1:T(8,128)(2,1)}, u32[]{:S(2)}) copy-start(bf16[112,10]{0,1:T(8,128)(2,1)} %constant.161.clone) | copy-start | bytes 6724
  38.2 21.8 %collective-permute-start.6 = (bf16[2,512,384]{2,1,0:T(8,128)(2,1)}, bf16[2,512,384]{2,1,0:T(8,128)(2,1)}, u32[]{:S(2)}, u32[]{:S(2)}) collective-permute-start(bf16[2,512,384]{2,1,0:T(8,128)(2,1)} %collective-permute-done.2.beside.refs_1_), channel_id=1, source_target_pairs={{0,8},{16,24},{8,0},{24,16},{1,9},{17,25},{9,1},{25,17},{2,10},{18... | collective-permute-start | bytes 2359304 | tf_op jit(solution)/shard_map/ppermute | solution.py:24
  41.8 18.3 %collective-permute-start.7 = (bf16[2,512,384]{2,1,0:T(8,128)(2,1)}, bf16[2,512,384]{2,1,0:T(8,128)(2,1)}, u32[]{:S(2)}, u32[]{:S(2)}) collective-permute-start(bf16[2,512,384]{2,1,0:T(8,128)(2,1)} %collective-permute-done.2.beside.refs_1_), channel_id=1, source_target_pairs={{8,16},{16,8},{9,17},{17,9},{10,18},{18,10},{11,19},{19,11},{12,20... | collective-permute-start | bytes 2359304 | tf_op jit(solution)/shard_map/ppermute | solution.py:24
  44.8 3.6 %collective-permute-start.10 = (s32[2,2,8]{2,1,0:T(2,128)S(1)}, s32[2,2,8]{2,1,0:T(2,128)S(1)}, u32[]{:S(2)}, u32[]{:S(2)}) collective-permute-start(s32[2,2,8]{2,1,0:T(2,128)S(1)} %pad_add_fusion.1), channel_id=1, source_target_pairs={{0,4},{4,0},{1,5},{5,1},{2,6},{6,2},{3,7},{7,3},{8,12},{12,8},{9,1... | collective-permute-start | bytes 392 | tf_op jit(solution)/shard_map/ppermute | solution.py:19
  48.3 3.9 %collective-permute-start.11 = (f32[2,1000]{1,0:T(2,128)}, f32[2,1000]{1,0:T(2,128)S(1)}, u32[]{:S(2)}, u32[]{:S(2)}) collective-permute-start(f32[2,1000]{1,0:T(2,128)} %param.16), channel_id=1, source_target_pairs={{0,4},{4,0},{1,5},{5,1},{2,6},{6,2},{3,7},{7,3},{8,12},{12,8},{9,1... | collective-permute-start | bytes 24008 | tf_op jit(solution)/shard_map/ppermute | solution.py:19
  52.2 18.2 %collective-permute-start.3 = (bf16[2,512,384]{2,1,0:T(8,128)(2,1)}, bf16[2,512,384]{2,1,0:T(8,128)(2,1)}, u32[]{:S(2)}, u32[]{:S(2)}) collective-permute-start(bf16[2,512,384]{2,1,0:T(8,128)(2,1)} %get-tuple-element.54.refs_0_), channel_id=1, source_target_pairs={{0,4},{4,0},{1,5},{5,1},{2,6},{6,2},{3,7},{7,3},{8,12},{12,8},{9,1... | collective-permute-start | bytes 2359304 | tf_op jit(solution)/shard_map/ppermute | solution.py:19
  58.5 17.4 %copy-start.8 = (bf16[2,3,112,112]{3,2,1,0:T(8,128)(2,1)S(1)}, bf16[2,3,112,112]{3,2,1,0:T(8,128)(2,1)}, u32[]{:S(2)}) copy-start(bf16[2,3,112,112]{3,2,1,0:T(8,128)(2,1)} %pad_maximum_fusion.6.refs_9_) | copy-start | bytes 451588
  58.5 17.4 %copy-start.9 = (bf16[160,480]{1,0:T(8,128)(2,1)S(1)}, bf16[160,480]{1,0:T(8,128)(2,1)}, u32[]{:S(2)}) copy-start(bf16[160,480]{1,0:T(8,128)(2,1)} %fusion.1.refs_8_) | copy-start | bytes 460804
  58.5 17.4 %copy-start.10 = (s32[8,10]{1,0:T(8,128)S(1)}, s32[8,10]{1,0:T(8,128)}, u32[]{:S(2)}) copy-start(s32[8,10]{1,0:T(8,128)} %stack.65.table) | copy-start | bytes 964
  58.5 39.4 %copy-start = (bf16[2,1000,384]{2,1,0:T(8,128)(2,1)}, bf16[2,1000,384]{2,1,0:T(8,128)(2,1)S(1)}, u32[]{:S(2)}) copy-start(bf16[2,1000,384]{2,1,0:T(8,128)(2,1)S(1)} %collective-permute-done) | copy-start | bytes 4608004
  73.5 23.9 %collective-permute-start.8 = (bf16[1008,384]{1,0:T(8,128)(2,1)S(1)}, bf16[1008,384]{1,0:T(8,128)(2,1)}, u32[]{:S(2)}, u32[]{:S(2)}) collective-permute-start(bf16[1008,384]{1,0:T(8,128)(2,1)S(1)} %get-tuple-element.57), channel_id=1, source_target_pairs={{0,2},{1,3},{2,0},{3,1},{4,6},{5,7},{6,4},{7,5},{8,10},{9,11},{10,... | collective-permute-start | bytes 2322440 | tf_op jit(solution)/shard_map/ppermute | solution.py:19
  75.0 23.0 %collective-permute-start.15 = (bf16[2,1000,384]{2,1,0:T(8,128)(2,1)S(1)}, bf16[2,1000,384]{2,1,0:T(8,128)(2,1)}, u32[]{:S(2)}, u32[]{:S(2)}) collective-permute-start(bf16[2,1000,384]{2,1,0:T(8,128)(2,1)S(1)} %collective-permute-done), channel_id=1, source_target_pairs={{0,1},{1,0},{2,3},{3,2},{4,5},{5,4},{6,7},{7,6},{8,9},{9,8},{10,11... | collective-permute-start | bytes 4608008 | tf_op jit(solution)/shard_map/ppermute | solution.py:19
  75.0 22.3 %collective-permute-start.9 = (bf16[992,384]{1,0:T(8,128)(2,1)S(1)}, bf16[992,384]{1,0:T(8,128)(2,1)}, u32[]{:S(2)}, u32[]{:S(2)}) collective-permute-start(bf16[992,384]{1,0:T(8,128)(2,1)S(1)} %slice.101), channel_id=1, source_target_pairs={{0,4},{4,0},{1,5},{5,1},{2,6},{6,2},{3,7},{7,3},{8,12},{12,8},{9,1... | collective-permute-start | bytes 2285576 | tf_op jit(solution)/shard_map/ppermute | solution.py:19
  75.6 26.4 %collective-permute-start.12 = (bf16[2000,384]{1,0:T(8,128)(2,1)}, bf16[2000,384]{1,0:T(8,128)(2,1)}, u32[]{:S(2)}, u32[]{:S(2)}) collective-permute-start(bf16[2000,384]{1,0:T(8,128)(2,1)} %get-tuple-element.73.refs_0_), channel_id=1, source_target_pairs={{0,1},{1,0},{2,3},{3,2},{4,5},{5,4},{6,7},{7,6},{8,9},{9,8},{10,11... | collective-permute-start | bytes 4608008 | tf_op jit(solution)/shard_map/ppermute | solution.py:19
  97.3 4.7 %collective-permute-start.13 = (bf16[1008,384]{1,0:T(8,128)(2,1)}, bf16[1008,384]{1,0:T(8,128)(2,1)}, u32[]{:S(2)}, u32[]{:S(2)}) collective-permute-start(bf16[1008,384]{1,0:T(8,128)(2,1)} %collective-permute-done.8.refs_2_), channel_id=1, source_target_pairs={{0,1},{1,0},{2,3},{3,2},{4,5},{5,4},{6,7},{7,6},{8,9},{9,8},{10,11... | collective-permute-start | bytes 2322440 | tf_op jit(solution)/shard_map/ppermute | solution.py:19
  97.7 4.3 %collective-permute-start.14 = (bf16[992,384]{1,0:T(8,128)(2,1)}, bf16[992,384]{1,0:T(8,128)(2,1)}, u32[]{:S(2)}, u32[]{:S(2)}) collective-permute-start(bf16[992,384]{1,0:T(8,128)(2,1)} %collective-permute-done.9.refs_3_), channel_id=1, source_target_pairs={{0,1},{1,0},{2,3},{3,2},{4,5},{5,4},{6,7},{7,6},{8,9},{9,8},{10,11... | collective-permute-start | bytes 2285576 | tf_op jit(solution)/shard_map/ppermute | solution.py:19
  108.3 24.4 %collective-permute-start.16 = (bf16[192,384]{0,1:T(8,128)(2,1)}, bf16[192,384]{0,1:T(8,128)(2,1)}, u32[]{:S(2)}, u32[]{:S(2)}) collective-permute-start(bf16[192,384]{0,1:T(8,128)(2,1)} %bitcast.37), channel_id=1, source_target_pairs={{0,8},{8,0},{16,24},{24,16},{1,9},{9,1},{17,25},{25,17},{2,10},{10... | collective-permute-start | bytes 442376 | tf_op jit(solution)/shard_map/ppermute | solution.py:19
  118.1 17.5 %collective-permute-start.17 = (bf16[192,384]{0,1:T(8,128)(2,1)}, bf16[192,384]{0,1:T(8,128)(2,1)}, u32[]{:S(2)}, u32[]{:S(2)}) collective-permute-start(bf16[192,384]{0,1:T(8,128)(2,1)} %bitcast.38), channel_id=1, source_target_pairs={{0,16},{8,24},{16,0},{24,8},{1,17},{9,25},{17,1},{25,9},{2,18},{10... | collective-permute-start | bytes 442376 | tf_op jit(solution)/shard_map/ppermute | solution.py:19
  120.1 15.4 %collective-permute-start.18 = (bf16[192,384]{0,1:T(8,128)(2,1)}, bf16[192,384]{0,1:T(8,128)(2,1)}, u32[]{:S(2)}, u32[]{:S(2)}) collective-permute-start(bf16[192,384]{0,1:T(8,128)(2,1)} %bitcast.39), channel_id=1, source_target_pairs={{0,24},{8,16},{16,8},{24,0},{1,25},{9,17},{17,9},{25,1},{2,26},{10... | collective-permute-start | bytes 442376 | tf_op jit(solution)/shard_map/ppermute | solution.py:19
  136.8 17.2 %collective-permute-start.19 = (bf16[192,384]{0,1:T(8,128)(2,1)S(1)}, bf16[192,384]{0,1:T(8,128)(2,1)S(1)}, u32[]{:S(2)}, u32[]{:S(2)}) collective-permute-start(bf16[192,384]{0,1:T(8,128)(2,1)S(1)} %get-tuple-element.84), channel_id=1, source_target_pairs={{0,8},{8,0},{16,24},{24,16},{1,9},{9,1},{17,25},{25,17},{2,10},{10... | collective-permute-start | bytes 442376 | tf_op jit(solution)/shard_map/ppermute | solution.py:19
  140.7 17.2 %collective-permute-start.20 = (bf16[192,384]{0,1:T(8,128)(2,1)S(1)}, bf16[192,384]{0,1:T(8,128)(2,1)S(1)}, u32[]{:S(2)}, u32[]{:S(2)}) collective-permute-start(bf16[192,384]{0,1:T(8,128)(2,1)S(1)} %get-tuple-element.84), channel_id=1, source_target_pairs={{0,16},{8,24},{16,0},{24,8},{1,17},{9,25},{17,1},{25,9},{2,18},{10... | collective-permute-start | bytes 442376 | tf_op jit(solution)/shard_map/ppermute | solution.py:19
  142.0 15.9 %collective-permute-start.21 = (bf16[192,384]{0,1:T(8,128)(2,1)S(1)}, bf16[192,384]{0,1:T(8,128)(2,1)S(1)}, u32[]{:S(2)}, u32[]{:S(2)}) collective-permute-start(bf16[192,384]{0,1:T(8,128)(2,1)S(1)} %get-tuple-element.84), channel_id=1, source_target_pairs={{0,24},{8,16},{16,8},{24,0},{1,25},{9,17},{17,9},{25,1},{2,26},{10... | collective-permute-start | bytes 442376 | tf_op jit(solution)/shard_map/ppermute | solution.py:19
  143.4 9.6 %collective-permute-start.22 = (f32[192,192]{0,1:T(8,128)S(1)}, f32[192,192]{0,1:T(8,128)S(1)}, u32[]{:S(2)}, u32[]{:S(2)}) collective-permute-start(f32[192,192]{0,1:T(8,128)S(1)} %slice_select_fusion), channel_id=1, source_target_pairs={{0,4},{4,0},{1,5},{5,1},{2,6},{6,2},{3,7},{7,3},{8,12},{12,8},{9,1... | collective-permute-start | bytes 442376 | tf_op jit(solution)/shard_map/ppermute | solution.py:19
  158.0 7.3 %collective-permute-start.25 = (bf16[384,384]{0,1:T(8,128)(2,1)S(1)}, bf16[384,384]{0,1:T(8,128)(2,1)S(1)}, u32[]{:S(2)}, u32[]{:S(2)}) collective-permute-start(bf16[384,384]{0,1:T(8,128)(2,1)S(1)} %pad_maximum_fusion.4), channel_id=1, source_target_pairs={{0,2},{1,3},{2,0},{3,1},{4,6},{5,7},{6,4},{7,5},{8,10},{9,11},{10,... | collective-permute-start | bytes 884744 | tf_op jit(solution)/shard_map/ppermute | solution.py:19
  158.7 9.7 %collective-permute-start.23 = (bf16[384,384]{0,1:T(8,128)(2,1)S(1)}, bf16[384,384]{0,1:T(8,128)(2,1)S(1)}, u32[]{:S(2)}, u32[]{:S(2)}) collective-permute-start(bf16[384,384]{0,1:T(8,128)(2,1)S(1)} %pad_maximum_fusion.3), channel_id=1, source_target_pairs={{0,4},{4,0},{1,5},{5,1},{2,6},{6,2},{3,7},{7,3},{8,12},{12,8},{9,1... | collective-permute-start | bytes 884744 | tf_op jit(solution)/shard_map/ppermute | solution.py:19
  165.5 12.8 %collective-permute-start.26 = (bf16[768,384]{0,1:T(8,128)(2,1)S(1)}, bf16[768,384]{0,1:T(8,128)(2,1)}, u32[]{:S(2)}, u32[]{:S(2)}) collective-permute-start(bf16[768,384]{0,1:T(8,128)(2,1)S(1)} %pad_maximum_fusion.1), channel_id=1, source_target_pairs={{0,4},{4,0},{1,5},{5,1},{2,6},{6,2},{3,7},{7,3},{8,12},{12,8},{9,1... | collective-permute-start | bytes 1769480 | tf_op jit(solution)/shard_map/ppermute | solution.py:19
  168.6 10.1 %collective-permute-start.24 = (bf16[768,384]{0,1:T(8,128)(2,1)S(1)}, bf16[768,384]{0,1:T(8,128)(2,1)}, u32[]{:S(2)}, u32[]{:S(2)}) collective-permute-start(bf16[768,384]{0,1:T(8,128)(2,1)S(1)} %pad_maximum_fusion), channel_id=1, source_target_pairs={{0,2},{1,3},{2,0},{3,1},{4,6},{5,7},{6,4},{7,5},{8,10},{9,11},{10,... | collective-permute-start | bytes 1769480 | tf_op jit(solution)/shard_map/ppermute | solution.py:19
  170.4 12.6 %collective-permute-start.29 = (bf16[768,384]{0,1:T(8,128)(2,1)S(1)}, bf16[768,384]{0,1:T(8,128)(2,1)S(1)}, u32[]{:S(2)}, u32[]{:S(2)}) collective-permute-start(bf16[768,384]{0,1:T(8,128)(2,1)S(1)} %pad_maximum_fusion.1), channel_id=1, source_target_pairs={{0,1},{1,0},{2,3},{3,2},{4,5},{5,4},{6,7},{7,6},{8,9},{9,8},{10,11... | collective-permute-start | bytes 1769480 | tf_op jit(solution)/shard_map/ppermute | solution.py:19
  170.4 15.2 %collective-permute-start.27 = (bf16[768,384]{0,1:T(8,128)(2,1)S(1)}, bf16[768,384]{0,1:T(8,128)(2,1)S(1)}, u32[]{:S(2)}, u32[]{:S(2)}) collective-permute-start(bf16[768,384]{0,1:T(8,128)(2,1)S(1)} %pad_maximum_fusion), channel_id=1, source_target_pairs={{0,1},{1,0},{2,3},{3,2},{4,5},{5,4},{6,7},{7,6},{8,9},{9,8},{10,11... | collective-permute-start | bytes 1769480 | tf_op jit(solution)/shard_map/ppermute | solution.py:19
  178.3 14.7 %collective-permute-start.30 = (bf16[768,384]{0,1:T(8,128)(2,1)}, bf16[768,384]{0,1:T(8,128)(2,1)}, u32[]{:S(2)}, u32[]{:S(2)}) collective-permute-start(bf16[768,384]{0,1:T(8,128)(2,1)} %collective-permute-done.26), channel_id=1, source_target_pairs={{0,1},{1,0},{2,3},{3,2},{4,5},{5,4},{6,7},{7,6},{8,9},{9,8},{10,11... | collective-permute-start | bytes 1769480 | tf_op jit(solution)/shard_map/ppermute | solution.py:19
  178.6 16.4 %collective-permute-start.28 = (bf16[768,384]{0,1:T(8,128)(2,1)}, bf16[768,384]{0,1:T(8,128)(2,1)}, u32[]{:S(2)}, u32[]{:S(2)}) collective-permute-start(bf16[768,384]{0,1:T(8,128)(2,1)} %collective-permute-done.24), channel_id=1, source_target_pairs={{0,1},{1,0},{2,3},{3,2},{4,5},{5,4},{6,7},{7,6},{8,9},{9,8},{10,11... | collective-permute-start | bytes 1769480 | tf_op jit(solution)/shard_map/ppermute | solution.py:19
  180.0 28.7 %collective-permute-start.31 = (bf16[3,192,384]{2,1,0:T(8,128)(2,1)}, bf16[3,192,384]{2,1,0:T(8,128)(2,1)}, u32[]{:S(2)}, u32[]{:S(2)}) collective-permute-start(bf16[3,192,384]{2,1,0:T(8,128)(2,1)} %get-tuple-element.105), channel_id=1, source_target_pairs={{0,8},{8,0},{16,24},{24,16},{1,9},{9,1},{17,25},{25,17},{2,10},{10... | collective-permute-start | bytes 1327112 | tf_op jit(solution)/shard_map/ppermute | solution.py:19
  182.9 25.8 %collective-permute-start.32 = (bf16[3,192,384]{2,1,0:T(8,128)(2,1)}, bf16[3,192,384]{2,1,0:T(8,128)(2,1)}, u32[]{:S(2)}, u32[]{:S(2)}) collective-permute-start(bf16[3,192,384]{2,1,0:T(8,128)(2,1)} %get-tuple-element.104), channel_id=1, source_target_pairs={{0,16},{8,24},{16,0},{24,8},{1,17},{9,25},{17,1},{25,9},{2,18},{10... | collective-permute-start | bytes 1327112 | tf_op jit(solution)/shard_map/ppermute | solution.py:19
  186.4 30.5 %collective-permute-start.33 = (bf16[3,192,384]{2,1,0:T(8,128)(2,1)}, bf16[3,192,384]{2,1,0:T(8,128)(2,1)}, u32[]{:S(2)}, u32[]{:S(2)}) collective-permute-start(bf16[3,192,384]{2,1,0:T(8,128)(2,1)} %get-tuple-element.103), channel_id=1, source_target_pairs={{0,24},{8,16},{16,8},{24,0},{1,25},{9,17},{17,9},{25,1},{2,26},{10... | collective-permute-start | bytes 1327112 | tf_op jit(solution)/shard_map/ppermute | solution.py:19
  200.3 16.6 %copy-start.11 = (bf16[3,192,384]{2,1,0:T(8,128)(2,1)S(1)}, bf16[3,192,384]{2,1,0:T(8,128)(2,1)}, u32[]{:S(2)}) copy-start(bf16[3,192,384]{2,1,0:T(8,128)(2,1)} %get-tuple-element.90) | copy-start | bytes 1327108
  218.9 14.3 %collective-permute-start.34 = (f32[192,192]{0,1:T(8,128)S(1)}, f32[192,192]{0,1:T(8,128)S(1)}, u32[]{:S(2)}, u32[]{:S(2)}) collective-permute-start(f32[192,192]{0,1:T(8,128)S(1)} %broadcast_select_fusion), channel_id=1, source_target_pairs={{0,4},{4,0},{1,5},{5,1},{2,6},{6,2},{3,7},{7,3},{8,12},{12,8},{9,1... | collective-permute-start | bytes 442376 | tf_op jit(solution)/shard_map/ppermute | solution.py:19
  219.5 18.6 %collective-permute-start.35 = (bf16[192,384]{1,0:T(8,128)(2,1)S(1)}, bf16[192,384]{1,0:T(8,128)(2,1)S(1)}, u32[]{:S(2)}, u32[]{:S(2)}) collective-permute-start(bf16[192,384]{1,0:T(8,128)(2,1)S(1)} %fusion.12), channel_id=1, source_target_pairs={{0,0},{1,8},{2,16},{3,24},{4,4},{5,12},{6,20},{7,28},{8,1},{9,9},{... | collective-permute-start | bytes 442376 | tf_op jit(solution)/shard_map/ppermute | solution.py:630
  (14 other events, 30.9 us)
where the time goes:
time: 240 us; the launch traced here: 239 us
  starting transfers between devices  63.1 us (26%)
  Pallas kernels  60.7 us (25%)
  waiting for transfers between devices  47.7 us (20%)
  local copies, waits for them, and re-layouts  37 us (15%)
  other arithmetic  18.8 us (8%)
  matrix products  9.83 us (4%)
    ppermute x31, waiting for transfers between devices, swap(): return lax.ppermute(value, axis, [(i, i ^ bit) for i in range(count)])  41.7 us
    ppermute x31, starting transfers between devices, swap(): return lax.ppermute(value, axis, [(i, i ^ bit) for i in range(count)])  41.1 us
    pallas_call x1, Pallas kernels, kinetic(): pl.pallas_call(functools.partial(kinetic_kernel, edge, slots), out_shape=...  21.5 us
    pallas_call x2, Pallas kernels, box_fock(): pl.pallas_call(functools.partial(fock_kernel, side, counts), out_shape=ja...  14.6 us
    ppermute x1, starting transfers between devices, body(): lax.ppermute(sums[2].astype(bf16), BOX + ('orb',), to).astype(f32)  13.7 us
    unnamed x52, local copies, waits for them, and re-layouts  9.14 us
    ppermute x7, local copies, waits for them, and re-layouts, swap(): return lax.ppermute(value, axis, [(i, i ^ bit) for i in range(count)])  8.8 us
    pallas_call x2, Pallas kernels, box_correlation(): pl.pallas_call(functools.partial(correlation_kernel, share, counts), out_...  8.77 us
  transfers between devices with their start and end apart: 36, of which 12 were waited for; matrix products, arithmetic and copies ran while one was open for 20% of the time, Pallas kernels for 20%

commit v1 on v0

--- a/solution.py
+++ b/solution.py
@@ -300,9 +300,52 @@
     )(meta, *pieces, offset)
 
 
-def kinetic_kernel(edge, slots, table, scale, *refs):
-    parts, (pot, fwd_in, fwd_out, back_in, back_mid, back_out), out = refs[:6], refs[6:12], refs[12]
-    raw, x, outer, inner, total, total_fix, columns, sems = refs[13:]
+def fill_tables(slots, levels, place_meta, own_facts, beside_facts, side_facts, across_facts, table, scale):
+    level, pair = place_meta[0], place_meta[1]
+    even = lax.rem(level, 2) == 0
+    none = 6 * slots
+
+    def place(slot_id):
+        box = lax.div(slot_id, slots)
+        apart = lax.div(box, PAIR) - level
+        base = jnp.where(apart == 0, 0, jnp.where((apart < 0) == even, 4, 2))
+        return (base + jnp.where(lax.rem(box, PAIR) != pair, 1, 0)) * slots + lax.rem(slot_id, slots)
+
+    for index in range(4 * slots):
+        group, r = divmod(index, slots)
+
+        def fact(c):
+            if group < 2:
+                return (own_facts, beside_facts)[group][r, c]
+            swap_id = jnp.where(even, 1, 0) if group == 2 else jnp.where(even, 0, 1)
+            near_pair = 1 if group == 2 else 0
+            return jnp.where(pair == near_pair, side_facts[swap_id, r, c], across_facts[swap_id, r, c])
+
+        box = (
+            level * PAIR + pair,
+            level * PAIR + 1 - pair,
+            jnp.maximum(level * PAIR - 1, 0),
+            jnp.minimum((level + 1) * PAIR, levels * PAIR - 1),
+        )[group]
+        there = (True, True, level > 0, level < levels - 1)[group]
+        own_id = box * slots + r
+        own_place = place(own_id)
+        table[index, 0] = jnp.where((fact(7) > 0) & there, own_place, -1)
+        for a in range(3):
+            for k in (0, 2):
+                distance = fact(2 * a + k // 2)
+                target = place(jnp.maximum(own_id + distance, 0))
+                target = jnp.where(distance < 16 * slots, target, none)
+                table[index, 1 + 3 * a + k] = jnp.clip(target, 0, none)
+            table[index, 2 + 3 * a] = own_place
+        level_of = fact(6)
+        scale[index] = jnp.where(level_of == 0, 0.5, jnp.where(level_of == 1, 1.0, 2.0))
+
+
+def kinetic_kernel(edge, slots, levels, place_meta, own_facts, beside_facts, side_facts, across_facts, *refs):
+    parts, refs = refs[:6], refs[6:]
+    (own_pot, beside_pot, fwd_in, fwd_out, back_in, back_mid, back_out), out, refs = refs[:7], refs[7], refs[8:]
+    raw, x, outer, inner, total, total_fix, columns, table, scale, sems = refs
     square = edge * edge
     own = PAIR * slots
     padded, width = x.shape[2:]
@@ -312,7 +355,9 @@
     x[...] = jnp.zeros_like(x)
     total[...] = jnp.zeros_like(total)
     total_fix[...] = jnp.zeros_like(total_fix)
-    columns[...] = pot[...].T
+    columns[0] = own_pot[...].T
+    columns[1] = beside_pot[...].T
+    fill_tables(slots, levels, place_meta, own_facts, beside_facts, side_facts, across_facts, table, scale)
     for copy in copies:
         copy.wait()
 
@@ -391,7 +436,7 @@
     for t in range(own):
         for i in range(edge):
             rows = slice(i * square, (i + 1) * square)
-            weighted = (columns[rows, t : t + 1] * x[t, i, :square, :].astype(f32)).astype(bf16)
+            weighted = (columns[t // slots, rows, t % slots : t % slots + 1] * x[t, i, :square, :].astype(f32)).astype(bf16)
             whole = total[t, i, :square, :] + weighted.astype(f32)
             top = whole.astype(bf16)
             low = (whole - top.astype(f32)).astype(bf16)
@@ -399,32 +444,59 @@
             out[t, rows, :] = jnp.concatenate([top, low, fix], axis=1)
 
 
+def matrices_kernel(stacked, blocks, *refs):
+    spots, outs = refs[:9], refs[9:]
+    fwd_in, fwd_out, back_in, back_mid, back_out = outs
+    for mode in range(3):
+        spot, spread, same = spots[3 * mode : 3 * mode + 3]
+        wide = matmul(matmul(spot[...], stacked[...]).astype(bf16), spread[...])
+        wide = (wide * jnp.concatenate([same[...]] * 3, axis=1)).astype(bf16)
+        if mode == 2:
+            fwd_out[...] = wide
+        else:
+            fwd_in[mode] = wide
+        for k in range(3):
+            turned = lax.dot_general(spot[...], blocks[k], (((1,), (1,)), ((), ())), preferred_element_type=f32)
+            turned = lax.dot_general(
+                turned.astype(bf16), spot[...], (((1,), (1,)), ((), ())), preferred_element_type=f32
+            )
+            turned = (turned * same[...]).astype(bf16)
+            if mode == 2:
+                back_out[k] = turned
+            else:
+                back_in[mode, k] = turned
+    back_mid[...] = jnp.concatenate([back_in[0, 1], back_in[1, 1]], axis=1)
+
+
 def block_matrices(deriv_blocks):
     edge = deriv_blocks.shape[1]
     square = edge * edge
     padded = -(-square // ROWS) * ROWS
+    tall = edge * ROWS
     ids = np.arange(padded)
     slow = ((ids[:, None] // edge) == np.arange(edge)).astype(np.float32)
     fast = (((ids[:, None] % edge) == np.arange(edge)) & (ids[:, None] < square)).astype(np.float32)
-    ids = np.arange(edge * ROWS)
+    ids = np.arange(tall)
     outer = ((ids[:, None] // ROWS) == np.arange(edge)).astype(np.float32)
     within = ((ids[:, None] % ROWS) == np.arange(ROWS)).astype(np.float32)
     stacked = jnp.moveaxis(deriv_blocks, 0, 1).reshape(edge, 3 * edge)
-    forward, backward = [], []
+    constants = []
     for spot, mask in ((slow, fast), (fast, slow), (outer, within)):
-        same = mask @ mask.T
-        spread_out = np.kron(np.eye(3, dtype=np.float32), spot.T)
-        spot_b, same_b = jnp.asarray(spot, bf16), jnp.asarray(same, f32)
-        wide = matmul(matmul(spot_b, stacked).astype(bf16), jnp.asarray(spread_out, bf16))
-        forward.append((wide * jnp.tile(same_b, (1, 3))).astype(bf16))
-        turned = jnp.einsum("ri,kji->krj", spot_b, deriv_blocks, preferred_element_type=f32).astype(bf16)
-        turned = jnp.einsum("krj,cj->krc", turned, spot_b, preferred_element_type=f32)
-        backward.append((turned * same_b).astype(bf16))
-    middle = jnp.concatenate([backward[0][1], backward[1][1]], axis=1)
-    return jnp.stack(forward[:2]), forward[2], jnp.stack(backward[:2]), middle, backward[2]
-
-
-def kinetic(parts, pot, matrices, table, scale, edge, coefficients):
+        spread = np.kron(np.eye(3, dtype=np.float32), spot.T)
+        constants += [jnp.asarray(spot, bf16), jnp.asarray(spread, bf16), jnp.asarray(mask @ mask.T, f32)]
+    vmem = pl.BlockSpec(memory_space=pltpu.VMEM)
+    shapes = [(2, padded, 3 * padded), (tall, 3 * tall), (2, 3, padded, padded), (padded, 2 * padded), (3, tall, tall)]
+    return pl.pallas_call(
+        matrices_kernel,
+        out_shape=[jax.ShapeDtypeStruct(shape, bf16) for shape in shapes],
+        in_specs=[vmem] * 11,
+        out_specs=[vmem] * 5,
+        compiler_params=params(24),
+        name="matrices",
+    )(stacked, deriv_blocks, *constants)
+
+
+def kinetic(parts, place_meta, all_facts, pots, matrices, edge, coefficients, levels):
     slots, folded, lanes = parts[0].shape
     width = lanes // 2
     padded = matrices[0].shape[1]
@@ -433,9 +505,9 @@
     smem = pl.BlockSpec(memory_space=pltpu.SMEM)
     anywhere = pl.BlockSpec(memory_space=pl.ANY)
     return pl.pallas_call(
-        functools.partial(kinetic_kernel, edge, slots),
+        functools.partial(kinetic_kernel, edge, slots, levels),
         out_shape=jax.ShapeDtypeStruct((own, coefficients, 3 * width), bf16),
-        in_specs=[smem, smem] + [anywhere] * 6 + [vmem] * 6,
+        in_specs=[smem] * 5 + [anywhere] * 6 + [vmem] * 7,
         out_specs=vmem,
         scratch_shapes=[
             pltpu.VMEM((6, slots, folded, lanes), bf16),
@@ -444,13 +516,59 @@
             pltpu.VMEM((2, edge, 2 * padded, width), bf16),
             pltpu.VMEM((own, edge, padded, width), f32),
             pltpu.VMEM((own, edge, padded, width), f32),
-            pltpu.VMEM(pot.shape[::-1], f32),
+            pltpu.VMEM((2,) + pots[0].shape[::-1], f32),
+            pltpu.SMEM((4 * slots, 10), jnp.int32),
+            pltpu.SMEM((4 * slots,), f32),
             pltpu.SemaphoreType.DMA((6,)),
         ],
         compiler_params=params(48),
         cost_estimate=pl.CostEstimate(flops=2 * 10**10, bytes_accessed=40 * 10**6, transcendentals=0),
         name="kinetic",
-    )(table, scale, *parts, pot, *matrices)
+    )(place_meta, *all_facts, *parts, *pots, *matrices)
+
+
+def offset_sum_kernel(meta, *refs):
+    blocks, (small, kept, sent) = refs[:-3], refs[-3:]
+    total = blocks[0][...].astype(f32)
+    for block in blocks[1:]:
+        total = total + block[...].astype(f32)
+    small[...] = total.astype(bf16)
+    half = kept.shape[0]
+    first = meta[0] == 0
+    low, high = total[:, :half].T, total[:, half:].T
+    kept[...] = jnp.where(first, low, high)
+    sent[...] = jnp.where(first, high, low)
+
+
+def fock_sum_kernel(meta, *refs):
+    blocks, (share, kept, sent) = refs[:-3], refs[-3:]
+    parts = []
+    for part in range(3):
+        total = blocks[0][part].astype(f32)
+        for block in blocks[1:]:
+            total = total + block[part].astype(f32)
+        parts.append(total)
+    main = parts[0] + parts[1]
+    share[...] = parts[2].astype(bf16)
+    half = kept.shape[0]
+    first = meta[0] == 0
+    low, high = main[:, :half].T, main[:, half:].T
+    kept[...] = jnp.where(first, low, high)
+    sent[...] = jnp.where(first, high, low)
+
+
+def level_sum(kernel, meta, blocks):
+    tall, width = blocks[0].shape[-2:]
+    vmem = pl.BlockSpec(memory_space=pltpu.VMEM)
+    turned = jax.ShapeDtypeStruct((width // PAIR, tall), f32)
+    return pl.pallas_call(
+        kernel,
+        out_shape=[jax.ShapeDtypeStruct((tall, width), bf16), turned, turned],
+        in_specs=[pl.BlockSpec(memory_space=pltpu.SMEM)] + [vmem] * len(blocks),
+        out_specs=[vmem] * 3,
+        compiler_params=params(24),
+        name="level_sum",
+    )(meta, *blocks)
 
 
 def body(orbitals, potential, deriv_blocks, levels, box_counts, neighbours):
@@ -473,6 +591,8 @@
     live = (slot_ids < box_counts[0]).astype(jnp.int32)
     facts = jnp.concatenate([apart_ids, levels[:, None], live[:, None]], axis=1)
     wide_facts = jnp.pad(facts.astype(f32), ((0, 0), (0, own_width - facts.shape[1])))
+    own_pot = jnp.pad(potential, ((0, -slots % 8), (0, -coefficients % 128)))
+    beside_pot = swap(own_pot, "pair", 1)
     pack_meta = jnp.stack([pair, box_counts[0]]).astype(jnp.int32)
     [theirs] = pack(pack_meta, orbitals, wide_facts, False)
     pack_meta, theirs = lax.optimization_barrier((pack_meta, theirs))
@@ -481,9 +601,7 @@
     far = {q: swap(active, "orb", q) for q in groups if q and q % 2 == 0}
     beside = swap(theirs, "pair", 1)
     first_mine, second_mine = trade(mine, "lvl", 0), trade(mine, "lvl", 1)
-    near_active = swap(active, "orb", 1)
-    later_pot, later_mine, beside = lax.optimization_barrier((potential, mine, beside))
-    beside_rest = swap(later_mine, "pair", 1)
+    beside_rest = swap(mine, "pair", 1)
     first_beside, second_beside = trade(beside, "lvl", 0), trade(beside, "lvl", 1)
 
     def facts_of(packed):
@@ -491,62 +609,26 @@
 
     side_facts = jnp.stack([facts_of(first_mine), facts_of(second_mine)])
     across_facts = swap(side_facts, "pair", 1)
-    other_pot = swap(later_pot, "pair", 1)
     matrices = block_matrices(deriv_blocks)
 
-    even = level % 2 == 0
-    box_of_level = level * PAIR
-    ids = jnp.concatenate(
-        [
-            own_ids,
-            (box_of_level + 1 - pair) * slots + slot_ids,
-            (box_of_level - 1) * slots + slot_ids,
-            (box_of_level + PAIR) * slots + slot_ids,
-        ]
-    ).astype(jnp.int32)
-    lower_own, lower_across = (jnp.where(even, both[1], both[0]) for both in (side_facts, across_facts))
-    upper_own, upper_across = (jnp.where(even, both[0], both[1]) for both in (side_facts, across_facts))
-    chosen = jnp.concatenate(
-        [
-            facts,
-            facts_of(beside),
-            jnp.where(first, lower_across, lower_own),
-            jnp.where(first, upper_own, upper_across),
-        ]
-    )
-    there = (ids >= 0) & (ids < level_count * PAIR * slots)
-
-    def place(slot_id):
-        box = slot_id // slots
-        apart = box // PAIR - level
-        base = jnp.where(apart == 0, 0, jnp.where((apart < 0) == even, 4, 2))
-        return (base + (box % PAIR != pair)) * slots + slot_id % slots
-
-    distance = chosen[:, :6]
-    near = jnp.where(distance < none, place(jnp.maximum(ids, 0)[:, None] + distance), 6 * slots)
-    near = jnp.clip(near, 0, 6 * slots)
-    self_place = place(jnp.maximum(ids, 0))
-    table = [jnp.where(there & (chosen[:, 7] > 0), self_place, -1)]
-    for a in range(3):
-        table += [near[:, 2 * a], self_place, near[:, 2 * a + 1]]
-    table = jnp.stack(table, axis=1).astype(jnp.int32)
-    level_of = chosen[:, 6]
-    scale = jnp.where(level_of == 0, 0.5, jnp.where(level_of == 1, 1.0, 2.0)).astype(f32)
-    pot = jnp.concatenate([potential, other_pot])
-    pot = jnp.pad(pot, ((0, -pot.shape[0] % 8), (0, -pot.shape[1] % 128)))
-
-    (far, near_active, beside, beside_rest, first_mine, second_mine, first_beside, second_beside, active, matrices) = (
-        lax.optimization_barrier(
-            (far, near_active, beside, beside_rest, first_mine, second_mine, first_beside, second_beside, active, matrices)
+    far, active, parts, beside_rest, matrices, all_facts, pots = lax.optimization_barrier(
+        (
+            far,
+            active,
+            [mine, beside, first_mine, first_beside, second_mine, second_beside],
+            beside_rest,
+            matrices,
+            [facts, facts_of(beside), side_facts, across_facts],
+            [own_pot, beside_pot],
         )
     )
-    table, scale, pot = lax.optimization_barrier((table, scale, pot))
+    beside = parts[1]
 
     flat = lambda block: block.reshape(-1, block.shape[-1])
     cut = -(-slots * coefficients // (2 * ROWS)) * ROWS
     beside_all, beside_top = unfold(pack_meta, beside, beside_rest, fold, cut)
     cross = {q: [swap(beside_top, "orb", q), swap(flat(far[q])[cut:], "pair", 1)] for q in far}
-    left_own = {0: active, 1: near_active, **far}
+    left_own = {0: active, 1: swap(active, "orb", 1), **far}
     left_beside = {0: [beside_all], 1: [swap(beside_all, "orb", 1)]}
     for q in far:
         left_own[q + 1] = swap(far[q], "orb", 1)
@@ -557,20 +639,11 @@
     def along_levels(blocks):
         mine_block = lambda target: lax.dynamic_index_in_dim(blocks, orb ^ target, keepdims=False)
         steps = range(1, level_count)
-        return mine_block(level), [swap(mine_block(level ^ step), "lvl", step) for step in steps]
-
-    def add(parts):
-        own, got = parts
-        return own.astype(f32) + sum(block.astype(f32) for block in got)
-
-    def turned_rows(strip):
-        pieces = []
-        for over in range(PAIR):
-            to_first = (pair ^ over) == 0
-            piece = jnp.where(to_first, strip[:, :half], strip[:, half:])
-            pieces.append((swap(piece, "pair", over) if over else piece).T)
-        own, other = pieces
-        return jnp.concatenate([jnp.where(first, own, other), jnp.where(first, other, own)], axis=1)
+        return [mine_block(level)] + [swap(mine_block(level ^ step), "lvl", step) for step in steps]
+
+    def both_halves(kept, sent):
+        got = swap(sent, "pair", 1)
+        return jnp.concatenate([jnp.where(first, kept, got), jnp.where(first, got, kept)], axis=1)
 
     def own_block(strip):
         strip = lax.all_gather(lax.psum(strip, "lvl"), ("orb", "pair"), axis=0, tiled=True)
@@ -579,8 +652,8 @@
 
     meta = jnp.stack([pair, level, orb]).astype(jnp.int32)
 
-    parts = [mine, beside, first_mine, first_beside, second_mine, second_beside]
-    right = kinetic(parts, pot, matrices, table, scale, edge, coefficients)
+    place_meta = jnp.stack([level, pair]).astype(jnp.int32)
+    right = kinetic(parts, place_meta, all_facts, pots, matrices, edge, coefficients, level_count)
 
     cross, right, meta = lax.optimization_barrier((cross, right, meta))
     lefts_own = [[flat(left_own[q])] for q in groups]
@@ -598,9 +671,8 @@
     if square_grid:
         sent = along_levels(blocks)
         sent, fock_part = lax.optimization_barrier((sent, fock_part))
-        offset_turned = add(sent)
-        small = offset_turned.astype(bf16)
-        offset = turned_rows(offset_turned)
+        small, kept, other = level_sum(offset_sum_kernel, meta, sent)
+        offset = both_halves(kept, other)
     else:
         offset = own_block(natural(blocks).astype(f32))
     row_ids = row0 + jnp.arange(box_rows, dtype=jnp.int32)
@@ -615,19 +687,18 @@
         sent = along_levels(fock_blocks)
         top, low = join([top, swap(top, "pair", 1)]), join([low, swap(low, "orb", 2)])
         pieces = [top, swap(top, "orb", 2), low, swap(low, "pair", 1)]
+        pieces, sent = lax.optimization_barrier((pieces, sent))
         pieces += [swap(piece, "orb", 1) for piece in pieces]
         root_meta = jnp.stack([level, pair, orb]).astype(jnp.int32)
         inverse_root = root_of(root_meta, pieces, offset, all_width, level_count)
-        inverse_root, sent = lax.optimization_barrier((inverse_root, sent))
-        sums = add(sent)
-        main = turned_rows(sums[0] + sums[1])
+        share, kept, other = level_sum(fock_sum_kernel, meta, sent)
         to = [
             ((z * PAIR + y) * orb_count + o, (o * PAIR + y) * orb_count + z)
             for z in range(level_count)
             for y in range(PAIR)
             for o in groups
         ]
-        fock = main + lax.ppermute(sums[2].astype(bf16), BOX + ("orb",), to).astype(f32)
+        fock = both_halves(kept, other) + lax.ppermute(share, BOX + ("orb",), to).astype(f32)
     else:
         main = natural(fock_blocks[:, 0]).astype(f32) + natural(fock_blocks[:, 1]).astype(f32)
         main = lax.all_gather(lax.psum(main, "lvl"), "pair", axis=0, tiled=True)

time: 240 us -> 206 us (0.86)
  local copies, waits for them, and re-layouts: 37 us -> 5.1 us
  waiting for transfers between devices: 47.7 us -> 68.3 us
  other arithmetic: 18.8 us -> 6.09 us
  matrix products: 9.83 us -> 0 us
    ppermute x31, waiting for transfers between devices: 41.7 us -> 62.5 us  [swap(): return lax.ppermute(value, axis, [(i, i ^ bit) for i in range(count)])]
    dot_general x6 -> x0, matrix products: 9.83 us -> none  [the longest x3 5.66 us: matmul(): return jnp.dot(left, right, preferred_element_type=f32)]
    ppermute x7 -> x0, local copies, waits for them, and re-layouts: 8.8 us -> none  [swap(): return lax.ppermute(value, axis, [(i, i ^ bit) for i in range(count)])]
    another operation x7 -> x0, local copies, waits for them, and re-layouts: 7.81 us -> none  [the longest x6 6.35 us: block_matrices(): forward.append((wide * jnp.tile(same_b, (1, 3))).astype(bf16))]
    unnamed x52 -> x29, local copies, waits for them, and re-layouts: 9.14 us -> 2.25 us
    ppermute x31, starting transfers between devices: 41.1 us -> 46.7 us  [swap(): return lax.ppermute(value, axis, [(i, i ^ bit) for i in range(count)])]
    dynamic_slice x5 -> x0, local copies, waits for them, and re-layouts: 4.92 us -> none  [along_levels(): lax.dynamic_index_in_dim(blocks, orb ^ target, keepdims=False)]
    select_n x9 -> x2, other arithmetic: 3.13 us -> 0.06 us  [both_halves(): jnp.where(first, kept, got)]
  transfers between devices with their start and end apart: 36 -> 36, of which waited for: 12 -> 10; matrix products, arithmetic and copies ran while one was open for 20% -> 4% of each run, Pallas kernels for 20% -> 19%
where the time goes in v1:
time: 206 us
  waiting for transfers between devices  68.3 us (33%)
  starting transfers between devices  64.5 us (31%)
  Pallas kernels  59.8 us (29%)
  other arithmetic  6.09 us (3%)
  local copies, waits for them, and re-layouts  5.1 us (2%)
    ppermute x31, waiting for transfers between devices, swap(): return lax.ppermute(value, axis, [(i, i ^ bit) for i in range(count)])  62.5 us
    ppermute x31, starting transfers between devices, swap(): return lax.ppermute(value, axis, [(i, i ^ bit) for i in range(count)])  46.7 us
    pallas_call x1, Pallas kernels, kinetic(): pl.pallas_call(functools.partial(kinetic_kernel, edge, slots, levels), ou...  17.8 us
    pallas_call x2, Pallas kernels, box_fock(): pl.pallas_call(functools.partial(fock_kernel, side, counts), out_shape=ja...  14.7 us
    ppermute x1, starting transfers between devices, body(): lax.ppermute(share, BOX + ('orb',), to).astype(f32)  11.5 us
    pallas_call x2, Pallas kernels, box_correlation(): pl.pallas_call(functools.partial(correlation_kernel, share, counts), out_...  8.8 us
    pallas_call x1, Pallas kernels, root_of(): pl.pallas_call(functools.partial(root_kernel, levels), out_shape=jax.Shap...  8.34 us
    ppermute x4, starting transfers between devices, trade(): return lax.ppermute(value, axis, pairs + [(b, a) for a, b in pairs])  6.25 us
  transfers between devices with their start and end apart: 36, of which 10 were waited for; matrix products, arithmetic and copies ran while one was open for 4% of the time, Pallas kernels for 19%

profile of v1, /device:TPU:2, one launch (start us, length us, event | category | flops | bytes accessed | tf_op | source)
XLA Modules:
  0.0 205.7 jit_solution(11269802528633483423)
XLA Ops:
  3.7 1.4 copy-done
  5.2 2.2 %pack.2 = bf16[2,512,384]{2,1,0:T(8,128)(2,1)} custom-call(s32[2]{0:T(128)S(1)} %pad_add_fusion.2.meta, bf16[2,1000,384]{2,1,0:T(8,128)(2,1)S(1)} %copy-done, f32[2,384]{1,0:T(2,128)S(1)} %pad.8.facts), custom_call_target="tpu_custom_call" | custom-call | tf_op jit(solution)/shard_map/pack/pallas_call | solution.py:60
  7.4 1.5 collective-permute-start.1
  8.9 2.3 %pack.3 = (bf16[2,512,384]{2,1,0:T(8,128)(2,1)}, bf16[2,1000,384]{2,1,0:T(8,128)(2,1)S(1)}) custom-call(s32[2]{0:T(128)S(1)} %pad_add_fusion.2.meta, bf16[2,1000,384]{2,1,0:T(8,128)(2,1)S(1)} %copy-done, f32[2,384]{1,0:T(2,128)S(1)} %pad.8.facts), custom_call_target="tpu_custom_call" | custom-call | tf_op jit(solution)/shard_map/pack/pallas_call | solution.py:60
  11.2 1.6 collective-permute-start.2
  13.3 1.6 collective-permute-start.4
  15.9 12.2 %collective-permute-done.1.beside.refs_1_ = bf16[2,512,384]{2,1,0:T(8,128)(2,1)} collective-permute-done((bf16[2,512,384]{2,1,0:T(8,128)(2,1)}, bf16[2,512,384]{2,1,0:T(8,128)(2,1)}, u32[]{:S(2)}, u32[]{:S(2)}) %collective-permute-start.1) | collective-permute-done | bytes 786464 | tf_op jit(solution)/shard_map/ppermute | solution.py:19
  28.1 1.6 collective-permute-start.3
  29.7 2.2 %collective-permute-done.2.refs_2_ = bf16[2,512,384]{2,1,0:T(8,128)(2,1)} collective-permute-done((bf16[2,512,384]{2,1,0:T(8,128)(2,1)}, bf16[2,512,384]{2,1,0:T(8,128)(2,1)}, u32[]{:S(2)}, u32[]{:S(2)}) %collective-permute-start.2) | collective-permute-done | bytes 786464 | tf_op jit(solution)/shard_map/ppermute | solution.py:24
  32.0 1.5 collective-permute-start.5
  34.3 0.8 reshape.83.stacked
  35.9 1.0 matrices.1
  38.2 6.2 %collective-permute-done.8.refs_7_ = f32[8,1024]{1,0:T(8,128)S(1)} collective-permute-done((f32[8,1024]{1,0:T(8,128)S(1)}, f32[8,1024]{1,0:T(8,128)S(1)}, u32[]{:S(2)}, u32[]{:S(2)}) %collective-permute-start.8) | collective-permute-done | bytes 32800 | tf_op jit(solution)/shard_map/ppermute | solution.py:19
  44.5 1.5 collective-permute-start.7
  46.7 1.4 collective-permute-done.7.across_facts
  48.1 3.0 %unfold.1 = (bf16[2000,384]{1,0:T(8,128)(2,1)}, bf16[1008,384]{1,0:T(8,128)(2,1)S(1)}) custom-call(s32[2]{0:T(128)S(1)} %pad_add_fusion.2.meta, bf16[2,512,384]{2,1,0:T(8,128)(2,1)} %collective-permute-done.1.beside.refs_1_, bf16[2,512,384]{2,1,0:T(8,128)(2,1)} %collective-permute-done.6.rest), custom_call_target="tpu_custom_call" | custom-call | tf_op jit(solution)/shard_map/unfold/pallas_call | solution.py:87
  51.5 1.8 collective-permute-start.10
  53.8 17.8 %kinetic.1 = bf16[4,1000,576]{2,1,0:T(8,128)(2,1)} custom-call(s32[2]{0:T(128)S(1)} %copy-done.11, s32[2,8]{1,0:T(2,128)S(1)} %copy-done.10, s32[2,8]{1,0:T(2,128)S(1)} %bitcast.36, s32[2,2,8]{2,1,0:T(2,128)S(1)} %pad_add_fusion.side_facts, s32[2,2,8]{2,1,0:T(2,128)S(1)} %collective-permute-done.7.across_facts, ...), custom_call_target="tpu_custom_call" | custom-call | flops 20000000000 | bytes 40000000 | tf_op jit(solution)/shard_map/kinetic/pallas_call | solution.py:507
  72.2 4.0 %correlation.2.refs_6_ = f32[4,192,384]{2,1,0:T(8,128)S(1)} custom-call(s32[3]{0:T(128)S(1)} %add_add_fusion.meta, bf16[2000,384]{1,0:T(8,128)(2,1)S(1)} %bitcast.34, bf16[2000,384]{1,0:T(8,128)(2,1)} %bitcast.11.refs_1_, bf16[2000,384]{1,0:T(8,128)(2,1)S(1)} %bitcast.32, bf16[2000,384]{1,0:T(8,128)(2,1)} %bitcast.12.refs_3_), custom_call_target="tpu_custom_call" | custom-call | flops 1179648000 | bytes 6144000 | tf_op jit(solution)/shard_map/correlation/pallas_call | solution.py:149
  76.3 4.8 %correlation.3 = bf16[4,192,384]{2,1,0:T(8,128)(2,1)S(1)} custom-call(s32[3]{0:T(128)S(1)} %add_add_fusion.meta, bf16[2000,384]{1,0:T(8,128)(2,1)} %get-tuple-element.93.refs_0_, bf16[2000,384]{1,0:T(8,128)(2,1)} %collective-permute-done.11.refs_1_, bf16[1008,384]{1,0:T(8,128)(2,1)} %collective-permute-done.9.refs_2_, ...), custom_call_target="tpu_custom_call" | custom-call | flops 1179648000 | bytes 6144000 | tf_op jit(solution)/shard_map/correlation/pallas_call | solution.py:149
  81.1 7.8 %collective-permute-start.16 = (bf16[192,384]{1,0:T(8,128)(2,1)S(1)}, bf16[192,384]{1,0:T(8,128)(2,1)S(1)}, u32[]{:S(2)}, u32[]{:S(2)}) collective-permute-start(bf16[192,384]{1,0:T(8,128)(2,1)S(1)} %get-tuple-element.133), channel_id=1, source_target_pairs={{0,8},{8,0},{16,24},{24,16},{1,9},{9,1},{17,25},{25,17},{2,10},{10... | collective-permute-start | bytes 442376 | tf_op jit(solution)/shard_map/ppermute | solution.py:19
  89.0 9.8 %collective-permute-start.17 = (bf16[192,384]{1,0:T(8,128)(2,1)S(1)}, bf16[192,384]{1,0:T(8,128)(2,1)S(1)}, u32[]{:S(2)}, u32[]{:S(2)}) collective-permute-start(bf16[192,384]{1,0:T(8,128)(2,1)S(1)} %get-tuple-element.132), channel_id=1, source_target_pairs={{0,16},{8,24},{16,0},{24,8},{1,17},{9,25},{17,1},{25,9},{2,18},{10... | collective-permute-start | bytes 442376 | tf_op jit(solution)/shard_map/ppermute | solution.py:19
  98.8 1.4 collective-permute-start.18
  100.2 6.6 %fock.2.refs_6_ = f32[4,576,384]{2,1,0:T(8,128)S(1)} custom-call(bf16[2,2000,576]{2,1,0:T(8,128)(2,1)} %bitcast.37, bf16[2000,384]{1,0:T(8,128)(2,1)S(1)} %bitcast.35, bf16[2000,384]{1,0:T(8,128)(2,1)} %bitcast.11.refs_1_, bf16[2000,384]{1,0:T(8,128)(2,1)S(1)} %bitcast.33, bf16[2000,384]{1,0:T(8,128)(2,1)} %bitcast.12.refs_3_), custom_call_target="tpu_custom_call" | custom-call | flops 3538944000 | bytes 6144000 | tf_op jit(solution)/shard_map/fock/pallas_call | solution.py:201
  106.8 3.7 %collective-permute-done.18.refs_3_ = bf16[192,384]{1,0:T(8,128)(2,1)S(1)} collective-permute-done((bf16[192,384]{1,0:T(8,128)(2,1)S(1)}, bf16[192,384]{1,0:T(8,128)(2,1)S(1)}, u32[]{:S(2)}, u32[]{:S(2)}) %collective-permute-start.18) | collective-permute-done | bytes 147488 | tf_op jit(solution)/shard_map/ppermute | solution.py:19
  110.5 0.8 level_sum.2
  111.3 2.7 %collective-permute-start.19 = (bf16[192,384]{1,0:T(8,128)(2,1)S(1)}, bf16[192,384]{1,0:T(8,128)(2,1)S(1)}, u32[]{:S(2)}, u32[]{:S(2)}) collective-permute-start(bf16[192,384]{1,0:T(8,128)(2,1)S(1)} %get-tuple-element.106), channel_id=1, source_target_pairs={{0,8},{8,0},{16,24},{24,16},{1,9},{9,1},{17,25},{25,17},{2,10},{10... | collective-permute-start | bytes 442376 | tf_op jit(solution)/shard_map/ppermute | solution.py:19
  114.1 2.0 collective-permute-start.20
  116.1 1.4 collective-permute-start.21
  117.5 1.5 collective-permute-start.22
  119.0 8.1 %fock.3 = bf16[4,3,192,384]{3,2,1,0:T(8,128)(2,1)S(1)} custom-call(bf16[2,2000,576]{2,1,0:T(8,128)(2,1)} %bitcast.38, bf16[2000,384]{1,0:T(8,128)(2,1)} %get-tuple-element.93.refs_0_, bf16[2000,384]{1,0:T(8,128)(2,1)} %collective-permute-done.11.refs_1_, bf16[1008,384]{1,0:T(8,128)(2,1)} %collective-permute-done.9.refs_2_, ...), custom_call_target="tpu_custom_call" | custom-call | flops 3538944000 | bytes 6144000 | tf_op jit(solution)/shard_map/fock/pallas_call | solution.py:201
  127.1 0.9 convert_add_fusion
  128.7 1.4 collective-permute-start.23
  130.2 6.0 %collective-permute-done.25 = bf16[384,384]{1,0:T(8,128)(2,1)S(1)} collective-permute-done((bf16[384,384]{1,0:T(8,128)(2,1)S(1)}, bf16[384,384]{1,0:T(8,128)(2,1)S(1)}, u32[]{:S(2)}, u32[]{:S(2)}) %collective-permute-start.25) | collective-permute-done | bytes 294944 | tf_op jit(solution)/shard_map/ppermute | solution.py:19
  136.2 1.1 collective-permute-start.26
  137.4 1.0 collective-permute-start.24
  138.6 2.9 %collective-permute-start.27 = (bf16[3,192,384]{2,1,0:T(8,128)(2,1)S(1)}, bf16[3,192,384]{2,1,0:T(8,128)(2,1)S(1)}, u32[]{:S(2)}, u32[]{:S(2)}) collective-permute-start(bf16[3,192,384]{2,1,0:T(8,128)(2,1)S(1)} %get-tuple-element.129), channel_id=1, source_target_pairs={{0,8},{8,0},{16,24},{24,16},{1,9},{9,1},{17,25},{25,17},{2,10},{10... | collective-permute-start | bytes 1327112 | tf_op jit(solution)/shard_map/ppermute | solution.py:19
  141.5 2.0 collective-permute-start.28
  143.5 1.4 collective-permute-start.29
  144.9 13.1 %collective-permute-done.27.refs_1_ = bf16[3,192,384]{2,1,0:T(8,128)(2,1)S(1)} collective-permute-done((bf16[3,192,384]{2,1,0:T(8,128)(2,1)S(1)}, bf16[3,192,384]{2,1,0:T(8,128)(2,1)S(1)}, u32[]{:S(2)}, u32[]{:S(2)}) %collective-permute-start.27) | collective-permute-done | bytes 442400 | tf_op jit(solution)/shard_map/ppermute | solution.py:19
  158.0 16.5 %collective-permute-done.28.refs_2_ = bf16[3,192,384]{2,1,0:T(8,128)(2,1)S(1)} collective-permute-done((bf16[3,192,384]{2,1,0:T(8,128)(2,1)S(1)}, bf16[3,192,384]{2,1,0:T(8,128)(2,1)S(1)}, u32[]{:S(2)}, u32[]{:S(2)}) %collective-permute-start.28) | collective-permute-done | bytes 442400 | tf_op jit(solution)/shard_map/ppermute | solution.py:19
  174.5 0.9 level_sum.3
  175.5 1.3 collective-permute-start.30
  177.9 3.3 %collective-permute-done.30 = f32[192,192]{1,0:T(8,128)S(1)} collective-permute-done((f32[192,192]{1,0:T(8,128)S(1)}, f32[192,192]{1,0:T(8,128)S(1)}, u32[]{:S(2)}, u32[]{:S(2)}) %collective-permute-start.30) | collective-permute-done | bytes 147488 | tf_op jit(solution)/shard_map/ppermute | solution.py:19
  181.2 11.5 %collective-permute-start.31 = (bf16[192,384]{1,0:T(8,128)(2,1)S(1)}, bf16[192,384]{1,0:T(8,128)(2,1)S(1)}, u32[]{:S(2)}, u32[]{:S(2)}) collective-permute-start(bf16[192,384]{1,0:T(8,128)(2,1)S(1)} %get-tuple-element.117), channel_id=1, source_target_pairs={{0,0},{1,8},{2,16},{3,24},{4,4},{5,12},{6,20},{7,28},{8,1},{9,9},{... | collective-permute-start | bytes 442376 | tf_op jit(solution)/shard_map/ppermute | solution.py:701
  192.7 3.6 %collective-permute-done.31 = bf16[192,384]{1,0:T(8,128)(2,1)S(1)} collective-permute-done((bf16[192,384]{1,0:T(8,128)(2,1)S(1)}, bf16[192,384]{1,0:T(8,128)(2,1)S(1)}, u32[]{:S(2)}, u32[]{:S(2)}) %collective-permute-start.31) | collective-permute-done | bytes 147488 | tf_op jit(solution)/shard_map/ppermute | solution.py:701
  196.3 0.8 maximum_add_fusion
  197.2 8.3 %root.1 = f32[192,384]{1,0:T(8,128)} custom-call(s32[3]{0:T(128)S(1)} %add_add_fusion.1.meta, bf16[768,384]{1,0:T(8,128)(2,1)S(1)} %constant_dynamic-update-slice_fusion.refs_0_, bf16[768,384]{1,0:T(8,128)(2,1)S(1)} %collective-permute-done.24.refs_1_, bf16[768,384]{1,0:T(8,128)(2,1)S(1)} %constant_dynamic-update-slice_fusion.3.refs_2_, ...), custom_call_target="tpu_custom_call" | custom-call | flops 3623878656 | bytes 9437184 | tf_op jit(solution)/shard_map/root/pallas_call | solution.py:286
  (96 shorter events, 11.5 us)
Async XLA Ops:
  3.7 1.4 copy-start
  5.1 30.7 %copy-start.1 = (f32[160,160]{1,0:T(8,128)S(1)}, f32[160,160]{1,0:T(8,128)}, u32[]{:S(2)}) copy-start(f32[160,160]{1,0:T(8,128)} %constant.76.clone.refs_8_) | copy-start | bytes 307204
  5.1 30.7 %copy-start.2 = (f32[112,112]{1,0:T(8,128)S(1)}, f32[112,112]{1,0:T(8,128)}, u32[]{:S(2)}) copy-start(f32[112,112]{1,0:T(8,128)} %constant.70.clone.refs_2_) | copy-start | bytes 150532
  5.1 30.7 %copy-start.3 = (f32[112,112]{1,0:T(8,128)S(1)}, f32[112,112]{1,0:T(8,128)}, u32[]{:S(2)}) copy-start(f32[112,112]{1,0:T(8,128)} %constant.73.clone.refs_5_) | copy-start | bytes 150532
  5.1 30.7 %copy-start.4 = (bf16[160,10]{1,0:T(8,128)(2,1)S(1)}, bf16[160,10]{1,0:T(8,128)(2,1)}, u32[]{:S(2)}) copy-start(bf16[160,10]{1,0:T(8,128)(2,1)} %constant.74.clone.refs_6_) | copy-start | bytes 9604
  5.1 30.7 %copy-start.5 = (bf16[30,480]{1,0:T(8,128)(2,1)S(1)}, bf16[30,480]{1,0:T(8,128)(2,1)}, u32[]{:S(2)}) copy-start(bf16[30,480]{1,0:T(8,128)(2,1)} %constant.75.clone.refs_7_) | copy-start | bytes 86404
  5.1 30.7 %copy-start.6 = (bf16[112,10]{1,0:T(8,128)(2,1)S(1)}, bf16[112,10]{1,0:T(8,128)(2,1)}, u32[]{:S(2)}) copy-start(bf16[112,10]{1,0:T(8,128)(2,1)} %constant.68.clone.refs_0_) | copy-start | bytes 6724
  5.2 30.7 %copy-start.7 = (bf16[112,10]{1,0:T(8,128)(2,1)S(1)}, bf16[112,10]{1,0:T(8,128)(2,1)}, u32[]{:S(2)}) copy-start(bf16[112,10]{1,0:T(8,128)(2,1)} %constant.71.clone.refs_3_) | copy-start | bytes 6724
  5.2 30.7 %copy-start.8 = (bf16[30,336]{1,0:T(8,128)(2,1)S(1)}, bf16[30,336]{1,0:T(8,128)(2,1)}, u32[]{:S(2)}) copy-start(bf16[30,336]{1,0:T(8,128)(2,1)} %constant.69.clone.refs_1_) | copy-start | bytes 60484
  5.2 30.7 %copy-start.9 = (bf16[30,336]{1,0:T(8,128)(2,1)S(1)}, bf16[30,336]{1,0:T(8,128)(2,1)}, u32[]{:S(2)}) copy-start(bf16[30,336]{1,0:T(8,128)(2,1)} %constant.72.clone.refs_4_) | copy-start | bytes 60484
  7.4 20.7 %collective-permute-start.1 = (bf16[2,512,384]{2,1,0:T(8,128)(2,1)}, bf16[2,512,384]{2,1,0:T(8,128)(2,1)}, u32[]{:S(2)}, u32[]{:S(2)}) collective-permute-start(bf16[2,512,384]{2,1,0:T(8,128)(2,1)} %pack.2), channel_id=1, source_target_pairs={{0,4},{4,0},{1,5},{5,1},{2,6},{6,2},{3,7},{7,3},{8,12},{12,8},{9,1... | collective-permute-start | bytes 2359304 | tf_op jit(solution)/shard_map/ppermute | solution.py:19
  11.2 20.8 %collective-permute-start.2 = (bf16[2,512,384]{2,1,0:T(8,128)(2,1)}, bf16[2,512,384]{2,1,0:T(8,128)(2,1)}, u32[]{:S(2)}, u32[]{:S(2)}) collective-permute-start(bf16[2,512,384]{2,1,0:T(8,128)(2,1)} %get-tuple-element.80.refs_0_), channel_id=1, source_target_pairs={{0,8},{16,24},{8,0},{24,16},{1,9},{17,25},{9,1},{25,17},{2,10},{18... | collective-permute-start | bytes 2359304 | tf_op jit(solution)/shard_map/ppermute | solution.py:24
  12.8 35.3 %collective-permute-start = (bf16[2,1000,384]{2,1,0:T(8,128)(2,1)S(1)}, bf16[2,1000,384]{2,1,0:T(8,128)(2,1)S(1)}, u32[]{:S(2)}, u32[]{:S(2)}) collective-permute-start(bf16[2,1000,384]{2,1,0:T(8,128)(2,1)S(1)} %get-tuple-element.96), channel_id=1, source_target_pairs={{0,2},{1,3},{2,0},{3,1},{4,6},{5,7},{6,4},{7,5},{8,10},{9,11},{10,... | collective-permute-start | bytes 4608008 | tf_op jit(solution)/shard_map/ppermute | solution.py:19
  13.3 24.2 %collective-permute-start.4 = (bf16[2,512,384]{2,1,0:T(8,128)(2,1)}, bf16[2,512,384]{2,1,0:T(8,128)(2,1)}, u32[]{:S(2)}, u32[]{:S(2)}) collective-permute-start(bf16[2,512,384]{2,1,0:T(8,128)(2,1)} %get-tuple-element.80.refs_0_), channel_id=1, source_target_pairs={{8,16},{16,8},{9,17},{17,9},{10,18},{18,10},{11,19},{19,11},{12,20... | collective-permute-start | bytes 2359304 | tf_op jit(solution)/shard_map/ppermute | solution.py:24
  14.8 31.8 %collective-permute-start.6 = (bf16[2,512,384]{2,1,0:T(8,128)(2,1)}, bf16[2,512,384]{2,1,0:T(8,128)(2,1)}, u32[]{:S(2)}, u32[]{:S(2)}) collective-permute-start(bf16[2,512,384]{2,1,0:T(8,128)(2,1)} %get-tuple-element.80.refs_0_), channel_id=1, source_target_pairs={{0,4},{4,0},{1,5},{5,1},{2,6},{6,2},{3,7},{7,3},{8,12},{12,8},{9,1... | collective-permute-start | bytes 2359304 | tf_op jit(solution)/shard_map/ppermute | solution.py:19
  28.1 19.9 %collective-permute-start.3 = (bf16[2,512,384]{2,1,0:T(8,128)(2,1)}, bf16[2,512,384]{2,1,0:T(8,128)(2,1)}, u32[]{:S(2)}, u32[]{:S(2)}) collective-permute-start(bf16[2,512,384]{2,1,0:T(8,128)(2,1)} %collective-permute-done.1.beside.refs_1_), channel_id=1, source_target_pairs={{0,8},{16,24},{8,0},{24,16},{1,9},{17,25},{9,1},{25,17},{2,10},{18... | collective-permute-start | bytes 2359304 | tf_op jit(solution)/shard_map/ppermute | solution.py:24
  32.0 16.1 %collective-permute-start.5 = (bf16[2,512,384]{2,1,0:T(8,128)(2,1)}, bf16[2,512,384]{2,1,0:T(8,128)(2,1)}, u32[]{:S(2)}, u32[]{:S(2)}) collective-permute-start(bf16[2,512,384]{2,1,0:T(8,128)(2,1)} %collective-permute-done.1.beside.refs_1_), channel_id=1, source_target_pairs={{8,16},{16,8},{9,17},{17,9},{10,18},{18,10},{11,19},{19,11},{12,20... | collective-permute-start | bytes 2359304 | tf_op jit(solution)/shard_map/ppermute | solution.py:24
  37.5 6.9 %collective-permute-start.8 = (f32[8,1024]{1,0:T(8,128)S(1)}, f32[8,1024]{1,0:T(8,128)S(1)}, u32[]{:S(2)}, u32[]{:S(2)}) collective-permute-start(f32[8,1024]{1,0:T(8,128)S(1)} %pad.9.refs_6_), channel_id=1, source_target_pairs={{0,4},{4,0},{1,5},{5,1},{2,6},{6,2},{3,7},{7,3},{8,12},{12,8},{9,1... | collective-permute-start | bytes 98312 | tf_op jit(solution)/shard_map/ppermute | solution.py:19
  44.5 3.6 %collective-permute-start.7 = (s32[2,2,8]{2,1,0:T(2,128)S(1)}, s32[2,2,8]{2,1,0:T(2,128)S(1)}, u32[]{:S(2)}, u32[]{:S(2)}) collective-permute-start(s32[2,2,8]{2,1,0:T(2,128)S(1)} %pad_add_fusion.side_facts), channel_id=1, source_target_pairs={{0,4},{4,0},{1,5},{5,1},{2,6},{6,2},{3,7},{7,3},{8,12},{12,8},{9,1... | collective-permute-start | bytes 392 | tf_op jit(solution)/shard_map/ppermute | solution.py:19
  48.0 5.8 %copy-start.10 = (s32[2,8]{1,0:T(2,128)S(1)}, s32[2,8]{1,0:T(2,128)}, u32[]{:S(2)}) copy-start(s32[2,8]{1,0:T(2,128)} %get-tuple-element.76.own_facts) | copy-start | bytes 196
  48.1 5.8 %copy-start.11 = (s32[2]{0:T(128)S(1)}, s32[2]{0:T(128)}, u32[]{:S(2)}) copy-start(s32[2]{0:T(128)} %pad_add_fusion.3.place_meta) | copy-start | bytes 28
  51.1 20.5 %collective-permute-start.9 = (bf16[1008,384]{1,0:T(8,128)(2,1)S(1)}, bf16[1008,384]{1,0:T(8,128)(2,1)}, u32[]{:S(2)}, u32[]{:S(2)}) collective-permute-start(bf16[1008,384]{1,0:T(8,128)(2,1)S(1)} %get-tuple-element.74), channel_id=1, source_target_pairs={{0,2},{1,3},{2,0},{3,1},{4,6},{5,7},{6,4},{7,5},{8,10},{9,11},{10,... | collective-permute-start | bytes 2322440 | tf_op jit(solution)/shard_map/ppermute | solution.py:19
  51.4 20.8 %collective-permute-start.15 = (bf16[2,1000,384]{2,1,0:T(8,128)(2,1)S(1)}, bf16[2,1000,384]{2,1,0:T(8,128)(2,1)}, u32[]{:S(2)}, u32[]{:S(2)}) collective-permute-start(bf16[2,1000,384]{2,1,0:T(8,128)(2,1)S(1)} %collective-permute-done), channel_id=1, source_target_pairs={{0,1},{1,0},{2,3},{3,2},{4,5},{5,4},{6,7},{7,6},{8,9},{9,8},{10,11... | collective-permute-start | bytes 4608008 | tf_op jit(solution)/shard_map/ppermute | solution.py:19
  51.5 20.1 %collective-permute-start.10 = (bf16[992,384]{1,0:T(8,128)(2,1)S(1)}, bf16[992,384]{1,0:T(8,128)(2,1)}, u32[]{:S(2)}, u32[]{:S(2)}) collective-permute-start(bf16[992,384]{1,0:T(8,128)(2,1)S(1)} %slice.19), channel_id=1, source_target_pairs={{0,4},{4,0},{1,5},{5,1},{2,6},{6,2},{3,7},{7,3},{8,12},{12,8},{9,1... | collective-permute-start | bytes 2285576 | tf_op jit(solution)/shard_map/ppermute | solution.py:19
  53.3 18.9 %collective-permute-start.14 = (bf16[2,1000,384]{2,1,0:T(8,128)(2,1)S(1)}, bf16[2,1000,384]{2,1,0:T(8,128)(2,1)}, u32[]{:S(2)}, u32[]{:S(2)}) collective-permute-start(bf16[2,1000,384]{2,1,0:T(8,128)(2,1)S(1)} %get-tuple-element.96), channel_id=1, source_target_pairs={{0,1},{1,0},{2,3},{3,2},{4,5},{5,4},{6,7},{7,6},{8,9},{9,8},{10,11... | collective-permute-start | bytes 4608008 | tf_op jit(solution)/shard_map/ppermute | solution.py:19
  53.5 22.7 %collective-permute-start.11 = (bf16[2000,384]{1,0:T(8,128)(2,1)}, bf16[2000,384]{1,0:T(8,128)(2,1)}, u32[]{:S(2)}, u32[]{:S(2)}) collective-permute-start(bf16[2000,384]{1,0:T(8,128)(2,1)} %get-tuple-element.93.refs_0_), channel_id=1, source_target_pairs={{0,1},{1,0},{2,3},{3,2},{4,5},{5,4},{6,7},{7,6},{8,9},{9,8},{10,11... | collective-permute-start | bytes 4608008 | tf_op jit(solution)/shard_map/ppermute | solution.py:19
  71.6 4.7 %collective-permute-start.12 = (bf16[1008,384]{1,0:T(8,128)(2,1)}, bf16[1008,384]{1,0:T(8,128)(2,1)}, u32[]{:S(2)}, u32[]{:S(2)}) collective-permute-start(bf16[1008,384]{1,0:T(8,128)(2,1)} %collective-permute-done.9.refs_2_), channel_id=1, source_target_pairs={{0,1},{1,0},{2,3},{3,2},{4,5},{5,4},{6,7},{7,6},{8,9},{9,8},{10,11... | collective-permute-start | bytes 2322440 | tf_op jit(solution)/shard_map/ppermute | solution.py:19
  71.9 4.3 %collective-permute-start.13 = (bf16[992,384]{1,0:T(8,128)(2,1)}, bf16[992,384]{1,0:T(8,128)(2,1)}, u32[]{:S(2)}, u32[]{:S(2)}) collective-permute-start(bf16[992,384]{1,0:T(8,128)(2,1)} %collective-permute-done.10.refs_3_), channel_id=1, source_target_pairs={{0,1},{1,0},{2,3},{3,2},{4,5},{5,4},{6,7},{7,6},{8,9},{9,8},{10,11... | collective-permute-start | bytes 2285576 | tf_op jit(solution)/shard_map/ppermute | solution.py:19
  81.1 25.7 %collective-permute-start.16 = (bf16[192,384]{1,0:T(8,128)(2,1)S(1)}, bf16[192,384]{1,0:T(8,128)(2,1)S(1)}, u32[]{:S(2)}, u32[]{:S(2)}) collective-permute-start(bf16[192,384]{1,0:T(8,128)(2,1)S(1)} %get-tuple-element.133), channel_id=1, source_target_pairs={{0,8},{8,0},{16,24},{24,16},{1,9},{9,1},{17,25},{25,17},{2,10},{10... | collective-permute-start | bytes 442376 | tf_op jit(solution)/shard_map/ppermute | solution.py:19
  89.0 17.8 %collective-permute-start.17 = (bf16[192,384]{1,0:T(8,128)(2,1)S(1)}, bf16[192,384]{1,0:T(8,128)(2,1)S(1)}, u32[]{:S(2)}, u32[]{:S(2)}) collective-permute-start(bf16[192,384]{1,0:T(8,128)(2,1)S(1)} %get-tuple-element.132), channel_id=1, source_target_pairs={{0,16},{8,24},{16,0},{24,8},{1,17},{9,25},{17,1},{25,9},{2,18},{10... | collective-permute-start | bytes 442376 | tf_op jit(solution)/shard_map/ppermute | solution.py:19
  98.8 11.8 %collective-permute-start.18 = (bf16[192,384]{1,0:T(8,128)(2,1)S(1)}, bf16[192,384]{1,0:T(8,128)(2,1)S(1)}, u32[]{:S(2)}, u32[]{:S(2)}) collective-permute-start(bf16[192,384]{1,0:T(8,128)(2,1)S(1)} %get-tuple-element.131), channel_id=1, source_target_pairs={{0,24},{8,16},{16,8},{24,0},{1,25},{9,17},{17,9},{25,1},{2,26},{10... | collective-permute-start | bytes 442376 | tf_op jit(solution)/shard_map/ppermute | solution.py:19
  111.3 16.6 %collective-permute-start.19 = (bf16[192,384]{1,0:T(8,128)(2,1)S(1)}, bf16[192,384]{1,0:T(8,128)(2,1)S(1)}, u32[]{:S(2)}, u32[]{:S(2)}) collective-permute-start(bf16[192,384]{1,0:T(8,128)(2,1)S(1)} %get-tuple-element.106), channel_id=1, source_target_pairs={{0,8},{8,0},{16,24},{24,16},{1,9},{9,1},{17,25},{25,17},{2,10},{10... | collective-permute-start | bytes 442376 | tf_op jit(solution)/shard_map/ppermute | solution.py:19
  114.1 13.9 %collective-permute-start.20 = (bf16[192,384]{1,0:T(8,128)(2,1)S(1)}, bf16[192,384]{1,0:T(8,128)(2,1)S(1)}, u32[]{:S(2)}, u32[]{:S(2)}) collective-permute-start(bf16[192,384]{1,0:T(8,128)(2,1)S(1)} %get-tuple-element.106), channel_id=1, source_target_pairs={{0,16},{8,24},{16,0},{24,8},{1,17},{9,25},{17,1},{25,9},{2,18},{10... | collective-permute-start | bytes 442376 | tf_op jit(solution)/shard_map/ppermute | solution.py:19
  116.1 11.9 %collective-permute-start.21 = (bf16[192,384]{1,0:T(8,128)(2,1)S(1)}, bf16[192,384]{1,0:T(8,128)(2,1)S(1)}, u32[]{:S(2)}, u32[]{:S(2)}) collective-permute-start(bf16[192,384]{1,0:T(8,128)(2,1)S(1)} %get-tuple-element.106), channel_id=1, source_target_pairs={{0,24},{8,16},{16,8},{24,0},{1,25},{9,17},{17,9},{25,1},{2,26},{10... | collective-permute-start | bytes 442376 | tf_op jit(solution)/shard_map/ppermute | solution.py:19
  117.5 9.6 %collective-permute-start.22 = (f32[192,192]{1,0:T(8,128)S(1)}, f32[192,192]{1,0:T(8,128)S(1)}, u32[]{:S(2)}, u32[]{:S(2)}) collective-permute-start(f32[192,192]{1,0:T(8,128)S(1)} %get-tuple-element.105), channel_id=1, source_target_pairs={{0,4},{4,0},{1,5},{5,1},{2,6},{6,2},{3,7},{7,3},{8,12},{12,8},{9,1... | collective-permute-start | bytes 442376 | tf_op jit(solution)/shard_map/ppermute | solution.py:19
  128.0 8.2 %collective-permute-start.25 = (bf16[384,384]{1,0:T(8,128)(2,1)S(1)}, bf16[384,384]{1,0:T(8,128)(2,1)S(1)}, u32[]{:S(2)}, u32[]{:S(2)}) collective-permute-start(bf16[384,384]{1,0:T(8,128)(2,1)S(1)} %pad_maximum_fusion.2), channel_id=1, source_target_pairs={{0,2},{1,3},{2,0},{3,1},{4,6},{5,7},{6,4},{7,5},{8,10},{9,11},{10,... | collective-permute-start | bytes 884744 | tf_op jit(solution)/shard_map/ppermute | solution.py:19
  128.7 8.7 %collective-permute-start.23 = (bf16[384,384]{1,0:T(8,128)(2,1)S(1)}, bf16[384,384]{1,0:T(8,128)(2,1)S(1)}, u32[]{:S(2)}, u32[]{:S(2)}) collective-permute-start(bf16[384,384]{1,0:T(8,128)(2,1)S(1)} %pad_maximum_fusion.1), channel_id=1, source_target_pairs={{0,4},{4,0},{1,5},{5,1},{2,6},{6,2},{3,7},{7,3},{8,12},{12,8},{9,1... | collective-permute-start | bytes 884744 | tf_op jit(solution)/shard_map/ppermute | solution.py:19
  136.2 38.3 %collective-permute-start.26 = (bf16[768,384]{1,0:T(8,128)(2,1)S(1)}, bf16[768,384]{1,0:T(8,128)(2,1)S(1)}, u32[]{:S(2)}, u32[]{:S(2)}) collective-permute-start(bf16[768,384]{1,0:T(8,128)(2,1)S(1)} %constant_dynamic-update-slice_fusion.3.refs_2_), channel_id=1, source_target_pairs={{0,4},{4,0},{1,5},{5,1},{2,6},{6,2},{3,7},{7,3},{8,12},{12,8},{9,1... | collective-permute-start | bytes 1769480 | tf_op jit(solution)/shard_map/ppermute | solution.py:19
  137.4 37.1 %collective-permute-start.24 = (bf16[768,384]{1,0:T(8,128)(2,1)S(1)}, bf16[768,384]{1,0:T(8,128)(2,1)S(1)}, u32[]{:S(2)}, u32[]{:S(2)}) collective-permute-start(bf16[768,384]{1,0:T(8,128)(2,1)S(1)} %constant_dynamic-update-slice_fusion.refs_0_), channel_id=1, source_target_pairs={{0,2},{1,3},{2,0},{3,1},{4,6},{5,7},{6,4},{7,5},{8,10},{9,11},{10,... | collective-permute-start | bytes 1769480 | tf_op jit(solution)/shard_map/ppermute | solution.py:19
  138.6 19.4 %collective-permute-start.27 = (bf16[3,192,384]{2,1,0:T(8,128)(2,1)S(1)}, bf16[3,192,384]{2,1,0:T(8,128)(2,1)S(1)}, u32[]{:S(2)}, u32[]{:S(2)}) collective-permute-start(bf16[3,192,384]{2,1,0:T(8,128)(2,1)S(1)} %get-tuple-element.129), channel_id=1, source_target_pairs={{0,8},{8,0},{16,24},{24,16},{1,9},{9,1},{17,25},{25,17},{2,10},{10... | collective-permute-start | bytes 1327112 | tf_op jit(solution)/shard_map/ppermute | solution.py:19
  141.5 33.0 %collective-permute-start.28 = (bf16[3,192,384]{2,1,0:T(8,128)(2,1)S(1)}, bf16[3,192,384]{2,1,0:T(8,128)(2,1)S(1)}, u32[]{:S(2)}, u32[]{:S(2)}) collective-permute-start(bf16[3,192,384]{2,1,0:T(8,128)(2,1)S(1)} %get-tuple-element.128), channel_id=1, source_target_pairs={{0,16},{8,24},{16,0},{24,8},{1,17},{9,25},{17,1},{25,9},{2,18},{10... | collective-permute-start | bytes 1327112 | tf_op jit(solution)/shard_map/ppermute | solution.py:19
  143.5 31.0 %collective-permute-start.29 = (bf16[3,192,384]{2,1,0:T(8,128)(2,1)S(1)}, bf16[3,192,384]{2,1,0:T(8,128)(2,1)S(1)}, u32[]{:S(2)}, u32[]{:S(2)}) collective-permute-start(bf16[3,192,384]{2,1,0:T(8,128)(2,1)S(1)} %get-tuple-element.127), channel_id=1, source_target_pairs={{0,24},{8,16},{16,8},{24,0},{1,25},{9,17},{17,9},{25,1},{2,26},{10... | collective-permute-start | bytes 1327112 | tf_op jit(solution)/shard_map/ppermute | solution.py:19
  175.5 5.7 %collective-permute-start.30 = (f32[192,192]{1,0:T(8,128)S(1)}, f32[192,192]{1,0:T(8,128)S(1)}, u32[]{:S(2)}, u32[]{:S(2)}) collective-permute-start(f32[192,192]{1,0:T(8,128)S(1)} %get-tuple-element.116), channel_id=1, source_target_pairs={{0,4},{4,0},{1,5},{5,1},{2,6},{6,2},{3,7},{7,3},{8,12},{12,8},{9,1... | collective-permute-start | bytes 442376 | tf_op jit(solution)/shard_map/ppermute | solution.py:19
  176.8 20.4 %collective-permute-start.32 = (bf16[768,384]{1,0:T(8,128)(2,1)S(1)}, bf16[768,384]{1,0:T(8,128)(2,1)S(1)}, u32[]{:S(2)}, u32[]{:S(2)}) collective-permute-start(bf16[768,384]{1,0:T(8,128)(2,1)S(1)} %constant_dynamic-update-slice_fusion.refs_0_), channel_id=1, source_target_pairs={{0,1},{1,0},{2,3},{3,2},{4,5},{5,4},{6,7},{7,6},{8,9},{9,8},{10,11... | collective-permute-start | bytes 1769480 | tf_op jit(solution)/shard_map/ppermute | solution.py:19
  176.8 20.4 %collective-permute-start.33 = (bf16[768,384]{1,0:T(8,128)(2,1)S(1)}, bf16[768,384]{1,0:T(8,128)(2,1)S(1)}, u32[]{:S(2)}, u32[]{:S(2)}) collective-permute-start(bf16[768,384]{1,0:T(8,128)(2,1)S(1)} %collective-permute-done.24.refs_1_), channel_id=1, source_target_pairs={{0,1},{1,0},{2,3},{3,2},{4,5},{5,4},{6,7},{7,6},{8,9},{9,8},{10,11... | collective-permute-start | bytes 1769480 | tf_op jit(solution)/shard_map/ppermute | solution.py:19
  177.3 19.9 %collective-permute-start.34 = (bf16[768,384]{1,0:T(8,128)(2,1)S(1)}, bf16[768,384]{1,0:T(8,128)(2,1)S(1)}, u32[]{:S(2)}, u32[]{:S(2)}) collective-permute-start(bf16[768,384]{1,0:T(8,128)(2,1)S(1)} %constant_dynamic-update-slice_fusion.3.refs_2_), channel_id=1, source_target_pairs={{0,1},{1,0},{2,3},{3,2},{4,5},{5,4},{6,7},{7,6},{8,9},{9,8},{10,11... | collective-permute-start | bytes 1769480 | tf_op jit(solution)/shard_map/ppermute | solution.py:19
  177.3 19.9 %collective-permute-start.35 = (bf16[768,384]{1,0:T(8,128)(2,1)S(1)}, bf16[768,384]{1,0:T(8,128)(2,1)S(1)}, u32[]{:S(2)}, u32[]{:S(2)}) collective-permute-start(bf16[768,384]{1,0:T(8,128)(2,1)S(1)} %collective-permute-done.26.refs_3_), channel_id=1, source_target_pairs={{0,1},{1,0},{2,3},{3,2},{4,5},{5,4},{6,7},{7,6},{8,9},{9,8},{10,11... | collective-permute-start | bytes 1769480 | tf_op jit(solution)/shard_map/ppermute | solution.py:19
  181.2 15.1 %collective-permute-start.31 = (bf16[192,384]{1,0:T(8,128)(2,1)S(1)}, bf16[192,384]{1,0:T(8,128)(2,1)S(1)}, u32[]{:S(2)}, u32[]{:S(2)}) collective-permute-start(bf16[192,384]{1,0:T(8,128)(2,1)S(1)} %get-tuple-element.117), channel_id=1, source_target_pairs={{0,0},{1,8},{2,16},{3,24},{4,4},{5,12},{6,20},{7,28},{8,1},{9,9},{... | collective-permute-start | bytes 442376 | tf_op jit(solution)/shard_map/ppermute | solution.py:701

commit v2 on v1

--- a/solution.py
+++ b/solution.py
@@ -32,39 +32,45 @@
     return pltpu.CompilerParams(vmem_limit_bytes=mebibytes * 1024 * 1024)
 
 
-def pack_kernel(own, meta, orbitals, facts, packed, *active):
+def pack_kernel(meta, neighbours, levels, orbitals, theirs, mine):
     slots, coefficients, width = orbitals.shape
     half, fold = width // PAIR, coefficients // 2
-    low_half = (meta[0] == 0) == own
+    first = meta[0] == 0
+    place = lax.broadcasted_iota(jnp.int32, (8, width), 1)
     for slot in range(slots):
         keep = slot < meta[1]
         for part in range(2):
-            rows = slice(part * fold, (part + 1) * fold)
-            here = orbitals[slot, rows, :]
+            here = orbitals[slot, part * fold : (part + 1) * fold, :]
             here = jnp.where(keep, here, jnp.zeros_like(here))
-            if active:
-                active[0][slot, rows, :] = here
+            low, high = here[:, :half], here[:, half:]
             lanes = slice(part * half, (part + 1) * half)
-            packed[slot, :fold, lanes] = jnp.where(low_half, here[:, :half], here[:, half:])
-        rest = packed.shape[1] - fold
-        packed[slot, fold:, :] = jnp.broadcast_to(facts[slot : slot + 1, :], (rest, width)).astype(bf16)
-
-
-def pack(meta, orbitals, facts, own):
+            theirs[slot, :fold, lanes] = jnp.where(first, high, low)
+            mine[slot, :fold, lanes] = jnp.where(first, low, high)
+        own_id = meta[2] + slot
+        facts = jnp.where(place == 6, levels[slot], jnp.where(place == 7, jnp.where(keep, 1, 0), 0))
+        for c in range(6):
+            target = neighbours[slot, c]
+            facts = jnp.where(place == c, jnp.where(target >= 0, target - own_id, 16 * slots), facts)
+        facts = facts.astype(f32).astype(bf16)
+        for packed in (theirs, mine):
+            packed[slot, fold : fold + 8, :] = facts
+            rest = packed.shape[1] - fold - 8
+            packed[slot, fold + 8 :, :] = jnp.zeros((rest, width), bf16)
+
+
+def pack(meta, neighbours, levels, orbitals):
     slots, coefficients, width = orbitals.shape
     fold = coefficients // 2
     padded = (fold // ROWS + 1) * ROWS
-    vmem = pl.BlockSpec(memory_space=pltpu.VMEM)
-    shapes = [jax.ShapeDtypeStruct((slots, padded, width), bf16)]
-    shapes += [jax.ShapeDtypeStruct(orbitals.shape, bf16)] * own
+    vmem, smem = pl.BlockSpec(memory_space=pltpu.VMEM), pl.BlockSpec(memory_space=pltpu.SMEM)
     return pl.pallas_call(
-        functools.partial(pack_kernel, own),
-        out_shape=shapes,
-        in_specs=[pl.BlockSpec(memory_space=pltpu.SMEM), vmem, vmem],
-        out_specs=[vmem] * len(shapes),
+        pack_kernel,
+        out_shape=[jax.ShapeDtypeStruct((slots, padded, width), bf16)] * 2,
+        in_specs=[smem, smem, smem, vmem],
+        out_specs=[vmem, vmem],
         compiler_params=params(24),
         name="pack",
-    )(meta, orbitals, facts)
+    )(meta, neighbours, levels, orbitals)
 
 
 def unfold_kernel(fold, meta, beside, rest, whole, top):
@@ -125,10 +131,12 @@
     for copy in copies[: counts[0]]:
         copy.wait()
     own = held[:, :width]
-    turned[...] = jnp.where(first, own[:, :half], own[:, half:]).T
-    for copy in copies[counts[0] :]:
-        copy.wait()
+    own = jnp.where(first, own[:, :half], own[:, half:]).T
+    live = lax.broadcasted_iota(jnp.int32, own.shape, 1) < meta[1 if before else 2]
+    turned[...] = jnp.where(live, own, jnp.zeros_like(own))
     for base in range(0, groups, 2):
+        for copy in copies[max(sum(counts[:base]), counts[0]) : sum(counts[: base + 2])]:
+            copy.wait()
         wide = matmul(turned[...], held[:, base * width : (base + 2) * width])
         for q in (base, base + 1):
             total = wide[:, (q - base) * width : (q - base + 1) * width]
@@ -175,9 +183,9 @@
     half, width = out.shape[-2] // (1 if before else 3), out.shape[-1]
     last.wait()
     turned[...] = raw[...].T
-    for copy in copies:
-        copy.wait()
     for base in range(0, len(lefts), 2):
+        for copy in copies[sum(counts[:base]) : sum(counts[: base + 2])]:
+            copy.wait()
         wide = matmul(turned[...], held[:, base * width : (base + 2) * width])
         for q in (base, base + 1):
             total = wide[:, (q - base) * width : (q - base + 1) * width]
@@ -352,7 +360,9 @@
     copies = [pltpu.make_async_copy(part, raw.at[place], sems.at[place]) for place, part in enumerate(parts)]
     for copy in copies:
         copy.start()
-    x[...] = jnp.zeros_like(x)
+    tail = padded - ROWS
+    x[:, :, tail:, :] = jnp.zeros((x.shape[0], edge, ROWS, width), bf16)
+    x[6 * slots] = jnp.zeros((edge, padded, width), bf16)
     total[...] = jnp.zeros_like(total)
     total_fix[...] = jnp.zeros_like(total_fix)
     columns[0] = own_pot[...].T
@@ -584,19 +594,12 @@
     square_grid = level_count == orb_count == 4 and box_rows == half
     row0, col0 = (level * PAIR + pair) * box_rows, orb * own_width
 
-    slot_ids = jnp.arange(slots, dtype=jnp.int32)
-    own_ids = (level * PAIR + pair) * slots + slot_ids
-    none = 16 * slots
-    apart_ids = jnp.where(neighbours >= 0, neighbours - own_ids[:, None, None], none).reshape(slots, 6)
-    live = (slot_ids < box_counts[0]).astype(jnp.int32)
-    facts = jnp.concatenate([apart_ids, levels[:, None], live[:, None]], axis=1)
-    wide_facts = jnp.pad(facts.astype(f32), ((0, 0), (0, own_width - facts.shape[1])))
     own_pot = jnp.pad(potential, ((0, -slots % 8), (0, -coefficients % 128)))
     beside_pot = swap(own_pot, "pair", 1)
-    pack_meta = jnp.stack([pair, box_counts[0]]).astype(jnp.int32)
-    [theirs] = pack(pack_meta, orbitals, wide_facts, False)
-    pack_meta, theirs = lax.optimization_barrier((pack_meta, theirs))
-    mine, active = pack(pack_meta, orbitals, wide_facts, True)
+    own_base = (level * PAIR + pair) * slots
+    pack_meta = jnp.stack([pair, box_counts[0], own_base]).astype(jnp.int32)
+    theirs, mine = pack(pack_meta, neighbours.reshape(slots, 6), levels, orbitals)
+    active = orbitals
 
     far = {q: swap(active, "orb", q) for q in groups if q and q % 2 == 0}
     beside = swap(theirs, "pair", 1)
@@ -605,7 +608,7 @@
     first_beside, second_beside = trade(beside, "lvl", 0), trade(beside, "lvl", 1)
 
     def facts_of(packed):
-        return packed[:, fold, : facts.shape[1]].astype(f32).astype(jnp.int32)
+        return packed[:, fold, :8].astype(f32).astype(jnp.int32)
 
     side_facts = jnp.stack([facts_of(first_mine), facts_of(second_mine)])
     across_facts = swap(side_facts, "pair", 1)
@@ -618,7 +621,7 @@
             [mine, beside, first_mine, first_beside, second_mine, second_beside],
             beside_rest,
             matrices,
-            [facts, facts_of(beside), side_facts, across_facts],
+            [facts_of(mine), facts_of(beside), side_facts, across_facts],
             [own_pot, beside_pot],
         )
     )
@@ -650,7 +653,8 @@
         strip = lax.dynamic_slice_in_dim(strip, row0, box_rows, axis=0)
         return lax.dynamic_slice_in_dim(strip, col0, own_width, axis=1)
 
-    meta = jnp.stack([pair, level, orb]).astype(jnp.int32)
+    live_rows = box_counts[0] * coefficients
+    meta = jnp.stack([pair, slots * coefficients, live_rows]).astype(jnp.int32)
 
     place_meta = jnp.stack([level, pair]).astype(jnp.int32)
     right = kinetic(parts, place_meta, all_facts, pots, matrices, edge, coefficients, level_count)
@@ -685,12 +689,15 @@
         join = functools.partial(jnp.concatenate, axis=0)
         top, low = join(pieces[: level_count // 2]), join(pieces[level_count // 2 :])
         sent = along_levels(fock_blocks)
-        top, low = join([top, swap(top, "pair", 1)]), join([low, swap(low, "orb", 2)])
+        got = [swap(top, "pair", 1), swap(low, "orb", 2)]
+        got, sent[1] = lax.optimization_barrier((got, sent[1]))
+        top, low = join([top, got[0]]), join([low, got[1]])
         pieces = [top, swap(top, "orb", 2), low, swap(low, "pair", 1)]
-        pieces, sent = lax.optimization_barrier((pieces, sent))
+        pieces, sent[2] = lax.optimization_barrier((pieces, sent[2]))
         pieces += [swap(piece, "orb", 1) for piece in pieces]
         root_meta = jnp.stack([level, pair, orb]).astype(jnp.int32)
         inverse_root = root_of(root_meta, pieces, offset, all_width, level_count)
+        inverse_root, sent = lax.optimization_barrier((inverse_root, sent))
         share, kept, other = level_sum(fock_sum_kernel, meta, sent)
         to = [
             ((z * PAIR + y) * orb_count + o, (o * PAIR + y) * orb_count + z)

time: 206 us -> 196 us (0.951)
  waiting for transfers between devices: 68.3 us -> 55.2 us
  local copies, waits for them, and re-layouts: 5.1 us -> 10.3 us
    ppermute x31, waiting for transfers between devices: 62.5 us -> 49.7 us  [swap(): return lax.ppermute(value, axis, [(i, i ^ bit) for i in range(count)])]
    unnamed x29 -> x50, local copies, waits for them, and re-layouts: 2.25 us -> 7.71 us
    pallas_call x1, Pallas kernels: 17.8 us -> 20.4 us  [kinetic(): pl.pallas_call(functools.partial(kinetic_kernel, edge, slots, levels), ou...]
    ppermute x4, waiting for transfers between devices: 2.24 us -> 0.01 us  [trade(): return lax.ppermute(value, axis, pairs + [(b, a) for a, b in pairs])]
    pallas_call x2 -> x1, Pallas kernels: 4.46 us -> 3.2 us  [pack(): pl.pallas_call(pack_kernel, out_shape=[jax.ShapeDtypeStruct((slots, padde...]
  transfers between devices with their start and end apart: 36 -> 36, of which waited for: 10 -> 12; matrix products, arithmetic and copies ran while one was open for 4% -> 4% of each run, Pallas kernels for 19% -> 26%
where the time goes in v2:
time: 196 us; the launch traced here: 197 us
  starting transfers between devices  63.1 us (32%)
  Pallas kernels  61 us (31%)
  waiting for transfers between devices  55.2 us (28%)
  local copies, waits for them, and re-layouts  10.3 us (5%)
  other arithmetic  5.84 us (3%)
    ppermute x31, waiting for transfers between devices, swap(): return lax.ppermute(value, axis, [(i, i ^ bit) for i in range(count)])  49.7 us
    ppermute x31, starting transfers between devices, swap(): return lax.ppermute(value, axis, [(i, i ^ bit) for i in range(count)])  46.9 us
    pallas_call x1, Pallas kernels, kinetic(): pl.pallas_call(functools.partial(kinetic_kernel, edge, slots, levels), ou...  20.4 us
    pallas_call x2, Pallas kernels, box_fock(): pl.pallas_call(functools.partial(fock_kernel, side, counts), out_shape=ja...  15.9 us
    ppermute x1, starting transfers between devices, body(): lax.ppermute(share, BOX + ('orb',), to).astype(f32)  9.93 us
    pallas_call x2, Pallas kernels, box_correlation(): pl.pallas_call(functools.partial(correlation_kernel, share, counts), out_...  9.16 us
    pallas_call x1, Pallas kernels, root_of(): pl.pallas_call(functools.partial(root_kernel, levels), out_shape=jax.Shap...  8.64 us
    unnamed x50, local copies, waits for them, and re-layouts  7.71 us
  transfers between devices with their start and end apart: 36, of which 12 were waited for; matrix products, arithmetic and copies ran while one was open for 4% of the time, Pallas kernels for 26%

profile of v2, /device:TPU:2, one launch (start us, length us, event | category | flops | bytes accessed | tf_op | source)
XLA Modules:
  0.0 197.2 jit_solution(7235686910773011356)
XLA Ops:
  3.0 3.2 %pack.1 = (bf16[2,512,384]{2,1,0:T(8,128)(2,1)S(1)}, bf16[2,512,384]{2,1,0:T(8,128)(2,1)}) custom-call(s32[3]{0:T(128)S(1)} %pad_add_fusion.1.meta, s32[2,6]{1,0:T(2,128)S(1)} %reshape.73.neighbours, s32[2]{0:T(128)S(1)} %copy-done.19, bf16[2,1000,384]{2,1,0:T(8,128)(2,1)} %orbitals.1), custom_call_target="tpu_custom_call" | custom-call | tf_op jit(solution)/shard_map/pack/pallas_call | solution.py:66
  6.2 1.5 collective-permute-start.1
  7.8 1.6 collective-permute-start.2
  9.9 1.5 collective-permute-start.4
  12.6 1.2 convert_convert_fusion
  13.8 12.8 %collective-permute-done.1.beside.refs_1_ = bf16[2,512,384]{2,1,0:T(8,128)(2,1)S(1)} collective-permute-done((bf16[2,512,384]{2,1,0:T(8,128)(2,1)S(1)}, bf16[2,512,384]{2,1,0:T(8,128)(2,1)S(1)}, u32[]{:S(2)}, u32[]{:S(2)}) %collective-permute-start.1) | collective-permute-done | bytes 786464 | tf_op jit(solution)/shard_map/ppermute | solution.py:19
  26.7 1.6 collective-permute-start.3
  28.3 1.5 collective-permute-start.5
  30.4 1.4 reshape.74.stacked
  34.0 1.0 matrices.1
  35.6 1.5 collective-permute-start.8
  37.9 5.2 %collective-permute-done.8.refs_7_ = f32[8,1024]{1,0:T(8,128)S(1)} collective-permute-done((f32[8,1024]{1,0:T(8,128)S(1)}, f32[8,1024]{1,0:T(8,128)S(1)}, u32[]{:S(2)}, u32[]{:S(2)}) %collective-permute-start.8) | collective-permute-done | bytes 32800 | tf_op jit(solution)/shard_map/ppermute | solution.py:19
  43.1 1.5 collective-permute-start.7
  44.6 0.9 copy-done
  45.5 0.9 copy-done.3
  46.7 1.1 copy-done.1
  47.8 1.1 copy-done.4
  49.6 1.0 unfold.1
  51.1 1.8 collective-permute-start.10
  53.5 20.4 %kinetic.1 = bf16[4,1000,576]{2,1,0:T(8,128)(2,1)} custom-call(s32[2]{0:T(128)S(1)} %copy-done.20, s32[2,8]{1,0:T(2,128)S(1)} %bitcast.33, s32[2,8]{1,0:T(2,128)S(1)} %bitcast.34, s32[2,2,8]{2,1,0:T(2,128)S(1)} %pad_add_fusion.side_facts, s32[2,2,8]{2,1,0:T(2,128)S(1)} %collective-permute-done.7.across_facts, ...), custom_call_target="tpu_custom_call" | custom-call | flops 20000000000 | bytes 40000000 | tf_op jit(solution)/shard_map/kinetic/pallas_call | solution.py:517
  74.5 4.8 %correlation.2.refs_6_ = f32[4,192,384]{2,1,0:T(8,128)S(1)} custom-call(s32[3]{0:T(128)S(1)} %copy-done.15, bf16[2000,384]{1,0:T(8,128)(2,1)} %bitcast.10.refs_0_, bf16[2000,384]{1,0:T(8,128)(2,1)} %bitcast.11.refs_1_, bf16[2000,384]{1,0:T(8,128)(2,1)S(1)} %bitcast.31, bf16[2000,384]{1,0:T(8,128)(2,1)} %bitcast.12.refs_3_), custom_call_target="tpu_custom_call" | custom-call | flops 1179648000 | bytes 6144000 | tf_op jit(solution)/shard_map/correlation/pallas_call | solution.py:157
  79.3 4.4 %correlation.3 = bf16[4,192,384]{2,1,0:T(8,128)(2,1)S(1)} custom-call(s32[3]{0:T(128)S(1)} %copy-done.15, bf16[2000,384]{1,0:T(8,128)(2,1)S(1)} %get-tuple-element.94.refs_0_, bf16[2000,384]{1,0:T(8,128)(2,1)} %collective-permute-done.11.refs_1_, bf16[1008,384]{1,0:T(8,128)(2,1)} %collective-permute-done.9.refs_2_, ...), custom_call_target="tpu_custom_call" | custom-call | flops 1179648000 | bytes 6144000 | tf_op jit(solution)/shard_map/correlation/pallas_call | solution.py:157
  83.7 4.8 %collective-permute-start.16 = (bf16[192,384]{1,0:T(8,128)(2,1)S(1)}, bf16[192,384]{1,0:T(8,128)(2,1)S(1)}, u32[]{:S(2)}, u32[]{:S(2)}) collective-permute-start(bf16[192,384]{1,0:T(8,128)(2,1)S(1)} %get-tuple-element.137), channel_id=1, source_target_pairs={{0,8},{8,0},{16,24},{24,16},{1,9},{9,1},{17,25},{25,17},{2,10},{10... | collective-permute-start | bytes 442376 | tf_op jit(solution)/shard_map/ppermute | solution.py:19
  88.5 9.2 %collective-permute-start.17 = (bf16[192,384]{1,0:T(8,128)(2,1)S(1)}, bf16[192,384]{1,0:T(8,128)(2,1)S(1)}, u32[]{:S(2)}, u32[]{:S(2)}) collective-permute-start(bf16[192,384]{1,0:T(8,128)(2,1)S(1)} %get-tuple-element.136), channel_id=1, source_target_pairs={{0,16},{8,24},{16,0},{24,8},{1,17},{9,25},{17,1},{25,9},{2,18},{10... | collective-permute-start | bytes 442376 | tf_op jit(solution)/shard_map/ppermute | solution.py:19
  97.8 1.4 collective-permute-start.18
  99.1 8.2 %fock.2.refs_6_ = f32[4,576,384]{2,1,0:T(8,128)S(1)} custom-call(bf16[2,2000,576]{2,1,0:T(8,128)(2,1)} %bitcast.35, bf16[2000,384]{1,0:T(8,128)(2,1)} %bitcast.10.refs_0_, bf16[2000,384]{1,0:T(8,128)(2,1)} %bitcast.11.refs_1_, bf16[2000,384]{1,0:T(8,128)(2,1)S(1)} %bitcast.32, bf16[2000,384]{1,0:T(8,128)(2,1)} %bitcast.12.refs_3_), custom_call_target="tpu_custom_call" | custom-call | flops 3538944000 | bytes 6144000 | tf_op jit(solution)/shard_map/fock/pallas_call | solution.py:209
  107.3 2.2 %collective-permute-done.18.refs_3_ = bf16[192,384]{1,0:T(8,128)(2,1)S(1)} collective-permute-done((bf16[192,384]{1,0:T(8,128)(2,1)S(1)}, bf16[192,384]{1,0:T(8,128)(2,1)S(1)}, u32[]{:S(2)}, u32[]{:S(2)}) %collective-permute-start.18) | collective-permute-done | bytes 147488 | tf_op jit(solution)/shard_map/ppermute | solution.py:19
  110.3 2.7 %collective-permute-start.19 = (bf16[192,384]{1,0:T(8,128)(2,1)S(1)}, bf16[192,384]{1,0:T(8,128)(2,1)S(1)}, u32[]{:S(2)}, u32[]{:S(2)}) collective-permute-start(bf16[192,384]{1,0:T(8,128)(2,1)S(1)} %get-tuple-element.107), channel_id=1, source_target_pairs={{0,8},{8,0},{16,24},{24,16},{1,9},{9,1},{17,25},{25,17},{2,10},{10... | collective-permute-start | bytes 442376 | tf_op jit(solution)/shard_map/ppermute | solution.py:19
  113.1 2.0 %collective-permute-start.20 = (bf16[192,384]{1,0:T(8,128)(2,1)S(1)}, bf16[192,384]{1,0:T(8,128)(2,1)S(1)}, u32[]{:S(2)}, u32[]{:S(2)}) collective-permute-start(bf16[192,384]{1,0:T(8,128)(2,1)S(1)} %get-tuple-element.107), channel_id=1, source_target_pairs={{0,16},{8,24},{16,0},{24,8},{1,17},{9,25},{17,1},{25,9},{2,18},{10... | collective-permute-start | bytes 442376 | tf_op jit(solution)/shard_map/ppermute | solution.py:19
  115.1 1.4 collective-permute-start.21
  116.5 1.5 collective-permute-start.22
  118.0 7.7 %fock.3 = bf16[4,3,192,384]{3,2,1,0:T(8,128)(2,1)S(1)} custom-call(bf16[2,2000,576]{2,1,0:T(8,128)(2,1)} %bitcast.36, bf16[2000,384]{1,0:T(8,128)(2,1)S(1)} %get-tuple-element.94.refs_0_, bf16[2000,384]{1,0:T(8,128)(2,1)} %collective-permute-done.11.refs_1_, bf16[1008,384]{1,0:T(8,128)(2,1)} %collective-permute-done.9.refs_2_, ...), custom_call_target="tpu_custom_call" | custom-call | flops 3538944000 | bytes 6144000 | tf_op jit(solution)/shard_map/fock/pallas_call | solution.py:209
  125.8 0.9 convert_add_fusion
  126.9 1.5 collective-permute-start.24
  128.6 2.8 %collective-permute-start.25 = (bf16[3,192,384]{2,1,0:T(8,128)(2,1)S(1)}, bf16[3,192,384]{2,1,0:T(8,128)(2,1)S(1)}, u32[]{:S(2)}, u32[]{:S(2)}) collective-permute-start(bf16[3,192,384]{2,1,0:T(8,128)(2,1)S(1)} %get-tuple-element.134), channel_id=1, source_target_pairs={{0,8},{8,0},{16,24},{24,16},{1,9},{9,1},{17,25},{25,17},{2,10},{10... | collective-permute-start | bytes 1327112 | tf_op jit(solution)/shard_map/ppermute | solution.py:19
  132.2 2.7 %collective-permute-done.24 = bf16[384,384]{1,0:T(8,128)(2,1)S(1)} collective-permute-done((bf16[384,384]{1,0:T(8,128)(2,1)S(1)}, bf16[384,384]{1,0:T(8,128)(2,1)S(1)}, u32[]{:S(2)}, u32[]{:S(2)}) %collective-permute-start.24) | collective-permute-done | bytes 294944 | tf_op jit(solution)/shard_map/ppermute | solution.py:19
  134.8 4.4 %collective-permute-done.23 = bf16[384,384]{1,0:T(8,128)(2,1)S(1)} collective-permute-done((bf16[384,384]{1,0:T(8,128)(2,1)S(1)}, bf16[384,384]{1,0:T(8,128)(2,1)S(1)}, u32[]{:S(2)}, u32[]{:S(2)}) %collective-permute-start.23) | collective-permute-done | bytes 294944 | tf_op jit(solution)/shard_map/ppermute | solution.py:19
  139.3 1.6 collective-permute-done.25.refs_1_
  141.6 1.6 collective-permute-start.26
  143.1 3.7 %collective-permute-start.28 = (bf16[3,192,384]{2,1,0:T(8,128)(2,1)S(1)}, bf16[3,192,384]{2,1,0:T(8,128)(2,1)S(1)}, u32[]{:S(2)}, u32[]{:S(2)}) collective-permute-start(bf16[3,192,384]{2,1,0:T(8,128)(2,1)S(1)} %get-tuple-element.133), channel_id=1, source_target_pairs={{0,16},{8,24},{16,0},{24,8},{1,17},{9,25},{17,1},{25,9},{2,18},{10... | collective-permute-start | bytes 1327112 | tf_op jit(solution)/shard_map/ppermute | solution.py:19
  146.8 17.5 %collective-permute-done.28.refs_2_ = bf16[3,192,384]{2,1,0:T(8,128)(2,1)S(1)} collective-permute-done((bf16[3,192,384]{2,1,0:T(8,128)(2,1)S(1)}, bf16[3,192,384]{2,1,0:T(8,128)(2,1)S(1)}, u32[]{:S(2)}, u32[]{:S(2)}) %collective-permute-start.28) | collective-permute-done | bytes 442400 | tf_op jit(solution)/shard_map/ppermute | solution.py:19
  165.3 2.6 %collective-permute-start.33 = (bf16[3,192,384]{2,1,0:T(8,128)(2,1)S(1)}, bf16[3,192,384]{2,1,0:T(8,128)(2,1)S(1)}, u32[]{:S(2)}, u32[]{:S(2)}) collective-permute-start(bf16[3,192,384]{2,1,0:T(8,128)(2,1)S(1)} %get-tuple-element.131), channel_id=1, source_target_pairs={{0,24},{8,16},{16,8},{24,0},{1,25},{9,17},{17,9},{25,1},{2,26},{10... | collective-permute-start | bytes 1327112 | tf_op jit(solution)/shard_map/ppermute | solution.py:19
  168.9 8.6 %root.1 = f32[192,384]{1,0:T(8,128)} custom-call(s32[3]{0:T(128)S(1)} %pad_add_fusion.4.meta, bf16[768,384]{1,0:T(8,128)(2,1)S(1)} %constant_dynamic-update-slice_fusion.refs_0_, bf16[768,384]{1,0:T(8,128)(2,1)S(1)} %collective-permute-done.26.refs_1_, bf16[768,384]{1,0:T(8,128)(2,1)S(1)} %constant_dynamic-update-slice_fusion.3.refs_2_, ...), custom_call_target="tpu_custom_call" | custom-call | flops 3623878656 | bytes 9437184 | tf_op jit(solution)/shard_map/root/pallas_call | solution.py:294
  177.5 1.9 collective-permute-done.33.refs_3_
  179.4 0.9 level_sum.3
  180.9 9.9 %collective-permute-start.35 = (bf16[192,384]{1,0:T(8,128)(2,1)S(1)}, bf16[192,384]{1,0:T(8,128)(2,1)S(1)}, u32[]{:S(2)}, u32[]{:S(2)}) collective-permute-start(bf16[192,384]{1,0:T(8,128)(2,1)S(1)} %get-tuple-element.127), channel_id=1, source_target_pairs={{0,0},{1,8},{2,16},{3,24},{4,4},{5,12},{6,20},{7,28},{8,1},{9,9},{... | collective-permute-start | bytes 442376 | tf_op jit(solution)/shard_map/ppermute | solution.py:708
  190.9 5.5 %collective-permute-done.35 = bf16[192,384]{1,0:T(8,128)(2,1)S(1)} collective-permute-done((bf16[192,384]{1,0:T(8,128)(2,1)S(1)}, bf16[192,384]{1,0:T(8,128)(2,1)S(1)}, u32[]{:S(2)}, u32[]{:S(2)}) %collective-permute-start.35) | collective-permute-done | bytes 147488 | tf_op jit(solution)/shard_map/ppermute | solution.py:708
  196.4 0.8 maximum_add_fusion
  (110 shorter events, 15.3 us)
Async XLA Ops:
  0.6 31.9 %copy-start.10 = (bf16[112,10]{1,0:T(8,128)(2,1)S(1)}, bf16[112,10]{1,0:T(8,128)(2,1)}, u32[]{:S(2)}) copy-start(bf16[112,10]{1,0:T(8,128)(2,1)} %constant.70.clone.refs_0_) | copy-start | bytes 6724
  0.6 31.8 %copy-start.12 = (bf16[30,336]{1,0:T(8,128)(2,1)S(1)}, bf16[30,336]{1,0:T(8,128)(2,1)}, u32[]{:S(2)}) copy-start(bf16[30,336]{1,0:T(8,128)(2,1)} %constant.71.clone.refs_1_) | copy-start | bytes 60484
  0.7 31.8 %copy-start.6 = (f32[112,112]{1,0:T(8,128)S(1)}, f32[112,112]{1,0:T(8,128)}, u32[]{:S(2)}) copy-start(f32[112,112]{1,0:T(8,128)} %constant.72.clone.refs_2_) | copy-start | bytes 150532
  0.7 31.8 %copy-start.11 = (bf16[112,10]{1,0:T(8,128)(2,1)S(1)}, bf16[112,10]{1,0:T(8,128)(2,1)}, u32[]{:S(2)}) copy-start(bf16[112,10]{1,0:T(8,128)(2,1)} %constant.73.clone.refs_3_) | copy-start | bytes 6724
  0.7 31.8 %copy-start.7 = (f32[112,112]{1,0:T(8,128)S(1)}, f32[112,112]{1,0:T(8,128)}, u32[]{:S(2)}) copy-start(f32[112,112]{1,0:T(8,128)} %constant.75.clone.refs_5_) | copy-start | bytes 150532
  0.7 31.8 %copy-start.8 = (bf16[160,10]{1,0:T(8,128)(2,1)S(1)}, bf16[160,10]{1,0:T(8,128)(2,1)}, u32[]{:S(2)}) copy-start(bf16[160,10]{1,0:T(8,128)(2,1)} %constant.76.clone.refs_6_) | copy-start | bytes 9604
  0.7 31.8 %copy-start.9 = (bf16[30,480]{1,0:T(8,128)(2,1)S(1)}, bf16[30,480]{1,0:T(8,128)(2,1)}, u32[]{:S(2)}) copy-start(bf16[30,480]{1,0:T(8,128)(2,1)} %constant.77.clone.refs_7_) | copy-start | bytes 86404
  0.7 31.8 %copy-start.5 = (f32[160,160]{1,0:T(8,128)S(1)}, f32[160,160]{1,0:T(8,128)}, u32[]{:S(2)}) copy-start(f32[160,160]{1,0:T(8,128)} %constant.78.clone.refs_8_) | copy-start | bytes 307204
  3.0 26.8 %copy-start.16 = (s32[3]{0:T(128)}, s32[3]{0:T(128)S(1)}, u32[]{:S(2)}) copy-start(s32[3]{0:T(128)S(1)} %pad_add_fusion.1.meta) | copy-start | bytes 40
  3.0 27.4 %copy-start.21 = (bf16[3,10,10]{2,0,1:T(4,128)(2,1)S(1)}, bf16[3,10,10]{2,0,1:T(4,128)(2,1)}, u32[]{:S(2)}) copy-start(bf16[3,10,10]{2,0,1:T(4,128)(2,1)} %param.17) | copy-start | bytes 1804
  6.2 20.4 %collective-permute-start.1 = (bf16[2,512,384]{2,1,0:T(8,128)(2,1)S(1)}, bf16[2,512,384]{2,1,0:T(8,128)(2,1)S(1)}, u32[]{:S(2)}, u32[]{:S(2)}) collective-permute-start(bf16[2,512,384]{2,1,0:T(8,128)(2,1)S(1)} %get-tuple-element.67), channel_id=1, source_target_pairs={{0,4},{4,0},{1,5},{5,1},{2,6},{6,2},{3,7},{7,3},{8,12},{12,8},{9,1... | collective-permute-start | bytes 2359304 | tf_op jit(solution)/shard_map/ppermute | solution.py:19
  7.8 20.5 %collective-permute-start.2 = (bf16[2,512,384]{2,1,0:T(8,128)(2,1)}, bf16[2,512,384]{2,1,0:T(8,128)(2,1)}, u32[]{:S(2)}, u32[]{:S(2)}) collective-permute-start(bf16[2,512,384]{2,1,0:T(8,128)(2,1)} %get-tuple-element.81.refs_0_), channel_id=1, source_target_pairs={{0,8},{16,24},{8,0},{24,16},{1,9},{17,25},{9,1},{25,17},{2,10},{18... | collective-permute-start | bytes 2359304 | tf_op jit(solution)/shard_map/ppermute | solution.py:24
  9.3 37.3 %collective-permute-start = (bf16[2,1000,384]{2,1,0:T(8,128)(2,1)}, bf16[2,1000,384]{2,1,0:T(8,128)(2,1)S(1)}, u32[]{:S(2)}, u32[]{:S(2)}) collective-permute-start(bf16[2,1000,384]{2,1,0:T(8,128)(2,1)} %orbitals.1), channel_id=1, source_target_pairs={{0,2},{1,3},{2,0},{3,1},{4,6},{5,7},{6,4},{7,5},{8,10},{9,11},{10,... | collective-permute-start | bytes 4608008 | tf_op jit(solution)/shard_map/ppermute | solution.py:19
  9.9 25.8 %collective-permute-start.4 = (bf16[2,512,384]{2,1,0:T(8,128)(2,1)}, bf16[2,512,384]{2,1,0:T(8,128)(2,1)}, u32[]{:S(2)}, u32[]{:S(2)}) collective-permute-start(bf16[2,512,384]{2,1,0:T(8,128)(2,1)} %get-tuple-element.81.refs_0_), channel_id=1, source_target_pairs={{8,16},{16,8},{9,17},{17,9},{10,18},{18,10},{11,19},{19,11},{12,20... | collective-permute-start | bytes 2359304 | tf_op jit(solution)/shard_map/ppermute | solution.py:24
  11.4 34.1 %collective-permute-start.6 = (bf16[2,512,384]{2,1,0:T(8,128)(2,1)}, bf16[2,512,384]{2,1,0:T(8,128)(2,1)S(1)}, u32[]{:S(2)}, u32[]{:S(2)}) collective-permute-start(bf16[2,512,384]{2,1,0:T(8,128)(2,1)} %get-tuple-element.81.refs_0_), channel_id=1, source_target_pairs={{0,4},{4,0},{1,5},{5,1},{2,6},{6,2},{3,7},{7,3},{8,12},{12,8},{9,1... | collective-permute-start | bytes 2359304 | tf_op jit(solution)/shard_map/ppermute | solution.py:19
  26.7 20.0 %collective-permute-start.3 = (bf16[2,512,384]{2,1,0:T(8,128)(2,1)S(1)}, bf16[2,512,384]{2,1,0:T(8,128)(2,1)}, u32[]{:S(2)}, u32[]{:S(2)}) collective-permute-start(bf16[2,512,384]{2,1,0:T(8,128)(2,1)S(1)} %collective-permute-done.1.beside.refs_1_), channel_id=1, source_target_pairs={{0,8},{16,24},{8,0},{24,16},{1,9},{17,25},{9,1},{25,17},{2,10},{18... | collective-permute-start | bytes 2359304 | tf_op jit(solution)/shard_map/ppermute | solution.py:24
  28.3 18.4 %collective-permute-start.5 = (bf16[2,512,384]{2,1,0:T(8,128)(2,1)S(1)}, bf16[2,512,384]{2,1,0:T(8,128)(2,1)}, u32[]{:S(2)}, u32[]{:S(2)}) collective-permute-start(bf16[2,512,384]{2,1,0:T(8,128)(2,1)S(1)} %collective-permute-done.1.beside.refs_1_), channel_id=1, source_target_pairs={{8,16},{16,8},{9,17},{17,9},{10,18},{18,10},{11,19},{19,11},{12,20... | collective-permute-start | bytes 2359304 | tf_op jit(solution)/shard_map/ppermute | solution.py:24
  35.6 7.4 %collective-permute-start.8 = (f32[8,1024]{1,0:T(8,128)S(1)}, f32[8,1024]{1,0:T(8,128)S(1)}, u32[]{:S(2)}, u32[]{:S(2)}) collective-permute-start(f32[8,1024]{1,0:T(8,128)S(1)} %pad.4.refs_6_), channel_id=1, source_target_pairs={{0,4},{4,0},{1,5},{5,1},{2,6},{6,2},{3,7},{7,3},{8,12},{12,8},{9,1... | collective-permute-start | bytes 98312 | tf_op jit(solution)/shard_map/ppermute | solution.py:19
  43.1 3.6 %collective-permute-start.7 = (s32[2,2,8]{2,1,0:T(2,128)S(1)}, s32[2,2,8]{2,1,0:T(2,128)S(1)}, u32[]{:S(2)}, u32[]{:S(2)}) collective-permute-start(s32[2,2,8]{2,1,0:T(2,128)S(1)} %pad_add_fusion.side_facts), channel_id=1, source_target_pairs={{0,4},{4,0},{1,5},{5,1},{2,6},{6,2},{3,7},{7,3},{8,12},{12,8},{9,1... | collective-permute-start | bytes 392 | tf_op jit(solution)/shard_map/ppermute | solution.py:19
  49.6 3.8 %copy-start.20 = (s32[2]{0:T(128)S(1)}, s32[2]{0:T(128)}, u32[]{:S(2)}) copy-start(s32[2]{0:T(128)} %pad_add_fusion.2.place_meta) | copy-start | bytes 28
  50.7 23.2 %collective-permute-start.9 = (bf16[1008,384]{1,0:T(8,128)(2,1)S(1)}, bf16[1008,384]{1,0:T(8,128)(2,1)}, u32[]{:S(2)}, u32[]{:S(2)}) collective-permute-start(bf16[1008,384]{1,0:T(8,128)(2,1)S(1)} %get-tuple-element.75), channel_id=1, source_target_pairs={{0,2},{1,3},{2,0},{3,1},{4,6},{5,7},{6,4},{7,5},{8,10},{9,11},{10,... | collective-permute-start | bytes 2322440 | tf_op jit(solution)/shard_map/ppermute | solution.py:19
  51.0 23.4 %collective-permute-start.15 = (bf16[2,1000,384]{2,1,0:T(8,128)(2,1)S(1)}, bf16[2,1000,384]{2,1,0:T(8,128)(2,1)}, u32[]{:S(2)}, u32[]{:S(2)}) collective-permute-start(bf16[2,1000,384]{2,1,0:T(8,128)(2,1)S(1)} %collective-permute-done), channel_id=1, source_target_pairs={{0,1},{1,0},{2,3},{3,2},{4,5},{5,4},{6,7},{7,6},{8,9},{9,8},{10,11... | collective-permute-start | bytes 4608008 | tf_op jit(solution)/shard_map/ppermute | solution.py:19
  51.1 22.7 %collective-permute-start.10 = (bf16[992,384]{1,0:T(8,128)(2,1)S(1)}, bf16[992,384]{1,0:T(8,128)(2,1)}, u32[]{:S(2)}, u32[]{:S(2)}) collective-permute-start(bf16[992,384]{1,0:T(8,128)(2,1)S(1)} %slice.23), channel_id=1, source_target_pairs={{0,4},{4,0},{1,5},{5,1},{2,6},{6,2},{3,7},{7,3},{8,12},{12,8},{9,1... | collective-permute-start | bytes 2285576 | tf_op jit(solution)/shard_map/ppermute | solution.py:19
  52.9 21.5 %collective-permute-start.14 = (bf16[2,1000,384]{2,1,0:T(8,128)(2,1)}, bf16[2,1000,384]{2,1,0:T(8,128)(2,1)}, u32[]{:S(2)}, u32[]{:S(2)}) collective-permute-start(bf16[2,1000,384]{2,1,0:T(8,128)(2,1)} %orbitals.1), channel_id=1, source_target_pairs={{0,1},{1,0},{2,3},{3,2},{4,5},{5,4},{6,7},{7,6},{8,9},{9,8},{10,11... | collective-permute-start | bytes 4608008 | tf_op jit(solution)/shard_map/ppermute | solution.py:19
  53.2 21.3 %copy-start.15 = (s32[3]{0:T(128)S(1)}, s32[3]{0:T(128)}, u32[]{:S(2)}) copy-start(s32[3]{0:T(128)} %pad_add_fusion.3.meta) | copy-start | bytes 40
  53.2 26.1 %collective-permute-start.11 = (bf16[2000,384]{1,0:T(8,128)(2,1)S(1)}, bf16[2000,384]{1,0:T(8,128)(2,1)}, u32[]{:S(2)}, u32[]{:S(2)}) collective-permute-start(bf16[2000,384]{1,0:T(8,128)(2,1)S(1)} %get-tuple-element.94.refs_0_), channel_id=1, source_target_pairs={{0,1},{1,0},{2,3},{3,2},{4,5},{5,4},{6,7},{7,6},{8,9},{9,8},{10,11... | collective-permute-start | bytes 4608008 | tf_op jit(solution)/shard_map/ppermute | solution.py:19
  73.8 5.4 %collective-permute-start.12 = (bf16[1008,384]{1,0:T(8,128)(2,1)}, bf16[1008,384]{1,0:T(8,128)(2,1)}, u32[]{:S(2)}, u32[]{:S(2)}) collective-permute-start(bf16[1008,384]{1,0:T(8,128)(2,1)} %collective-permute-done.9.refs_2_), channel_id=1, source_target_pairs={{0,1},{1,0},{2,3},{3,2},{4,5},{5,4},{6,7},{7,6},{8,9},{9,8},{10,11... | collective-permute-start | bytes 2322440 | tf_op jit(solution)/shard_map/ppermute | solution.py:19
  74.1 5.1 %collective-permute-start.13 = (bf16[992,384]{1,0:T(8,128)(2,1)}, bf16[992,384]{1,0:T(8,128)(2,1)}, u32[]{:S(2)}, u32[]{:S(2)}) collective-permute-start(bf16[992,384]{1,0:T(8,128)(2,1)} %collective-permute-done.10.refs_3_), channel_id=1, source_target_pairs={{0,1},{1,0},{2,3},{3,2},{4,5},{5,4},{6,7},{7,6},{8,9},{9,8},{10,11... | collective-permute-start | bytes 2285576 | tf_op jit(solution)/shard_map/ppermute | solution.py:19
  83.7 23.6 %collective-permute-start.16 = (bf16[192,384]{1,0:T(8,128)(2,1)S(1)}, bf16[192,384]{1,0:T(8,128)(2,1)S(1)}, u32[]{:S(2)}, u32[]{:S(2)}) collective-permute-start(bf16[192,384]{1,0:T(8,128)(2,1)S(1)} %get-tuple-element.137), channel_id=1, source_target_pairs={{0,8},{8,0},{16,24},{24,16},{1,9},{9,1},{17,25},{25,17},{2,10},{10... | collective-permute-start | bytes 442376 | tf_op jit(solution)/shard_map/ppermute | solution.py:19
  88.5 18.8 %collective-permute-start.17 = (bf16[192,384]{1,0:T(8,128)(2,1)S(1)}, bf16[192,384]{1,0:T(8,128)(2,1)S(1)}, u32[]{:S(2)}, u32[]{:S(2)}) collective-permute-start(bf16[192,384]{1,0:T(8,128)(2,1)S(1)} %get-tuple-element.136), channel_id=1, source_target_pairs={{0,16},{8,24},{16,0},{24,8},{1,17},{9,25},{17,1},{25,9},{2,18},{10... | collective-permute-start | bytes 442376 | tf_op jit(solution)/shard_map/ppermute | solution.py:19
  97.8 11.8 %collective-permute-start.18 = (bf16[192,384]{1,0:T(8,128)(2,1)S(1)}, bf16[192,384]{1,0:T(8,128)(2,1)S(1)}, u32[]{:S(2)}, u32[]{:S(2)}) collective-permute-start(bf16[192,384]{1,0:T(8,128)(2,1)S(1)} %get-tuple-element.135), channel_id=1, source_target_pairs={{0,24},{8,16},{16,8},{24,0},{1,25},{9,17},{17,9},{25,1},{2,26},{10... | collective-permute-start | bytes 442376 | tf_op jit(solution)/shard_map/ppermute | solution.py:19
  110.3 16.3 %collective-permute-start.19 = (bf16[192,384]{1,0:T(8,128)(2,1)S(1)}, bf16[192,384]{1,0:T(8,128)(2,1)S(1)}, u32[]{:S(2)}, u32[]{:S(2)}) collective-permute-start(bf16[192,384]{1,0:T(8,128)(2,1)S(1)} %get-tuple-element.107), channel_id=1, source_target_pairs={{0,8},{8,0},{16,24},{24,16},{1,9},{9,1},{17,25},{25,17},{2,10},{10... | collective-permute-start | bytes 442376 | tf_op jit(solution)/shard_map/ppermute | solution.py:19
  113.1 13.8 %collective-permute-start.20 = (bf16[192,384]{1,0:T(8,128)(2,1)S(1)}, bf16[192,384]{1,0:T(8,128)(2,1)S(1)}, u32[]{:S(2)}, u32[]{:S(2)}) collective-permute-start(bf16[192,384]{1,0:T(8,128)(2,1)S(1)} %get-tuple-element.107), channel_id=1, source_target_pairs={{0,16},{8,24},{16,0},{24,8},{1,17},{9,25},{17,1},{25,9},{2,18},{10... | collective-permute-start | bytes 442376 | tf_op jit(solution)/shard_map/ppermute | solution.py:19
  115.1 11.8 %collective-permute-start.21 = (bf16[192,384]{1,0:T(8,128)(2,1)S(1)}, bf16[192,384]{1,0:T(8,128)(2,1)S(1)}, u32[]{:S(2)}, u32[]{:S(2)}) collective-permute-start(bf16[192,384]{1,0:T(8,128)(2,1)S(1)} %get-tuple-element.107), channel_id=1, source_target_pairs={{0,24},{8,16},{16,8},{24,0},{1,25},{9,17},{17,9},{25,1},{2,26},{10... | collective-permute-start | bytes 442376 | tf_op jit(solution)/shard_map/ppermute | solution.py:19
  116.5 9.3 %collective-permute-start.22 = (f32[192,192]{1,0:T(8,128)S(1)}, f32[192,192]{1,0:T(8,128)S(1)}, u32[]{:S(2)}, u32[]{:S(2)}) collective-permute-start(f32[192,192]{1,0:T(8,128)S(1)} %get-tuple-element.106), channel_id=1, source_target_pairs={{0,4},{4,0},{1,5},{5,1},{2,6},{6,2},{3,7},{7,3},{8,12},{12,8},{9,1... | collective-permute-start | bytes 442376 | tf_op jit(solution)/shard_map/ppermute | solution.py:19
  126.9 7.9 %collective-permute-start.24 = (bf16[384,384]{1,0:T(8,128)(2,1)S(1)}, bf16[384,384]{1,0:T(8,128)(2,1)S(1)}, u32[]{:S(2)}, u32[]{:S(2)}) collective-permute-start(bf16[384,384]{1,0:T(8,128)(2,1)S(1)} %pad_maximum_fusion.2), channel_id=1, source_target_pairs={{0,2},{1,3},{2,0},{3,1},{4,6},{5,7},{6,4},{7,5},{8,10},{9,11},{10,... | collective-permute-start | bytes 884744 | tf_op jit(solution)/shard_map/ppermute | solution.py:19
  128.6 12.2 %collective-permute-start.25 = (bf16[3,192,384]{2,1,0:T(8,128)(2,1)S(1)}, bf16[3,192,384]{2,1,0:T(8,128)(2,1)S(1)}, u32[]{:S(2)}, u32[]{:S(2)}) collective-permute-start(bf16[3,192,384]{2,1,0:T(8,128)(2,1)S(1)} %get-tuple-element.134), channel_id=1, source_target_pairs={{0,8},{8,0},{16,24},{24,16},{1,9},{9,1},{17,25},{25,17},{2,10},{10... | collective-permute-start | bytes 1327112 | tf_op jit(solution)/shard_map/ppermute | solution.py:19
  131.4 7.8 %collective-permute-start.23 = (bf16[384,384]{1,0:T(8,128)(2,1)S(1)}, bf16[384,384]{1,0:T(8,128)(2,1)S(1)}, u32[]{:S(2)}, u32[]{:S(2)}) collective-permute-start(bf16[384,384]{1,0:T(8,128)(2,1)S(1)} %pad_maximum_fusion.1), channel_id=1, source_target_pairs={{0,4},{4,0},{1,5},{5,1},{2,6},{6,2},{3,7},{7,3},{8,12},{12,8},{9,1... | collective-permute-start | bytes 884744 | tf_op jit(solution)/shard_map/ppermute | solution.py:19
  140.9 23.4 %collective-permute-start.27 = (bf16[768,384]{1,0:T(8,128)(2,1)S(1)}, bf16[768,384]{1,0:T(8,128)(2,1)S(1)}, u32[]{:S(2)}, u32[]{:S(2)}) collective-permute-start(bf16[768,384]{1,0:T(8,128)(2,1)S(1)} %constant_dynamic-update-slice_fusion.3.refs_2_), channel_id=1, source_target_pairs={{0,4},{4,0},{1,5},{5,1},{2,6},{6,2},{3,7},{7,3},{8,12},{12,8},{9,1... | collective-permute-start | bytes 1769480 | tf_op jit(solution)/shard_map/ppermute | solution.py:19
  141.6 22.7 %collective-permute-start.26 = (bf16[768,384]{1,0:T(8,128)(2,1)S(1)}, bf16[768,384]{1,0:T(8,128)(2,1)S(1)}, u32[]{:S(2)}, u32[]{:S(2)}) collective-permute-start(bf16[768,384]{1,0:T(8,128)(2,1)S(1)} %constant_dynamic-update-slice_fusion.refs_0_), channel_id=1, source_target_pairs={{0,2},{1,3},{2,0},{3,1},{4,6},{5,7},{6,4},{7,5},{8,10},{9,11},{10,... | collective-permute-start | bytes 1769480 | tf_op jit(solution)/shard_map/ppermute | solution.py:19
  143.1 21.2 %collective-permute-start.28 = (bf16[3,192,384]{2,1,0:T(8,128)(2,1)S(1)}, bf16[3,192,384]{2,1,0:T(8,128)(2,1)S(1)}, u32[]{:S(2)}, u32[]{:S(2)}) collective-permute-start(bf16[3,192,384]{2,1,0:T(8,128)(2,1)S(1)} %get-tuple-element.133), channel_id=1, source_target_pairs={{0,16},{8,24},{16,0},{24,8},{1,17},{9,25},{17,1},{25,9},{2,18},{10... | collective-permute-start | bytes 1327112 | tf_op jit(solution)/shard_map/ppermute | solution.py:19
  164.3 3.7 %collective-permute-start.29 = (bf16[768,384]{1,0:T(8,128)(2,1)S(1)}, bf16[768,384]{1,0:T(8,128)(2,1)S(1)}, u32[]{:S(2)}, u32[]{:S(2)}) collective-permute-start(bf16[768,384]{1,0:T(8,128)(2,1)S(1)} %constant_dynamic-update-slice_fusion.refs_0_), channel_id=1, source_target_pairs={{0,1},{1,0},{2,3},{3,2},{4,5},{5,4},{6,7},{7,6},{8,9},{9,8},{10,11... | collective-permute-start | bytes 1769480 | tf_op jit(solution)/shard_map/ppermute | solution.py:19
  164.3 3.7 %collective-permute-start.30 = (bf16[768,384]{1,0:T(8,128)(2,1)S(1)}, bf16[768,384]{1,0:T(8,128)(2,1)S(1)}, u32[]{:S(2)}, u32[]{:S(2)}) collective-permute-start(bf16[768,384]{1,0:T(8,128)(2,1)S(1)} %collective-permute-done.26.refs_1_), channel_id=1, source_target_pairs={{0,1},{1,0},{2,3},{3,2},{4,5},{5,4},{6,7},{7,6},{8,9},{9,8},{10,11... | collective-permute-start | bytes 1769480 | tf_op jit(solution)/shard_map/ppermute | solution.py:19
  164.8 3.2 %collective-permute-start.31 = (bf16[768,384]{1,0:T(8,128)(2,1)S(1)}, bf16[768,384]{1,0:T(8,128)(2,1)S(1)}, u32[]{:S(2)}, u32[]{:S(2)}) collective-permute-start(bf16[768,384]{1,0:T(8,128)(2,1)S(1)} %constant_dynamic-update-slice_fusion.3.refs_2_), channel_id=1, source_target_pairs={{0,1},{1,0},{2,3},{3,2},{4,5},{5,4},{6,7},{7,6},{8,9},{9,8},{10,11... | collective-permute-start | bytes 1769480 | tf_op jit(solution)/shard_map/ppermute | solution.py:19
  164.9 4.0 %collective-permute-start.32 = (bf16[768,384]{1,0:T(8,128)(2,1)S(1)}, bf16[768,384]{1,0:T(8,128)(2,1)S(1)}, u32[]{:S(2)}, u32[]{:S(2)}) collective-permute-start(bf16[768,384]{1,0:T(8,128)(2,1)S(1)} %collective-permute-done.27.refs_3_), channel_id=1, source_target_pairs={{0,1},{1,0},{2,3},{3,2},{4,5},{5,4},{6,7},{7,6},{8,9},{9,8},{10,11... | collective-permute-start | bytes 1769480 | tf_op jit(solution)/shard_map/ppermute | solution.py:19
  165.3 14.0 %collective-permute-start.33 = (bf16[3,192,384]{2,1,0:T(8,128)(2,1)S(1)}, bf16[3,192,384]{2,1,0:T(8,128)(2,1)S(1)}, u32[]{:S(2)}, u32[]{:S(2)}) collective-permute-start(bf16[3,192,384]{2,1,0:T(8,128)(2,1)S(1)} %get-tuple-element.131), channel_id=1, source_target_pairs={{0,24},{8,16},{16,8},{24,0},{1,25},{9,17},{17,9},{25,1},{2,26},{10... | collective-permute-start | bytes 1327112 | tf_op jit(solution)/shard_map/ppermute | solution.py:19
  180.3 10.5 %collective-permute-start.34 = (f32[192,192]{1,0:T(8,128)S(1)}, f32[192,192]{1,0:T(8,128)S(1)}, u32[]{:S(2)}, u32[]{:S(2)}) collective-permute-start(f32[192,192]{1,0:T(8,128)S(1)} %get-tuple-element.126), channel_id=1, source_target_pairs={{0,4},{4,0},{1,5},{5,1},{2,6},{6,2},{3,7},{7,3},{8,12},{12,8},{9,1... | collective-permute-start | bytes 442376 | tf_op jit(solution)/shard_map/ppermute | solution.py:19
  180.9 15.5 %collective-permute-start.35 = (bf16[192,384]{1,0:T(8,128)(2,1)S(1)}, bf16[192,384]{1,0:T(8,128)(2,1)S(1)}, u32[]{:S(2)}, u32[]{:S(2)}) collective-permute-start(bf16[192,384]{1,0:T(8,128)(2,1)S(1)} %get-tuple-element.127), channel_id=1, source_target_pairs={{0,0},{1,8},{2,16},{3,24},{4,4},{5,12},{6,20},{7,28},{8,1},{9,9},{... | collective-permute-start | bytes 442376 | tf_op jit(solution)/shard_map/ppermute | solution.py:708
  (10 other events, 14.5 us)

commit v3 on v2

--- a/solution.py
+++ b/solution.py
@@ -32,7 +32,7 @@
     return pltpu.CompilerParams(vmem_limit_bytes=mebibytes * 1024 * 1024)
 
 
-def pack_kernel(meta, neighbours, levels, orbitals, theirs, mine):
+def pack_kernel(meta, neighbours, levels, orbitals, pot, theirs, mine):
     slots, coefficients, width = orbitals.shape
     half, fold = width // PAIR, coefficients // 2
     first = meta[0] == 0
@@ -54,29 +54,46 @@
         facts = facts.astype(f32).astype(bf16)
         for packed in (theirs, mine):
             packed[slot, fold : fold + 8, :] = facts
-            rest = packed.shape[1] - fold - 8
-            packed[slot, fold + 8 :, :] = jnp.zeros((rest, width), bf16)
-
-
-def pack(meta, neighbours, levels, orbitals):
+        row = fold + 8
+        for start in range(0, pot.shape[1], width):
+            exact = pot[slot : slot + 1, start : start + width]
+            for _ in range(3):
+                part = exact.astype(bf16)
+                exact = exact - part.astype(f32)
+                for packed in (theirs, mine):
+                    packed[slot, row : row + 1, :] = part
+                row += 1
+        for packed in (theirs, mine):
+            packed[slot, row:, :] = jnp.zeros((packed.shape[1] - row, width), bf16)
+
+
+def pack(meta, neighbours, levels, orbitals, pot):
     slots, coefficients, width = orbitals.shape
     fold = coefficients // 2
-    padded = (fold // ROWS + 1) * ROWS
+    padded = -(-(fold + 8 + 3 * (pot.shape[1] // width)) // ROWS) * ROWS
     vmem, smem = pl.BlockSpec(memory_space=pltpu.VMEM), pl.BlockSpec(memory_space=pltpu.SMEM)
     return pl.pallas_call(
         pack_kernel,
         out_shape=[jax.ShapeDtypeStruct((slots, padded, width), bf16)] * 2,
-        in_specs=[smem, smem, smem, vmem],
+        in_specs=[smem, smem, smem, vmem, vmem],
         out_specs=[vmem, vmem],
         compiler_params=params(24),
         name="pack",
-    )(meta, neighbours, levels, orbitals)
-
-
-def unfold_kernel(fold, meta, beside, rest, whole, top):
+    )(meta, neighbours, levels, orbitals, pot)
+
+
+def unfold_kernel(fold, meta, beside_in, rest_in, whole, top, beside, rest, sems):
+    copies = [
+        pltpu.make_async_copy(source, target, sems.at[i])
+        for i, (source, target) in enumerate(((beside_in, beside), (rest_in, rest)))
+    ]
+    for copy in copies:
+        copy.start()
     slots, _, width = beside.shape
     half = width // PAIR
     first = meta[0] == 0
+    for copy in copies:
+        copy.wait()
     for slot in range(slots):
         for part in range(2):
             lanes = slice(part * half, (part + 1) * half)
@@ -96,8 +113,13 @@
             jax.ShapeDtypeStruct((2 * slots * fold, width), bf16),
             jax.ShapeDtypeStruct((cut, width), bf16),
         ],
-        in_specs=[pl.BlockSpec(memory_space=pltpu.SMEM), vmem, vmem],
+        in_specs=[pl.BlockSpec(memory_space=pltpu.SMEM)] + [pl.BlockSpec(memory_space=pl.ANY)] * 2,
         out_specs=[vmem, vmem],
+        scratch_shapes=[
+            pltpu.VMEM(beside.shape, bf16),
+            pltpu.VMEM(beside.shape, bf16),
+            pltpu.SemaphoreType.DMA((2,)),
+        ],
         compiler_params=params(24),
         name="unfold",
     )(meta, beside, rest)
@@ -175,12 +197,14 @@
 
 
 def fock_kernel(side, counts, right, *refs):
-    refs, (out, held, raw, turned, sems, last_sem) = refs[:-6], refs[-6:]
-    lefts, before = grouped(refs, counts), refs[sum(counts) :]
+    outs, (held, raw, turned, sems, last_sem) = refs[sum(counts) : -5], refs[-5:]
+    lefts = grouped(refs, counts)
+    before, apart, sent, kept = outs if len(outs) == 4 else (None, None, None, None)
+    out = outs[-1]
     last = pltpu.make_async_copy(right.at[side], raw, last_sem)
     last.start()
     copies = load_left(lefts, held, sems)
-    half, width = out.shape[-2] // (1 if before else 3), out.shape[-1]
+    half, width = out.shape[-2] // (3 if before is None else 1), out.shape[-1]
     last.wait()
     turned[...] = raw[...].T
     for base in range(0, len(lefts), 2):
@@ -189,28 +213,37 @@
         wide = matmul(turned[...], held[:, base * width : (base + 2) * width])
         for q in (base, base + 1):
             total = wide[:, (q - base) * width : (q - base + 1) * width]
-            if before:
-                total = total + before[0][q]
-                main = total[:half] + total[half : 2 * half]
-                top = main.astype(bf16)
-                out[q, 0], out[q, 1] = top, (main - top.astype(f32)).astype(bf16)
-                out[q, 2] = total[2 * half :].astype(bf16)
-            else:
+            if before is None:
                 out[q] = total
-
-
-def box_fock(side, lefts, right, before):
+                continue
+            total = total + before[q]
+            main = total[:half] + total[half : 2 * half]
+            top = main.astype(bf16)
+            parts = (top, (main - top.astype(f32)).astype(bf16), total[2 * half :].astype(bf16))
+            distance = q ^ apart[0]
+
+            def store(target):
+                for i in range(3):
+                    target[lax.shift_right_logical(distance, 1), i] = parts[i]
+
+            pl.when(lax.rem(distance, 2) == 1)(functools.partial(store, sent))
+            pl.when(lax.rem(distance, 2) == 0)(functools.partial(store, kept))
+
+
+def box_fock(side, lefts, right, before, apart):
     depth, width = sum(piece.shape[0] for piece in lefts[0]), lefts[0][0].shape[1]
     counts = [len(pieces) for pieces in lefts]
     tall = right.shape[-1]
     anywhere, vmem = pl.BlockSpec(memory_space=pl.ANY), pl.BlockSpec(memory_space=pltpu.VMEM)
-    extra = [] if before is None else [before]
-    out = ((len(lefts), tall, width), f32) if before is None else ((len(lefts), 3, tall // 3, width), bf16)
+    extra = [] if before is None else [before, apart]
+    out = jax.ShapeDtypeStruct((len(lefts), tall, width), f32)
+    if before is not None:
+        out = [jax.ShapeDtypeStruct((len(lefts) // 2, 3, tall // 3, width), bf16)] * 2
     return pl.pallas_call(
         functools.partial(fock_kernel, side, counts),
-        out_shape=jax.ShapeDtypeStruct(*out),
-        in_specs=[anywhere] * (sum(counts) + 1) + [vmem] * len(extra),
-        out_specs=vmem,
+        out_shape=out,
+        in_specs=[anywhere] * (sum(counts) + 1) + [vmem, pl.BlockSpec(memory_space=pltpu.SMEM)][: len(extra)],
+        out_specs=vmem if before is None else [vmem, vmem],
         scratch_shapes=[
             pltpu.VMEM((depth, len(lefts) * width), bf16),
             pltpu.VMEM(right.shape[1:], bf16),
@@ -308,7 +341,7 @@
     )(meta, *pieces, offset)
 
 
-def fill_tables(slots, levels, place_meta, own_facts, beside_facts, side_facts, across_facts, table, scale):
+def fill_tables(slots, levels, place_meta, facts, table, scale):
     level, pair = place_meta[0], place_meta[1]
     even = lax.rem(level, 2) == 0
     none = 6 * slots
@@ -324,10 +357,10 @@
 
         def fact(c):
             if group < 2:
-                return (own_facts, beside_facts)[group][r, c]
+                return facts[group, r, c]
             swap_id = jnp.where(even, 1, 0) if group == 2 else jnp.where(even, 0, 1)
             near_pair = 1 if group == 2 else 0
-            return jnp.where(pair == near_pair, side_facts[swap_id, r, c], across_facts[swap_id, r, c])
+            return facts[2 + 2 * swap_id + jnp.where(pair == near_pair, 0, 1), r, c]
 
         box = (
             level * PAIR + pair,
@@ -350,10 +383,10 @@
         scale[index] = jnp.where(level_of == 0, 0.5, jnp.where(level_of == 1, 1.0, 2.0))
 
 
-def kinetic_kernel(edge, slots, levels, place_meta, own_facts, beside_facts, side_facts, across_facts, *refs):
+def kinetic_kernel(edge, slots, levels, place_meta, facts, *refs):
     parts, refs = refs[:6], refs[6:]
-    (own_pot, beside_pot, fwd_in, fwd_out, back_in, back_mid, back_out), out, refs = refs[:7], refs[7], refs[8:]
-    raw, x, outer, inner, total, total_fix, columns, table, scale, sems = refs
+    (fwd_in, fwd_out, back_in, back_mid, back_out), out, refs = refs[:5], refs[5], refs[6:]
+    raw, x, outer, inner, total, total_fix, lines, columns, table, scale, sems = refs
     square = edge * edge
     own = PAIR * slots
     padded, width = x.shape[2:]
@@ -365,11 +398,19 @@
     x[6 * slots] = jnp.zeros((edge, padded, width), bf16)
     total[...] = jnp.zeros_like(total)
     total_fix[...] = jnp.zeros_like(total_fix)
-    columns[0] = own_pot[...].T
-    columns[1] = beside_pot[...].T
-    fill_tables(slots, levels, place_meta, own_facts, beside_facts, side_facts, across_facts, table, scale)
+    fill_tables(slots, levels, place_meta, facts, table, scale)
+    lines[...] = jnp.zeros_like(lines)
     for copy in copies:
         copy.wait()
+    lanes = raw.shape[3]
+    for t in range(own):
+        for start in range(0, lines.shape[1], lanes):
+            row = edge * square // 2 + 8 + 3 * (start // lanes)
+            high, middle, low = (
+                raw[t // slots, t % slots, row + i : row + i + 1, :].astype(f32) for i in range(3)
+            )
+            lines[t : t + 1, start : start + lanes] = (high + middle) + low
+    columns[...] = lines[...].T
 
     def lay_out(place, carry):
         for slot in range(slots):
@@ -396,18 +437,24 @@
                 return (half * value).astype(bf16), (half * (value - exact)).astype(bf16)
 
             sources = [[table[s, 1 + 3 * a + k] for k in range(3)] for a in range(3)]
-            for i in range(chunks):
-                rows = slice(i * ROWS, (i + 1) * ROWS)
-                block = [x[t, :, rows, :].reshape(edge * ROWS, width) for t in sources[0]]
-                fields = split(matmul(fwd_out[...], jnp.concatenate(block, axis=0)))
-                for field in range(2):
-                    outer[field, :, rows, :] = fields[field].reshape(edge, ROWS, width)
-            for i in range(edge):
-                for a in (1, 2):
-                    block = jnp.concatenate([x[t, i] for t in sources[a]], axis=0)
-                    fields = split(matmul(fwd_in[a - 1], block))
-                    for field in range(2):
-                        inner[field, i, (a - 1) * padded : a * padded, :] = fields[field]
+            here = sources[0][1]
+            for a in range(3):
+
+                @pl.when((here < own) | (sources[a][0] < own) | (sources[a][2] < own))
+                def _():
+                    if a == 0:
+                        for i in range(chunks):
+                            rows = slice(i * ROWS, (i + 1) * ROWS)
+                            block = [x[t, :, rows, :].reshape(edge * ROWS, width) for t in sources[0]]
+                            fields = split(matmul(fwd_out[...], jnp.concatenate(block, axis=0)))
+                            for field in range(2):
+                                outer[field, :, rows, :] = fields[field].reshape(edge, ROWS, width)
+                    else:
+                        for i in range(edge):
+                            block = jnp.concatenate([x[t, i] for t in sources[a]], axis=0)
+                            fields = split(matmul(fwd_in[a - 1], block))
+                            for field in range(2):
+                                inner[field, i, (a - 1) * padded : a * padded, :] = fields[field]
 
             def back_outer(k, target):
                 for i in range(chunks):
@@ -430,8 +477,6 @@
                                     here = inner[field, i, (a - 1) * padded : a * padded, :]
                                     sums[field][target, i] += matmul(back_in[a - 1, k], here)
 
-            here = sources[0][1]
-
             @pl.when(here < own)
             def _():
                 back_outer(1, here)
@@ -446,7 +491,7 @@
     for t in range(own):
         for i in range(edge):
             rows = slice(i * square, (i + 1) * square)
-            weighted = (columns[t // slots, rows, t % slots : t % slots + 1] * x[t, i, :square, :].astype(f32)).astype(bf16)
+            weighted = (columns[rows, t : t + 1] * x[t, i, :square, :].astype(f32)).astype(bf16)
             whole = total[t, i, :square, :] + weighted.astype(f32)
             top = whole.astype(bf16)
             low = (whole - top.astype(f32)).astype(bf16)
@@ -506,7 +551,7 @@
     )(stacked, deriv_blocks, *constants)
 
 
-def kinetic(parts, place_meta, all_facts, pots, matrices, edge, coefficients, levels):
+def kinetic(parts, place_meta, facts, matrices, edge, coefficients, levels):
     slots, folded, lanes = parts[0].shape
     width = lanes // 2
     padded = matrices[0].shape[1]
@@ -517,7 +562,7 @@
     return pl.pallas_call(
         functools.partial(kinetic_kernel, edge, slots, levels),
         out_shape=jax.ShapeDtypeStruct((own, coefficients, 3 * width), bf16),
-        in_specs=[smem] * 5 + [anywhere] * 6 + [vmem] * 7,
+        in_specs=[smem] * 2 + [anywhere] * 6 + [vmem] * 5,
         out_specs=vmem,
         scratch_shapes=[
             pltpu.VMEM((6, slots, folded, lanes), bf16),
@@ -526,7 +571,8 @@
             pltpu.VMEM((2, edge, 2 * padded, width), bf16),
             pltpu.VMEM((own, edge, padded, width), f32),
             pltpu.VMEM((own, edge, padded, width), f32),
-            pltpu.VMEM((2,) + pots[0].shape[::-1], f32),
+            pltpu.VMEM((own + -own % 8, coefficients + -coefficients % lanes), f32),
+            pltpu.VMEM((coefficients + -coefficients % lanes, own + -own % 8), f32),
             pltpu.SMEM((4 * slots, 10), jnp.int32),
             pltpu.SMEM((4 * slots,), f32),
             pltpu.SemaphoreType.DMA((6,)),
@@ -534,7 +580,7 @@
         compiler_params=params(48),
         cost_estimate=pl.CostEstimate(flops=2 * 10**10, bytes_accessed=40 * 10**6, transcendentals=0),
         name="kinetic",
-    )(place_meta, *all_facts, *parts, *pots, *matrices)
+    )(place_meta, facts, *parts, *matrices)
 
 
 def offset_sum_kernel(meta, *refs):
@@ -550,16 +596,34 @@
     sent[...] = jnp.where(first, high, low)
 
 
-def fock_sum_kernel(meta, *refs):
-    blocks, (share, kept, sent) = refs[:-3], refs[-3:]
-    parts = []
-    for part in range(3):
-        total = blocks[0][part].astype(f32)
-        for block in blocks[1:]:
-            total = total + block[part].astype(f32)
-        parts.append(total)
-    main = parts[0] + parts[1]
-    share[...] = parts[2].astype(bf16)
+def fock_pair_kernel(kept, got, own, sent):
+    for j in range(2):
+        main, share = (
+            sum((block[j, i].astype(f32) for block in (kept, got) for i in parts), 0.0) for parts in ((0, 1), (2,))
+        )
+        if j == 0:
+            own[0], own[1] = main, share
+        else:
+            top = main.astype(bf16)
+            sent[0], sent[1], sent[2] = top, (main - top.astype(f32)).astype(bf16), share.astype(bf16)
+
+
+def fock_pair(kept, got):
+    vmem = pl.BlockSpec(memory_space=pltpu.VMEM)
+    tall, width = kept.shape[2:]
+    return pl.pallas_call(
+        fock_pair_kernel,
+        out_shape=[jax.ShapeDtypeStruct((2, tall, width), f32), jax.ShapeDtypeStruct((3, tall, width), bf16)],
+        in_specs=[vmem, vmem],
+        out_specs=[vmem, vmem],
+        compiler_params=params(24),
+        name="fock_pair",
+    )(kept, got)
+
+
+def fock_sum_kernel(meta, own, got, share, kept, sent):
+    main = own[0] + got[0].astype(f32) + got[1].astype(f32)
+    share[...] = (own[1] + got[2].astype(f32)).astype(bf16)
     half = kept.shape[0]
     first = meta[0] == 0
     low, high = main[:, :half].T, main[:, half:].T
@@ -594,11 +658,10 @@
     square_grid = level_count == orb_count == 4 and box_rows == half
     row0, col0 = (level * PAIR + pair) * box_rows, orb * own_width
 
-    own_pot = jnp.pad(potential, ((0, -slots % 8), (0, -coefficients % 128)))
-    beside_pot = swap(own_pot, "pair", 1)
+    pot = jnp.pad(potential, ((0, 0), (0, -coefficients % own_width)))
     own_base = (level * PAIR + pair) * slots
     pack_meta = jnp.stack([pair, box_counts[0], own_base]).astype(jnp.int32)
-    theirs, mine = pack(pack_meta, neighbours.reshape(slots, 6), levels, orbitals)
+    theirs, mine = pack(pack_meta, neighbours.reshape(slots, 6), levels, orbitals, pot)
     active = orbitals
 
     far = {q: swap(active, "orb", q) for q in groups if q and q % 2 == 0}
@@ -607,25 +670,19 @@
     beside_rest = swap(mine, "pair", 1)
     first_beside, second_beside = trade(beside, "lvl", 0), trade(beside, "lvl", 1)
 
-    def facts_of(packed):
-        return packed[:, fold, :8].astype(f32).astype(jnp.int32)
-
-    side_facts = jnp.stack([facts_of(first_mine), facts_of(second_mine)])
-    across_facts = swap(side_facts, "pair", 1)
     matrices = block_matrices(deriv_blocks)
 
-    far, active, parts, beside_rest, matrices, all_facts, pots = lax.optimization_barrier(
+    far, active, parts, beside_rest, matrices = lax.optimization_barrier(
         (
             far,
             active,
             [mine, beside, first_mine, first_beside, second_mine, second_beside],
             beside_rest,
             matrices,
-            [facts_of(mine), facts_of(beside), side_facts, across_facts],
-            [own_pot, beside_pot],
         )
     )
     beside = parts[1]
+    facts = jnp.stack([part[:, fold, :8] for part in parts]).astype(f32).astype(jnp.int32)
 
     flat = lambda block: block.reshape(-1, block.shape[-1])
     cut = -(-slots * coefficients // (2 * ROWS)) * ROWS
@@ -657,7 +714,7 @@
     meta = jnp.stack([pair, slots * coefficients, live_rows]).astype(jnp.int32)
 
     place_meta = jnp.stack([level, pair]).astype(jnp.int32)
-    right = kinetic(parts, place_meta, all_facts, pots, matrices, edge, coefficients, level_count)
+    right = kinetic(parts, place_meta, facts, matrices, edge, coefficients, level_count)
 
     cross, right, meta = lax.optimization_barrier((cross, right, meta))
     lefts_own = [[flat(left_own[q])] for q in groups]
@@ -671,7 +728,7 @@
     blocks = box_correlation(share, meta, lefts_own, None, half)
     blocks = box_correlation(share, meta, lefts_beside, blocks, half)
     right = right.reshape(2, slots * coefficients, 3 * half)
-    fock_part = box_fock(0, lefts_own, right, None)
+    fock_part = box_fock(0, lefts_own, right, None, None)
     if square_grid:
         sent = along_levels(blocks)
         sent, fock_part = lax.optimization_barrier((sent, fock_part))
@@ -682,23 +739,24 @@
     row_ids = row0 + jnp.arange(box_rows, dtype=jnp.int32)
     col_ids = col0 + jnp.arange(own_width, dtype=jnp.int32)
     correlation = offset + (row_ids[:, None] == col_ids[None, :]).astype(f32)
-    fock_blocks = box_fock(1, lefts_beside, right, fock_part)
+    apart = (orb ^ level if square_grid else 0 * orb).reshape(1).astype(jnp.int32)
+    odd, even = box_fock(1, lefts_beside, right, fock_part, apart)
     if square_grid:
         pieces = [small] + [swap(small, "lvl", z) for z in range(1, level_count)]
-        pieces, fock_blocks, offset = lax.optimization_barrier((pieces, fock_blocks, offset))
+        pieces, odd, even, offset = lax.optimization_barrier((pieces, odd, even, offset))
         join = functools.partial(jnp.concatenate, axis=0)
         top, low = join(pieces[: level_count // 2]), join(pieces[level_count // 2 :])
-        sent = along_levels(fock_blocks)
+        paired = swap(odd, "lvl", 1)
         got = [swap(top, "pair", 1), swap(low, "orb", 2)]
-        got, sent[1] = lax.optimization_barrier((got, sent[1]))
+        got, paired = lax.optimization_barrier((got, paired))
+        own_sum, fock_sent = fock_pair(even, paired)
+        fock_got = swap(fock_sent, "lvl", 2)
         top, low = join([top, got[0]]), join([low, got[1]])
         pieces = [top, swap(top, "orb", 2), low, swap(low, "pair", 1)]
-        pieces, sent[2] = lax.optimization_barrier((pieces, sent[2]))
         pieces += [swap(piece, "orb", 1) for piece in pieces]
         root_meta = jnp.stack([level, pair, orb]).astype(jnp.int32)
         inverse_root = root_of(root_meta, pieces, offset, all_width, level_count)
-        inverse_root, sent = lax.optimization_barrier((inverse_root, sent))
-        share, kept, other = level_sum(fock_sum_kernel, meta, sent)
+        share, kept, other = level_sum(fock_sum_kernel, meta, [own_sum, fock_got])
         to = [
             ((z * PAIR + y) * orb_count + o, (o * PAIR + y) * orb_count + z)
             for z in range(level_count)
@@ -707,6 +765,7 @@
         ]
         fock = both_halves(kept, other) + lax.ppermute(share, BOX + ("orb",), to).astype(f32)
     else:
+        fock_blocks = jnp.stack([even, odd], axis=1).reshape(orb_count, 3, half, own_width)
         main = natural(fock_blocks[:, 0]).astype(f32) + natural(fock_blocks[:, 1]).astype(f32)
         main = lax.all_gather(lax.psum(main, "lvl"), "pair", axis=0, tiled=True)
         fock = lax.dynamic_slice_in_dim(main, row0, box_rows, axis=1).T + own_block(natural(fock_blocks[:, 2]).astype(f32))

time: 196 us -> 203 us (1.036)
  waiting for transfers between devices: 55.2 us -> 73.2 us
  starting transfers between devices: 63.1 us -> 46.5 us
  local copies, waits for them, and re-layouts: 10.3 us -> 14.7 us
  Pallas kernels: 61 us -> 65.1 us
  other arithmetic: 5.84 us -> 2.13 us
    ppermute x31 -> x28, waiting for transfers between devices: 49.7 us -> 64.4 us  [swap(): return lax.ppermute(value, axis, [(i, i ^ bit) for i in range(count)])]
    ppermute x31 -> x28, starting transfers between devices: 46.9 us -> 38.3 us  [swap(): return lax.ppermute(value, axis, [(i, i ^ bit) for i in range(count)])]
    ppermute x1, starting transfers between devices: 9.93 us -> 1.91 us  [body(): lax.ppermute(share, BOX + ('orb',), to).astype(f32)]
    slice x0 -> x6, local copies, waits for them, and re-layouts: none -> 3.41 us  [body(): part[:, fold, :8]]
    pallas_call x1, Pallas kernels: 20.4 us -> 23.5 us  [kinetic(): pl.pallas_call(functools.partial(kinetic_kernel, edge, slots, levels), ou...]
    convert_element_type x4 -> x1, other arithmetic: 2.61 us -> 0.01 us  [body(): jnp.stack([part[:, fold, :8] for part in parts]).astype(f32)]
    ppermute x1, waiting for transfers between devices: 5.51 us -> 8 us  [body(): lax.ppermute(share, BOX + ('orb',), to).astype(f32)]
    unnamed x50 -> x51, local copies, waits for them, and re-layouts: 7.71 us -> 9.47 us
  transfers between devices with their start and end apart: 36 -> 33, of which waited for: 12 -> 11; matrix products, arithmetic and copies ran while one was open for 4% -> 2% of each run, Pallas kernels for 26% -> 23%
where the time goes in v3:
time: 203 us
  waiting for transfers between devices  73.2 us (36%)
  Pallas kernels  65.1 us (32%)
  starting transfers between devices  46.5 us (23%)
  local copies, waits for them, and re-layouts  14.7 us (7%)
  other arithmetic  2.13 us (1%)
    ppermute x28, waiting for transfers between devices, swap(): return lax.ppermute(value, axis, [(i, i ^ bit) for i in range(count)])  64.4 us
    ppermute x28, starting transfers between devices, swap(): return lax.ppermute(value, axis, [(i, i ^ bit) for i in range(count)])  38.3 us
    pallas_call x1, Pallas kernels, kinetic(): pl.pallas_call(functools.partial(kinetic_kernel, edge, slots, levels), ou...  23.5 us
    pallas_call x2, Pallas kernels, box_fock(): pl.pallas_call(functools.partial(fock_kernel, side, counts), out_shape=ou...  16.6 us
    unnamed x51, local copies, waits for them, and re-layouts  9.47 us
    pallas_call x2, Pallas kernels, box_correlation(): pl.pallas_call(functools.partial(correlation_kernel, share, counts), out_...  9.16 us
    pallas_call x1, Pallas kernels, root_of(): pl.pallas_call(functools.partial(root_kernel, levels), out_shape=jax.Shap...  8.34 us
    ppermute x1, waiting for transfers between devices, body(): lax.ppermute(share, BOX + ('orb',), to).astype(f32)  8 us
  transfers between devices with their start and end apart: 33, of which 11 were waited for; matrix products, arithmetic and copies ran while one was open for 2% of the time, Pallas kernels for 23%

profile of v3, /device:TPU:2, one launch (start us, length us, event | category | flops | bytes accessed | tf_op | source)
XLA Modules:
  0.0 203.5 jit_solution(7358023645963213647)
XLA Ops:
  1.4 0.8 copy.20
  3.7 3.2 %pack.1 = (bf16[2,528,384]{2,1,0:T(8,128)(2,1)S(1)}, bf16[2,528,384]{2,1,0:T(8,128)(2,1)}) custom-call(s32[3]{0:T(128)S(1)} %pad_add_fusion.meta, s32[2,6]{1,0:T(2,128)S(1)} %reshape.42.neighbours, s32[2]{0:T(128)S(1)} %copy-done.16, bf16[2,1000,384]{2,1,0:T(8,128)(2,1)} %orbitals.1, f32[2,1152]{1,0:T(2,128)S(1)} %pad.4.pot), custom_call_target="tpu_custom_call" | custom-call | tf_op jit(solution)/shard_map/pack/pallas_call | solution.py:75
  6.9 1.5 collective-permute-start.1
  8.5 1.6 collective-permute-start.2
  10.6 1.6 collective-permute-start.4
  12.7 15.2 %collective-permute-done.1.beside_in.refs_1_ = bf16[2,528,384]{2,1,0:T(8,128)(2,1)S(1)} collective-permute-done((bf16[2,528,384]{2,1,0:T(8,128)(2,1)S(1)}, bf16[2,528,384]{2,1,0:T(8,128)(2,1)S(1)}, u32[]{:S(2)}, u32[]{:S(2)}) %collective-permute-start.1) | collective-permute-done | bytes 811040 | tf_op jit(solution)/shard_map/ppermute | solution.py:19
  27.9 1.6 collective-permute-start.3
  29.5 0.9 copy-done.17
  30.4 1.6 collective-permute-start.5
  32.0 0.8 reshape.43.stacked
  35.0 1.0 matrices.1
  36.2 7.9 %collective-permute-done.6.rest_in = bf16[2,528,384]{2,1,0:T(8,128)(2,1)S(1)} collective-permute-done((bf16[2,528,384]{2,1,0:T(8,128)(2,1)}, bf16[2,528,384]{2,1,0:T(8,128)(2,1)S(1)}, u32[]{:S(2)}, u32[]{:S(2)}) %collective-permute-start.6) | collective-permute-done | bytes 811040 | tf_op jit(solution)/shard_map/ppermute | solution.py:19
  44.1 0.9 copy-done.3
  45.8 0.9 copy-done
  50.2 1.1 copy-done.1
  51.3 1.1 copy-done.4
  53.1 1.4 unfold.1
  55.3 1.5 collective-permute-start.8
  57.3 23.5 %kinetic.1 = bf16[4,1000,576]{2,1,0:T(8,128)(2,1)} custom-call(s32[2]{0:T(128)S(1)} %pad_add_fusion.1.place_meta, s32[6,2,8]{2,1,0:T(2,128)S(1)} %convert_convert_fusion.facts, bf16[2,528,384]{2,1,0:T(8,128)(2,1)} %get-tuple-element.66.refs_0_, bf16[2,528,384]{2,1,0:T(8,128)(2,1)S(1)} %copy-done.2, bf16[2,528,384]{2,1,0:T(8,128)(2,1)S(1)} %copy-done.18, ...), custom_call_target="tpu_custom_call" | custom-call | flops 20000000000 | bytes 40000000 | tf_op jit(solution)/shard_map/kinetic/pallas_call | solution.py:562
  81.5 4.8 %correlation.2.refs_6_ = f32[4,192,384]{2,1,0:T(8,128)S(1)} custom-call(s32[3]{0:T(128)S(1)} %pad_add_fusion.2.meta, bf16[2000,384]{1,0:T(8,128)(2,1)} %bitcast.5.refs_0_, bf16[2000,384]{1,0:T(8,128)(2,1)} %bitcast.6.refs_1_, bf16[2000,384]{1,0:T(8,128)(2,1)S(1)} %bitcast.32, bf16[2000,384]{1,0:T(8,128)(2,1)} %bitcast.7.refs_3_), custom_call_target="tpu_custom_call" | custom-call | flops 1179648000 | bytes 6144000 | tf_op jit(solution)/shard_map/correlation/pallas_call | solution.py:179
  86.3 4.4 %correlation.3 = bf16[4,192,384]{2,1,0:T(8,128)(2,1)S(1)} custom-call(s32[3]{0:T(128)S(1)} %pad_add_fusion.2.meta, bf16[2000,384]{1,0:T(8,128)(2,1)S(1)} %get-tuple-element.77.refs_0_, bf16[2000,384]{1,0:T(8,128)(2,1)} %collective-permute-done.9.refs_1_, bf16[1008,384]{1,0:T(8,128)(2,1)} %collective-permute-done.7.refs_2_, ...), custom_call_target="tpu_custom_call" | custom-call | flops 1179648000 | bytes 6144000 | tf_op jit(solution)/shard_map/correlation/pallas_call | solution.py:179
  90.7 3.3 %collective-permute-start.14 = (bf16[192,384]{1,0:T(8,128)(2,1)S(1)}, bf16[192,384]{1,0:T(8,128)(2,1)S(1)}, u32[]{:S(2)}, u32[]{:S(2)}) collective-permute-start(bf16[192,384]{1,0:T(8,128)(2,1)S(1)} %get-tuple-element.111), channel_id=1, source_target_pairs={{0,8},{8,0},{16,24},{24,16},{1,9},{9,1},{17,25},{25,17},{2,10},{10... | collective-permute-start | bytes 442376 | tf_op jit(solution)/shard_map/ppermute | solution.py:19
  94.1 7.5 %collective-permute-start.15 = (bf16[192,384]{1,0:T(8,128)(2,1)S(1)}, bf16[192,384]{1,0:T(8,128)(2,1)S(1)}, u32[]{:S(2)}, u32[]{:S(2)}) collective-permute-start(bf16[192,384]{1,0:T(8,128)(2,1)S(1)} %get-tuple-element.110), channel_id=1, source_target_pairs={{0,16},{8,24},{16,0},{24,8},{1,17},{9,25},{17,1},{25,9},{2,18},{10... | collective-permute-start | bytes 442376 | tf_op jit(solution)/shard_map/ppermute | solution.py:19
  101.6 1.4 collective-permute-start.16
  103.0 8.2 %fock.2.refs_6_ = f32[4,576,384]{2,1,0:T(8,128)S(1)} custom-call(bf16[2,2000,576]{2,1,0:T(8,128)(2,1)} %bitcast.34, bf16[2000,384]{1,0:T(8,128)(2,1)} %bitcast.5.refs_0_, bf16[2000,384]{1,0:T(8,128)(2,1)} %bitcast.6.refs_1_, bf16[2000,384]{1,0:T(8,128)(2,1)S(1)} %bitcast.33, bf16[2000,384]{1,0:T(8,128)(2,1)} %bitcast.7.refs_3_), custom_call_target="tpu_custom_call" | custom-call | flops 3538944000 | bytes 6144000 | tf_op jit(solution)/shard_map/fock/pallas_call | solution.py:242
  111.2 2.1 %collective-permute-done.16.refs_3_ = bf16[192,384]{1,0:T(8,128)(2,1)S(1)} collective-permute-done((bf16[192,384]{1,0:T(8,128)(2,1)S(1)}, bf16[192,384]{1,0:T(8,128)(2,1)S(1)}, u32[]{:S(2)}, u32[]{:S(2)}) %collective-permute-start.16) | collective-permute-done | bytes 147488 | tf_op jit(solution)/shard_map/ppermute | solution.py:19
  113.3 0.8 level_sum.2
  114.1 2.7 %collective-permute-start.17 = (bf16[192,384]{1,0:T(8,128)(2,1)S(1)}, bf16[192,384]{1,0:T(8,128)(2,1)S(1)}, u32[]{:S(2)}, u32[]{:S(2)}) collective-permute-start(bf16[192,384]{1,0:T(8,128)(2,1)S(1)} %get-tuple-element.93), channel_id=1, source_target_pairs={{0,8},{8,0},{16,24},{24,16},{1,9},{9,1},{17,25},{25,17},{2,10},{10... | collective-permute-start | bytes 442376 | tf_op jit(solution)/shard_map/ppermute | solution.py:19
  116.8 2.0 collective-permute-start.18
  118.8 1.4 collective-permute-start.19
  120.9 8.4 %fock.3 = (bf16[2,3,192,384]{3,2,1,0:T(8,128)(2,1)S(1)}, bf16[2,3,192,384]{3,2,1,0:T(8,128)(2,1)S(1)}) custom-call(bf16[2,2000,576]{2,1,0:T(8,128)(2,1)} %bitcast.35, bf16[2000,384]{1,0:T(8,128)(2,1)S(1)} %get-tuple-element.77.refs_0_, bf16[2000,384]{1,0:T(8,128)(2,1)} %collective-permute-done.9.refs_1_, bf16[1008,384]{1,0:T(8,128)(2,1)} %collective-permute-done.7.refs_2_, ...), custom_call_target="tpu_custom_call" | custom-call | flops 3538944000 | bytes 6144000 | tf_op jit(solution)/shard_map/fock/pallas_call | solution.py:242
  129.4 0.9 convert_add_fusion
  130.6 2.7 %collective-permute-start.23 = (bf16[2,3,192,384]{3,2,1,0:T(8,128)(2,1)S(1)}, bf16[2,3,192,384]{3,2,1,0:T(8,128)(2,1)S(1)}, u32[]{:S(2)}, u32[]{:S(2)}) collective-permute-start(bf16[2,3,192,384]{3,2,1,0:T(8,128)(2,1)S(1)} %get-tuple-element.97), channel_id=1, source_target_pairs={{0,8},{8,0},{16,24},{24,16},{1,9},{9,1},{17,25},{25,17},{2,10},{10... | collective-permute-start | bytes 2654216 | tf_op jit(solution)/shard_map/ppermute | solution.py:19
  133.3 1.6 collective-permute-start.22
  135.7 5.8 %collective-permute-done.22 = bf16[384,384]{1,0:T(8,128)(2,1)S(1)} collective-permute-done((bf16[384,384]{1,0:T(8,128)(2,1)S(1)}, bf16[384,384]{1,0:T(8,128)(2,1)S(1)}, u32[]{:S(2)}, u32[]{:S(2)}) %collective-permute-start.22) | collective-permute-done | bytes 294944 | tf_op jit(solution)/shard_map/ppermute | solution.py:19
  141.5 1.4 collective-permute-done.21
  142.8 9.7 %collective-permute-done.23.got = bf16[2,3,192,384]{3,2,1,0:T(8,128)(2,1)S(1)} collective-permute-done((bf16[2,3,192,384]{3,2,1,0:T(8,128)(2,1)S(1)}, bf16[2,3,192,384]{3,2,1,0:T(8,128)(2,1)S(1)}, u32[]{:S(2)}, u32[]{:S(2)}) %collective-permute-start.23) | collective-permute-done | bytes 884768 | tf_op jit(solution)/shard_map/ppermute | solution.py:19
  152.6 0.8 collective-permute-start.28
  153.4 1.4 collective-permute-start.27
  155.0 3.7 %collective-permute-start.24 = (bf16[3,192,384]{2,1,0:T(8,128)(2,1)S(1)}, bf16[3,192,384]{2,1,0:T(8,128)(2,1)S(1)}, u32[]{:S(2)}, u32[]{:S(2)}) collective-permute-start(bf16[3,192,384]{2,1,0:T(8,128)(2,1)S(1)} %get-tuple-element.100), channel_id=1, source_target_pairs={{0,16},{8,24},{16,0},{24,8},{1,17},{9,25},{17,1},{25,9},{2,18},{10... | collective-permute-start | bytes 1327112 | tf_op jit(solution)/shard_map/ppermute | solution.py:19
  158.8 17.8 %collective-permute-done.24.got = bf16[3,192,384]{2,1,0:T(8,128)(2,1)S(1)} collective-permute-done((bf16[3,192,384]{2,1,0:T(8,128)(2,1)S(1)}, bf16[3,192,384]{2,1,0:T(8,128)(2,1)S(1)}, u32[]{:S(2)}, u32[]{:S(2)}) %collective-permute-start.24) | collective-permute-done | bytes 442400 | tf_op jit(solution)/shard_map/ppermute | solution.py:19
  176.5 0.8 level_sum.3
  177.4 1.6 collective-permute-start.25
  180.1 4.0 %collective-permute-done.25 = f32[192,192]{1,0:T(8,128)S(1)} collective-permute-done((f32[192,192]{1,0:T(8,128)S(1)}, f32[192,192]{1,0:T(8,128)S(1)}, u32[]{:S(2)}, u32[]{:S(2)}) %collective-permute-start.25) | collective-permute-done | bytes 147488 | tf_op jit(solution)/shard_map/ppermute | solution.py:19
  184.1 1.9 collective-permute-start.26
  186.1 8.0 %collective-permute-done.26 = bf16[192,384]{1,0:T(8,128)(2,1)S(1)} collective-permute-done((bf16[192,384]{1,0:T(8,128)(2,1)S(1)}, bf16[192,384]{1,0:T(8,128)(2,1)S(1)}, u32[]{:S(2)}, u32[]{:S(2)}) %collective-permute-start.26) | collective-permute-done | bytes 147488 | tf_op jit(solution)/shard_map/ppermute | solution.py:766
  194.1 0.8 maximum_add_fusion
  195.0 8.3 %root.1 = f32[192,384]{1,0:T(8,128)} custom-call(s32[3]{0:T(128)S(1)} %pad_add_fusion.3.meta, bf16[768,384]{1,0:T(8,128)(2,1)S(1)} %constant_dynamic-update-slice_fusion.6.refs_0_, bf16[768,384]{1,0:T(8,128)(2,1)S(1)} %collective-permute-done.27.refs_1_, bf16[768,384]{1,0:T(8,128)(2,1)S(1)} %constant_dynamic-update-slice_fusion.9.refs_2_, ...), custom_call_target="tpu_custom_call" | custom-call | flops 3623878656 | bytes 9437184 | tf_op jit(solution)/shard_map/root/pallas_call | solution.py:327
  (108 shorter events, 15.1 us)
Async XLA Ops:
  0.6 32.1 %copy-start.10 = (bf16[112,10]{1,0:T(8,128)(2,1)S(1)}, bf16[112,10]{1,0:T(8,128)(2,1)}, u32[]{:S(2)}) copy-start(bf16[112,10]{1,0:T(8,128)(2,1)} %constant.60.clone.refs_0_) | copy-start | bytes 6724
  0.6 32.1 %copy-start.6 = (f32[112,112]{1,0:T(8,128)S(1)}, f32[112,112]{1,0:T(8,128)}, u32[]{:S(2)}) copy-start(f32[112,112]{1,0:T(8,128)} %constant.62.clone.refs_2_) | copy-start | bytes 150532
  0.7 32.1 %copy-start.7 = (f32[112,112]{1,0:T(8,128)S(1)}, f32[112,112]{1,0:T(8,128)}, u32[]{:S(2)}) copy-start(f32[112,112]{1,0:T(8,128)} %constant.65.clone.refs_5_) | copy-start | bytes 150532
  0.7 32.1 %copy-start.8 = (bf16[160,10]{1,0:T(8,128)(2,1)S(1)}, bf16[160,10]{1,0:T(8,128)(2,1)}, u32[]{:S(2)}) copy-start(bf16[160,10]{1,0:T(8,128)(2,1)} %constant.66.clone.refs_6_) | copy-start | bytes 9604
  0.7 32.1 %copy-start.9 = (bf16[30,480]{1,0:T(8,128)(2,1)S(1)}, bf16[30,480]{1,0:T(8,128)(2,1)}, u32[]{:S(2)}) copy-start(bf16[30,480]{1,0:T(8,128)(2,1)} %constant.67.clone.refs_7_) | copy-start | bytes 86404
  0.7 32.1 %copy-start.5 = (f32[160,160]{1,0:T(8,128)S(1)}, f32[160,160]{1,0:T(8,128)}, u32[]{:S(2)}) copy-start(f32[160,160]{1,0:T(8,128)} %constant.68.clone.refs_8_) | copy-start | bytes 307204
  3.7 28.3 %copy-start.14 = (s32[3]{0:T(128)}, s32[3]{0:T(128)S(1)}, u32[]{:S(2)}) copy-start(s32[3]{0:T(128)S(1)} %pad_add_fusion.meta) | copy-start | bytes 40
  3.7 28.3 %copy-start.19 = (bf16[3,10,10]{2,0,1:T(4,128)(2,1)S(1)}, bf16[3,10,10]{2,0,1:T(4,128)(2,1)}, u32[]{:S(2)}) copy-start(bf16[3,10,10]{2,0,1:T(4,128)(2,1)} %param.17) | copy-start | bytes 1804
  6.9 21.0 %collective-permute-start.1 = (bf16[2,528,384]{2,1,0:T(8,128)(2,1)S(1)}, bf16[2,528,384]{2,1,0:T(8,128)(2,1)S(1)}, u32[]{:S(2)}, u32[]{:S(2)}) collective-permute-start(bf16[2,528,384]{2,1,0:T(8,128)(2,1)S(1)} %get-tuple-element.56), channel_id=1, source_target_pairs={{0,4},{4,0},{1,5},{5,1},{2,6},{6,2},{3,7},{7,3},{8,12},{12,8},{9,1... | collective-permute-start | bytes 2433032 | tf_op jit(solution)/shard_map/ppermute | solution.py:19
  8.5 21.0 %collective-permute-start.2 = (bf16[2,528,384]{2,1,0:T(8,128)(2,1)}, bf16[2,528,384]{2,1,0:T(8,128)(2,1)S(1)}, u32[]{:S(2)}, u32[]{:S(2)}) collective-permute-start(bf16[2,528,384]{2,1,0:T(8,128)(2,1)} %get-tuple-element.66.refs_0_), channel_id=1, source_target_pairs={{0,8},{16,24},{8,0},{24,16},{1,9},{17,25},{9,1},{25,17},{2,10},{18... | collective-permute-start | bytes 2433032 | tf_op jit(solution)/shard_map/ppermute | solution.py:24
  10.0 35.0 %collective-permute-start = (bf16[2,1000,384]{2,1,0:T(8,128)(2,1)}, bf16[2,1000,384]{2,1,0:T(8,128)(2,1)S(1)}, u32[]{:S(2)}, u32[]{:S(2)}) collective-permute-start(bf16[2,1000,384]{2,1,0:T(8,128)(2,1)} %orbitals.1), channel_id=1, source_target_pairs={{0,2},{1,3},{2,0},{3,1},{4,6},{5,7},{6,4},{7,5},{8,10},{9,11},{10,... | collective-permute-start | bytes 4608008 | tf_op jit(solution)/shard_map/ppermute | solution.py:19
  10.6 25.6 %collective-permute-start.4 = (bf16[2,528,384]{2,1,0:T(8,128)(2,1)}, bf16[2,528,384]{2,1,0:T(8,128)(2,1)}, u32[]{:S(2)}, u32[]{:S(2)}) collective-permute-start(bf16[2,528,384]{2,1,0:T(8,128)(2,1)} %get-tuple-element.66.refs_0_), channel_id=1, source_target_pairs={{8,16},{16,8},{9,17},{17,9},{10,18},{18,10},{11,19},{19,11},{12,20... | collective-permute-start | bytes 2433032 | tf_op jit(solution)/shard_map/ppermute | solution.py:24
  12.2 32.0 %collective-permute-start.6 = (bf16[2,528,384]{2,1,0:T(8,128)(2,1)}, bf16[2,528,384]{2,1,0:T(8,128)(2,1)S(1)}, u32[]{:S(2)}, u32[]{:S(2)}) collective-permute-start(bf16[2,528,384]{2,1,0:T(8,128)(2,1)} %get-tuple-element.66.refs_0_), channel_id=1, source_target_pairs={{0,4},{4,0},{1,5},{5,1},{2,6},{6,2},{3,7},{7,3},{8,12},{12,8},{9,1... | collective-permute-start | bytes 2433032 | tf_op jit(solution)/shard_map/ppermute | solution.py:19
  27.9 17.9 %collective-permute-start.3 = (bf16[2,528,384]{2,1,0:T(8,128)(2,1)S(1)}, bf16[2,528,384]{2,1,0:T(8,128)(2,1)}, u32[]{:S(2)}, u32[]{:S(2)}) collective-permute-start(bf16[2,528,384]{2,1,0:T(8,128)(2,1)S(1)} %collective-permute-done.1.beside_in.refs_1_), channel_id=1, source_target_pairs={{0,8},{16,24},{8,0},{24,16},{1,9},{17,25},{9,1},{25,17},{2,10},{18... | collective-permute-start | bytes 2433032 | tf_op jit(solution)/shard_map/ppermute | solution.py:24
  29.5 0.9 copy-start.17
  30.4 15.4 %collective-permute-start.5 = (bf16[2,528,384]{2,1,0:T(8,128)(2,1)S(1)}, bf16[2,528,384]{2,1,0:T(8,128)(2,1)}, u32[]{:S(2)}, u32[]{:S(2)}) collective-permute-start(bf16[2,528,384]{2,1,0:T(8,128)(2,1)S(1)} %collective-permute-done.1.beside_in.refs_1_), channel_id=1, source_target_pairs={{8,16},{16,8},{9,17},{17,9},{10,18},{18,10},{11,19},{19,11},{12,20... | collective-permute-start | bytes 2433032 | tf_op jit(solution)/shard_map/ppermute | solution.py:24
  44.1 0.9 copy-start.3
  45.8 0.9 copy-start
  50.2 1.1 copy-start.1
  51.3 1.1 copy-start.4
  53.1 4.2 %copy-start.2 = (bf16[2,528,384]{2,1,0:T(8,128)(2,1)S(1)}, bf16[2,528,384]{2,1,0:T(8,128)(2,1)}, u32[]{:S(2)}) copy-start(bf16[2,528,384]{2,1,0:T(8,128)(2,1)} %copy-done) | copy-start | bytes 2433028
  53.1 4.2 %copy-start.18 = (bf16[2,528,384]{2,1,0:T(8,128)(2,1)S(1)}, bf16[2,528,384]{2,1,0:T(8,128)(2,1)}, u32[]{:S(2)}) copy-start(bf16[2,528,384]{2,1,0:T(8,128)(2,1)} %copy-done.17) | copy-start | bytes 2433028
  54.5 26.3 %collective-permute-start.7 = (bf16[1008,384]{1,0:T(8,128)(2,1)S(1)}, bf16[1008,384]{1,0:T(8,128)(2,1)}, u32[]{:S(2)}, u32[]{:S(2)}) collective-permute-start(bf16[1008,384]{1,0:T(8,128)(2,1)S(1)} %get-tuple-element.64), channel_id=1, source_target_pairs={{0,2},{1,3},{2,0},{3,1},{4,6},{5,7},{6,4},{7,5},{8,10},{9,11},{10,... | collective-permute-start | bytes 2322440 | tf_op jit(solution)/shard_map/ppermute | solution.py:19
  55.2 26.2 %collective-permute-start.13 = (bf16[2,1000,384]{2,1,0:T(8,128)(2,1)S(1)}, bf16[2,1000,384]{2,1,0:T(8,128)(2,1)}, u32[]{:S(2)}, u32[]{:S(2)}) collective-permute-start(bf16[2,1000,384]{2,1,0:T(8,128)(2,1)S(1)} %collective-permute-done), channel_id=1, source_target_pairs={{0,1},{1,0},{2,3},{3,2},{4,5},{5,4},{6,7},{7,6},{8,9},{9,8},{10,11... | collective-permute-start | bytes 4608008 | tf_op jit(solution)/shard_map/ppermute | solution.py:19
  55.3 25.5 %collective-permute-start.8 = (bf16[992,384]{1,0:T(8,128)(2,1)S(1)}, bf16[992,384]{1,0:T(8,128)(2,1)}, u32[]{:S(2)}, u32[]{:S(2)}) collective-permute-start(bf16[992,384]{1,0:T(8,128)(2,1)S(1)} %slice.28), channel_id=1, source_target_pairs={{0,4},{4,0},{1,5},{5,1},{2,6},{6,2},{3,7},{7,3},{8,12},{12,8},{9,1... | collective-permute-start | bytes 2285576 | tf_op jit(solution)/shard_map/ppermute | solution.py:19
  56.8 24.6 %collective-permute-start.12 = (bf16[2,1000,384]{2,1,0:T(8,128)(2,1)}, bf16[2,1000,384]{2,1,0:T(8,128)(2,1)}, u32[]{:S(2)}, u32[]{:S(2)}) collective-permute-start(bf16[2,1000,384]{2,1,0:T(8,128)(2,1)} %orbitals.1), channel_id=1, source_target_pairs={{0,1},{1,0},{2,3},{3,2},{4,5},{5,4},{6,7},{7,6},{8,9},{9,8},{10,11... | collective-permute-start | bytes 4608008 | tf_op jit(solution)/shard_map/ppermute | solution.py:19
  57.0 29.2 %collective-permute-start.9 = (bf16[2000,384]{1,0:T(8,128)(2,1)S(1)}, bf16[2000,384]{1,0:T(8,128)(2,1)}, u32[]{:S(2)}, u32[]{:S(2)}) collective-permute-start(bf16[2000,384]{1,0:T(8,128)(2,1)S(1)} %get-tuple-element.77.refs_0_), channel_id=1, source_target_pairs={{0,1},{1,0},{2,3},{3,2},{4,5},{5,4},{6,7},{7,6},{8,9},{9,8},{10,11... | collective-permute-start | bytes 4608008 | tf_op jit(solution)/shard_map/ppermute | solution.py:19
  80.9 5.4 %collective-permute-start.10 = (bf16[1008,384]{1,0:T(8,128)(2,1)}, bf16[1008,384]{1,0:T(8,128)(2,1)}, u32[]{:S(2)}, u32[]{:S(2)}) collective-permute-start(bf16[1008,384]{1,0:T(8,128)(2,1)} %collective-permute-done.7.refs_2_), channel_id=1, source_target_pairs={{0,1},{1,0},{2,3},{3,2},{4,5},{5,4},{6,7},{7,6},{8,9},{9,8},{10,11... | collective-permute-start | bytes 2322440 | tf_op jit(solution)/shard_map/ppermute | solution.py:19
  81.2 5.1 %collective-permute-start.11 = (bf16[992,384]{1,0:T(8,128)(2,1)}, bf16[992,384]{1,0:T(8,128)(2,1)}, u32[]{:S(2)}, u32[]{:S(2)}) collective-permute-start(bf16[992,384]{1,0:T(8,128)(2,1)} %collective-permute-done.8.refs_3_), channel_id=1, source_target_pairs={{0,1},{1,0},{2,3},{3,2},{4,5},{5,4},{6,7},{7,6},{8,9},{9,8},{10,11... | collective-permute-start | bytes 2285576 | tf_op jit(solution)/shard_map/ppermute | solution.py:19
  90.7 20.4 %collective-permute-start.14 = (bf16[192,384]{1,0:T(8,128)(2,1)S(1)}, bf16[192,384]{1,0:T(8,128)(2,1)S(1)}, u32[]{:S(2)}, u32[]{:S(2)}) collective-permute-start(bf16[192,384]{1,0:T(8,128)(2,1)S(1)} %get-tuple-element.111), channel_id=1, source_target_pairs={{0,8},{8,0},{16,24},{24,16},{1,9},{9,1},{17,25},{25,17},{2,10},{10... | collective-permute-start | bytes 442376 | tf_op jit(solution)/shard_map/ppermute | solution.py:19
  94.1 17.1 %collective-permute-start.15 = (bf16[192,384]{1,0:T(8,128)(2,1)S(1)}, bf16[192,384]{1,0:T(8,128)(2,1)S(1)}, u32[]{:S(2)}, u32[]{:S(2)}) collective-permute-start(bf16[192,384]{1,0:T(8,128)(2,1)S(1)} %get-tuple-element.110), channel_id=1, source_target_pairs={{0,16},{8,24},{16,0},{24,8},{1,17},{9,25},{17,1},{25,9},{2,18},{10... | collective-permute-start | bytes 442376 | tf_op jit(solution)/shard_map/ppermute | solution.py:19
  101.6 11.7 %collective-permute-start.16 = (bf16[192,384]{1,0:T(8,128)(2,1)S(1)}, bf16[192,384]{1,0:T(8,128)(2,1)S(1)}, u32[]{:S(2)}, u32[]{:S(2)}) collective-permute-start(bf16[192,384]{1,0:T(8,128)(2,1)S(1)} %get-tuple-element.109), channel_id=1, source_target_pairs={{0,24},{8,16},{16,8},{24,0},{1,25},{9,17},{17,9},{25,1},{2,26},{10... | collective-permute-start | bytes 442376 | tf_op jit(solution)/shard_map/ppermute | solution.py:19
  114.1 16.2 %collective-permute-start.17 = (bf16[192,384]{1,0:T(8,128)(2,1)S(1)}, bf16[192,384]{1,0:T(8,128)(2,1)S(1)}, u32[]{:S(2)}, u32[]{:S(2)}) collective-permute-start(bf16[192,384]{1,0:T(8,128)(2,1)S(1)} %get-tuple-element.93), channel_id=1, source_target_pairs={{0,8},{8,0},{16,24},{24,16},{1,9},{9,1},{17,25},{25,17},{2,10},{10... | collective-permute-start | bytes 442376 | tf_op jit(solution)/shard_map/ppermute | solution.py:19
  116.8 13.8 %collective-permute-start.18 = (bf16[192,384]{1,0:T(8,128)(2,1)S(1)}, bf16[192,384]{1,0:T(8,128)(2,1)S(1)}, u32[]{:S(2)}, u32[]{:S(2)}) collective-permute-start(bf16[192,384]{1,0:T(8,128)(2,1)S(1)} %get-tuple-element.93), channel_id=1, source_target_pairs={{0,16},{8,24},{16,0},{24,8},{1,17},{9,25},{17,1},{25,9},{2,18},{10... | collective-permute-start | bytes 442376 | tf_op jit(solution)/shard_map/ppermute | solution.py:19
  118.8 11.8 %collective-permute-start.19 = (bf16[192,384]{1,0:T(8,128)(2,1)S(1)}, bf16[192,384]{1,0:T(8,128)(2,1)S(1)}, u32[]{:S(2)}, u32[]{:S(2)}) collective-permute-start(bf16[192,384]{1,0:T(8,128)(2,1)S(1)} %get-tuple-element.93), channel_id=1, source_target_pairs={{0,24},{8,16},{16,8},{24,0},{1,25},{9,17},{17,9},{25,1},{2,26},{10... | collective-permute-start | bytes 442376 | tf_op jit(solution)/shard_map/ppermute | solution.py:19
  120.2 9.2 %collective-permute-start.20 = (f32[192,192]{1,0:T(8,128)S(1)}, f32[192,192]{1,0:T(8,128)S(1)}, u32[]{:S(2)}, u32[]{:S(2)}) collective-permute-start(f32[192,192]{1,0:T(8,128)S(1)} %get-tuple-element.91), channel_id=1, source_target_pairs={{0,4},{4,0},{1,5},{5,1},{2,6},{6,2},{3,7},{7,3},{8,12},{12,8},{9,1... | collective-permute-start | bytes 442376 | tf_op jit(solution)/shard_map/ppermute | solution.py:19
  130.6 21.9 %collective-permute-start.23 = (bf16[2,3,192,384]{3,2,1,0:T(8,128)(2,1)S(1)}, bf16[2,3,192,384]{3,2,1,0:T(8,128)(2,1)S(1)}, u32[]{:S(2)}, u32[]{:S(2)}) collective-permute-start(bf16[2,3,192,384]{3,2,1,0:T(8,128)(2,1)S(1)} %get-tuple-element.97), channel_id=1, source_target_pairs={{0,8},{8,0},{16,24},{24,16},{1,9},{9,1},{17,25},{25,17},{2,10},{10... | collective-permute-start | bytes 2654216 | tf_op jit(solution)/shard_map/ppermute | solution.py:19
  133.3 8.1 %collective-permute-start.22 = (bf16[384,384]{1,0:T(8,128)(2,1)S(1)}, bf16[384,384]{1,0:T(8,128)(2,1)S(1)}, u32[]{:S(2)}, u32[]{:S(2)}) collective-permute-start(bf16[384,384]{1,0:T(8,128)(2,1)S(1)} %pad_maximum_fusion.2), channel_id=1, source_target_pairs={{0,2},{1,3},{2,0},{3,1},{4,6},{5,7},{6,4},{7,5},{8,10},{9,11},{10,... | collective-permute-start | bytes 884744 | tf_op jit(solution)/shard_map/ppermute | solution.py:19
  135.0 7.8 %collective-permute-start.21 = (bf16[384,384]{1,0:T(8,128)(2,1)S(1)}, bf16[384,384]{1,0:T(8,128)(2,1)S(1)}, u32[]{:S(2)}, u32[]{:S(2)}) collective-permute-start(bf16[384,384]{1,0:T(8,128)(2,1)S(1)} %pad_maximum_fusion.1), channel_id=1, source_target_pairs={{0,4},{4,0},{1,5},{5,1},{2,6},{6,2},{3,7},{7,3},{8,12},{12,8},{9,1... | collective-permute-start | bytes 884744 | tf_op jit(solution)/shard_map/ppermute | solution.py:19
  152.6 26.9 %collective-permute-start.28 = (bf16[768,384]{1,0:T(8,128)(2,1)S(1)}, bf16[768,384]{1,0:T(8,128)(2,1)S(1)}, u32[]{:S(2)}, u32[]{:S(2)}) collective-permute-start(bf16[768,384]{1,0:T(8,128)(2,1)S(1)} %constant_dynamic-update-slice_fusion.9.refs_2_), channel_id=1, source_target_pairs={{0,4},{4,0},{1,5},{5,1},{2,6},{6,2},{3,7},{7,3},{8,12},{12,8},{9,1... | collective-permute-start | bytes 1769480 | tf_op jit(solution)/shard_map/ppermute | solution.py:19
  153.4 26.1 %collective-permute-start.27 = (bf16[768,384]{1,0:T(8,128)(2,1)S(1)}, bf16[768,384]{1,0:T(8,128)(2,1)S(1)}, u32[]{:S(2)}, u32[]{:S(2)}) collective-permute-start(bf16[768,384]{1,0:T(8,128)(2,1)S(1)} %constant_dynamic-update-slice_fusion.6.refs_0_), channel_id=1, source_target_pairs={{0,2},{1,3},{2,0},{3,1},{4,6},{5,7},{6,4},{7,5},{8,10},{9,11},{10,... | collective-permute-start | bytes 1769480 | tf_op jit(solution)/shard_map/ppermute | solution.py:19
  155.0 21.5 %collective-permute-start.24 = (bf16[3,192,384]{2,1,0:T(8,128)(2,1)S(1)}, bf16[3,192,384]{2,1,0:T(8,128)(2,1)S(1)}, u32[]{:S(2)}, u32[]{:S(2)}) collective-permute-start(bf16[3,192,384]{2,1,0:T(8,128)(2,1)S(1)} %get-tuple-element.100), channel_id=1, source_target_pairs={{0,16},{8,24},{16,0},{24,8},{1,17},{9,25},{17,1},{25,9},{2,18},{10... | collective-permute-start | bytes 1327112 | tf_op jit(solution)/shard_map/ppermute | solution.py:19
  177.4 6.8 %collective-permute-start.25 = (f32[192,192]{1,0:T(8,128)S(1)}, f32[192,192]{1,0:T(8,128)S(1)}, u32[]{:S(2)}, u32[]{:S(2)}) collective-permute-start(f32[192,192]{1,0:T(8,128)S(1)} %get-tuple-element.102), channel_id=1, source_target_pairs={{0,4},{4,0},{1,5},{5,1},{2,6},{6,2},{3,7},{7,3},{8,12},{12,8},{9,1... | collective-permute-start | bytes 442376 | tf_op jit(solution)/shard_map/ppermute | solution.py:19
  179.0 15.9 %collective-permute-start.31 = (bf16[768,384]{1,0:T(8,128)(2,1)S(1)}, bf16[768,384]{1,0:T(8,128)(2,1)S(1)}, u32[]{:S(2)}, u32[]{:S(2)}) collective-permute-start(bf16[768,384]{1,0:T(8,128)(2,1)S(1)} %constant_dynamic-update-slice_fusion.9.refs_2_), channel_id=1, source_target_pairs={{0,1},{1,0},{2,3},{3,2},{4,5},{5,4},{6,7},{7,6},{8,9},{9,8},{10,11... | collective-permute-start | bytes 1769480 | tf_op jit(solution)/shard_map/ppermute | solution.py:19
  179.0 15.9 %collective-permute-start.29 = (bf16[768,384]{1,0:T(8,128)(2,1)S(1)}, bf16[768,384]{1,0:T(8,128)(2,1)S(1)}, u32[]{:S(2)}, u32[]{:S(2)}) collective-permute-start(bf16[768,384]{1,0:T(8,128)(2,1)S(1)} %constant_dynamic-update-slice_fusion.6.refs_0_), channel_id=1, source_target_pairs={{0,1},{1,0},{2,3},{3,2},{4,5},{5,4},{6,7},{7,6},{8,9},{9,8},{10,11... | collective-permute-start | bytes 1769480 | tf_op jit(solution)/shard_map/ppermute | solution.py:19
  179.5 15.4 %collective-permute-start.32 = (bf16[768,384]{1,0:T(8,128)(2,1)S(1)}, bf16[768,384]{1,0:T(8,128)(2,1)S(1)}, u32[]{:S(2)}, u32[]{:S(2)}) collective-permute-start(bf16[768,384]{1,0:T(8,128)(2,1)S(1)} %collective-permute-done.28.refs_3_), channel_id=1, source_target_pairs={{0,1},{1,0},{2,3},{3,2},{4,5},{5,4},{6,7},{7,6},{8,9},{9,8},{10,11... | collective-permute-start | bytes 1769480 | tf_op jit(solution)/shard_map/ppermute | solution.py:19
  179.5 15.4 %collective-permute-start.30 = (bf16[768,384]{1,0:T(8,128)(2,1)S(1)}, bf16[768,384]{1,0:T(8,128)(2,1)S(1)}, u32[]{:S(2)}, u32[]{:S(2)}) collective-permute-start(bf16[768,384]{1,0:T(8,128)(2,1)S(1)} %collective-permute-done.27.refs_1_), channel_id=1, source_target_pairs={{0,1},{1,0},{2,3},{3,2},{4,5},{5,4},{6,7},{7,6},{8,9},{9,8},{10,11... | collective-permute-start | bytes 1769480 | tf_op jit(solution)/shard_map/ppermute | solution.py:19
  184.1 10.0 %collective-permute-start.26 = (bf16[192,384]{1,0:T(8,128)(2,1)S(1)}, bf16[192,384]{1,0:T(8,128)(2,1)S(1)}, u32[]{:S(2)}, u32[]{:S(2)}) collective-permute-start(bf16[192,384]{1,0:T(8,128)(2,1)S(1)} %get-tuple-element.103), channel_id=1, source_target_pairs={{0,0},{1,8},{2,16},{3,24},{4,4},{5,12},{6,20},{7,28},{8,1},{9,9},{... | collective-permute-start | bytes 442376 | tf_op jit(solution)/shard_map/ppermute | solution.py:766
  (5 other events, 3.5 us)

commit v4 on v3

--- a/solution.py
+++ b/solution.py
@@ -199,8 +199,8 @@
 def fock_kernel(side, counts, right, *refs):
     outs, (held, raw, turned, sems, last_sem) = refs[sum(counts) : -5], refs[-5:]
     lefts = grouped(refs, counts)
-    before, apart, sent, kept = outs if len(outs) == 4 else (None, None, None, None)
-    out = outs[-1]
+    before, apart, outs = (None, None, outs) if len(outs) == 1 else (outs[0], outs[1], outs[2:])
+    out = outs[0]
     last = pltpu.make_async_copy(right.at[side], raw, last_sem)
     last.start()
     copies = load_left(lefts, held, sems)
@@ -220,14 +220,13 @@
             main = total[:half] + total[half : 2 * half]
             top = main.astype(bf16)
             parts = (top, (main - top.astype(f32)).astype(bf16), total[2 * half :].astype(bf16))
-            distance = q ^ apart[0]
 
             def store(target):
                 for i in range(3):
-                    target[lax.shift_right_logical(distance, 1), i] = parts[i]
-
-            pl.when(lax.rem(distance, 2) == 1)(functools.partial(store, sent))
-            pl.when(lax.rem(distance, 2) == 0)(functools.partial(store, kept))
+                    target[i] = parts[i]
+
+            for distance, target in enumerate(outs):
+                pl.when(q ^ apart[0] == distance)(functools.partial(store, target))
 
 
 def box_fock(side, lefts, right, before, apart):
@@ -238,12 +237,12 @@
     extra = [] if before is None else [before, apart]
     out = jax.ShapeDtypeStruct((len(lefts), tall, width), f32)
     if before is not None:
-        out = [jax.ShapeDtypeStruct((len(lefts) // 2, 3, tall // 3, width), bf16)] * 2
+        out = [jax.ShapeDtypeStruct((3, tall // 3, width), bf16)] * len(lefts)
     return pl.pallas_call(
         functools.partial(fock_kernel, side, counts),
         out_shape=out,
         in_specs=[anywhere] * (sum(counts) + 1) + [vmem, pl.BlockSpec(memory_space=pltpu.SMEM)][: len(extra)],
-        out_specs=vmem if before is None else [vmem, vmem],
+        out_specs=vmem if before is None else [vmem] * len(lefts),
         scratch_shapes=[
             pltpu.VMEM((depth, len(lefts) * width), bf16),
             pltpu.VMEM(right.shape[1:], bf16),
@@ -336,7 +335,7 @@
             pltpu.SemaphoreType.DMA((side // coarse * (side // width),)),
         ],
         compiler_params=params(40),
-        cost_estimate=pl.CostEstimate(flops=4 * side * side * width, bytes_accessed=4 * side * side, transcendentals=0),
+        cost_estimate=pl.CostEstimate(flops=16 * side * side * width, bytes_accessed=4 * side * side, transcendentals=0),
         name="root",
     )(meta, *pieces, offset)
 
@@ -360,7 +359,7 @@
                 return facts[group, r, c]
             swap_id = jnp.where(even, 1, 0) if group == 2 else jnp.where(even, 0, 1)
             near_pair = 1 if group == 2 else 0
-            return facts[2 + 2 * swap_id + jnp.where(pair == near_pair, 0, 1), r, c]
+            return facts[2 + swap_id + jnp.where(pair == near_pair, 0, 2), r, c]
 
         box = (
             level * PAIR + pair,
@@ -596,34 +595,11 @@
     sent[...] = jnp.where(first, high, low)
 
 
-def fock_pair_kernel(kept, got, own, sent):
-    for j in range(2):
-        main, share = (
-            sum((block[j, i].astype(f32) for block in (kept, got) for i in parts), 0.0) for parts in ((0, 1), (2,))
-        )
-        if j == 0:
-            own[0], own[1] = main, share
-        else:
-            top = main.astype(bf16)
-            sent[0], sent[1], sent[2] = top, (main - top.astype(f32)).astype(bf16), share.astype(bf16)
-
-
-def fock_pair(kept, got):
-    vmem = pl.BlockSpec(memory_space=pltpu.VMEM)
-    tall, width = kept.shape[2:]
-    return pl.pallas_call(
-        fock_pair_kernel,
-        out_shape=[jax.ShapeDtypeStruct((2, tall, width), f32), jax.ShapeDtypeStruct((3, tall, width), bf16)],
-        in_specs=[vmem, vmem],
-        out_specs=[vmem, vmem],
-        compiler_params=params(24),
-        name="fock_pair",
-    )(kept, got)
-
-
-def fock_sum_kernel(meta, own, got, share, kept, sent):
-    main = own[0] + got[0].astype(f32) + got[1].astype(f32)
-    share[...] = (own[1] + got[2].astype(f32)).astype(bf16)
+def fock_sum_kernel(meta, *refs):
+    blocks, (share, kept, sent) = refs[:-3], refs[-3:]
+    sums = [sum((block[part].astype(f32) for block in blocks[1:]), blocks[0][part].astype(f32)) for part in range(3)]
+    main = sums[0] + sums[1]
+    share[...] = sums[2].astype(bf16)
     half = kept.shape[0]
     first = meta[0] == 0
     low, high = main[:, :half].T, main[:, half:].T
@@ -672,21 +648,19 @@
 
     matrices = block_matrices(deriv_blocks)
 
-    far, active, parts, beside_rest, matrices = lax.optimization_barrier(
-        (
-            far,
-            active,
-            [mine, beside, first_mine, first_beside, second_mine, second_beside],
-            beside_rest,
-            matrices,
-        )
-    )
-    beside = parts[1]
-    facts = jnp.stack([part[:, fold, :8] for part in parts]).astype(f32).astype(jnp.int32)
-
+    def facts_of(parts):
+        return jnp.stack([part[:, fold, :8] for part in parts]).astype(f32).astype(jnp.int32)
+
+    early_facts = facts_of([mine, beside, first_mine, second_mine])
     flat = lambda block: block.reshape(-1, block.shape[-1])
     cut = -(-slots * coefficients // (2 * ROWS)) * ROWS
     beside_all, beside_top = unfold(pack_meta, beside, beside_rest, fold, cut)
+
+    parts = [mine, beside, first_mine, first_beside, second_mine, second_beside]
+    far, active, parts, beside_all, beside_top, matrices, early_facts = lax.optimization_barrier(
+        (far, active, parts, beside_all, beside_top, matrices, early_facts)
+    )
+    facts = jnp.concatenate([early_facts, facts_of([parts[3], parts[5]])])
     cross = {q: [swap(beside_top, "orb", q), swap(flat(far[q])[cut:], "pair", 1)] for q in far}
     left_own = {0: active, 1: swap(active, "orb", 1), **far}
     left_beside = {0: [beside_all], 1: [swap(beside_all, "orb", 1)]}
@@ -701,8 +675,7 @@
         steps = range(1, level_count)
         return [mine_block(level)] + [swap(mine_block(level ^ step), "lvl", step) for step in steps]
 
-    def both_halves(kept, sent):
-        got = swap(sent, "pair", 1)
+    def both_halves(kept, got):
         return jnp.concatenate([jnp.where(first, kept, got), jnp.where(first, got, kept)], axis=1)
 
     def own_block(strip):
@@ -733,39 +706,40 @@
         sent = along_levels(blocks)
         sent, fock_part = lax.optimization_barrier((sent, fock_part))
         small, kept, other = level_sum(offset_sum_kernel, meta, sent)
-        offset = both_halves(kept, other)
+        offset = both_halves(kept, swap(other, "pair", 1))
     else:
         offset = own_block(natural(blocks).astype(f32))
     row_ids = row0 + jnp.arange(box_rows, dtype=jnp.int32)
     col_ids = col0 + jnp.arange(own_width, dtype=jnp.int32)
     correlation = offset + (row_ids[:, None] == col_ids[None, :]).astype(f32)
     apart = (orb ^ level if square_grid else 0 * orb).reshape(1).astype(jnp.int32)
-    odd, even = box_fock(1, lefts_beside, right, fock_part, apart)
+    fock_blocks = box_fock(1, lefts_beside, right, fock_part, apart)
     if square_grid:
         pieces = [small] + [swap(small, "lvl", z) for z in range(1, level_count)]
-        pieces, odd, even, offset = lax.optimization_barrier((pieces, odd, even, offset))
+        pieces, fock_blocks, offset = lax.optimization_barrier((pieces, fock_blocks, offset))
         join = functools.partial(jnp.concatenate, axis=0)
         top, low = join(pieces[: level_count // 2]), join(pieces[level_count // 2 :])
-        paired = swap(odd, "lvl", 1)
+        sent = [fock_blocks[0]] + [swap(fock_blocks[step], "lvl", step) for step in range(1, level_count)]
         got = [swap(top, "pair", 1), swap(low, "orb", 2)]
-        got, paired = lax.optimization_barrier((got, paired))
-        own_sum, fock_sent = fock_pair(even, paired)
-        fock_got = swap(fock_sent, "lvl", 2)
+        got, sent[2] = lax.optimization_barrier((got, sent[2]))
         top, low = join([top, got[0]]), join([low, got[1]])
         pieces = [top, swap(top, "orb", 2), low, swap(low, "pair", 1)]
+        pieces, sent = lax.optimization_barrier((pieces, sent))
         pieces += [swap(piece, "orb", 1) for piece in pieces]
         root_meta = jnp.stack([level, pair, orb]).astype(jnp.int32)
         inverse_root = root_of(root_meta, pieces, offset, all_width, level_count)
-        share, kept, other = level_sum(fock_sum_kernel, meta, [own_sum, fock_got])
+        share, kept, other = level_sum(fock_sum_kernel, meta, sent)
         to = [
             ((z * PAIR + y) * orb_count + o, (o * PAIR + y) * orb_count + z)
             for z in range(level_count)
             for y in range(PAIR)
             for o in groups
         ]
-        fock = both_halves(kept, other) + lax.ppermute(share, BOX + ("orb",), to).astype(f32)
+        got = swap(other, "pair", 1), lax.ppermute(share, BOX + ("orb",), to)
+        inverse_root, got = lax.optimization_barrier((inverse_root, got))
+        fock = both_halves(kept, got[0]) + got[1].astype(f32)
     else:
-        fock_blocks = jnp.stack([even, odd], axis=1).reshape(orb_count, 3, half, own_width)
+        fock_blocks = jnp.stack(fock_blocks)
         main = natural(fock_blocks[:, 0]).astype(f32) + natural(fock_blocks[:, 1]).astype(f32)
         main = lax.all_gather(lax.psum(main, "lvl"), "pair", axis=0, tiled=True)
         fock = lax.dynamic_slice_in_dim(main, row0, box_rows, axis=1).T + own_block(natural(fock_blocks[:, 2]).astype(f32))

time: 203 us -> 192 us (0.946); the launches traced: 203 us -> 196 us
  waiting for transfers between devices: 73.2 us -> 62.7 us
  local copies, waits for them, and re-layouts: 14.7 us -> 8.89 us
  starting transfers between devices: 46.5 us -> 52.3 us
  Pallas kernels: 65.1 us -> 67.7 us
    ppermute x1, waiting for transfers between devices: 8 us -> 0.01 us  [body(): got = (swap(other, 'pair', 1), lax.ppermute(share, BOX + ('orb',), to))]
    unnamed x51 -> x37, local copies, waits for them, and re-layouts: 9.47 us -> 3.67 us
    ppermute x1, starting transfers between devices: 1.91 us -> 4.73 us  [body(): got = (swap(other, 'pair', 1), lax.ppermute(share, BOX + ('orb',), to))]
    ppermute x28 -> x29, waiting for transfers between devices: 64.4 us -> 62.1 us  [swap(): return lax.ppermute(value, axis, [(i, i ^ bit) for i in range(count)])]
    ppermute x28 -> x29, starting transfers between devices: 38.3 us -> 39.3 us  [swap(): return lax.ppermute(value, axis, [(i, i ^ bit) for i in range(count)])]
  transfers between devices with their start and end apart: 33 -> 34, of which waited for: 11 -> 9; matrix products, arithmetic and copies ran while one was open for 2% -> 2% of each run, Pallas kernels for 23% -> 30%
where the time goes in v4:
time: 192 us; the launch traced here: 196 us
  Pallas kernels  67.7 us (35%)
  waiting for transfers between devices  62.7 us (33%)
  starting transfers between devices  52.3 us (27%)
  local copies, waits for them, and re-layouts  8.89 us (5%)
  other arithmetic  2.16 us (1%)
    ppermute x29, waiting for transfers between devices, swap(): return lax.ppermute(value, axis, [(i, i ^ bit) for i in range(count)])  62.1 us
    ppermute x29, starting transfers between devices, swap(): return lax.ppermute(value, axis, [(i, i ^ bit) for i in range(count)])  39.3 us
    pallas_call x1, Pallas kernels, kinetic(): pl.pallas_call(functools.partial(kinetic_kernel, edge, slots, levels), ou...  25.4 us
    pallas_call x2, Pallas kernels, box_fock(): pl.pallas_call(functools.partial(fock_kernel, side, counts), out_shape=ou...  16.7 us
    pallas_call x2, Pallas kernels, box_correlation(): pl.pallas_call(functools.partial(correlation_kernel, share, counts), out_...  9.16 us
    pallas_call x1, Pallas kernels, root_of(): pl.pallas_call(functools.partial(root_kernel, levels), out_shape=jax.Shap...  8.39 us
    ppermute x4, starting transfers between devices, trade(): return lax.ppermute(value, axis, pairs + [(b, a) for a, b in pairs])  8.27 us
    ppermute x1, starting transfers between devices, body(): got = (swap(other, 'pair', 1), lax.ppermute(share, BOX + ('orb',), to))  4.73 us
  transfers between devices with their start and end apart: 34, of which 9 were waited for; matrix products, arithmetic and copies ran while one was open for 2% of the time, Pallas kernels for 30%

profile of v4, /device:TPU:2, one launch (start us, length us, event | category | flops | bytes accessed | tf_op | source)
XLA Modules:
  0.0 195.6 jit_solution(17861881087347809570)
XLA Ops:
  1.5 0.8 copy.20
  2.3 0.7 pad.4.pot
  3.8 3.2 %pack.1 = (bf16[2,528,384]{2,1,0:T(8,128)(2,1)S(1)}, bf16[2,528,384]{2,1,0:T(8,128)(2,1)}) custom-call(s32[3]{0:T(128)S(1)} %pad_add_fusion.1.meta, s32[2,6]{1,0:T(2,128)S(1)} %reshape.42.neighbours, s32[2]{0:T(128)S(1)} %copy-done.11, bf16[2,1000,384]{2,1,0:T(8,128)(2,1)} %orbitals.1, f32[2,1152]{1,0:T(2,128)S(1)} %pad.4.pot), custom_call_target="tpu_custom_call" | custom-call | tf_op jit(solution)/shard_map/pack/pallas_call | solution.py:75
  7.0 1.5 collective-permute-start.1
  8.5 1.6 collective-permute-start.4
  10.6 3.6 %collective-permute-start.2 = (bf16[2,528,384]{2,1,0:T(8,128)(2,1)}, bf16[2,528,384]{2,1,0:T(8,128)(2,1)}, u32[]{:S(2)}, u32[]{:S(2)}) collective-permute-start(bf16[2,528,384]{2,1,0:T(8,128)(2,1)} %get-tuple-element.84.refs_0_), channel_id=1, source_target_pairs={{0,8},{16,24},{8,0},{24,16},{1,9},{17,25},{9,1},{25,17},{2,10},{18... | collective-permute-start | bytes 2433032 | tf_op jit(solution)/shard_map/ppermute | solution.py:24
  14.7 13.4 %collective-permute-done.1.beside_in.refs_1_ = bf16[2,528,384]{2,1,0:T(8,128)(2,1)} collective-permute-done((bf16[2,528,384]{2,1,0:T(8,128)(2,1)S(1)}, bf16[2,528,384]{2,1,0:T(8,128)(2,1)}, u32[]{:S(2)}, u32[]{:S(2)}) %collective-permute-start.1) | collective-permute-done | bytes 811040 | tf_op jit(solution)/shard_map/ppermute | solution.py:19
  28.1 1.6 collective-permute-start.3
  29.6 1.6 collective-permute-start.5
  31.2 0.7 slice.21
  32.1 1.0 matrices.1
  33.2 0.7 slice.30
  35.3 8.9 %collective-permute-done.6.rest_in = bf16[2,528,384]{2,1,0:T(8,128)(2,1)S(1)} collective-permute-done((bf16[2,528,384]{2,1,0:T(8,128)(2,1)}, bf16[2,528,384]{2,1,0:T(8,128)(2,1)S(1)}, u32[]{:S(2)}, u32[]{:S(2)}) %collective-permute-start.6) | collective-permute-done | bytes 811040 | tf_op jit(solution)/shard_map/ppermute | solution.py:19
  44.2 0.9 copy-done
  45.1 1.1 copy-done.1
  46.2 2.2 %unfold.1 = (bf16[2000,384]{1,0:T(8,128)(2,1)S(1)}, bf16[1008,384]{1,0:T(8,128)(2,1)S(1)}) custom-call(s32[3]{0:T(128)S(1)} %pad_add_fusion.1.meta, bf16[2,528,384]{2,1,0:T(8,128)(2,1)} %collective-permute-done.1.beside_in.refs_1_, bf16[2,528,384]{2,1,0:T(8,128)(2,1)S(1)} %copy-done.1), custom_call_target="tpu_custom_call" | custom-call | tf_op jit(solution)/shard_map/unfold/pallas_call | solution.py:110
  49.1 0.7 slice.26
  49.8 0.7 slice.27
  50.5 1.0 collective-permute-start.8
  51.5 1.1 collective-permute-start.7
  53.2 25.4 %kinetic.1 = bf16[4,1000,576]{2,1,0:T(8,128)(2,1)} custom-call(s32[2]{0:T(128)S(1)} %pad_add_fusion.2.place_meta, s32[6,2,8]{2,1,0:T(2,128)S(1)} %pad_add_fusion.facts, bf16[2,528,384]{2,1,0:T(8,128)(2,1)} %get-tuple-element.84.refs_0_, bf16[2,528,384]{2,1,0:T(8,128)(2,1)} %collective-permute-done.1.beside_in.refs_1_, ...), custom_call_target="tpu_custom_call" | custom-call | flops 20000000000 | bytes 40000000 | tf_op jit(solution)/shard_map/kinetic/pallas_call | solution.py:561
  79.1 4.8 %correlation.2.refs_6_ = f32[4,192,384]{2,1,0:T(8,128)S(1)} custom-call(s32[3]{0:T(128)S(1)} %pad_add_fusion.3.meta, bf16[2000,384]{1,0:T(8,128)(2,1)} %bitcast.5.refs_0_, bf16[2000,384]{1,0:T(8,128)(2,1)} %bitcast.6.refs_1_, bf16[2000,384]{1,0:T(8,128)(2,1)S(1)} %bitcast.36, bf16[2000,384]{1,0:T(8,128)(2,1)} %bitcast.7.refs_3_), custom_call_target="tpu_custom_call" | custom-call | flops 1179648000 | bytes 6144000 | tf_op jit(solution)/shard_map/correlation/pallas_call | solution.py:179
  84.0 4.4 %correlation.3 = bf16[4,192,384]{2,1,0:T(8,128)(2,1)S(1)} custom-call(s32[3]{0:T(128)S(1)} %pad_add_fusion.3.meta, bf16[2000,384]{1,0:T(8,128)(2,1)S(1)} %get-tuple-element.94.refs_0_, bf16[2000,384]{1,0:T(8,128)(2,1)} %collective-permute-done.9.refs_1_, bf16[1008,384]{1,0:T(8,128)(2,1)} %collective-permute-done.7.refs_2_, ...), custom_call_target="tpu_custom_call" | custom-call | flops 1179648000 | bytes 6144000 | tf_op jit(solution)/shard_map/correlation/pallas_call | solution.py:179
  88.4 11.1 %collective-permute-start.14 = (bf16[192,384]{1,0:T(8,128)(2,1)S(1)}, bf16[192,384]{1,0:T(8,128)(2,1)S(1)}, u32[]{:S(2)}, u32[]{:S(2)}) collective-permute-start(bf16[192,384]{1,0:T(8,128)(2,1)S(1)} %get-tuple-element.141), channel_id=1, source_target_pairs={{0,8},{8,0},{16,24},{24,16},{1,9},{9,1},{17,25},{25,17},{2,10},{10... | collective-permute-start | bytes 442376 | tf_op jit(solution)/shard_map/ppermute | solution.py:19
  99.6 2.4 %collective-permute-start.16 = (bf16[192,384]{1,0:T(8,128)(2,1)S(1)}, bf16[192,384]{1,0:T(8,128)(2,1)S(1)}, u32[]{:S(2)}, u32[]{:S(2)}) collective-permute-start(bf16[192,384]{1,0:T(8,128)(2,1)S(1)} %get-tuple-element.139), channel_id=1, source_target_pairs={{0,24},{8,16},{16,8},{24,0},{1,25},{9,17},{17,9},{25,1},{2,26},{10... | collective-permute-start | bytes 442376 | tf_op jit(solution)/shard_map/ppermute | solution.py:19
  102.0 8.2 %fock.2.refs_6_ = f32[4,576,384]{2,1,0:T(8,128)S(1)} custom-call(bf16[2,2000,576]{2,1,0:T(8,128)(2,1)} %bitcast.38, bf16[2000,384]{1,0:T(8,128)(2,1)} %bitcast.5.refs_0_, bf16[2000,384]{1,0:T(8,128)(2,1)} %bitcast.6.refs_1_, bf16[2000,384]{1,0:T(8,128)(2,1)S(1)} %bitcast.37, bf16[2000,384]{1,0:T(8,128)(2,1)} %bitcast.7.refs_3_), custom_call_target="tpu_custom_call" | custom-call | flops 3538944000 | bytes 6144000 | tf_op jit(solution)/shard_map/fock/pallas_call | solution.py:241
  110.2 2.0 %collective-permute-done.15.refs_2_ = bf16[192,384]{1,0:T(8,128)(2,1)S(1)} collective-permute-done((bf16[192,384]{1,0:T(8,128)(2,1)S(1)}, bf16[192,384]{1,0:T(8,128)(2,1)S(1)}, u32[]{:S(2)}, u32[]{:S(2)}) %collective-permute-start.15) | collective-permute-done | bytes 147488 | tf_op jit(solution)/shard_map/ppermute | solution.py:19
  112.2 0.8 level_sum.2
  113.0 3.7 %collective-permute-start.17 = (bf16[192,384]{1,0:T(8,128)(2,1)S(1)}, bf16[192,384]{1,0:T(8,128)(2,1)S(1)}, u32[]{:S(2)}, u32[]{:S(2)}) collective-permute-start(bf16[192,384]{1,0:T(8,128)(2,1)S(1)} %get-tuple-element.111), channel_id=1, source_target_pairs={{0,8},{8,0},{16,24},{24,16},{1,9},{9,1},{17,25},{25,17},{2,10},{10... | collective-permute-start | bytes 442376 | tf_op jit(solution)/shard_map/ppermute | solution.py:19
  116.7 2.4 %collective-permute-start.19 = (bf16[192,384]{1,0:T(8,128)(2,1)S(1)}, bf16[192,384]{1,0:T(8,128)(2,1)S(1)}, u32[]{:S(2)}, u32[]{:S(2)}) collective-permute-start(bf16[192,384]{1,0:T(8,128)(2,1)S(1)} %get-tuple-element.111), channel_id=1, source_target_pairs={{0,24},{8,16},{16,8},{24,0},{1,25},{9,17},{17,9},{25,1},{2,26},{10... | collective-permute-start | bytes 442376 | tf_op jit(solution)/shard_map/ppermute | solution.py:19
  119.2 1.5 collective-permute-start.20
  120.7 8.5 %fock.3 = (bf16[3,192,384]{2,1,0:T(8,128)(2,1)S(1)}, bf16[3,192,384]{2,1,0:T(8,128)(2,1)S(1)}, bf16[3,192,384]{2,1,0:T(8,128)(2,1)S(1)}, bf16[3,192,384]{2,1,0:T(8,128)(2,1)S(1)}) custom-call(bf16[2,2000,576]{2,1,0:T(8,128)(2,1)} %bitcast.39, bf16[2000,384]{1,0:T(8,128)(2,1)S(1)} %get-tuple-element.94.refs_0_, ...), custom_call_target="tpu_custom_call" | custom-call | flops 3538944000 | bytes 6144000 | tf_op jit(solution)/shard_map/fock/pallas_call | solution.py:241
  129.3 0.9 convert_add_fusion
  130.2 1.5 collective-permute-start.22
  131.8 1.6 collective-permute-start.21
  133.3 2.1 %collective-permute-start.23 = (bf16[3,192,384]{2,1,0:T(8,128)(2,1)S(1)}, bf16[3,192,384]{2,1,0:T(8,128)(2,1)S(1)}, u32[]{:S(2)}, u32[]{:S(2)}) collective-permute-start(bf16[3,192,384]{2,1,0:T(8,128)(2,1)S(1)} %get-tuple-element.115), channel_id=1, source_target_pairs={{0,16},{8,24},{16,0},{24,8},{1,17},{9,25},{17,1},{25,9},{2,18},{10... | collective-permute-start | bytes 1327112 | tf_op jit(solution)/shard_map/ppermute | solution.py:19
  135.5 2.8 %collective-permute-done.22 = bf16[384,384]{1,0:T(8,128)(2,1)S(1)} collective-permute-done((bf16[384,384]{1,0:T(8,128)(2,1)S(1)}, bf16[384,384]{1,0:T(8,128)(2,1)S(1)}, u32[]{:S(2)}, u32[]{:S(2)}) %collective-permute-start.22) | collective-permute-done | bytes 294944 | tf_op jit(solution)/shard_map/ppermute | solution.py:19
  138.3 1.3 collective-permute-done.21
  139.6 14.4 %collective-permute-done.23.refs_2_ = bf16[3,192,384]{2,1,0:T(8,128)(2,1)S(1)} collective-permute-done((bf16[3,192,384]{2,1,0:T(8,128)(2,1)S(1)}, bf16[3,192,384]{2,1,0:T(8,128)(2,1)S(1)}, u32[]{:S(2)}, u32[]{:S(2)}) %collective-permute-start.23) | collective-permute-done | bytes 442400 | tf_op jit(solution)/shard_map/ppermute | solution.py:19
  154.1 0.9 collective-permute-start.25
  155.9 2.8 %collective-permute-start.27 = (bf16[3,192,384]{2,1,0:T(8,128)(2,1)S(1)}, bf16[3,192,384]{2,1,0:T(8,128)(2,1)S(1)}, u32[]{:S(2)}, u32[]{:S(2)}) collective-permute-start(bf16[3,192,384]{2,1,0:T(8,128)(2,1)S(1)} %get-tuple-element.121), channel_id=1, source_target_pairs={{0,24},{8,16},{16,8},{24,0},{1,25},{9,17},{17,9},{25,1},{2,26},{10... | collective-permute-start | bytes 1327112 | tf_op jit(solution)/shard_map/ppermute | solution.py:19
  158.7 7.8 %collective-permute-done.26.refs_1_ = bf16[3,192,384]{2,1,0:T(8,128)(2,1)S(1)} collective-permute-done((bf16[3,192,384]{2,1,0:T(8,128)(2,1)S(1)}, bf16[3,192,384]{2,1,0:T(8,128)(2,1)S(1)}, u32[]{:S(2)}, u32[]{:S(2)}) %collective-permute-start.26) | collective-permute-done | bytes 442400 | tf_op jit(solution)/shard_map/ppermute | solution.py:19
  166.5 11.4 %collective-permute-done.27.refs_3_ = bf16[3,192,384]{2,1,0:T(8,128)(2,1)S(1)} collective-permute-done((bf16[3,192,384]{2,1,0:T(8,128)(2,1)S(1)}, bf16[3,192,384]{2,1,0:T(8,128)(2,1)S(1)}, u32[]{:S(2)}, u32[]{:S(2)}) %collective-permute-start.27) | collective-permute-done | bytes 442400 | tf_op jit(solution)/shard_map/ppermute | solution.py:19
  179.0 0.9 level_sum.3
  180.0 1.6 collective-permute-start.32
  181.6 4.7 %collective-permute-start.33 = (bf16[192,384]{1,0:T(8,128)(2,1)S(1)}, bf16[192,384]{1,0:T(8,128)(2,1)S(1)}, u32[]{:S(2)}, u32[]{:S(2)}) collective-permute-start(bf16[192,384]{1,0:T(8,128)(2,1)S(1)} %get-tuple-element.133), channel_id=1, source_target_pairs={{0,0},{1,8},{2,16},{3,24},{4,4},{5,12},{6,20},{7,28},{8,1},{9,9},{... | collective-permute-start | bytes 442376 | tf_op jit(solution)/shard_map/ppermute | solution.py:738
  186.3 8.4 %root.1 = f32[192,384]{1,0:T(8,128)} custom-call(s32[3]{0:T(128)S(1)} %pad_add_fusion.4.meta, bf16[768,384]{1,0:T(8,128)(2,1)S(1)} %constant_dynamic-update-slice_fusion.refs_0_, bf16[768,384]{1,0:T(8,128)(2,1)S(1)} %collective-permute-done.24.refs_1_, bf16[768,384]{1,0:T(8,128)(2,1)S(1)} %constant_dynamic-update-slice_fusion.3.refs_2_, ...), custom_call_target="tpu_custom_call" | custom-call | flops 14495514624 | bytes 9437184 | tf_op jit(solution)/shard_map/root/pallas_call | solution.py:326
  194.8 0.8 maximum_add_fusion
  (96 shorter events, 7.7 us)
Async XLA Ops:
  0.6 31.4 %copy-start.7 = (bf16[112,10]{1,0:T(8,128)(2,1)S(1)}, bf16[112,10]{1,0:T(8,128)(2,1)}, u32[]{:S(2)}) copy-start(bf16[112,10]{1,0:T(8,128)(2,1)} %constant.60.clone.refs_0_) | copy-start | bytes 6724
  0.6 31.4 %copy-start.9 = (bf16[30,336]{1,0:T(8,128)(2,1)S(1)}, bf16[30,336]{1,0:T(8,128)(2,1)}, u32[]{:S(2)}) copy-start(bf16[30,336]{1,0:T(8,128)(2,1)} %constant.61.clone.refs_1_) | copy-start | bytes 60484
  0.7 31.4 %copy-start.3 = (f32[112,112]{1,0:T(8,128)S(1)}, f32[112,112]{1,0:T(8,128)}, u32[]{:S(2)}) copy-start(f32[112,112]{1,0:T(8,128)} %constant.62.clone.refs_2_) | copy-start | bytes 150532
  0.7 31.3 %copy-start.8 = (bf16[112,10]{1,0:T(8,128)(2,1)S(1)}, bf16[112,10]{1,0:T(8,128)(2,1)}, u32[]{:S(2)}) copy-start(bf16[112,10]{1,0:T(8,128)(2,1)} %constant.63.clone.refs_3_) | copy-start | bytes 6724
  0.7 31.3 %copy-start.10 = (bf16[30,336]{1,0:T(8,128)(2,1)S(1)}, bf16[30,336]{1,0:T(8,128)(2,1)}, u32[]{:S(2)}) copy-start(bf16[30,336]{1,0:T(8,128)(2,1)} %constant.64.clone.refs_4_) | copy-start | bytes 60484
  0.7 31.3 %copy-start.4 = (f32[112,112]{1,0:T(8,128)S(1)}, f32[112,112]{1,0:T(8,128)}, u32[]{:S(2)}) copy-start(f32[112,112]{1,0:T(8,128)} %constant.65.clone.refs_5_) | copy-start | bytes 150532
  0.7 31.3 %copy-start.5 = (bf16[160,10]{1,0:T(8,128)(2,1)S(1)}, bf16[160,10]{1,0:T(8,128)(2,1)}, u32[]{:S(2)}) copy-start(bf16[160,10]{1,0:T(8,128)(2,1)} %constant.66.clone.refs_6_) | copy-start | bytes 9604
  0.7 31.3 %copy-start.6 = (bf16[30,480]{1,0:T(8,128)(2,1)S(1)}, bf16[30,480]{1,0:T(8,128)(2,1)}, u32[]{:S(2)}) copy-start(bf16[30,480]{1,0:T(8,128)(2,1)} %constant.67.clone.refs_7_) | copy-start | bytes 86404
  0.7 31.3 %copy-start.2 = (f32[160,160]{1,0:T(8,128)S(1)}, f32[160,160]{1,0:T(8,128)}, u32[]{:S(2)}) copy-start(f32[160,160]{1,0:T(8,128)} %constant.68.clone.refs_8_) | copy-start | bytes 307204
  3.1 0.7 copy-start.11
  3.8 28.1 %copy-start.12 = (bf16[3,10,10]{2,0,1:T(4,128)(2,1)S(1)}, bf16[3,10,10]{2,0,1:T(4,128)(2,1)}, u32[]{:S(2)}) copy-start(bf16[3,10,10]{2,0,1:T(4,128)(2,1)} %param.17) | copy-start | bytes 1804
  7.0 21.1 %collective-permute-start.1 = (bf16[2,528,384]{2,1,0:T(8,128)(2,1)S(1)}, bf16[2,528,384]{2,1,0:T(8,128)(2,1)}, u32[]{:S(2)}, u32[]{:S(2)}) collective-permute-start(bf16[2,528,384]{2,1,0:T(8,128)(2,1)S(1)} %get-tuple-element.71), channel_id=1, source_target_pairs={{0,4},{4,0},{1,5},{5,1},{2,6},{6,2},{3,7},{7,3},{8,12},{12,8},{9,1... | collective-permute-start | bytes 2433032 | tf_op jit(solution)/shard_map/ppermute | solution.py:19
  8.5 21.1 %collective-permute-start.4 = (bf16[2,528,384]{2,1,0:T(8,128)(2,1)}, bf16[2,528,384]{2,1,0:T(8,128)(2,1)}, u32[]{:S(2)}, u32[]{:S(2)}) collective-permute-start(bf16[2,528,384]{2,1,0:T(8,128)(2,1)} %get-tuple-element.84.refs_0_), channel_id=1, source_target_pairs={{8,16},{16,8},{9,17},{17,9},{10,18},{18,10},{11,19},{19,11},{12,20... | collective-permute-start | bytes 2433032 | tf_op jit(solution)/shard_map/ppermute | solution.py:24
  10.1 38.4 %collective-permute-start = (bf16[2,1000,384]{2,1,0:T(8,128)(2,1)}, bf16[2,1000,384]{2,1,0:T(8,128)(2,1)S(1)}, u32[]{:S(2)}, u32[]{:S(2)}) collective-permute-start(bf16[2,1000,384]{2,1,0:T(8,128)(2,1)} %orbitals.1), channel_id=1, source_target_pairs={{0,2},{1,3},{2,0},{3,1},{4,6},{5,7},{6,4},{7,5},{8,10},{9,11},{10,... | collective-permute-start | bytes 4608008 | tf_op jit(solution)/shard_map/ppermute | solution.py:19
  10.6 23.3 %collective-permute-start.2 = (bf16[2,528,384]{2,1,0:T(8,128)(2,1)}, bf16[2,528,384]{2,1,0:T(8,128)(2,1)}, u32[]{:S(2)}, u32[]{:S(2)}) collective-permute-start(bf16[2,528,384]{2,1,0:T(8,128)(2,1)} %get-tuple-element.84.refs_0_), channel_id=1, source_target_pairs={{0,8},{16,24},{8,0},{24,16},{1,9},{17,25},{9,1},{25,17},{2,10},{18... | collective-permute-start | bytes 2433032 | tf_op jit(solution)/shard_map/ppermute | solution.py:24
  14.2 30.0 %collective-permute-start.6 = (bf16[2,528,384]{2,1,0:T(8,128)(2,1)}, bf16[2,528,384]{2,1,0:T(8,128)(2,1)S(1)}, u32[]{:S(2)}, u32[]{:S(2)}) collective-permute-start(bf16[2,528,384]{2,1,0:T(8,128)(2,1)} %get-tuple-element.84.refs_0_), channel_id=1, source_target_pairs={{0,4},{4,0},{1,5},{5,1},{2,6},{6,2},{3,7},{7,3},{8,12},{12,8},{9,1... | collective-permute-start | bytes 2433032 | tf_op jit(solution)/shard_map/ppermute | solution.py:19
  28.1 21.0 %collective-permute-start.3 = (bf16[2,528,384]{2,1,0:T(8,128)(2,1)}, bf16[2,528,384]{2,1,0:T(8,128)(2,1)}, u32[]{:S(2)}, u32[]{:S(2)}) collective-permute-start(bf16[2,528,384]{2,1,0:T(8,128)(2,1)} %collective-permute-done.1.beside_in.refs_1_), channel_id=1, source_target_pairs={{0,8},{16,24},{8,0},{24,16},{1,9},{17,25},{9,1},{25,17},{2,10},{18... | collective-permute-start | bytes 2433032 | tf_op jit(solution)/shard_map/ppermute | solution.py:24
  29.6 19.5 %collective-permute-start.5 = (bf16[2,528,384]{2,1,0:T(8,128)(2,1)}, bf16[2,528,384]{2,1,0:T(8,128)(2,1)}, u32[]{:S(2)}, u32[]{:S(2)}) collective-permute-start(bf16[2,528,384]{2,1,0:T(8,128)(2,1)} %collective-permute-done.1.beside_in.refs_1_), channel_id=1, source_target_pairs={{8,16},{16,8},{9,17},{17,9},{10,18},{18,10},{11,19},{19,11},{12,20... | collective-permute-start | bytes 2433032 | tf_op jit(solution)/shard_map/ppermute | solution.py:24
  44.2 0.9 copy-start
  45.1 1.1 copy-start.1
  50.5 28.7 %collective-permute-start.13 = (bf16[2,1000,384]{2,1,0:T(8,128)(2,1)S(1)}, bf16[2,1000,384]{2,1,0:T(8,128)(2,1)}, u32[]{:S(2)}, u32[]{:S(2)}) collective-permute-start(bf16[2,1000,384]{2,1,0:T(8,128)(2,1)S(1)} %collective-permute-done), channel_id=1, source_target_pairs={{0,1},{1,0},{2,3},{3,2},{4,5},{5,4},{6,7},{7,6},{8,9},{9,8},{10,11... | collective-permute-start | bytes 4608008 | tf_op jit(solution)/shard_map/ppermute | solution.py:19
  50.5 28.0 %collective-permute-start.8 = (bf16[992,384]{1,0:T(8,128)(2,1)S(1)}, bf16[992,384]{1,0:T(8,128)(2,1)}, u32[]{:S(2)}, u32[]{:S(2)}) collective-permute-start(bf16[992,384]{1,0:T(8,128)(2,1)S(1)} %slice.31), channel_id=1, source_target_pairs={{0,4},{4,0},{1,5},{5,1},{2,6},{6,2},{3,7},{7,3},{8,12},{12,8},{9,1... | collective-permute-start | bytes 2285576 | tf_op jit(solution)/shard_map/ppermute | solution.py:19
  51.5 27.0 %collective-permute-start.7 = (bf16[1008,384]{1,0:T(8,128)(2,1)S(1)}, bf16[1008,384]{1,0:T(8,128)(2,1)}, u32[]{:S(2)}, u32[]{:S(2)}) collective-permute-start(bf16[1008,384]{1,0:T(8,128)(2,1)S(1)} %get-tuple-element.79), channel_id=1, source_target_pairs={{0,2},{1,3},{2,0},{3,1},{4,6},{5,7},{6,4},{7,5},{8,10},{9,11},{10,... | collective-permute-start | bytes 2322440 | tf_op jit(solution)/shard_map/ppermute | solution.py:19
  52.6 26.5 %collective-permute-start.12 = (bf16[2,1000,384]{2,1,0:T(8,128)(2,1)}, bf16[2,1000,384]{2,1,0:T(8,128)(2,1)}, u32[]{:S(2)}, u32[]{:S(2)}) collective-permute-start(bf16[2,1000,384]{2,1,0:T(8,128)(2,1)} %orbitals.1), channel_id=1, source_target_pairs={{0,1},{1,0},{2,3},{3,2},{4,5},{5,4},{6,7},{7,6},{8,9},{9,8},{10,11... | collective-permute-start | bytes 4608008 | tf_op jit(solution)/shard_map/ppermute | solution.py:19
  52.6 31.3 %collective-permute-start.9 = (bf16[2000,384]{1,0:T(8,128)(2,1)S(1)}, bf16[2000,384]{1,0:T(8,128)(2,1)}, u32[]{:S(2)}, u32[]{:S(2)}) collective-permute-start(bf16[2000,384]{1,0:T(8,128)(2,1)S(1)} %get-tuple-element.94.refs_0_), channel_id=1, source_target_pairs={{0,1},{1,0},{2,3},{3,2},{4,5},{5,4},{6,7},{7,6},{8,9},{9,8},{10,11... | collective-permute-start | bytes 4608008 | tf_op jit(solution)/shard_map/ppermute | solution.py:19
  78.5 5.4 %collective-permute-start.10 = (bf16[1008,384]{1,0:T(8,128)(2,1)}, bf16[1008,384]{1,0:T(8,128)(2,1)}, u32[]{:S(2)}, u32[]{:S(2)}) collective-permute-start(bf16[1008,384]{1,0:T(8,128)(2,1)} %collective-permute-done.7.refs_2_), channel_id=1, source_target_pairs={{0,1},{1,0},{2,3},{3,2},{4,5},{5,4},{6,7},{7,6},{8,9},{9,8},{10,11... | collective-permute-start | bytes 2322440 | tf_op jit(solution)/shard_map/ppermute | solution.py:19
  78.6 5.3 %collective-permute-start.11 = (bf16[992,384]{1,0:T(8,128)(2,1)}, bf16[992,384]{1,0:T(8,128)(2,1)}, u32[]{:S(2)}, u32[]{:S(2)}) collective-permute-start(bf16[992,384]{1,0:T(8,128)(2,1)} %collective-permute-done.8.refs_3_), channel_id=1, source_target_pairs={{0,1},{1,0},{2,3},{3,2},{4,5},{5,4},{6,7},{7,6},{8,9},{9,8},{10,11... | collective-permute-start | bytes 2285576 | tf_op jit(solution)/shard_map/ppermute | solution.py:19
  88.4 21.7 %collective-permute-start.14 = (bf16[192,384]{1,0:T(8,128)(2,1)S(1)}, bf16[192,384]{1,0:T(8,128)(2,1)S(1)}, u32[]{:S(2)}, u32[]{:S(2)}) collective-permute-start(bf16[192,384]{1,0:T(8,128)(2,1)S(1)} %get-tuple-element.141), channel_id=1, source_target_pairs={{0,8},{8,0},{16,24},{24,16},{1,9},{9,1},{17,25},{25,17},{2,10},{10... | collective-permute-start | bytes 442376 | tf_op jit(solution)/shard_map/ppermute | solution.py:19
  99.6 12.7 %collective-permute-start.15 = (bf16[192,384]{1,0:T(8,128)(2,1)S(1)}, bf16[192,384]{1,0:T(8,128)(2,1)S(1)}, u32[]{:S(2)}, u32[]{:S(2)}) collective-permute-start(bf16[192,384]{1,0:T(8,128)(2,1)S(1)} %get-tuple-element.140), channel_id=1, source_target_pairs={{0,16},{8,24},{16,0},{24,8},{1,17},{9,25},{17,1},{25,9},{2,18},{10... | collective-permute-start | bytes 442376 | tf_op jit(solution)/shard_map/ppermute | solution.py:19
  99.6 12.7 %collective-permute-start.16 = (bf16[192,384]{1,0:T(8,128)(2,1)S(1)}, bf16[192,384]{1,0:T(8,128)(2,1)S(1)}, u32[]{:S(2)}, u32[]{:S(2)}) collective-permute-start(bf16[192,384]{1,0:T(8,128)(2,1)S(1)} %get-tuple-element.139), channel_id=1, source_target_pairs={{0,24},{8,16},{16,8},{24,0},{1,25},{9,17},{17,9},{25,1},{2,26},{10... | collective-permute-start | bytes 442376 | tf_op jit(solution)/shard_map/ppermute | solution.py:19
  113.0 17.1 %collective-permute-start.17 = (bf16[192,384]{1,0:T(8,128)(2,1)S(1)}, bf16[192,384]{1,0:T(8,128)(2,1)S(1)}, u32[]{:S(2)}, u32[]{:S(2)}) collective-permute-start(bf16[192,384]{1,0:T(8,128)(2,1)S(1)} %get-tuple-element.111), channel_id=1, source_target_pairs={{0,8},{8,0},{16,24},{24,16},{1,9},{9,1},{17,25},{25,17},{2,10},{10... | collective-permute-start | bytes 442376 | tf_op jit(solution)/shard_map/ppermute | solution.py:19
  116.7 13.4 %collective-permute-start.18 = (bf16[192,384]{1,0:T(8,128)(2,1)S(1)}, bf16[192,384]{1,0:T(8,128)(2,1)S(1)}, u32[]{:S(2)}, u32[]{:S(2)}) collective-permute-start(bf16[192,384]{1,0:T(8,128)(2,1)S(1)} %get-tuple-element.111), channel_id=1, source_target_pairs={{0,16},{8,24},{16,0},{24,8},{1,17},{9,25},{17,1},{25,9},{2,18},{10... | collective-permute-start | bytes 442376 | tf_op jit(solution)/shard_map/ppermute | solution.py:19
  116.7 13.4 %collective-permute-start.19 = (bf16[192,384]{1,0:T(8,128)(2,1)S(1)}, bf16[192,384]{1,0:T(8,128)(2,1)S(1)}, u32[]{:S(2)}, u32[]{:S(2)}) collective-permute-start(bf16[192,384]{1,0:T(8,128)(2,1)S(1)} %get-tuple-element.111), channel_id=1, source_target_pairs={{0,24},{8,16},{16,8},{24,0},{1,25},{9,17},{17,9},{25,1},{2,26},{10... | collective-permute-start | bytes 442376 | tf_op jit(solution)/shard_map/ppermute | solution.py:19
  119.2 10.1 %collective-permute-start.20 = (f32[192,192]{1,0:T(8,128)S(1)}, f32[192,192]{1,0:T(8,128)S(1)}, u32[]{:S(2)}, u32[]{:S(2)}) collective-permute-start(f32[192,192]{1,0:T(8,128)S(1)} %get-tuple-element.110), channel_id=1, source_target_pairs={{0,4},{4,0},{1,5},{5,1},{2,6},{6,2},{3,7},{7,3},{8,12},{12,8},{9,1... | collective-permute-start | bytes 442376 | tf_op jit(solution)/shard_map/ppermute | solution.py:19
  130.2 8.2 %collective-permute-start.22 = (bf16[384,384]{1,0:T(8,128)(2,1)S(1)}, bf16[384,384]{1,0:T(8,128)(2,1)S(1)}, u32[]{:S(2)}, u32[]{:S(2)}) collective-permute-start(bf16[384,384]{1,0:T(8,128)(2,1)S(1)} %pad_maximum_fusion.2), channel_id=1, source_target_pairs={{0,2},{1,3},{2,0},{3,1},{4,6},{5,7},{6,4},{7,5},{8,10},{9,11},{10,... | collective-permute-start | bytes 884744 | tf_op jit(solution)/shard_map/ppermute | solution.py:19
  131.8 7.9 %collective-permute-start.21 = (bf16[384,384]{1,0:T(8,128)(2,1)S(1)}, bf16[384,384]{1,0:T(8,128)(2,1)S(1)}, u32[]{:S(2)}, u32[]{:S(2)}) collective-permute-start(bf16[384,384]{1,0:T(8,128)(2,1)S(1)} %pad_maximum_fusion.1), channel_id=1, source_target_pairs={{0,4},{4,0},{1,5},{5,1},{2,6},{6,2},{3,7},{7,3},{8,12},{12,8},{9,1... | collective-permute-start | bytes 884744 | tf_op jit(solution)/shard_map/ppermute | solution.py:19
  133.3 20.8 %collective-permute-start.23 = (bf16[3,192,384]{2,1,0:T(8,128)(2,1)S(1)}, bf16[3,192,384]{2,1,0:T(8,128)(2,1)S(1)}, u32[]{:S(2)}, u32[]{:S(2)}) collective-permute-start(bf16[3,192,384]{2,1,0:T(8,128)(2,1)S(1)} %get-tuple-element.115), channel_id=1, source_target_pairs={{0,16},{8,24},{16,0},{24,8},{1,17},{9,25},{17,1},{25,9},{2,18},{10... | collective-permute-start | bytes 1327112 | tf_op jit(solution)/shard_map/ppermute | solution.py:19
  154.1 23.8 %collective-permute-start.25 = (bf16[768,384]{1,0:T(8,128)(2,1)S(1)}, bf16[768,384]{1,0:T(8,128)(2,1)S(1)}, u32[]{:S(2)}, u32[]{:S(2)}) collective-permute-start(bf16[768,384]{1,0:T(8,128)(2,1)S(1)} %constant_dynamic-update-slice_fusion.3.refs_2_), channel_id=1, source_target_pairs={{0,4},{4,0},{1,5},{5,1},{2,6},{6,2},{3,7},{7,3},{8,12},{12,8},{9,1... | collective-permute-start | bytes 1769480 | tf_op jit(solution)/shard_map/ppermute | solution.py:19
  155.1 22.8 %collective-permute-start.24 = (bf16[768,384]{1,0:T(8,128)(2,1)S(1)}, bf16[768,384]{1,0:T(8,128)(2,1)S(1)}, u32[]{:S(2)}, u32[]{:S(2)}) collective-permute-start(bf16[768,384]{1,0:T(8,128)(2,1)S(1)} %constant_dynamic-update-slice_fusion.refs_0_), channel_id=1, source_target_pairs={{0,2},{1,3},{2,0},{3,1},{4,6},{5,7},{6,4},{7,5},{8,10},{9,11},{10,... | collective-permute-start | bytes 1769480 | tf_op jit(solution)/shard_map/ppermute | solution.py:19
  155.7 10.8 %collective-permute-start.26 = (bf16[3,192,384]{2,1,0:T(8,128)(2,1)S(1)}, bf16[3,192,384]{2,1,0:T(8,128)(2,1)S(1)}, u32[]{:S(2)}, u32[]{:S(2)}) collective-permute-start(bf16[3,192,384]{2,1,0:T(8,128)(2,1)S(1)} %get-tuple-element.119), channel_id=1, source_target_pairs={{0,8},{8,0},{16,24},{24,16},{1,9},{9,1},{17,25},{25,17},{2,10},{10... | collective-permute-start | bytes 1327112 | tf_op jit(solution)/shard_map/ppermute | solution.py:19
  155.9 22.0 %collective-permute-start.27 = (bf16[3,192,384]{2,1,0:T(8,128)(2,1)S(1)}, bf16[3,192,384]{2,1,0:T(8,128)(2,1)S(1)}, u32[]{:S(2)}, u32[]{:S(2)}) collective-permute-start(bf16[3,192,384]{2,1,0:T(8,128)(2,1)S(1)} %get-tuple-element.121), channel_id=1, source_target_pairs={{0,24},{8,16},{16,8},{24,0},{1,25},{9,17},{17,9},{25,1},{2,26},{10... | collective-permute-start | bytes 1327112 | tf_op jit(solution)/shard_map/ppermute | solution.py:19
  177.9 3.7 %collective-permute-start.28 = (bf16[768,384]{1,0:T(8,128)(2,1)S(1)}, bf16[768,384]{1,0:T(8,128)(2,1)S(1)}, u32[]{:S(2)}, u32[]{:S(2)}) collective-permute-start(bf16[768,384]{1,0:T(8,128)(2,1)S(1)} %constant_dynamic-update-slice_fusion.refs_0_), channel_id=1, source_target_pairs={{0,1},{1,0},{2,3},{3,2},{4,5},{5,4},{6,7},{7,6},{8,9},{9,8},{10,11... | collective-permute-start | bytes 1769480 | tf_op jit(solution)/shard_map/ppermute | solution.py:19
  177.9 8.4 %collective-permute-start.29 = (bf16[768,384]{1,0:T(8,128)(2,1)S(1)}, bf16[768,384]{1,0:T(8,128)(2,1)S(1)}, u32[]{:S(2)}, u32[]{:S(2)}) collective-permute-start(bf16[768,384]{1,0:T(8,128)(2,1)S(1)} %collective-permute-done.24.refs_1_), channel_id=1, source_target_pairs={{0,1},{1,0},{2,3},{3,2},{4,5},{5,4},{6,7},{7,6},{8,9},{9,8},{10,11... | collective-permute-start | bytes 1769480 | tf_op jit(solution)/shard_map/ppermute | solution.py:19
  178.4 7.9 %collective-permute-start.30 = (bf16[768,384]{1,0:T(8,128)(2,1)S(1)}, bf16[768,384]{1,0:T(8,128)(2,1)S(1)}, u32[]{:S(2)}, u32[]{:S(2)}) collective-permute-start(bf16[768,384]{1,0:T(8,128)(2,1)S(1)} %constant_dynamic-update-slice_fusion.3.refs_2_), channel_id=1, source_target_pairs={{0,1},{1,0},{2,3},{3,2},{4,5},{5,4},{6,7},{7,6},{8,9},{9,8},{10,11... | collective-permute-start | bytes 1769480 | tf_op jit(solution)/shard_map/ppermute | solution.py:19
  178.5 7.8 %collective-permute-start.31 = (bf16[768,384]{1,0:T(8,128)(2,1)S(1)}, bf16[768,384]{1,0:T(8,128)(2,1)S(1)}, u32[]{:S(2)}, u32[]{:S(2)}) collective-permute-start(bf16[768,384]{1,0:T(8,128)(2,1)S(1)} %collective-permute-done.25.refs_3_), channel_id=1, source_target_pairs={{0,1},{1,0},{2,3},{3,2},{4,5},{5,4},{6,7},{7,6},{8,9},{9,8},{10,11... | collective-permute-start | bytes 1769480 | tf_op jit(solution)/shard_map/ppermute | solution.py:19
  180.0 14.8 %collective-permute-start.32 = (f32[192,192]{1,0:T(8,128)S(1)}, f32[192,192]{1,0:T(8,128)S(1)}, u32[]{:S(2)}, u32[]{:S(2)}) collective-permute-start(f32[192,192]{1,0:T(8,128)S(1)} %get-tuple-element.132), channel_id=1, source_target_pairs={{0,4},{4,0},{1,5},{5,1},{2,6},{6,2},{3,7},{7,3},{8,12},{12,8},{9,1... | collective-permute-start | bytes 442376 | tf_op jit(solution)/shard_map/ppermute | solution.py:19
  181.6 13.2 %collective-permute-start.33 = (bf16[192,384]{1,0:T(8,128)(2,1)S(1)}, bf16[192,384]{1,0:T(8,128)(2,1)S(1)}, u32[]{:S(2)}, u32[]{:S(2)}) collective-permute-start(bf16[192,384]{1,0:T(8,128)(2,1)S(1)} %get-tuple-element.133), channel_id=1, source_target_pairs={{0,0},{1,8},{2,16},{3,24},{4,4},{5,12},{6,20},{7,28},{8,1},{9,9},{... | collective-permute-start | bytes 442376 | tf_op jit(solution)/shard_map/ppermute | solution.py:738

commit v5 on v4

--- a/solution.py
+++ b/solution.py
@@ -265,9 +265,9 @@
     side = whole.shape[0]
     groups = side // width
     copies = []
-    for piece, (z, y, q) in zip(pieces, piece_places(levels, groups)):
+    for piece, (z, y, q) in zip(pieces, piece_places(levels)):
         for i in range(len(z)):
-            start = ((orb ^ q[i]) * PAIR + (pair ^ y[i])) * coarse
+            start = ((orb ^ q) * PAIR + (pair ^ y)) * coarse
             rows = pl.ds(pl.multiple_of(start, coarse), coarse)
             lanes = pl.ds(pl.multiple_of((level ^ z[i]) * width, width), width)
             copies.append(
@@ -283,21 +283,14 @@
     own_lanes = pl.ds(pl.multiple_of(orb * width, width), width)
     rows = whole[pl.ds(row0, coarse), :]
 
-    def across(j, carry):
-        lanes = pl.ds(pl.multiple_of(j * width, width), width)
+    for j in range(groups):
+        lanes = slice(j * width, (j + 1) * width)
         rows_f[:, lanes] = matmul(rows, whole[:, lanes])
-        return carry
-
-    lax.fori_loop(0, groups, across, 0)
     columns = whole[:, own_lanes]
-
-    def down(i, carry):
-        here = pl.ds(pl.multiple_of(i * coarse, coarse), coarse)
+    for i in range(groups):
+        here = slice(i * width, (i + 1) * width)
         square = matmul(whole[here, :], columns)
         cols_b[here, :] = (0.25 * (whole[here, own_lanes].astype(f32) - square)).astype(bf16)
-        return carry
-
-    lax.fori_loop(0, side // coarse, down, 0)
     left = (rows.astype(f32) - 0.25 * rows_f[...]).astype(bf16)
     value = matmul(left, cols_b[...]) + 0.125 * rows_f[:, own_lanes] - 0.5 * offset[...]
     row_ids = lax.broadcasted_iota(jnp.int32, value.shape, 0) + row0
@@ -305,18 +298,15 @@
     root[...] = value + jnp.where(row_ids == col_ids, 1.0, 0.0)
 
 
-def piece_places(levels, groups):
+def piece_places(levels):
     places = []
     for core in (0, 1):
         for half in range(2):
-            low = [half * levels // 2 + z for z in range(levels // 2)]
+            z = [half * levels // 2 + i for i in range(levels // 2)]
             for second in (0, 1):
-                z, y, q = [], [], []
                 for inner in (0, 1):
-                    z += low
-                    y += [second if half else inner] * len(low)
-                    q += [2 * (inner if half else second) + core] * len(low)
-                places.append((z, y, q))
+                    y, far = (second, inner) if half else (inner, second)
+                    places.append((z, y, 2 * far + core))
     return places
 
 
@@ -643,7 +633,8 @@
     far = {q: swap(active, "orb", q) for q in groups if q and q % 2 == 0}
     beside = swap(theirs, "pair", 1)
     first_mine, second_mine = trade(mine, "lvl", 0), trade(mine, "lvl", 1)
-    beside_rest = swap(mine, "pair", 1)
+    later_mine, beside = lax.optimization_barrier((mine, beside))
+    beside_rest = swap(later_mine, "pair", 1)
     first_beside, second_beside = trade(beside, "lvl", 0), trade(beside, "lvl", 1)
 
     matrices = block_matrices(deriv_blocks)
@@ -721,9 +712,9 @@
         top, low = join(pieces[: level_count // 2]), join(pieces[level_count // 2 :])
         sent = [fock_blocks[0]] + [swap(fock_blocks[step], "lvl", step) for step in range(1, level_count)]
         got = [swap(top, "pair", 1), swap(low, "orb", 2)]
-        got, sent[2] = lax.optimization_barrier((got, sent[2]))
-        top, low = join([top, got[0]]), join([low, got[1]])
-        pieces = [top, swap(top, "orb", 2), low, swap(low, "pair", 1)]
+        got, sent[:3] = lax.optimization_barrier((got, sent[:3]))
+        tops, lows = [top, got[0]], [low, got[1]]
+        pieces = tops + [swap(piece, "orb", 2) for piece in tops] + lows + [swap(piece, "pair", 1) for piece in lows]
         pieces, sent = lax.optimization_barrier((pieces, sent))
         pieces += [swap(piece, "orb", 1) for piece in pieces]
         root_meta = jnp.stack([level, pair, orb]).astype(jnp.int32)

time: 192 us -> 190 us (0.990); the launches traced: 196 us -> 187 us
  Pallas kernels: 67.7 us -> 62.9 us
  waiting for transfers between devices: 62.7 us -> 60.1 us
    ppermute x29 -> x35, waiting for transfers between devices: 62.1 us -> 58.8 us  [swap(): return lax.ppermute(value, axis, [(i, i ^ bit) for i in range(count)])]
    pallas_call x1, Pallas kernels: 25.4 us -> 22.5 us  [kinetic(): pl.pallas_call(functools.partial(kinetic_kernel, edge, slots, levels), ou...]
    pallas_call x1, Pallas kernels: 8.39 us -> 6.38 us  [root_of(): pl.pallas_call(functools.partial(root_kernel, levels), out_shape=jax.Shap...]
    ppermute x29 -> x35, starting transfers between devices: 39.3 us -> 38.4 us  [swap(): return lax.ppermute(value, axis, [(i, i ^ bit) for i in range(count)])]
  transfers between devices with their start and end apart: 34 -> 40, of which waited for: 9 -> 12; matrix products, arithmetic and copies ran while one was open for 2% -> 2% of each run, Pallas kernels for 30% -> 29%
where the time goes in v5:
time: 190 us; the launch traced here: 187 us
  Pallas kernels  62.9 us (33%)
  waiting for transfers between devices  60.1 us (32%)
  starting transfers between devices  51.1 us (27%)
  local copies, waits for them, and re-layouts  8.79 us (5%)
  other arithmetic  2.09 us (1%)
    ppermute x35, waiting for transfers between devices, swap(): return lax.ppermute(value, axis, [(i, i ^ bit) for i in range(count)])  58.8 us
    ppermute x35, starting transfers between devices, swap(): return lax.ppermute(value, axis, [(i, i ^ bit) for i in range(count)])  38.4 us
    pallas_call x1, Pallas kernels, kinetic(): pl.pallas_call(functools.partial(kinetic_kernel, edge, slots, levels), ou...  22.5 us
    pallas_call x2, Pallas kernels, box_fock(): pl.pallas_call(functools.partial(fock_kernel, side, counts), out_shape=ou...  16.7 us
    pallas_call x2, Pallas kernels, box_correlation(): pl.pallas_call(functools.partial(correlation_kernel, share, counts), out_...  9.17 us
    ppermute x4, starting transfers between devices, trade(): return lax.ppermute(value, axis, pairs + [(b, a) for a, b in pairs])  8.29 us
    pallas_call x1, Pallas kernels, root_of(): pl.pallas_call(functools.partial(root_kernel, levels), out_shape=jax.Shap...  6.38 us
    ppermute x1, starting transfers between devices, body(): got = (swap(other, 'pair', 1), lax.ppermute(share, BOX + ('orb',), to))  4.44 us
  transfers between devices with their start and end apart: 40, of which 12 were waited for; matrix products, arithmetic and copies ran while one was open for 2% of the time, Pallas kernels for 29%

profile of v5, /device:TPU:2, one launch (start us, length us, event | category | flops | bytes accessed | tf_op | source)
XLA Modules:
  0.0 186.7 jit_solution(16605764870257709479)
XLA Ops:
  1.5 0.8 copy.20
  2.3 0.7 pad.4.pot
  3.8 3.2 %pack.1 = (bf16[2,528,384]{2,1,0:T(8,128)(2,1)S(1)}, bf16[2,528,384]{2,1,0:T(8,128)(2,1)}) custom-call(s32[3]{0:T(128)S(1)} %pad_add_fusion.1.meta, s32[2,6]{1,0:T(2,128)S(1)} %reshape.42.neighbours, s32[2]{0:T(128)S(1)} %copy-done.11, bf16[2,1000,384]{2,1,0:T(8,128)(2,1)} %orbitals.1, f32[2,1152]{1,0:T(2,128)S(1)} %pad.4.pot), custom_call_target="tpu_custom_call" | custom-call | tf_op jit(solution)/shard_map/pack/pallas_call | solution.py:75
  7.0 1.5 collective-permute-start.1
  8.5 1.5 collective-permute-start.4
  10.6 3.6 %collective-permute-start.2 = (bf16[2,528,384]{2,1,0:T(8,128)(2,1)}, bf16[2,528,384]{2,1,0:T(8,128)(2,1)}, u32[]{:S(2)}, u32[]{:S(2)}) collective-permute-start(bf16[2,528,384]{2,1,0:T(8,128)(2,1)} %get-tuple-element.94.refs_0_), channel_id=1, source_target_pairs={{0,8},{16,24},{8,0},{24,16},{1,9},{17,25},{9,1},{25,17},{2,10},{18... | collective-permute-start | bytes 2433032 | tf_op jit(solution)/shard_map/ppermute | solution.py:24
  14.2 12.7 %collective-permute-done.1.beside_in.refs_1_ = bf16[2,528,384]{2,1,0:T(8,128)(2,1)} collective-permute-done((bf16[2,528,384]{2,1,0:T(8,128)(2,1)S(1)}, bf16[2,528,384]{2,1,0:T(8,128)(2,1)}, u32[]{:S(2)}, u32[]{:S(2)}) %collective-permute-start.1) | collective-permute-done | bytes 811040 | tf_op jit(solution)/shard_map/ppermute | solution.py:19
  26.9 1.5 collective-permute-start.6
  28.4 1.6 collective-permute-start.3
  30.0 1.6 collective-permute-start.5
  32.4 1.0 matrices.1
  35.7 10.4 %collective-permute-done.6.rest_in = bf16[2,528,384]{2,1,0:T(8,128)(2,1)S(1)} collective-permute-done((bf16[2,528,384]{2,1,0:T(8,128)(2,1)}, bf16[2,528,384]{2,1,0:T(8,128)(2,1)S(1)}, u32[]{:S(2)}, u32[]{:S(2)}) %collective-permute-start.6) | collective-permute-done | bytes 811040 | tf_op jit(solution)/shard_map/ppermute | solution.py:19
  46.0 0.9 copy-done
  47.0 1.1 copy-done.1
  48.1 2.2 %unfold.1 = (bf16[2000,384]{1,0:T(8,128)(2,1)S(1)}, bf16[1008,384]{1,0:T(8,128)(2,1)S(1)}) custom-call(s32[3]{0:T(128)S(1)} %pad_add_fusion.1.meta, bf16[2,528,384]{2,1,0:T(8,128)(2,1)} %collective-permute-done.1.beside_in.refs_1_, bf16[2,528,384]{2,1,0:T(8,128)(2,1)S(1)} %copy-done.1), custom_call_target="tpu_custom_call" | custom-call | tf_op jit(solution)/shard_map/unfold/pallas_call | solution.py:110
  51.8 1.6 collective-permute-start.8
  54.5 22.5 %kinetic.1 = bf16[4,1000,576]{2,1,0:T(8,128)(2,1)} custom-call(s32[2]{0:T(128)S(1)} %pad_add_fusion.2.place_meta, s32[6,2,8]{2,1,0:T(2,128)S(1)} %pad_add_fusion.facts, bf16[2,528,384]{2,1,0:T(8,128)(2,1)} %get-tuple-element.94.refs_0_, bf16[2,528,384]{2,1,0:T(8,128)(2,1)} %collective-permute-done.1.beside_in.refs_1_, ...), custom_call_target="tpu_custom_call" | custom-call | flops 20000000000 | bytes 40000000 | tf_op jit(solution)/shard_map/kinetic/pallas_call | solution.py:551
  77.6 4.8 %correlation.2.refs_6_ = f32[4,192,384]{2,1,0:T(8,128)S(1)} custom-call(s32[3]{0:T(128)S(1)} %pad_add_fusion.3.meta, bf16[2000,384]{1,0:T(8,128)(2,1)} %bitcast.5.refs_0_, bf16[2000,384]{1,0:T(8,128)(2,1)} %bitcast.6.refs_1_, bf16[2000,384]{1,0:T(8,128)(2,1)S(1)} %bitcast.36, bf16[2000,384]{1,0:T(8,128)(2,1)} %bitcast.7.refs_3_), custom_call_target="tpu_custom_call" | custom-call | flops 1179648000 | bytes 6144000 | tf_op jit(solution)/shard_map/correlation/pallas_call | solution.py:179
  82.5 4.4 %correlation.3 = bf16[4,192,384]{2,1,0:T(8,128)(2,1)S(1)} custom-call(s32[3]{0:T(128)S(1)} %pad_add_fusion.3.meta, bf16[2000,384]{1,0:T(8,128)(2,1)S(1)} %get-tuple-element.104.refs_0_, bf16[2000,384]{1,0:T(8,128)(2,1)} %collective-permute-done.9.refs_1_, bf16[1008,384]{1,0:T(8,128)(2,1)} %collective-permute-done.7.refs_2_, ...), custom_call_target="tpu_custom_call" | custom-call | flops 1179648000 | bytes 6144000 | tf_op jit(solution)/shard_map/correlation/pallas_call | solution.py:179
  86.9 5.3 %collective-permute-start.14 = (bf16[192,384]{1,0:T(8,128)(2,1)S(1)}, bf16[192,384]{1,0:T(8,128)(2,1)S(1)}, u32[]{:S(2)}, u32[]{:S(2)}) collective-permute-start(bf16[192,384]{1,0:T(8,128)(2,1)S(1)} %get-tuple-element.157), channel_id=1, source_target_pairs={{0,8},{8,0},{16,24},{24,16},{1,9},{9,1},{17,25},{25,17},{2,10},{10... | collective-permute-start | bytes 442376 | tf_op jit(solution)/shard_map/ppermute | solution.py:19
  92.2 3.1 %collective-permute-start.15 = (bf16[192,384]{1,0:T(8,128)(2,1)S(1)}, bf16[192,384]{1,0:T(8,128)(2,1)S(1)}, u32[]{:S(2)}, u32[]{:S(2)}) collective-permute-start(bf16[192,384]{1,0:T(8,128)(2,1)S(1)} %get-tuple-element.156), channel_id=1, source_target_pairs={{0,16},{8,24},{16,0},{24,8},{1,17},{9,25},{17,1},{25,9},{2,18},{10... | collective-permute-start | bytes 442376 | tf_op jit(solution)/shard_map/ppermute | solution.py:19
  95.3 1.4 collective-permute-start.16
  96.7 8.2 %fock.2.refs_6_ = f32[4,576,384]{2,1,0:T(8,128)S(1)} custom-call(bf16[2,2000,576]{2,1,0:T(8,128)(2,1)} %bitcast.38, bf16[2000,384]{1,0:T(8,128)(2,1)} %bitcast.5.refs_0_, bf16[2000,384]{1,0:T(8,128)(2,1)} %bitcast.6.refs_1_, bf16[2000,384]{1,0:T(8,128)(2,1)S(1)} %bitcast.37, bf16[2000,384]{1,0:T(8,128)(2,1)} %bitcast.7.refs_3_), custom_call_target="tpu_custom_call" | custom-call | flops 3538944000 | bytes 6144000 | tf_op jit(solution)/shard_map/fock/pallas_call | solution.py:241
  104.9 2.0 %collective-permute-done.16.refs_3_ = bf16[192,384]{1,0:T(8,128)(2,1)S(1)} collective-permute-done((bf16[192,384]{1,0:T(8,128)(2,1)S(1)}, bf16[192,384]{1,0:T(8,128)(2,1)S(1)}, u32[]{:S(2)}, u32[]{:S(2)}) %collective-permute-start.16) | collective-permute-done | bytes 147488 | tf_op jit(solution)/shard_map/ppermute | solution.py:19
  106.9 0.8 level_sum.2
  107.7 2.8 %collective-permute-start.17 = (bf16[192,384]{1,0:T(8,128)(2,1)S(1)}, bf16[192,384]{1,0:T(8,128)(2,1)S(1)}, u32[]{:S(2)}, u32[]{:S(2)}) collective-permute-start(bf16[192,384]{1,0:T(8,128)(2,1)S(1)} %get-tuple-element.121), channel_id=1, source_target_pairs={{0,8},{8,0},{16,24},{24,16},{1,9},{9,1},{17,25},{25,17},{2,10},{10... | collective-permute-start | bytes 442376 | tf_op jit(solution)/shard_map/ppermute | solution.py:19
  110.5 2.0 %collective-permute-start.18 = (bf16[192,384]{1,0:T(8,128)(2,1)S(1)}, bf16[192,384]{1,0:T(8,128)(2,1)S(1)}, u32[]{:S(2)}, u32[]{:S(2)}) collective-permute-start(bf16[192,384]{1,0:T(8,128)(2,1)S(1)} %get-tuple-element.121), channel_id=1, source_target_pairs={{0,16},{8,24},{16,0},{24,8},{1,17},{9,25},{17,1},{25,9},{2,18},{10... | collective-permute-start | bytes 442376 | tf_op jit(solution)/shard_map/ppermute | solution.py:19
  112.5 1.4 collective-permute-start.19
  113.9 1.2 collective-permute-start.20
  115.1 8.5 %fock.3 = (bf16[3,192,384]{2,1,0:T(8,128)(2,1)S(1)}, bf16[3,192,384]{2,1,0:T(8,128)(2,1)S(1)}, bf16[3,192,384]{2,1,0:T(8,128)(2,1)S(1)}, bf16[3,192,384]{2,1,0:T(8,128)(2,1)S(1)}) custom-call(bf16[2,2000,576]{2,1,0:T(8,128)(2,1)} %bitcast.39, bf16[2000,384]{1,0:T(8,128)(2,1)S(1)} %get-tuple-element.104.refs_0_, ...), custom_call_target="tpu_custom_call" | custom-call | flops 3538944000 | bytes 6144000 | tf_op jit(solution)/shard_map/fock/pallas_call | solution.py:241
  123.7 0.9 convert_add_fusion
  124.6 1.6 collective-permute-start.22
  126.1 2.5 %collective-permute-start.23 = (bf16[3,192,384]{2,1,0:T(8,128)(2,1)S(1)}, bf16[3,192,384]{2,1,0:T(8,128)(2,1)S(1)}, u32[]{:S(2)}, u32[]{:S(2)}) collective-permute-start(bf16[3,192,384]{2,1,0:T(8,128)(2,1)S(1)} %get-tuple-element.126), channel_id=1, source_target_pairs={{0,8},{8,0},{16,24},{24,16},{1,9},{9,1},{17,25},{25,17},{2,10},{10... | collective-permute-start | bytes 1327112 | tf_op jit(solution)/shard_map/ppermute | solution.py:19
  128.6 1.9 %collective-permute-start.24 = (bf16[3,192,384]{2,1,0:T(8,128)(2,1)S(1)}, bf16[3,192,384]{2,1,0:T(8,128)(2,1)S(1)}, u32[]{:S(2)}, u32[]{:S(2)}) collective-permute-start(bf16[3,192,384]{2,1,0:T(8,128)(2,1)S(1)} %get-tuple-element.127), channel_id=1, source_target_pairs={{0,16},{8,24},{16,0},{24,8},{1,17},{9,25},{17,1},{25,9},{2,18},{10... | collective-permute-start | bytes 1327112 | tf_op jit(solution)/shard_map/ppermute | solution.py:19
  130.5 1.3 collective-permute-start.21
  131.8 1.5 collective-permute-start.29
  133.3 0.8 collective-permute-start.27
  134.1 6.5 %collective-permute-done.21.refs_1_ = bf16[384,384]{1,0:T(8,128)(2,1)S(1)} collective-permute-done((bf16[384,384]{1,0:T(8,128)(2,1)S(1)}, bf16[384,384]{1,0:T(8,128)(2,1)S(1)}, u32[]{:S(2)}, u32[]{:S(2)}) %collective-permute-start.21) | collective-permute-done | bytes 294944 | tf_op jit(solution)/shard_map/ppermute | solution.py:19
  141.1 5.8 %collective-permute-done.23.refs_1_ = bf16[3,192,384]{2,1,0:T(8,128)(2,1)S(1)} collective-permute-done((bf16[3,192,384]{2,1,0:T(8,128)(2,1)S(1)}, bf16[3,192,384]{2,1,0:T(8,128)(2,1)S(1)}, u32[]{:S(2)}, u32[]{:S(2)}) %collective-permute-start.23) | collective-permute-done | bytes 442400 | tf_op jit(solution)/shard_map/ppermute | solution.py:19
  146.9 14.7 %collective-permute-done.24.refs_2_ = bf16[3,192,384]{2,1,0:T(8,128)(2,1)S(1)} collective-permute-done((bf16[3,192,384]{2,1,0:T(8,128)(2,1)S(1)}, bf16[3,192,384]{2,1,0:T(8,128)(2,1)S(1)}, u32[]{:S(2)}, u32[]{:S(2)}) %collective-permute-start.24) | collective-permute-done | bytes 442400 | tf_op jit(solution)/shard_map/ppermute | solution.py:19
  162.1 1.2 collective-permute-start.28
  163.3 5.0 %collective-permute-done.26.refs_3_ = bf16[384,384]{1,0:T(8,128)(2,1)S(1)} collective-permute-done((bf16[384,384]{1,0:T(8,128)(2,1)S(1)}, bf16[384,384]{1,0:T(8,128)(2,1)S(1)}, u32[]{:S(2)}, u32[]{:S(2)}) %collective-permute-start.26) | collective-permute-done | bytes 294944 | tf_op jit(solution)/shard_map/ppermute | solution.py:19
  171.5 0.9 level_sum.3
  172.4 1.3 collective-permute-start.38
  173.7 4.4 %collective-permute-start.39 = (bf16[192,384]{1,0:T(8,128)(2,1)S(1)}, bf16[192,384]{1,0:T(8,128)(2,1)S(1)}, u32[]{:S(2)}, u32[]{:S(2)}) collective-permute-start(bf16[192,384]{1,0:T(8,128)(2,1)S(1)} %get-tuple-element.149), channel_id=1, source_target_pairs={{0,0},{1,8},{2,16},{3,24},{4,4},{5,12},{6,20},{7,28},{8,1},{9,9},{... | collective-permute-start | bytes 442376 | tf_op jit(solution)/shard_map/ppermute | solution.py:729
  178.2 6.4 %root.1 = f32[192,384]{1,0:T(8,128)} custom-call(s32[3]{0:T(128)S(1)} %pad_add_fusion.4.meta, bf16[384,384]{1,0:T(8,128)(2,1)S(1)} %constant_dynamic-update-slice_fusion.refs_0_, bf16[384,384]{1,0:T(8,128)(2,1)S(1)} %collective-permute-done.21.refs_1_, bf16[384,384]{1,0:T(8,128)(2,1)S(1)} %collective-permute-done.25.refs_2_, ...), custom_call_target="tpu_custom_call" | custom-call | flops 14495514624 | bytes 9437184 | tf_op jit(solution)/shard_map/root/pallas_call | solution.py:316
  184.6 1.3 collective-permute-done.39
  185.9 0.8 maximum_add_fusion
  (104 shorter events, 12.0 us)
Async XLA Ops:
  0.6 31.7 %copy-start.7 = (bf16[112,10]{1,0:T(8,128)(2,1)S(1)}, bf16[112,10]{1,0:T(8,128)(2,1)}, u32[]{:S(2)}) copy-start(bf16[112,10]{1,0:T(8,128)(2,1)} %constant.60.clone.refs_0_) | copy-start | bytes 6724
  0.6 31.7 %copy-start.9 = (bf16[30,336]{1,0:T(8,128)(2,1)S(1)}, bf16[30,336]{1,0:T(8,128)(2,1)}, u32[]{:S(2)}) copy-start(bf16[30,336]{1,0:T(8,128)(2,1)} %constant.61.clone.refs_1_) | copy-start | bytes 60484
  0.7 31.7 %copy-start.3 = (f32[112,112]{1,0:T(8,128)S(1)}, f32[112,112]{1,0:T(8,128)}, u32[]{:S(2)}) copy-start(f32[112,112]{1,0:T(8,128)} %constant.62.clone.refs_2_) | copy-start | bytes 150532
  0.7 31.7 %copy-start.8 = (bf16[112,10]{1,0:T(8,128)(2,1)S(1)}, bf16[112,10]{1,0:T(8,128)(2,1)}, u32[]{:S(2)}) copy-start(bf16[112,10]{1,0:T(8,128)(2,1)} %constant.63.clone.refs_3_) | copy-start | bytes 6724
  0.7 31.7 %copy-start.10 = (bf16[30,336]{1,0:T(8,128)(2,1)S(1)}, bf16[30,336]{1,0:T(8,128)(2,1)}, u32[]{:S(2)}) copy-start(bf16[30,336]{1,0:T(8,128)(2,1)} %constant.64.clone.refs_4_) | copy-start | bytes 60484
  0.7 31.7 %copy-start.4 = (f32[112,112]{1,0:T(8,128)S(1)}, f32[112,112]{1,0:T(8,128)}, u32[]{:S(2)}) copy-start(f32[112,112]{1,0:T(8,128)} %constant.65.clone.refs_5_) | copy-start | bytes 150532
  0.7 31.7 %copy-start.5 = (bf16[160,10]{1,0:T(8,128)(2,1)S(1)}, bf16[160,10]{1,0:T(8,128)(2,1)}, u32[]{:S(2)}) copy-start(bf16[160,10]{1,0:T(8,128)(2,1)} %constant.66.clone.refs_6_) | copy-start | bytes 9604
  0.7 31.7 %copy-start.6 = (bf16[30,480]{1,0:T(8,128)(2,1)S(1)}, bf16[30,480]{1,0:T(8,128)(2,1)}, u32[]{:S(2)}) copy-start(bf16[30,480]{1,0:T(8,128)(2,1)} %constant.67.clone.refs_7_) | copy-start | bytes 86404
  7.0 19.9 %collective-permute-start.1 = (bf16[2,528,384]{2,1,0:T(8,128)(2,1)S(1)}, bf16[2,528,384]{2,1,0:T(8,128)(2,1)}, u32[]{:S(2)}, u32[]{:S(2)}) collective-permute-start(bf16[2,528,384]{2,1,0:T(8,128)(2,1)S(1)} %get-tuple-element.79), channel_id=1, source_target_pairs={{0,4},{4,0},{1,5},{5,1},{2,6},{6,2},{3,7},{7,3},{8,12},{12,8},{9,1... | collective-permute-start | bytes 2433032 | tf_op jit(solution)/shard_map/ppermute | solution.py:19
  8.5 21.5 %collective-permute-start.4 = (bf16[2,528,384]{2,1,0:T(8,128)(2,1)}, bf16[2,528,384]{2,1,0:T(8,128)(2,1)}, u32[]{:S(2)}, u32[]{:S(2)}) collective-permute-start(bf16[2,528,384]{2,1,0:T(8,128)(2,1)} %get-tuple-element.94.refs_0_), channel_id=1, source_target_pairs={{8,16},{16,8},{9,17},{17,9},{10,18},{18,10},{11,19},{19,11},{12,20... | collective-permute-start | bytes 2433032 | tf_op jit(solution)/shard_map/ppermute | solution.py:24
  10.0 40.3 %collective-permute-start = (bf16[2,1000,384]{2,1,0:T(8,128)(2,1)}, bf16[2,1000,384]{2,1,0:T(8,128)(2,1)S(1)}, u32[]{:S(2)}, u32[]{:S(2)}) collective-permute-start(bf16[2,1000,384]{2,1,0:T(8,128)(2,1)} %orbitals.1), channel_id=1, source_target_pairs={{0,2},{1,3},{2,0},{3,1},{4,6},{5,7},{6,4},{7,5},{8,10},{9,11},{10,... | collective-permute-start | bytes 4608008 | tf_op jit(solution)/shard_map/ppermute | solution.py:19
  10.6 24.4 %collective-permute-start.2 = (bf16[2,528,384]{2,1,0:T(8,128)(2,1)}, bf16[2,528,384]{2,1,0:T(8,128)(2,1)}, u32[]{:S(2)}, u32[]{:S(2)}) collective-permute-start(bf16[2,528,384]{2,1,0:T(8,128)(2,1)} %get-tuple-element.94.refs_0_), channel_id=1, source_target_pairs={{0,8},{16,24},{8,0},{24,16},{1,9},{17,25},{9,1},{25,17},{2,10},{18... | collective-permute-start | bytes 2433032 | tf_op jit(solution)/shard_map/ppermute | solution.py:24
  26.9 19.1 %collective-permute-start.6 = (bf16[2,528,384]{2,1,0:T(8,128)(2,1)}, bf16[2,528,384]{2,1,0:T(8,128)(2,1)S(1)}, u32[]{:S(2)}, u32[]{:S(2)}) collective-permute-start(bf16[2,528,384]{2,1,0:T(8,128)(2,1)} %get-tuple-element.94.refs_0_), channel_id=1, source_target_pairs={{0,4},{4,0},{1,5},{5,1},{2,6},{6,2},{3,7},{7,3},{8,12},{12,8},{9,1... | collective-permute-start | bytes 2433032 | tf_op jit(solution)/shard_map/ppermute | solution.py:19
  28.4 21.9 %collective-permute-start.3 = (bf16[2,528,384]{2,1,0:T(8,128)(2,1)}, bf16[2,528,384]{2,1,0:T(8,128)(2,1)}, u32[]{:S(2)}, u32[]{:S(2)}) collective-permute-start(bf16[2,528,384]{2,1,0:T(8,128)(2,1)} %collective-permute-done.1.beside_in.refs_1_), channel_id=1, source_target_pairs={{0,8},{16,24},{8,0},{24,16},{1,9},{17,25},{9,1},{25,17},{2,10},{18... | collective-permute-start | bytes 2433032 | tf_op jit(solution)/shard_map/ppermute | solution.py:24
  30.0 20.3 %collective-permute-start.5 = (bf16[2,528,384]{2,1,0:T(8,128)(2,1)}, bf16[2,528,384]{2,1,0:T(8,128)(2,1)}, u32[]{:S(2)}, u32[]{:S(2)}) collective-permute-start(bf16[2,528,384]{2,1,0:T(8,128)(2,1)} %collective-permute-done.1.beside_in.refs_1_), channel_id=1, source_target_pairs={{8,16},{16,8},{9,17},{17,9},{10,18},{18,10},{11,19},{19,11},{12,20... | collective-permute-start | bytes 2433032 | tf_op jit(solution)/shard_map/ppermute | solution.py:24
  51.7 25.9 %collective-permute-start.13 = (bf16[2,1000,384]{2,1,0:T(8,128)(2,1)S(1)}, bf16[2,1000,384]{2,1,0:T(8,128)(2,1)}, u32[]{:S(2)}, u32[]{:S(2)}) collective-permute-start(bf16[2,1000,384]{2,1,0:T(8,128)(2,1)S(1)} %collective-permute-done), channel_id=1, source_target_pairs={{0,1},{1,0},{2,3},{3,2},{4,5},{5,4},{6,7},{7,6},{8,9},{9,8},{10,11... | collective-permute-start | bytes 4608008 | tf_op jit(solution)/shard_map/ppermute | solution.py:19
  51.8 25.2 %collective-permute-start.8 = (bf16[992,384]{1,0:T(8,128)(2,1)S(1)}, bf16[992,384]{1,0:T(8,128)(2,1)}, u32[]{:S(2)}, u32[]{:S(2)}) collective-permute-start(bf16[992,384]{1,0:T(8,128)(2,1)S(1)} %slice.30), channel_id=1, source_target_pairs={{0,4},{4,0},{1,5},{5,1},{2,6},{6,2},{3,7},{7,3},{8,12},{12,8},{9,1... | collective-permute-start | bytes 2285576 | tf_op jit(solution)/shard_map/ppermute | solution.py:19
  53.4 23.6 %collective-permute-start.7 = (bf16[1008,384]{1,0:T(8,128)(2,1)S(1)}, bf16[1008,384]{1,0:T(8,128)(2,1)}, u32[]{:S(2)}, u32[]{:S(2)}) collective-permute-start(bf16[1008,384]{1,0:T(8,128)(2,1)S(1)} %get-tuple-element.89), channel_id=1, source_target_pairs={{0,2},{1,3},{2,0},{3,1},{4,6},{5,7},{6,4},{7,5},{8,10},{9,11},{10,... | collective-permute-start | bytes 2322440 | tf_op jit(solution)/shard_map/ppermute | solution.py:19
  53.9 23.7 %collective-permute-start.12 = (bf16[2,1000,384]{2,1,0:T(8,128)(2,1)}, bf16[2,1000,384]{2,1,0:T(8,128)(2,1)}, u32[]{:S(2)}, u32[]{:S(2)}) collective-permute-start(bf16[2,1000,384]{2,1,0:T(8,128)(2,1)} %orbitals.1), channel_id=1, source_target_pairs={{0,1},{1,0},{2,3},{3,2},{4,5},{5,4},{6,7},{7,6},{8,9},{9,8},{10,11... | collective-permute-start | bytes 4608008 | tf_op jit(solution)/shard_map/ppermute | solution.py:19
  53.9 28.5 %collective-permute-start.9 = (bf16[2000,384]{1,0:T(8,128)(2,1)S(1)}, bf16[2000,384]{1,0:T(8,128)(2,1)}, u32[]{:S(2)}, u32[]{:S(2)}) collective-permute-start(bf16[2000,384]{1,0:T(8,128)(2,1)S(1)} %get-tuple-element.104.refs_0_), channel_id=1, source_target_pairs={{0,1},{1,0},{2,3},{3,2},{4,5},{5,4},{6,7},{7,6},{8,9},{9,8},{10,11... | collective-permute-start | bytes 4608008 | tf_op jit(solution)/shard_map/ppermute | solution.py:19
  77.0 5.4 %collective-permute-start.10 = (bf16[1008,384]{1,0:T(8,128)(2,1)}, bf16[1008,384]{1,0:T(8,128)(2,1)}, u32[]{:S(2)}, u32[]{:S(2)}) collective-permute-start(bf16[1008,384]{1,0:T(8,128)(2,1)} %collective-permute-done.7.refs_2_), channel_id=1, source_target_pairs={{0,1},{1,0},{2,3},{3,2},{4,5},{5,4},{6,7},{7,6},{8,9},{9,8},{10,11... | collective-permute-start | bytes 2322440 | tf_op jit(solution)/shard_map/ppermute | solution.py:19
  77.1 5.3 %collective-permute-start.11 = (bf16[992,384]{1,0:T(8,128)(2,1)}, bf16[992,384]{1,0:T(8,128)(2,1)}, u32[]{:S(2)}, u32[]{:S(2)}) collective-permute-start(bf16[992,384]{1,0:T(8,128)(2,1)} %collective-permute-done.8.refs_3_), channel_id=1, source_target_pairs={{0,1},{1,0},{2,3},{3,2},{4,5},{5,4},{6,7},{7,6},{8,9},{9,8},{10,11... | collective-permute-start | bytes 2285576 | tf_op jit(solution)/shard_map/ppermute | solution.py:19
  86.9 17.9 %collective-permute-start.14 = (bf16[192,384]{1,0:T(8,128)(2,1)S(1)}, bf16[192,384]{1,0:T(8,128)(2,1)S(1)}, u32[]{:S(2)}, u32[]{:S(2)}) collective-permute-start(bf16[192,384]{1,0:T(8,128)(2,1)S(1)} %get-tuple-element.157), channel_id=1, source_target_pairs={{0,8},{8,0},{16,24},{24,16},{1,9},{9,1},{17,25},{25,17},{2,10},{10... | collective-permute-start | bytes 442376 | tf_op jit(solution)/shard_map/ppermute | solution.py:19
  92.2 12.7 %collective-permute-start.15 = (bf16[192,384]{1,0:T(8,128)(2,1)S(1)}, bf16[192,384]{1,0:T(8,128)(2,1)S(1)}, u32[]{:S(2)}, u32[]{:S(2)}) collective-permute-start(bf16[192,384]{1,0:T(8,128)(2,1)S(1)} %get-tuple-element.156), channel_id=1, source_target_pairs={{0,16},{8,24},{16,0},{24,8},{1,17},{9,25},{17,1},{25,9},{2,18},{10... | collective-permute-start | bytes 442376 | tf_op jit(solution)/shard_map/ppermute | solution.py:19
  95.3 11.6 %collective-permute-start.16 = (bf16[192,384]{1,0:T(8,128)(2,1)S(1)}, bf16[192,384]{1,0:T(8,128)(2,1)S(1)}, u32[]{:S(2)}, u32[]{:S(2)}) collective-permute-start(bf16[192,384]{1,0:T(8,128)(2,1)S(1)} %get-tuple-element.155), channel_id=1, source_target_pairs={{0,24},{8,16},{16,8},{24,0},{1,25},{9,17},{17,9},{25,1},{2,26},{10... | collective-permute-start | bytes 442376 | tf_op jit(solution)/shard_map/ppermute | solution.py:19
  107.7 16.8 %collective-permute-start.17 = (bf16[192,384]{1,0:T(8,128)(2,1)S(1)}, bf16[192,384]{1,0:T(8,128)(2,1)S(1)}, u32[]{:S(2)}, u32[]{:S(2)}) collective-permute-start(bf16[192,384]{1,0:T(8,128)(2,1)S(1)} %get-tuple-element.121), channel_id=1, source_target_pairs={{0,8},{8,0},{16,24},{24,16},{1,9},{9,1},{17,25},{25,17},{2,10},{10... | collective-permute-start | bytes 442376 | tf_op jit(solution)/shard_map/ppermute | solution.py:19
  110.5 14.0 %collective-permute-start.18 = (bf16[192,384]{1,0:T(8,128)(2,1)S(1)}, bf16[192,384]{1,0:T(8,128)(2,1)S(1)}, u32[]{:S(2)}, u32[]{:S(2)}) collective-permute-start(bf16[192,384]{1,0:T(8,128)(2,1)S(1)} %get-tuple-element.121), channel_id=1, source_target_pairs={{0,16},{8,24},{16,0},{24,8},{1,17},{9,25},{17,1},{25,9},{2,18},{10... | collective-permute-start | bytes 442376 | tf_op jit(solution)/shard_map/ppermute | solution.py:19
  112.5 12.0 %collective-permute-start.19 = (bf16[192,384]{1,0:T(8,128)(2,1)S(1)}, bf16[192,384]{1,0:T(8,128)(2,1)S(1)}, u32[]{:S(2)}, u32[]{:S(2)}) collective-permute-start(bf16[192,384]{1,0:T(8,128)(2,1)S(1)} %get-tuple-element.121), channel_id=1, source_target_pairs={{0,24},{8,16},{16,8},{24,0},{1,25},{9,17},{17,9},{25,1},{2,26},{10... | collective-permute-start | bytes 442376 | tf_op jit(solution)/shard_map/ppermute | solution.py:19
  113.9 9.7 %collective-permute-start.20 = (f32[192,192]{1,0:T(8,128)S(1)}, f32[192,192]{1,0:T(8,128)S(1)}, u32[]{:S(2)}, u32[]{:S(2)}) collective-permute-start(f32[192,192]{1,0:T(8,128)S(1)} %get-tuple-element.120), channel_id=1, source_target_pairs={{0,4},{4,0},{1,5},{5,1},{2,6},{6,2},{3,7},{7,3},{8,12},{12,8},{9,1... | collective-permute-start | bytes 442376 | tf_op jit(solution)/shard_map/ppermute | solution.py:19
  124.6 8.7 %collective-permute-start.22 = (bf16[384,384]{1,0:T(8,128)(2,1)S(1)}, bf16[384,384]{1,0:T(8,128)(2,1)S(1)}, u32[]{:S(2)}, u32[]{:S(2)}) collective-permute-start(bf16[384,384]{1,0:T(8,128)(2,1)S(1)} %constant_dynamic-update-slice_fusion.2.refs_4_), channel_id=1, source_target_pairs={{0,2},{1,3},{2,0},{3,1},{4,6},{5,7},{6,4},{7,5},{8,10},{9,11},{10,... | collective-permute-start | bytes 884744 | tf_op jit(solution)/shard_map/ppermute | solution.py:19
  126.1 20.7 %collective-permute-start.23 = (bf16[3,192,384]{2,1,0:T(8,128)(2,1)S(1)}, bf16[3,192,384]{2,1,0:T(8,128)(2,1)S(1)}, u32[]{:S(2)}, u32[]{:S(2)}) collective-permute-start(bf16[3,192,384]{2,1,0:T(8,128)(2,1)S(1)} %get-tuple-element.126), channel_id=1, source_target_pairs={{0,8},{8,0},{16,24},{24,16},{1,9},{9,1},{17,25},{25,17},{2,10},{10... | collective-permute-start | bytes 1327112 | tf_op jit(solution)/shard_map/ppermute | solution.py:19
  128.6 33.0 %collective-permute-start.24 = (bf16[3,192,384]{2,1,0:T(8,128)(2,1)S(1)}, bf16[3,192,384]{2,1,0:T(8,128)(2,1)S(1)}, u32[]{:S(2)}, u32[]{:S(2)}) collective-permute-start(bf16[3,192,384]{2,1,0:T(8,128)(2,1)S(1)} %get-tuple-element.127), channel_id=1, source_target_pairs={{0,16},{8,24},{16,0},{24,8},{1,17},{9,25},{17,1},{25,9},{2,18},{10... | collective-permute-start | bytes 1327112 | tf_op jit(solution)/shard_map/ppermute | solution.py:19
  130.5 10.0 %collective-permute-start.21 = (bf16[384,384]{1,0:T(8,128)(2,1)S(1)}, bf16[384,384]{1,0:T(8,128)(2,1)S(1)}, u32[]{:S(2)}, u32[]{:S(2)}) collective-permute-start(bf16[384,384]{1,0:T(8,128)(2,1)S(1)} %constant_dynamic-update-slice_fusion.refs_0_), channel_id=1, source_target_pairs={{0,4},{4,0},{1,5},{5,1},{2,6},{6,2},{3,7},{7,3},{8,12},{12,8},{9,1... | collective-permute-start | bytes 884744 | tf_op jit(solution)/shard_map/ppermute | solution.py:19
  131.8 31.5 %collective-permute-start.29 = (bf16[3,192,384]{2,1,0:T(8,128)(2,1)S(1)}, bf16[3,192,384]{2,1,0:T(8,128)(2,1)S(1)}, u32[]{:S(2)}, u32[]{:S(2)}) collective-permute-start(bf16[3,192,384]{2,1,0:T(8,128)(2,1)S(1)} %get-tuple-element.133), channel_id=1, source_target_pairs={{0,24},{8,16},{16,8},{24,0},{1,25},{9,17},{17,9},{25,1},{2,26},{10... | collective-permute-start | bytes 1327112 | tf_op jit(solution)/shard_map/ppermute | solution.py:19
  133.3 30.1 %collective-permute-start.27 = (bf16[384,384]{1,0:T(8,128)(2,1)S(1)}, bf16[384,384]{1,0:T(8,128)(2,1)S(1)}, u32[]{:S(2)}, u32[]{:S(2)}) collective-permute-start(bf16[384,384]{1,0:T(8,128)(2,1)S(1)} %constant_dynamic-update-slice_fusion.2.refs_4_), channel_id=1, source_target_pairs={{0,4},{4,0},{1,5},{5,1},{2,6},{6,2},{3,7},{7,3},{8,12},{12,8},{9,1... | collective-permute-start | bytes 884744 | tf_op jit(solution)/shard_map/ppermute | solution.py:19
  140.5 22.8 %collective-permute-start.25 = (bf16[384,384]{1,0:T(8,128)(2,1)S(1)}, bf16[384,384]{1,0:T(8,128)(2,1)S(1)}, u32[]{:S(2)}, u32[]{:S(2)}) collective-permute-start(bf16[384,384]{1,0:T(8,128)(2,1)S(1)} %constant_dynamic-update-slice_fusion.refs_0_), channel_id=1, source_target_pairs={{0,2},{1,3},{2,0},{3,1},{4,6},{5,7},{6,4},{7,5},{8,10},{9,11},{10,... | collective-permute-start | bytes 884744 | tf_op jit(solution)/shard_map/ppermute | solution.py:19
  161.6 6.7 %collective-permute-start.26 = (bf16[384,384]{1,0:T(8,128)(2,1)S(1)}, bf16[384,384]{1,0:T(8,128)(2,1)S(1)}, u32[]{:S(2)}, u32[]{:S(2)}) collective-permute-start(bf16[384,384]{1,0:T(8,128)(2,1)S(1)} %collective-permute-done.21.refs_1_), channel_id=1, source_target_pairs={{0,2},{1,3},{2,0},{3,1},{4,6},{5,7},{6,4},{7,5},{8,10},{9,11},{10,... | collective-permute-start | bytes 884744 | tf_op jit(solution)/shard_map/ppermute | solution.py:19
  162.1 6.7 %collective-permute-start.28 = (bf16[384,384]{1,0:T(8,128)(2,1)S(1)}, bf16[384,384]{1,0:T(8,128)(2,1)S(1)}, u32[]{:S(2)}, u32[]{:S(2)}) collective-permute-start(bf16[384,384]{1,0:T(8,128)(2,1)S(1)} %collective-permute-done.22.refs_5_), channel_id=1, source_target_pairs={{0,4},{4,0},{1,5},{5,1},{2,6},{6,2},{3,7},{7,3},{8,12},{12,8},{9,1... | collective-permute-start | bytes 884744 | tf_op jit(solution)/shard_map/ppermute | solution.py:19
  168.8 1.6 collective-permute-start.30
  168.8 2.0 %collective-permute-start.31 = (bf16[384,384]{1,0:T(8,128)(2,1)S(1)}, bf16[384,384]{1,0:T(8,128)(2,1)S(1)}, u32[]{:S(2)}, u32[]{:S(2)}) collective-permute-start(bf16[384,384]{1,0:T(8,128)(2,1)S(1)} %collective-permute-done.21.refs_1_), channel_id=1, source_target_pairs={{0,1},{1,0},{2,3},{3,2},{4,5},{5,4},{6,7},{7,6},{8,9},{9,8},{10,11... | collective-permute-start | bytes 884744 | tf_op jit(solution)/shard_map/ppermute | solution.py:19
  169.3 1.9 %collective-permute-start.32 = (bf16[384,384]{1,0:T(8,128)(2,1)S(1)}, bf16[384,384]{1,0:T(8,128)(2,1)S(1)}, u32[]{:S(2)}, u32[]{:S(2)}) collective-permute-start(bf16[384,384]{1,0:T(8,128)(2,1)S(1)} %collective-permute-done.25.refs_2_), channel_id=1, source_target_pairs={{0,1},{1,0},{2,3},{3,2},{4,5},{5,4},{6,7},{7,6},{8,9},{9,8},{10,11... | collective-permute-start | bytes 884744 | tf_op jit(solution)/shard_map/ppermute | solution.py:19
  169.3 3.1 %collective-permute-start.33 = (bf16[384,384]{1,0:T(8,128)(2,1)S(1)}, bf16[384,384]{1,0:T(8,128)(2,1)S(1)}, u32[]{:S(2)}, u32[]{:S(2)}) collective-permute-start(bf16[384,384]{1,0:T(8,128)(2,1)S(1)} %collective-permute-done.26.refs_3_), channel_id=1, source_target_pairs={{0,1},{1,0},{2,3},{3,2},{4,5},{5,4},{6,7},{7,6},{8,9},{9,8},{10,11... | collective-permute-start | bytes 884744 | tf_op jit(solution)/shard_map/ppermute | solution.py:19
  169.8 3.9 %collective-permute-start.34 = (bf16[384,384]{1,0:T(8,128)(2,1)S(1)}, bf16[384,384]{1,0:T(8,128)(2,1)S(1)}, u32[]{:S(2)}, u32[]{:S(2)}) collective-permute-start(bf16[384,384]{1,0:T(8,128)(2,1)S(1)} %constant_dynamic-update-slice_fusion.2.refs_4_), channel_id=1, source_target_pairs={{0,1},{1,0},{2,3},{3,2},{4,5},{5,4},{6,7},{7,6},{8,9},{9,8},{10,11... | collective-permute-start | bytes 884744 | tf_op jit(solution)/shard_map/ppermute | solution.py:19
  170.4 7.7 %collective-permute-start.35 = (bf16[384,384]{1,0:T(8,128)(2,1)S(1)}, bf16[384,384]{1,0:T(8,128)(2,1)S(1)}, u32[]{:S(2)}, u32[]{:S(2)}) collective-permute-start(bf16[384,384]{1,0:T(8,128)(2,1)S(1)} %collective-permute-done.22.refs_5_), channel_id=1, source_target_pairs={{0,1},{1,0},{2,3},{3,2},{4,5},{5,4},{6,7},{7,6},{8,9},{9,8},{10,11... | collective-permute-start | bytes 884744 | tf_op jit(solution)/shard_map/ppermute | solution.py:19
  170.8 7.3 %collective-permute-start.36 = (bf16[384,384]{1,0:T(8,128)(2,1)S(1)}, bf16[384,384]{1,0:T(8,128)(2,1)S(1)}, u32[]{:S(2)}, u32[]{:S(2)}) collective-permute-start(bf16[384,384]{1,0:T(8,128)(2,1)S(1)} %collective-permute-done.27.refs_6_), channel_id=1, source_target_pairs={{0,1},{1,0},{2,3},{3,2},{4,5},{5,4},{6,7},{7,6},{8,9},{9,8},{10,11... | collective-permute-start | bytes 884744 | tf_op jit(solution)/shard_map/ppermute | solution.py:19
  171.2 6.9 %collective-permute-start.37 = (bf16[384,384]{1,0:T(8,128)(2,1)S(1)}, bf16[384,384]{1,0:T(8,128)(2,1)S(1)}, u32[]{:S(2)}, u32[]{:S(2)}) collective-permute-start(bf16[384,384]{1,0:T(8,128)(2,1)S(1)} %collective-permute-done.28.refs_7_), channel_id=1, source_target_pairs={{0,1},{1,0},{2,3},{3,2},{4,5},{5,4},{6,7},{7,6},{8,9},{9,8},{10,11... | collective-permute-start | bytes 884744 | tf_op jit(solution)/shard_map/ppermute | solution.py:19
  172.4 12.2 %collective-permute-start.38 = (f32[192,192]{1,0:T(8,128)S(1)}, f32[192,192]{1,0:T(8,128)S(1)}, u32[]{:S(2)}, u32[]{:S(2)}) collective-permute-start(f32[192,192]{1,0:T(8,128)S(1)} %get-tuple-element.148), channel_id=1, source_target_pairs={{0,4},{4,0},{1,5},{5,1},{2,6},{6,2},{3,7},{7,3},{8,12},{12,8},{9,1... | collective-permute-start | bytes 442376 | tf_op jit(solution)/shard_map/ppermute | solution.py:19
  173.7 12.2 %collective-permute-start.39 = (bf16[192,384]{1,0:T(8,128)(2,1)S(1)}, bf16[192,384]{1,0:T(8,128)(2,1)S(1)}, u32[]{:S(2)}, u32[]{:S(2)}) collective-permute-start(bf16[192,384]{1,0:T(8,128)(2,1)S(1)} %get-tuple-element.149), channel_id=1, source_target_pairs={{0,0},{1,8},{2,16},{3,24},{4,4},{5,12},{6,20},{7,28},{8,1},{9,9},{... | collective-permute-start | bytes 442376 | tf_op jit(solution)/shard_map/ppermute | solution.py:729
  (5 other events, 62.9 us)

commit v6 on v5

--- a/solution.py
+++ b/solution.py
@@ -49,19 +49,22 @@
         own_id = meta[2] + slot
         facts = jnp.where(place == 6, levels[slot], jnp.where(place == 7, jnp.where(keep, 1, 0), 0))
         for c in range(6):
-            target = neighbours[slot, c]
+            target = neighbours[slot, c // 2, c % 2]
             facts = jnp.where(place == c, jnp.where(target >= 0, target - own_id, 16 * slots), facts)
         facts = facts.astype(f32).astype(bf16)
         for packed in (theirs, mine):
             packed[slot, fold : fold + 8, :] = facts
         row = fold + 8
         for start in range(0, pot.shape[1], width):
-            exact = pot[slot : slot + 1, start : start + width]
+            stop = min(start + width, pot.shape[1])
+            exact = pot[slot : slot + 1, start:stop]
             for _ in range(3):
                 part = exact.astype(bf16)
                 exact = exact - part.astype(f32)
                 for packed in (theirs, mine):
-                    packed[slot, row : row + 1, :] = part
+                    packed[slot, row : row + 1, : stop - start] = part
+                    if stop - start < width:
+                        packed[slot, row : row + 1, stop - start :] = jnp.zeros((1, width - stop + start), bf16)
                 row += 1
         for packed in (theirs, mine):
             packed[slot, row:, :] = jnp.zeros((packed.shape[1] - row, width), bf16)
@@ -70,7 +73,7 @@
 def pack(meta, neighbours, levels, orbitals, pot):
     slots, coefficients, width = orbitals.shape
     fold = coefficients // 2
-    padded = -(-(fold + 8 + 3 * (pot.shape[1] // width)) // ROWS) * ROWS
+    padded = -(-(fold + 8 + 3 * -(-coefficients // width)) // ROWS) * ROWS
     vmem, smem = pl.BlockSpec(memory_space=pltpu.VMEM), pl.BlockSpec(memory_space=pltpu.SMEM)
     return pl.pallas_call(
         pack_kernel,
@@ -144,56 +147,110 @@
     return [[refs.pop(0) for _ in range(count)] for count in counts]
 
 
-def correlation_kernel(share, counts, meta, *refs):
-    refs, (out, held, turned, sems) = refs[:-4], refs[-4:]
-    groups, half, width = out.shape
-    lefts, before = grouped(refs, counts), refs[sum(counts) :]
-    copies = load_left(lefts, held, sems)
+def correlation_kernel(share, boxes, bases, meta, *refs):
+    extra = 2 if share else 0
+    blocks, refs = refs[: sum(map(sum, boxes))], refs[sum(map(sum, boxes)) :]
+    refs, (out, held, turned, sems) = refs[:extra], refs[extra:]
     first = meta[0] == 0
-    for copy in copies[: counts[0]]:
-        copy.wait()
-    own = held[:, :width]
-    own = jnp.where(first, own[:, :half], own[:, half:]).T
-    live = lax.broadcasted_iota(jnp.int32, own.shape, 1) < meta[1 if before else 2]
-    turned[...] = jnp.where(live, own, jnp.zeros_like(own))
-    for base in range(0, groups, 2):
-        for copy in copies[max(sum(counts[:base]), counts[0]) : sum(counts[: base + 2])]:
-            copy.wait()
-        wide = matmul(turned[...], held[:, base * width : (base + 2) * width])
-        for q in (base, base + 1):
-            total = wide[:, (q - base) * width : (q - base + 1) * width]
-            if before:
-                total = total + before[0][q]
-                if q == 0:
-                    rows = lax.broadcasted_iota(jnp.int32, (half, width), 0) + jnp.where(first, 0, half)
-                    columns = lax.broadcasted_iota(jnp.int32, (half, width), 1)
-                    total = total - jnp.where(rows == columns, share, 0.0)
-            out[q] = total.astype(out.dtype)
-
-
-def box_correlation(share, meta, lefts, before, half):
-    depth, width = sum(piece.shape[0] for piece in lefts[0]), lefts[0][0].shape[1]
-    counts = [len(pieces) for pieces in lefts]
+    half, width = out.shape[1:]
+    lefts, used = [], 0
+    for counts in boxes:
+        lefts.append(grouped(blocks[used : used + sum(counts)], counts))
+        used += sum(counts)
+    copies = [load_left(left, held.at[box], sems.at[box]) for box, left in enumerate(lefts)]
+    if share:
+        before, own_turned = refs
+    for box, counts in enumerate(boxes):
+        done = 0
+        if share and box == 0:
+            right = own_turned
+        else:
+            for copy in copies[box][: counts[0]]:
+                copy.wait()
+            done = counts[0]
+            own = held[box, :, :width]
+            own = jnp.where(first, own[:, :half], own[:, half:]).T
+            if not share:
+                live = lax.broadcasted_iota(jnp.int32, own.shape, 1) < meta[1]
+                own = jnp.where(live, own, jnp.zeros_like(own))
+            right = turned
+            right[...] = own
+        for base in range(0, len(counts), 2):
+            upto = sum(counts[: base + 2])
+            for copy in copies[box][done:upto]:
+                copy.wait()
+            done = upto
+            wide = matmul(right[...], held[box, :, base * width : (base + 2) * width])
+            for q in (base, base + 1):
+                target = bases[box] + q
+                total = wide[:, (q - base) * width : (q - base + 1) * width]
+                out[target] = total if box == 0 else out[target] + total
+
+
+def early_correlation(meta, lefts, half):
+    depth, width = lefts[0].shape
     vmem = pl.BlockSpec(memory_space=pltpu.VMEM)
-    extra = [] if before is None else [before]
+
+    def kernel(meta, *refs):
+        blocks, (out, turned, held, sems) = refs[: len(lefts)], refs[len(lefts) :]
+        correlation_kernel(None, [[1] * len(lefts)], [0], meta, *blocks, out, held, turned, sems)
+
     return pl.pallas_call(
-        functools.partial(correlation_kernel, share, counts),
-        out_shape=jax.ShapeDtypeStruct((len(lefts), half, width), f32 if before is None else bf16),
+        kernel,
+        out_shape=[
+            jax.ShapeDtypeStruct((len(lefts), half, width), f32),
+            jax.ShapeDtypeStruct((half, depth), bf16),
+        ],
+        in_specs=[pl.BlockSpec(memory_space=pltpu.SMEM)] + [pl.BlockSpec(memory_space=pl.ANY)] * len(lefts),
+        out_specs=[vmem, vmem],
+        scratch_shapes=[
+            pltpu.VMEM((1, depth, len(lefts) * width), bf16),
+            pltpu.SemaphoreType.DMA((1, len(lefts))),
+        ],
+        compiler_params=params(24),
+        name="early_correlation",
+    )(meta, *lefts)
+
+
+def late_correlation(share, meta, lefts_own, lefts_beside, before, own_turned):
+    half, width = before.shape[1:]
+    depth = own_turned.shape[1]
+    boxes = [[len(pieces) for pieces in lefts] for lefts in (lefts_own, lefts_beside)]
+    groups, early = len(lefts_beside), before.shape[0]
+    operands = [piece for lefts in (lefts_own, lefts_beside) for pieces in lefts for piece in pieces]
+    vmem = pl.BlockSpec(memory_space=pltpu.VMEM)
+
+    def kernel(meta, *refs):
+        out, total, held, turned, sems = refs[-5:]
+        before = refs[-7]
+        for q in range(early):
+            total[q] = before[q]
+        correlation_kernel(share, boxes, [early, 0], meta, *refs[:-5], total, held, turned, sems)
+        first = meta[0] == 0
+        rows = lax.broadcasted_iota(jnp.int32, (half, width), 0) + jnp.where(first, 0, half)
+        columns = lax.broadcasted_iota(jnp.int32, (half, width), 1)
+        total[0] = total[0] - jnp.where(rows == columns, share, 0.0)
+        out[...] = total[...].astype(bf16)
+
+    return pl.pallas_call(
+        kernel,
+        out_shape=jax.ShapeDtypeStruct((groups, half, width), bf16),
         in_specs=[pl.BlockSpec(memory_space=pltpu.SMEM)]
-        + [pl.BlockSpec(memory_space=pl.ANY)] * sum(counts)
-        + [vmem] * len(extra),
+        + [pl.BlockSpec(memory_space=pl.ANY)] * len(operands)
+        + [vmem, vmem],
         out_specs=vmem,
         scratch_shapes=[
-            pltpu.VMEM((depth, len(lefts) * width), bf16),
+            pltpu.VMEM((groups, half, width), f32),
+            pltpu.VMEM((2, depth, groups * width), bf16),
             pltpu.VMEM((half, depth), bf16),
-            pltpu.SemaphoreType.DMA((sum(counts),)),
+            pltpu.SemaphoreType.DMA((2, max(map(sum, boxes)))),
         ],
-        compiler_params=params(32),
+        compiler_params=params(40),
         cost_estimate=pl.CostEstimate(
-            flops=2 * len(lefts) * depth * width * half, bytes_accessed=2 * len(lefts) * depth * width, transcendentals=0
+            flops=2 * 2 * groups * depth * width * half, bytes_accessed=4 * groups * depth * width, transcendentals=0
         ),
         name="correlation",
-    )(meta, *[piece for pieces in lefts for piece in pieces], *extra)
+    )(meta, *operands, before, own_turned)
 
 
 def fock_kernel(side, counts, right, *refs):
@@ -325,7 +382,7 @@
             pltpu.SemaphoreType.DMA((side // coarse * (side // width),)),
         ],
         compiler_params=params(40),
-        cost_estimate=pl.CostEstimate(flops=16 * side * side * width, bytes_accessed=4 * side * side, transcendentals=0),
+        cost_estimate=pl.CostEstimate(flops=side * side, bytes_accessed=side, transcendentals=0),
         name="root",
     )(meta, *pieces, offset)
 
@@ -624,11 +681,15 @@
     square_grid = level_count == orb_count == 4 and box_rows == half
     row0, col0 = (level * PAIR + pair) * box_rows, orb * own_width
 
-    pot = jnp.pad(potential, ((0, 0), (0, -coefficients % own_width)))
     own_base = (level * PAIR + pair) * slots
     pack_meta = jnp.stack([pair, box_counts[0], own_base]).astype(jnp.int32)
-    theirs, mine = pack(pack_meta, neighbours.reshape(slots, 6), levels, orbitals, pot)
+    theirs, mine = pack(pack_meta, neighbours, levels, orbitals, potential)
     active = orbitals
+
+    meta = jnp.stack([pair, box_counts[0] * coefficients]).astype(jnp.int32)
+    near_active = swap(active, "orb", 1)
+    flat = lambda block: block.reshape(-1, block.shape[-1])
+    early_blocks, own_turned = early_correlation(meta, [flat(active), flat(near_active)], half)
 
     far = {q: swap(active, "orb", q) for q in groups if q and q % 2 == 0}
     beside = swap(theirs, "pair", 1)
@@ -643,17 +704,16 @@
         return jnp.stack([part[:, fold, :8] for part in parts]).astype(f32).astype(jnp.int32)
 
     early_facts = facts_of([mine, beside, first_mine, second_mine])
-    flat = lambda block: block.reshape(-1, block.shape[-1])
     cut = -(-slots * coefficients // (2 * ROWS)) * ROWS
     beside_all, beside_top = unfold(pack_meta, beside, beside_rest, fold, cut)
 
     parts = [mine, beside, first_mine, first_beside, second_mine, second_beside]
-    far, active, parts, beside_all, beside_top, matrices, early_facts = lax.optimization_barrier(
-        (far, active, parts, beside_all, beside_top, matrices, early_facts)
+    far, early_blocks, parts, beside_all, beside_top, matrices, early_facts = lax.optimization_barrier(
+        (far, early_blocks, parts, beside_all, beside_top, matrices, early_facts)
     )
     facts = jnp.concatenate([early_facts, facts_of([parts[3], parts[5]])])
     cross = {q: [swap(beside_top, "orb", q), swap(flat(far[q])[cut:], "pair", 1)] for q in far}
-    left_own = {0: active, 1: swap(active, "orb", 1), **far}
+    left_own = {0: active, 1: near_active, **far}
     left_beside = {0: [beside_all], 1: [swap(beside_all, "orb", 1)]}
     for q in far:
         left_own[q + 1] = swap(far[q], "orb", 1)
@@ -674,8 +734,6 @@
         strip = lax.dynamic_slice_in_dim(strip, row0, box_rows, axis=0)
         return lax.dynamic_slice_in_dim(strip, col0, own_width, axis=1)
 
-    live_rows = box_counts[0] * coefficients
-    meta = jnp.stack([pair, slots * coefficients, live_rows]).astype(jnp.int32)
 
     place_meta = jnp.stack([level, pair]).astype(jnp.int32)
     right = kinetic(parts, place_meta, facts, matrices, edge, coefficients, level_count)
@@ -689,8 +747,7 @@
     lefts_beside = [lefts_beside[q] for q in groups]
 
     share = 1.0 / level_count
-    blocks = box_correlation(share, meta, lefts_own, None, half)
-    blocks = box_correlation(share, meta, lefts_beside, blocks, half)
+    blocks = late_correlation(share, meta, lefts_own[2:], lefts_beside, early_blocks, own_turned)
     right = right.reshape(2, slots * coefficients, 3 * half)
     fock_part = box_fock(0, lefts_own, right, None, None)
     if square_grid:
@@ -712,13 +769,14 @@
         top, low = join(pieces[: level_count // 2]), join(pieces[level_count // 2 :])
         sent = [fock_blocks[0]] + [swap(fock_blocks[step], "lvl", step) for step in range(1, level_count)]
         got = [swap(top, "pair", 1), swap(low, "orb", 2)]
-        got, sent[:3] = lax.optimization_barrier((got, sent[:3]))
+        got, sent[:2] = lax.optimization_barrier((got, sent[:2]))
         tops, lows = [top, got[0]], [low, got[1]]
         pieces = tops + [swap(piece, "orb", 2) for piece in tops] + lows + [swap(piece, "pair", 1) for piece in lows]
-        pieces, sent = lax.optimization_barrier((pieces, sent))
+        pieces, sent[:3] = lax.optimization_barrier((pieces, sent[:3]))
         pieces += [swap(piece, "orb", 1) for piece in pieces]
         root_meta = jnp.stack([level, pair, orb]).astype(jnp.int32)
         inverse_root = root_of(root_meta, pieces, offset, all_width, level_count)
+        inverse_root, sent = lax.optimization_barrier((inverse_root, sent))
         share, kept, other = level_sum(fock_sum_kernel, meta, sent)
         to = [
             ((z * PAIR + y) * orb_count + o, (o * PAIR + y) * orb_count + z)
@@ -727,7 +785,6 @@
             for o in groups
         ]
         got = swap(other, "pair", 1), lax.ppermute(share, BOX + ("orb",), to)
-        inverse_root, got = lax.optimization_barrier((inverse_root, got))
         fock = both_halves(kept, got[0]) + got[1].astype(f32)
     else:
         fock_blocks = jnp.stack(fock_blocks)

time: 190 us -> 192 us (1.011); the launches traced: 187 us -> 192 us
  waiting for transfers between devices: 60.1 us -> 49.9 us
  starting transfers between devices: 51.1 us -> 58.4 us
  Pallas kernels: 62.9 us -> 68.9 us
    ppermute x35, waiting for transfers between devices: 58.8 us -> 44.4 us  [swap(): return lax.ppermute(value, axis, [(i, i ^ bit) for i in range(count)])]
    ppermute x1, starting transfers between devices: 4.44 us -> 11.4 us  [body(): got = (swap(other, 'pair', 1), lax.ppermute(share, BOX + ('orb',), to))]
    pallas_call x1, Pallas kernels: 22.5 us -> 28.6 us  [kinetic(): pl.pallas_call(functools.partial(kinetic_kernel, edge, slots, levels), ou...]
    ppermute x1, waiting for transfers between devices: 1.3 us -> 5.53 us  [body(): got = (swap(other, 'pair', 1), lax.ppermute(share, BOX + ('orb',), to))]
    unnamed x35 -> x45, local copies, waits for them, and re-layouts: 3.63 us -> 5.36 us
  transfers between devices with their start and end apart: 40 -> 40, of which waited for: 12 -> 17; matrix products, arithmetic and copies ran while one was open for 2% -> 3% of each run, Pallas kernels for 29% -> 30%
where the time goes in v6:
time: 192 us
  Pallas kernels  68.9 us (36%)
  starting transfers between devices  58.4 us (30%)
  waiting for transfers between devices  49.9 us (26%)
  local copies, waits for them, and re-layouts  10.4 us (5%)
  other arithmetic  2.1 us (1%)
    ppermute x35, waiting for transfers between devices, swap(): return lax.ppermute(value, axis, [(i, i ^ bit) for i in range(count)])  44.4 us
    ppermute x35, starting transfers between devices, swap(): return lax.ppermute(value, axis, [(i, i ^ bit) for i in range(count)])  37 us
    pallas_call x1, Pallas kernels, kinetic(): pl.pallas_call(functools.partial(kinetic_kernel, edge, slots, levels), ou...  28.6 us
    pallas_call x2, Pallas kernels, box_fock(): pl.pallas_call(functools.partial(fock_kernel, side, counts), out_shape=ou...  16.2 us
    ppermute x1, starting transfers between devices, body(): got = (swap(other, 'pair', 1), lax.ppermute(share, BOX + ('orb',), to))  11.4 us
    ppermute x4, starting transfers between devices, trade(): return lax.ppermute(value, axis, pairs + [(b, a) for a, b in pairs])  10.1 us
    pallas_call x1, Pallas kernels, root_of(): pl.pallas_call(functools.partial(root_kernel, levels), out_shape=jax.Shap...  6.36 us
    pallas_call x1, Pallas kernels, late_correlation(): pl.pallas_call(kernel, out_shape=jax.ShapeDtypeStruct((groups, half, widt...  5.83 us
  transfers between devices with their start and end apart: 40, of which 17 were waited for; matrix products, arithmetic and copies ran while one was open for 3% of the time, Pallas kernels for 30%

profile of v6, /device:TPU:2, one launch (start us, length us, event | category | flops | bytes accessed | tf_op | source)
XLA Modules:
  0.0 191.6 jit_solution(16361851878269716043)
XLA Ops:
  3.7 3.2 %pack.1 = (bf16[2,528,384]{2,1,0:T(8,128)(2,1)S(1)}, bf16[2,528,384]{2,1,0:T(8,128)(2,1)}) custom-call(s32[3]{0:T(128)S(1)} %pad_add_fusion.2.meta, s32[2,3,2]{2,1,0:T(4,128)S(1)} %copy.20.neighbours, s32[2]{0:T(128)S(1)} %copy-done.16, bf16[2,1000,384]{2,1,0:T(8,128)(2,1)} %orbitals.1, f32[2,1000]{1,0:T(2,128)S(1)} %copy-done.15), custom_call_target="tpu_custom_call" | custom-call | tf_op jit(solution)/shard_map/pack/pallas_call | solution.py:78
  6.9 1.5 collective-permute-start.2
  8.4 1.6 collective-permute-start.5
  10.0 3.6 %collective-permute-start.3 = (bf16[2,528,384]{2,1,0:T(8,128)(2,1)}, bf16[2,528,384]{2,1,0:T(8,128)(2,1)}, u32[]{:S(2)}, u32[]{:S(2)}) collective-permute-start(bf16[2,528,384]{2,1,0:T(8,128)(2,1)} %get-tuple-element.97.refs_0_), channel_id=1, source_target_pairs={{0,8},{16,24},{8,0},{24,16},{1,9},{17,25},{9,1},{25,17},{2,10},{18... | collective-permute-start | bytes 2433032 | tf_op jit(solution)/shard_map/ppermute | solution.py:24
  14.1 12.7 %collective-permute-done.2.beside_in.refs_1_ = bf16[2,528,384]{2,1,0:T(8,128)(2,1)} collective-permute-done((bf16[2,528,384]{2,1,0:T(8,128)(2,1)S(1)}, bf16[2,528,384]{2,1,0:T(8,128)(2,1)}, u32[]{:S(2)}, u32[]{:S(2)}) %collective-permute-start.2) | collective-permute-done | bytes 811040 | tf_op jit(solution)/shard_map/ppermute | solution.py:19
  26.8 1.5 collective-permute-start.7
  28.3 3.4 %collective-permute-start.4 = (bf16[2,528,384]{2,1,0:T(8,128)(2,1)}, bf16[2,528,384]{2,1,0:T(8,128)(2,1)}, u32[]{:S(2)}, u32[]{:S(2)}) collective-permute-start(bf16[2,528,384]{2,1,0:T(8,128)(2,1)} %collective-permute-done.2.beside_in.refs_1_), channel_id=1, source_target_pairs={{0,8},{16,24},{8,0},{24,16},{1,9},{17,25},{9,1},{25,17},{2,10},{18... | collective-permute-start | bytes 2433032 | tf_op jit(solution)/shard_map/ppermute | solution.py:24
  31.7 1.5 collective-permute-start.6
  34.0 0.8 reshape.43.stacked
  34.8 1.0 matrices.1
  38.1 3.6 %early_correlation.1 = (f32[2,192,384]{2,1,0:T(8,128)S(1)}, bf16[192,2000]{1,0:T(8,128)(2,1)S(1)}) custom-call(s32[2]{0:T(128)S(1)} %pad_add_fusion.1.meta, bf16[2000,384]{1,0:T(8,128)(2,1)} %bitcast.1.refs_0_, bf16[2000,384]{1,0:T(8,128)(2,1)S(1)} %bitcast.38), custom_call_target="tpu_custom_call" | custom-call | tf_op jit(solution)/shard_map/early_correlation/pallas_call | solution.py:198
  41.7 0.9 copy-done.2
  42.6 3.5 %collective-permute-done.7.rest_in = bf16[2,528,384]{2,1,0:T(8,128)(2,1)} collective-permute-done((bf16[2,528,384]{2,1,0:T(8,128)(2,1)}, bf16[2,528,384]{2,1,0:T(8,128)(2,1)}, u32[]{:S(2)}, u32[]{:S(2)}) %collective-permute-start.7) | collective-permute-done | bytes 811040 | tf_op jit(solution)/shard_map/ppermute | solution.py:19
  46.1 2.4 %unfold.1 = (bf16[2000,384]{1,0:T(8,128)(2,1)S(1)}, bf16[1008,384]{1,0:T(8,128)(2,1)S(1)}) custom-call(s32[3]{0:T(128)S(1)} %pad_add_fusion.2.meta, bf16[2,528,384]{2,1,0:T(8,128)(2,1)} %collective-permute-done.2.beside_in.refs_1_, bf16[2,528,384]{2,1,0:T(8,128)(2,1)} %collective-permute-done.7.rest_in), custom_call_target="tpu_custom_call" | custom-call | tf_op jit(solution)/shard_map/unfold/pallas_call | solution.py:113
  48.5 1.3 collective-permute-done
  52.4 28.6 %kinetic.1 = bf16[4,1000,576]{2,1,0:T(8,128)(2,1)} custom-call(s32[2]{0:T(128)S(1)} %pad_add_fusion.3.place_meta, s32[6,2,8]{2,1,0:T(2,128)S(1)} %pad_add_fusion.facts, bf16[2,528,384]{2,1,0:T(8,128)(2,1)} %get-tuple-element.97.refs_0_, bf16[2,528,384]{2,1,0:T(8,128)(2,1)} %collective-permute-done.2.beside_in.refs_1_, ...), custom_call_target="tpu_custom_call" | custom-call | flops 20000000000 | bytes 40000000 | tf_op jit(solution)/shard_map/kinetic/pallas_call | solution.py:608
  81.7 3.2 %collective-permute-done.13.refs_7_.refs_5_ = bf16[992,384]{1,0:T(8,128)(2,1)} collective-permute-done((bf16[992,384]{1,0:T(8,128)(2,1)}, bf16[992,384]{1,0:T(8,128)(2,1)}, u32[]{:S(2)}, u32[]{:S(2)}) %collective-permute-start.13) | collective-permute-done | bytes 761888 | tf_op jit(solution)/shard_map/ppermute | solution.py:19
  84.9 1.1 copy-done.3
  86.1 1.1 copy-done.5
  87.1 5.8 %correlation.1 = bf16[4,192,384]{2,1,0:T(8,128)(2,1)S(1)} custom-call(s32[2]{0:T(128)S(1)} %pad_add_fusion.1.meta, bf16[2000,384]{1,0:T(8,128)(2,1)S(1)} %bitcast.36, bf16[2000,384]{1,0:T(8,128)(2,1)} %bitcast.8.refs_1_.refs_3_, bf16[2000,384]{1,0:T(8,128)(2,1)S(1)} %get-tuple-element.107.refs_2_.refs_0_, ...), custom_call_target="tpu_custom_call" | custom-call | flops 2359296000 | bytes 12288000 | tf_op jit(solution)/shard_map/correlation/pallas_call | solution.py:235
  93.0 3.5 %collective-permute-start.14 = (bf16[192,384]{1,0:T(8,128)(2,1)S(1)}, bf16[192,384]{1,0:T(8,128)(2,1)S(1)}, u32[]{:S(2)}, u32[]{:S(2)}) collective-permute-start(bf16[192,384]{1,0:T(8,128)(2,1)S(1)} %get-tuple-element.161), channel_id=1, source_target_pairs={{0,8},{8,0},{16,24},{24,16},{1,9},{9,1},{17,25},{25,17},{2,10},{10... | collective-permute-start | bytes 442376 | tf_op jit(solution)/shard_map/ppermute | solution.py:19
  96.5 2.4 %collective-permute-start.16 = (bf16[192,384]{1,0:T(8,128)(2,1)S(1)}, bf16[192,384]{1,0:T(8,128)(2,1)S(1)}, u32[]{:S(2)}, u32[]{:S(2)}) collective-permute-start(bf16[192,384]{1,0:T(8,128)(2,1)S(1)} %get-tuple-element.159), channel_id=1, source_target_pairs={{0,24},{8,16},{16,8},{24,0},{1,25},{9,17},{17,9},{25,1},{2,26},{10... | collective-permute-start | bytes 442376 | tf_op jit(solution)/shard_map/ppermute | solution.py:19
  99.0 7.7 %fock.2.refs_6_ = f32[4,576,384]{2,1,0:T(8,128)S(1)} custom-call(bf16[2,2000,576]{2,1,0:T(8,128)(2,1)} %bitcast.40, bf16[2000,384]{1,0:T(8,128)(2,1)} %bitcast.1.refs_0_, bf16[2000,384]{1,0:T(8,128)(2,1)S(1)} %bitcast.39, bf16[2000,384]{1,0:T(8,128)(2,1)S(1)} %bitcast.37, bf16[2000,384]{1,0:T(8,128)(2,1)} %bitcast.8.refs_1_.refs_3_), custom_call_target="tpu_custom_call" | custom-call | flops 3538944000 | bytes 6144000 | tf_op jit(solution)/shard_map/fock/pallas_call | solution.py:298
  106.7 2.8 %collective-permute-done.15.refs_2_ = bf16[192,384]{1,0:T(8,128)(2,1)S(1)} collective-permute-done((bf16[192,384]{1,0:T(8,128)(2,1)S(1)}, bf16[192,384]{1,0:T(8,128)(2,1)S(1)}, u32[]{:S(2)}, u32[]{:S(2)}) %collective-permute-start.15) | collective-permute-done | bytes 147488 | tf_op jit(solution)/shard_map/ppermute | solution.py:19
  109.5 0.8 level_sum.2
  110.3 3.7 %collective-permute-start.17 = (bf16[192,384]{1,0:T(8,128)(2,1)S(1)}, bf16[192,384]{1,0:T(8,128)(2,1)S(1)}, u32[]{:S(2)}, u32[]{:S(2)}) collective-permute-start(bf16[192,384]{1,0:T(8,128)(2,1)S(1)} %get-tuple-element.125), channel_id=1, source_target_pairs={{0,8},{8,0},{16,24},{24,16},{1,9},{9,1},{17,25},{25,17},{2,10},{10... | collective-permute-start | bytes 442376 | tf_op jit(solution)/shard_map/ppermute | solution.py:19
  114.0 2.4 %collective-permute-start.19 = (bf16[192,384]{1,0:T(8,128)(2,1)S(1)}, bf16[192,384]{1,0:T(8,128)(2,1)S(1)}, u32[]{:S(2)}, u32[]{:S(2)}) collective-permute-start(bf16[192,384]{1,0:T(8,128)(2,1)S(1)} %get-tuple-element.125), channel_id=1, source_target_pairs={{0,24},{8,16},{16,8},{24,0},{1,25},{9,17},{17,9},{25,1},{2,26},{10... | collective-permute-start | bytes 442376 | tf_op jit(solution)/shard_map/ppermute | solution.py:19
  116.4 1.5 collective-permute-start.20
  118.0 8.5 %fock.3 = (bf16[3,192,384]{2,1,0:T(8,128)(2,1)S(1)}, bf16[3,192,384]{2,1,0:T(8,128)(2,1)S(1)}, bf16[3,192,384]{2,1,0:T(8,128)(2,1)S(1)}, bf16[3,192,384]{2,1,0:T(8,128)(2,1)S(1)}) custom-call(bf16[2,2000,576]{2,1,0:T(8,128)(2,1)} %bitcast.41, bf16[2000,384]{1,0:T(8,128)(2,1)S(1)} %get-tuple-element.107.refs_2_.refs_0_, ...), custom_call_target="tpu_custom_call" | custom-call | flops 3538944000 | bytes 6144000 | tf_op jit(solution)/shard_map/fock/pallas_call | solution.py:298
  126.5 0.9 convert_add_fusion
  127.4 1.6 collective-permute-start.22
  129.0 3.1 %collective-permute-start.23 = (bf16[3,192,384]{2,1,0:T(8,128)(2,1)S(1)}, bf16[3,192,384]{2,1,0:T(8,128)(2,1)S(1)}, u32[]{:S(2)}, u32[]{:S(2)}) collective-permute-start(bf16[3,192,384]{2,1,0:T(8,128)(2,1)S(1)} %get-tuple-element.130), channel_id=1, source_target_pairs={{0,8},{8,0},{16,24},{24,16},{1,9},{9,1},{17,25},{25,17},{2,10},{10... | collective-permute-start | bytes 1327112 | tf_op jit(solution)/shard_map/ppermute | solution.py:19
  132.1 1.6 collective-permute-start.21
  134.2 1.4 collective-permute-done.22.refs_5_
  135.6 1.5 collective-permute-start.24
  137.1 5.0 %collective-permute-done.21.refs_1_ = bf16[384,384]{1,0:T(8,128)(2,1)S(1)} collective-permute-done((bf16[384,384]{1,0:T(8,128)(2,1)S(1)}, bf16[384,384]{1,0:T(8,128)(2,1)S(1)}, u32[]{:S(2)}, u32[]{:S(2)}) %collective-permute-start.21) | collective-permute-done | bytes 294944 | tf_op jit(solution)/shard_map/ppermute | solution.py:19
  142.1 5.4 %collective-permute-done.23.refs_1_ = bf16[3,192,384]{2,1,0:T(8,128)(2,1)S(1)} collective-permute-done((bf16[3,192,384]{2,1,0:T(8,128)(2,1)S(1)}, bf16[3,192,384]{2,1,0:T(8,128)(2,1)S(1)}, u32[]{:S(2)}, u32[]{:S(2)}) %collective-permute-start.23) | collective-permute-done | bytes 442400 | tf_op jit(solution)/shard_map/ppermute | solution.py:19
  148.1 2.6 %collective-permute-start.27 = (bf16[384,384]{1,0:T(8,128)(2,1)S(1)}, bf16[384,384]{1,0:T(8,128)(2,1)S(1)}, u32[]{:S(2)}, u32[]{:S(2)}) collective-permute-start(bf16[384,384]{1,0:T(8,128)(2,1)S(1)} %collective-permute-done.22.refs_5_), channel_id=1, source_target_pairs={{0,4},{4,0},{1,5},{5,1},{2,6},{6,2},{3,7},{7,3},{8,12},{12,8},{9,1... | collective-permute-start | bytes 884744 | tf_op jit(solution)/shard_map/ppermute | solution.py:19
  150.6 4.2 %collective-permute-done.28.refs_2_ = bf16[3,192,384]{2,1,0:T(8,128)(2,1)S(1)} collective-permute-done((bf16[3,192,384]{2,1,0:T(8,128)(2,1)S(1)}, bf16[3,192,384]{2,1,0:T(8,128)(2,1)S(1)}, u32[]{:S(2)}, u32[]{:S(2)}) %collective-permute-start.28) | collective-permute-done | bytes 442400 | tf_op jit(solution)/shard_map/ppermute | solution.py:19
  155.0 1.1 collective-permute-done.27.refs_7_
  157.1 2.9 %collective-permute-start.37 = (bf16[3,192,384]{2,1,0:T(8,128)(2,1)S(1)}, bf16[3,192,384]{2,1,0:T(8,128)(2,1)S(1)}, u32[]{:S(2)}, u32[]{:S(2)}) collective-permute-start(bf16[3,192,384]{2,1,0:T(8,128)(2,1)S(1)} %get-tuple-element.148), channel_id=1, source_target_pairs={{0,24},{8,16},{16,8},{24,0},{1,25},{9,17},{17,9},{25,1},{2,26},{10... | collective-permute-start | bytes 1327112 | tf_op jit(solution)/shard_map/ppermute | solution.py:19
  162.8 6.4 %root.1 = f32[192,384]{1,0:T(8,128)} custom-call(s32[3]{0:T(128)S(1)} %pad_add_fusion.4.meta, bf16[384,384]{1,0:T(8,128)(2,1)S(1)} %constant_dynamic-update-slice_fusion.refs_0_, bf16[384,384]{1,0:T(8,128)(2,1)S(1)} %collective-permute-done.21.refs_1_, bf16[384,384]{1,0:T(8,128)(2,1)S(1)} %collective-permute-done.24.refs_2_, ...), custom_call_target="tpu_custom_call" | custom-call | flops 2359296 | bytes 1536 | tf_op jit(solution)/shard_map/root/pallas_call | solution.py:373
  169.2 1.9 collective-permute-done.37.refs_3_
  171.0 0.9 level_sum.3
  172.0 1.8 collective-permute-start.38
  173.8 11.4 %collective-permute-start.39 = (bf16[192,384]{1,0:T(8,128)(2,1)S(1)}, bf16[192,384]{1,0:T(8,128)(2,1)S(1)}, u32[]{:S(2)}, u32[]{:S(2)}) collective-permute-start(bf16[192,384]{1,0:T(8,128)(2,1)S(1)} %get-tuple-element.155), channel_id=1, source_target_pairs={{0,0},{1,8},{2,16},{3,24},{4,4},{5,12},{6,20},{7,28},{8,1},{9,9},{... | collective-permute-start | bytes 442376 | tf_op jit(solution)/shard_map/ppermute | solution.py:787
  185.2 5.5 %collective-permute-done.39 = bf16[192,384]{1,0:T(8,128)(2,1)S(1)} collective-permute-done((bf16[192,384]{1,0:T(8,128)(2,1)S(1)}, bf16[192,384]{1,0:T(8,128)(2,1)S(1)}, u32[]{:S(2)}, u32[]{:S(2)}) %collective-permute-start.39) | collective-permute-done | bytes 147488 | tf_op jit(solution)/shard_map/ppermute | solution.py:787
  190.7 0.8 maximum_add_fusion
  (112 shorter events, 14.3 us)
Async XLA Ops:
  0.6 34.1 %copy-start.11 = (bf16[112,10]{1,0:T(8,128)(2,1)S(1)}, bf16[112,10]{1,0:T(8,128)(2,1)}, u32[]{:S(2)}) copy-start(bf16[112,10]{1,0:T(8,128)(2,1)} %constant.56.clone.refs_0_) | copy-start | bytes 6724
  0.6 34.1 %copy-start.13 = (bf16[30,336]{1,0:T(8,128)(2,1)S(1)}, bf16[30,336]{1,0:T(8,128)(2,1)}, u32[]{:S(2)}) copy-start(bf16[30,336]{1,0:T(8,128)(2,1)} %constant.57.clone.refs_1_) | copy-start | bytes 60484
  0.7 34.1 %copy-start.7 = (f32[112,112]{1,0:T(8,128)S(1)}, f32[112,112]{1,0:T(8,128)}, u32[]{:S(2)}) copy-start(f32[112,112]{1,0:T(8,128)} %constant.58.clone.refs_2_) | copy-start | bytes 150532
  0.7 34.1 %copy-start.12 = (bf16[112,10]{1,0:T(8,128)(2,1)S(1)}, bf16[112,10]{1,0:T(8,128)(2,1)}, u32[]{:S(2)}) copy-start(bf16[112,10]{1,0:T(8,128)(2,1)} %constant.59.clone.refs_3_) | copy-start | bytes 6724
  0.7 34.1 %copy-start.14 = (bf16[30,336]{1,0:T(8,128)(2,1)S(1)}, bf16[30,336]{1,0:T(8,128)(2,1)}, u32[]{:S(2)}) copy-start(bf16[30,336]{1,0:T(8,128)(2,1)} %constant.60.clone.refs_4_) | copy-start | bytes 60484
  0.7 34.1 %copy-start.8 = (f32[112,112]{1,0:T(8,128)S(1)}, f32[112,112]{1,0:T(8,128)}, u32[]{:S(2)}) copy-start(f32[112,112]{1,0:T(8,128)} %constant.61.clone.refs_5_) | copy-start | bytes 150532
  0.7 34.1 %copy-start.9 = (bf16[160,10]{1,0:T(8,128)(2,1)S(1)}, bf16[160,10]{1,0:T(8,128)(2,1)}, u32[]{:S(2)}) copy-start(bf16[160,10]{1,0:T(8,128)(2,1)} %constant.62.clone.refs_6_) | copy-start | bytes 9604
  0.7 34.1 %copy-start.10 = (bf16[30,480]{1,0:T(8,128)(2,1)S(1)}, bf16[30,480]{1,0:T(8,128)(2,1)}, u32[]{:S(2)}) copy-start(bf16[30,480]{1,0:T(8,128)(2,1)} %constant.63.clone.refs_7_) | copy-start | bytes 86404
  6.9 19.9 %collective-permute-start.2 = (bf16[2,528,384]{2,1,0:T(8,128)(2,1)S(1)}, bf16[2,528,384]{2,1,0:T(8,128)(2,1)}, u32[]{:S(2)}, u32[]{:S(2)}) collective-permute-start(bf16[2,528,384]{2,1,0:T(8,128)(2,1)S(1)} %get-tuple-element.82), channel_id=1, source_target_pairs={{0,4},{4,0},{1,5},{5,1},{2,6},{6,2},{3,7},{7,3},{8,12},{12,8},{9,1... | collective-permute-start | bytes 2433032 | tf_op jit(solution)/shard_map/ppermute | solution.py:19
  8.4 19.9 %collective-permute-start.5 = (bf16[2,528,384]{2,1,0:T(8,128)(2,1)}, bf16[2,528,384]{2,1,0:T(8,128)(2,1)}, u32[]{:S(2)}, u32[]{:S(2)}) collective-permute-start(bf16[2,528,384]{2,1,0:T(8,128)(2,1)} %get-tuple-element.97.refs_0_), channel_id=1, source_target_pairs={{8,16},{16,8},{9,17},{17,9},{10,18},{18,10},{11,19},{19,11},{12,20... | collective-permute-start | bytes 2433032 | tf_op jit(solution)/shard_map/ppermute | solution.py:24
  10.0 21.8 %collective-permute-start.3 = (bf16[2,528,384]{2,1,0:T(8,128)(2,1)}, bf16[2,528,384]{2,1,0:T(8,128)(2,1)}, u32[]{:S(2)}, u32[]{:S(2)}) collective-permute-start(bf16[2,528,384]{2,1,0:T(8,128)(2,1)} %get-tuple-element.97.refs_0_), channel_id=1, source_target_pairs={{0,8},{16,24},{8,0},{24,16},{1,9},{17,25},{9,1},{25,17},{2,10},{18... | collective-permute-start | bytes 2433032 | tf_op jit(solution)/shard_map/ppermute | solution.py:24
  13.5 24.5 %collective-permute-start.1 = (bf16[2,1000,384]{2,1,0:T(8,128)(2,1)}, bf16[2,1000,384]{2,1,0:T(8,128)(2,1)S(1)}, u32[]{:S(2)}, u32[]{:S(2)}) collective-permute-start(bf16[2,1000,384]{2,1,0:T(8,128)(2,1)} %orbitals.1), channel_id=1, source_target_pairs={{0,1},{1,0},{2,3},{3,2},{4,5},{5,4},{6,7},{7,6},{8,9},{9,8},{10,11... | collective-permute-start | bytes 4608008 | tf_op jit(solution)/shard_map/ppermute | solution.py:19
  13.5 36.2 %collective-permute-start = (bf16[2,1000,384]{2,1,0:T(8,128)(2,1)}, bf16[2,1000,384]{2,1,0:T(8,128)(2,1)S(1)}, u32[]{:S(2)}, u32[]{:S(2)}) collective-permute-start(bf16[2,1000,384]{2,1,0:T(8,128)(2,1)} %orbitals.1), channel_id=1, source_target_pairs={{0,2},{1,3},{2,0},{3,1},{4,6},{5,7},{6,4},{7,5},{8,10},{9,11},{10,... | collective-permute-start | bytes 4608008 | tf_op jit(solution)/shard_map/ppermute | solution.py:19
  26.8 19.3 %collective-permute-start.7 = (bf16[2,528,384]{2,1,0:T(8,128)(2,1)}, bf16[2,528,384]{2,1,0:T(8,128)(2,1)}, u32[]{:S(2)}, u32[]{:S(2)}) collective-permute-start(bf16[2,528,384]{2,1,0:T(8,128)(2,1)} %get-tuple-element.97.refs_0_), channel_id=1, source_target_pairs={{0,4},{4,0},{1,5},{5,1},{2,6},{6,2},{3,7},{7,3},{8,12},{12,8},{9,1... | collective-permute-start | bytes 2433032 | tf_op jit(solution)/shard_map/ppermute | solution.py:19
  28.3 21.4 %collective-permute-start.4 = (bf16[2,528,384]{2,1,0:T(8,128)(2,1)}, bf16[2,528,384]{2,1,0:T(8,128)(2,1)}, u32[]{:S(2)}, u32[]{:S(2)}) collective-permute-start(bf16[2,528,384]{2,1,0:T(8,128)(2,1)} %collective-permute-done.2.beside_in.refs_1_), channel_id=1, source_target_pairs={{0,8},{16,24},{8,0},{24,16},{1,9},{17,25},{9,1},{25,17},{2,10},{18... | collective-permute-start | bytes 2433032 | tf_op jit(solution)/shard_map/ppermute | solution.py:24
  31.7 18.1 %collective-permute-start.6 = (bf16[2,528,384]{2,1,0:T(8,128)(2,1)}, bf16[2,528,384]{2,1,0:T(8,128)(2,1)}, u32[]{:S(2)}, u32[]{:S(2)}) collective-permute-start(bf16[2,528,384]{2,1,0:T(8,128)(2,1)} %collective-permute-done.2.beside_in.refs_1_), channel_id=1, source_target_pairs={{8,16},{16,8},{9,17},{17,9},{10,18},{18,10},{11,19},{19,11},{12,20... | collective-permute-start | bytes 2433032 | tf_op jit(solution)/shard_map/ppermute | solution.py:24
  51.2 30.5 %collective-permute-start.10 = (bf16[2,1000,384]{2,1,0:T(8,128)(2,1)S(1)}, bf16[2,1000,384]{2,1,0:T(8,128)(2,1)}, u32[]{:S(2)}, u32[]{:S(2)}) collective-permute-start(bf16[2,1000,384]{2,1,0:T(8,128)(2,1)S(1)} %collective-permute-done), channel_id=1, source_target_pairs={{0,1},{1,0},{2,3},{3,2},{4,5},{5,4},{6,7},{7,6},{8,9},{9,8},{10,11... | collective-permute-start | bytes 4608008 | tf_op jit(solution)/shard_map/ppermute | solution.py:19
  51.2 29.8 %collective-permute-start.9 = (bf16[992,384]{1,0:T(8,128)(2,1)S(1)}, bf16[992,384]{1,0:T(8,128)(2,1)}, u32[]{:S(2)}, u32[]{:S(2)}) collective-permute-start(bf16[992,384]{1,0:T(8,128)(2,1)S(1)} %slice.30), channel_id=1, source_target_pairs={{0,4},{4,0},{1,5},{5,1},{2,6},{6,2},{3,7},{7,3},{8,12},{12,8},{9,1... | collective-permute-start | bytes 2285576 | tf_op jit(solution)/shard_map/ppermute | solution.py:19
  51.8 29.2 %collective-permute-start.8 = (bf16[1008,384]{1,0:T(8,128)(2,1)S(1)}, bf16[1008,384]{1,0:T(8,128)(2,1)}, u32[]{:S(2)}, u32[]{:S(2)}) collective-permute-start(bf16[1008,384]{1,0:T(8,128)(2,1)S(1)} %get-tuple-element.92), channel_id=1, source_target_pairs={{0,2},{1,3},{2,0},{3,1},{4,6},{5,7},{6,4},{7,5},{8,10},{9,11},{10,... | collective-permute-start | bytes 2322440 | tf_op jit(solution)/shard_map/ppermute | solution.py:19
  52.4 29.3 %collective-permute-start.11 = (bf16[2000,384]{1,0:T(8,128)(2,1)S(1)}, bf16[2000,384]{1,0:T(8,128)(2,1)}, u32[]{:S(2)}, u32[]{:S(2)}) collective-permute-start(bf16[2000,384]{1,0:T(8,128)(2,1)S(1)} %get-tuple-element.107.refs_2_.refs_0_), channel_id=1, source_target_pairs={{0,1},{1,0},{2,3},{3,2},{4,5},{5,4},{6,7},{7,6},{8,9},{9,8},{10,11... | collective-permute-start | bytes 4608008 | tf_op jit(solution)/shard_map/ppermute | solution.py:19
  81.0 3.9 %collective-permute-start.12 = (bf16[1008,384]{1,0:T(8,128)(2,1)}, bf16[1008,384]{1,0:T(8,128)(2,1)}, u32[]{:S(2)}, u32[]{:S(2)}) collective-permute-start(bf16[1008,384]{1,0:T(8,128)(2,1)} %collective-permute-done.8.refs_4_.refs_2_), channel_id=1, source_target_pairs={{0,1},{1,0},{2,3},{3,2},{4,5},{5,4},{6,7},{7,6},{8,9},{9,8},{10,11... | collective-permute-start | bytes 2322440 | tf_op jit(solution)/shard_map/ppermute | solution.py:19
  81.6 3.3 %collective-permute-start.13 = (bf16[992,384]{1,0:T(8,128)(2,1)}, bf16[992,384]{1,0:T(8,128)(2,1)}, u32[]{:S(2)}, u32[]{:S(2)}) collective-permute-start(bf16[992,384]{1,0:T(8,128)(2,1)} %collective-permute-done.9.refs_5_.refs_3_), channel_id=1, source_target_pairs={{0,1},{1,0},{2,3},{3,2},{4,5},{5,4},{6,7},{7,6},{8,9},{9,8},{10,11... | collective-permute-start | bytes 2285576 | tf_op jit(solution)/shard_map/ppermute | solution.py:19
  93.0 13.7 %collective-permute-start.14 = (bf16[192,384]{1,0:T(8,128)(2,1)S(1)}, bf16[192,384]{1,0:T(8,128)(2,1)S(1)}, u32[]{:S(2)}, u32[]{:S(2)}) collective-permute-start(bf16[192,384]{1,0:T(8,128)(2,1)S(1)} %get-tuple-element.161), channel_id=1, source_target_pairs={{0,8},{8,0},{16,24},{24,16},{1,9},{9,1},{17,25},{25,17},{2,10},{10... | collective-permute-start | bytes 442376 | tf_op jit(solution)/shard_map/ppermute | solution.py:19
  96.5 12.9 %collective-permute-start.15 = (bf16[192,384]{1,0:T(8,128)(2,1)S(1)}, bf16[192,384]{1,0:T(8,128)(2,1)S(1)}, u32[]{:S(2)}, u32[]{:S(2)}) collective-permute-start(bf16[192,384]{1,0:T(8,128)(2,1)S(1)} %get-tuple-element.160), channel_id=1, source_target_pairs={{0,16},{8,24},{16,0},{24,8},{1,17},{9,25},{17,1},{25,9},{2,18},{10... | collective-permute-start | bytes 442376 | tf_op jit(solution)/shard_map/ppermute | solution.py:19
  96.5 12.9 %collective-permute-start.16 = (bf16[192,384]{1,0:T(8,128)(2,1)S(1)}, bf16[192,384]{1,0:T(8,128)(2,1)S(1)}, u32[]{:S(2)}, u32[]{:S(2)}) collective-permute-start(bf16[192,384]{1,0:T(8,128)(2,1)S(1)} %get-tuple-element.159), channel_id=1, source_target_pairs={{0,24},{8,16},{16,8},{24,0},{1,25},{9,17},{17,9},{25,1},{2,26},{10... | collective-permute-start | bytes 442376 | tf_op jit(solution)/shard_map/ppermute | solution.py:19
  110.3 17.1 %collective-permute-start.17 = (bf16[192,384]{1,0:T(8,128)(2,1)S(1)}, bf16[192,384]{1,0:T(8,128)(2,1)S(1)}, u32[]{:S(2)}, u32[]{:S(2)}) collective-permute-start(bf16[192,384]{1,0:T(8,128)(2,1)S(1)} %get-tuple-element.125), channel_id=1, source_target_pairs={{0,8},{8,0},{16,24},{24,16},{1,9},{9,1},{17,25},{25,17},{2,10},{10... | collective-permute-start | bytes 442376 | tf_op jit(solution)/shard_map/ppermute | solution.py:19
  114.0 13.4 %collective-permute-start.18 = (bf16[192,384]{1,0:T(8,128)(2,1)S(1)}, bf16[192,384]{1,0:T(8,128)(2,1)S(1)}, u32[]{:S(2)}, u32[]{:S(2)}) collective-permute-start(bf16[192,384]{1,0:T(8,128)(2,1)S(1)} %get-tuple-element.125), channel_id=1, source_target_pairs={{0,16},{8,24},{16,0},{24,8},{1,17},{9,25},{17,1},{25,9},{2,18},{10... | collective-permute-start | bytes 442376 | tf_op jit(solution)/shard_map/ppermute | solution.py:19
  114.0 13.4 %collective-permute-start.19 = (bf16[192,384]{1,0:T(8,128)(2,1)S(1)}, bf16[192,384]{1,0:T(8,128)(2,1)S(1)}, u32[]{:S(2)}, u32[]{:S(2)}) collective-permute-start(bf16[192,384]{1,0:T(8,128)(2,1)S(1)} %get-tuple-element.125), channel_id=1, source_target_pairs={{0,24},{8,16},{16,8},{24,0},{1,25},{9,17},{17,9},{25,1},{2,26},{10... | collective-permute-start | bytes 442376 | tf_op jit(solution)/shard_map/ppermute | solution.py:19
  116.4 10.0 %collective-permute-start.20 = (f32[192,192]{1,0:T(8,128)S(1)}, f32[192,192]{1,0:T(8,128)S(1)}, u32[]{:S(2)}, u32[]{:S(2)}) collective-permute-start(f32[192,192]{1,0:T(8,128)S(1)} %get-tuple-element.124), channel_id=1, source_target_pairs={{0,4},{4,0},{1,5},{5,1},{2,6},{6,2},{3,7},{7,3},{8,12},{12,8},{9,1... | collective-permute-start | bytes 442376 | tf_op jit(solution)/shard_map/ppermute | solution.py:19
  127.4 8.2 %collective-permute-start.22 = (bf16[384,384]{1,0:T(8,128)(2,1)S(1)}, bf16[384,384]{1,0:T(8,128)(2,1)S(1)}, u32[]{:S(2)}, u32[]{:S(2)}) collective-permute-start(bf16[384,384]{1,0:T(8,128)(2,1)S(1)} %constant_dynamic-update-slice_fusion.2.refs_4_), channel_id=1, source_target_pairs={{0,2},{1,3},{2,0},{3,1},{4,6},{5,7},{6,4},{7,5},{8,10},{9,11},{10,... | collective-permute-start | bytes 884744 | tf_op jit(solution)/shard_map/ppermute | solution.py:19
  129.0 18.5 %collective-permute-start.23 = (bf16[3,192,384]{2,1,0:T(8,128)(2,1)S(1)}, bf16[3,192,384]{2,1,0:T(8,128)(2,1)S(1)}, u32[]{:S(2)}, u32[]{:S(2)}) collective-permute-start(bf16[3,192,384]{2,1,0:T(8,128)(2,1)S(1)} %get-tuple-element.130), channel_id=1, source_target_pairs={{0,8},{8,0},{16,24},{24,16},{1,9},{9,1},{17,25},{25,17},{2,10},{10... | collective-permute-start | bytes 1327112 | tf_op jit(solution)/shard_map/ppermute | solution.py:19
  132.1 10.0 %collective-permute-start.21 = (bf16[384,384]{1,0:T(8,128)(2,1)S(1)}, bf16[384,384]{1,0:T(8,128)(2,1)S(1)}, u32[]{:S(2)}, u32[]{:S(2)}) collective-permute-start(bf16[384,384]{1,0:T(8,128)(2,1)S(1)} %constant_dynamic-update-slice_fusion.refs_0_), channel_id=1, source_target_pairs={{0,4},{4,0},{1,5},{5,1},{2,6},{6,2},{3,7},{7,3},{8,12},{12,8},{9,1... | collective-permute-start | bytes 884744 | tf_op jit(solution)/shard_map/ppermute | solution.py:19
  133.7 21.1 %collective-permute-start.28 = (bf16[3,192,384]{2,1,0:T(8,128)(2,1)S(1)}, bf16[3,192,384]{2,1,0:T(8,128)(2,1)S(1)}, u32[]{:S(2)}, u32[]{:S(2)}) collective-permute-start(bf16[3,192,384]{2,1,0:T(8,128)(2,1)S(1)} %get-tuple-element.135), channel_id=1, source_target_pairs={{0,16},{8,24},{16,0},{24,8},{1,17},{9,25},{17,1},{25,9},{2,18},{10... | collective-permute-start | bytes 1327112 | tf_op jit(solution)/shard_map/ppermute | solution.py:19
  133.7 16.9 %collective-permute-start.26 = (bf16[384,384]{1,0:T(8,128)(2,1)S(1)}, bf16[384,384]{1,0:T(8,128)(2,1)S(1)}, u32[]{:S(2)}, u32[]{:S(2)}) collective-permute-start(bf16[384,384]{1,0:T(8,128)(2,1)S(1)} %constant_dynamic-update-slice_fusion.2.refs_4_), channel_id=1, source_target_pairs={{0,4},{4,0},{1,5},{5,1},{2,6},{6,2},{3,7},{7,3},{8,12},{12,8},{9,1... | collective-permute-start | bytes 884744 | tf_op jit(solution)/shard_map/ppermute | solution.py:19
  135.6 15.1 %collective-permute-start.24 = (bf16[384,384]{1,0:T(8,128)(2,1)S(1)}, bf16[384,384]{1,0:T(8,128)(2,1)S(1)}, u32[]{:S(2)}, u32[]{:S(2)}) collective-permute-start(bf16[384,384]{1,0:T(8,128)(2,1)S(1)} %constant_dynamic-update-slice_fusion.refs_0_), channel_id=1, source_target_pairs={{0,2},{1,3},{2,0},{3,1},{4,6},{5,7},{6,4},{7,5},{8,10},{9,11},{10,... | collective-permute-start | bytes 884744 | tf_op jit(solution)/shard_map/ppermute | solution.py:19
  147.5 7.5 %collective-permute-start.25 = (bf16[384,384]{1,0:T(8,128)(2,1)S(1)}, bf16[384,384]{1,0:T(8,128)(2,1)S(1)}, u32[]{:S(2)}, u32[]{:S(2)}) collective-permute-start(bf16[384,384]{1,0:T(8,128)(2,1)S(1)} %collective-permute-done.21.refs_1_), channel_id=1, source_target_pairs={{0,2},{1,3},{2,0},{3,1},{4,6},{5,7},{6,4},{7,5},{8,10},{9,11},{10,... | collective-permute-start | bytes 884744 | tf_op jit(solution)/shard_map/ppermute | solution.py:19
  148.1 8.0 %collective-permute-start.27 = (bf16[384,384]{1,0:T(8,128)(2,1)S(1)}, bf16[384,384]{1,0:T(8,128)(2,1)S(1)}, u32[]{:S(2)}, u32[]{:S(2)}) collective-permute-start(bf16[384,384]{1,0:T(8,128)(2,1)S(1)} %collective-permute-done.22.refs_5_), channel_id=1, source_target_pairs={{0,4},{4,0},{1,5},{5,1},{2,6},{6,2},{3,7},{7,3},{8,12},{12,8},{9,1... | collective-permute-start | bytes 884744 | tf_op jit(solution)/shard_map/ppermute | solution.py:19
  156.0 3.9 %collective-permute-start.29 = (bf16[384,384]{1,0:T(8,128)(2,1)S(1)}, bf16[384,384]{1,0:T(8,128)(2,1)S(1)}, u32[]{:S(2)}, u32[]{:S(2)}) collective-permute-start(bf16[384,384]{1,0:T(8,128)(2,1)S(1)} %constant_dynamic-update-slice_fusion.refs_0_), channel_id=1, source_target_pairs={{0,1},{1,0},{2,3},{3,2},{4,5},{5,4},{6,7},{7,6},{8,9},{9,8},{10,11... | collective-permute-start | bytes 884744 | tf_op jit(solution)/shard_map/ppermute | solution.py:19
  156.0 3.9 %collective-permute-start.30 = (bf16[384,384]{1,0:T(8,128)(2,1)S(1)}, bf16[384,384]{1,0:T(8,128)(2,1)S(1)}, u32[]{:S(2)}, u32[]{:S(2)}) collective-permute-start(bf16[384,384]{1,0:T(8,128)(2,1)S(1)} %collective-permute-done.21.refs_1_), channel_id=1, source_target_pairs={{0,1},{1,0},{2,3},{3,2},{4,5},{5,4},{6,7},{7,6},{8,9},{9,8},{10,11... | collective-permute-start | bytes 884744 | tf_op jit(solution)/shard_map/ppermute | solution.py:19
  156.6 3.9 %collective-permute-start.31 = (bf16[384,384]{1,0:T(8,128)(2,1)S(1)}, bf16[384,384]{1,0:T(8,128)(2,1)S(1)}, u32[]{:S(2)}, u32[]{:S(2)}) collective-permute-start(bf16[384,384]{1,0:T(8,128)(2,1)S(1)} %collective-permute-done.24.refs_2_), channel_id=1, source_target_pairs={{0,1},{1,0},{2,3},{3,2},{4,5},{5,4},{6,7},{7,6},{8,9},{9,8},{10,11... | collective-permute-start | bytes 884744 | tf_op jit(solution)/shard_map/ppermute | solution.py:19
  156.6 4.0 %collective-permute-start.32 = (bf16[384,384]{1,0:T(8,128)(2,1)S(1)}, bf16[384,384]{1,0:T(8,128)(2,1)S(1)}, u32[]{:S(2)}, u32[]{:S(2)}) collective-permute-start(bf16[384,384]{1,0:T(8,128)(2,1)S(1)} %collective-permute-done.25.refs_3_), channel_id=1, source_target_pairs={{0,1},{1,0},{2,3},{3,2},{4,5},{5,4},{6,7},{7,6},{8,9},{9,8},{10,11... | collective-permute-start | bytes 884744 | tf_op jit(solution)/shard_map/ppermute | solution.py:19
  157.1 14.0 %collective-permute-start.37 = (bf16[3,192,384]{2,1,0:T(8,128)(2,1)S(1)}, bf16[3,192,384]{2,1,0:T(8,128)(2,1)S(1)}, u32[]{:S(2)}, u32[]{:S(2)}) collective-permute-start(bf16[3,192,384]{2,1,0:T(8,128)(2,1)S(1)} %get-tuple-element.148), channel_id=1, source_target_pairs={{0,24},{8,16},{16,8},{24,0},{1,25},{9,17},{17,9},{25,1},{2,26},{10... | collective-permute-start | bytes 1327112 | tf_op jit(solution)/shard_map/ppermute | solution.py:19
  159.9 1.6 collective-permute-start.33
  160.0 2.0 %collective-permute-start.34 = (bf16[384,384]{1,0:T(8,128)(2,1)S(1)}, bf16[384,384]{1,0:T(8,128)(2,1)S(1)}, u32[]{:S(2)}, u32[]{:S(2)}) collective-permute-start(bf16[384,384]{1,0:T(8,128)(2,1)S(1)} %collective-permute-done.22.refs_5_), channel_id=1, source_target_pairs={{0,1},{1,0},{2,3},{3,2},{4,5},{5,4},{6,7},{7,6},{8,9},{9,8},{10,11... | collective-permute-start | bytes 884744 | tf_op jit(solution)/shard_map/ppermute | solution.py:19
  160.5 1.9 collective-permute-start.35
  160.5 2.3 %collective-permute-start.36 = (bf16[384,384]{1,0:T(8,128)(2,1)S(1)}, bf16[384,384]{1,0:T(8,128)(2,1)S(1)}, u32[]{:S(2)}, u32[]{:S(2)}) collective-permute-start(bf16[384,384]{1,0:T(8,128)(2,1)S(1)} %collective-permute-done.27.refs_7_), channel_id=1, source_target_pairs={{0,1},{1,0},{2,3},{3,2},{4,5},{5,4},{6,7},{7,6},{8,9},{9,8},{10,11... | collective-permute-start | bytes 884744 | tf_op jit(solution)/shard_map/ppermute | solution.py:19
  172.0 13.2 %collective-permute-start.38 = (f32[192,192]{1,0:T(8,128)S(1)}, f32[192,192]{1,0:T(8,128)S(1)}, u32[]{:S(2)}, u32[]{:S(2)}) collective-permute-start(f32[192,192]{1,0:T(8,128)S(1)} %get-tuple-element.154), channel_id=1, source_target_pairs={{0,4},{4,0},{1,5},{5,1},{2,6},{6,2},{3,7},{7,3},{8,12},{12,8},{9,1... | collective-permute-start | bytes 442376 | tf_op jit(solution)/shard_map/ppermute | solution.py:19
  173.8 17.0 %collective-permute-start.39 = (bf16[192,384]{1,0:T(8,128)(2,1)S(1)}, bf16[192,384]{1,0:T(8,128)(2,1)S(1)}, u32[]{:S(2)}, u32[]{:S(2)}) collective-permute-start(bf16[192,384]{1,0:T(8,128)(2,1)S(1)} %get-tuple-element.155), channel_id=1, source_target_pairs={{0,0},{1,8},{2,16},{3,24},{4,4},{5,12},{6,20},{7,28},{8,1},{9,9},{... | collective-permute-start | bytes 442376 | tf_op jit(solution)/shard_map/ppermute | solution.py:787
  (10 other events, 93.0 us)

commit v7 on v5

--- a/solution.py
+++ b/solution.py
@@ -49,19 +49,22 @@
         own_id = meta[2] + slot
         facts = jnp.where(place == 6, levels[slot], jnp.where(place == 7, jnp.where(keep, 1, 0), 0))
         for c in range(6):
-            target = neighbours[slot, c]
+            target = neighbours[slot, c // 2, c % 2]
             facts = jnp.where(place == c, jnp.where(target >= 0, target - own_id, 16 * slots), facts)
         facts = facts.astype(f32).astype(bf16)
         for packed in (theirs, mine):
             packed[slot, fold : fold + 8, :] = facts
         row = fold + 8
         for start in range(0, pot.shape[1], width):
-            exact = pot[slot : slot + 1, start : start + width]
+            stop = min(start + width, pot.shape[1])
+            exact = pot[slot : slot + 1, start:stop]
             for _ in range(3):
                 part = exact.astype(bf16)
                 exact = exact - part.astype(f32)
                 for packed in (theirs, mine):
-                    packed[slot, row : row + 1, :] = part
+                    packed[slot, row : row + 1, : stop - start] = part
+                    if stop - start < width:
+                        packed[slot, row : row + 1, stop - start :] = jnp.zeros((1, width - stop + start), bf16)
                 row += 1
         for packed in (theirs, mine):
             packed[slot, row:, :] = jnp.zeros((packed.shape[1] - row, width), bf16)
@@ -70,7 +73,7 @@
 def pack(meta, neighbours, levels, orbitals, pot):
     slots, coefficients, width = orbitals.shape
     fold = coefficients // 2
-    padded = -(-(fold + 8 + 3 * (pot.shape[1] // width)) // ROWS) * ROWS
+    padded = -(-(fold + 8 + 3 * -(-coefficients // width)) // ROWS) * ROWS
     vmem, smem = pl.BlockSpec(memory_space=pltpu.VMEM), pl.BlockSpec(memory_space=pltpu.SMEM)
     return pl.pallas_call(
         pack_kernel,
@@ -624,10 +627,9 @@
     square_grid = level_count == orb_count == 4 and box_rows == half
     row0, col0 = (level * PAIR + pair) * box_rows, orb * own_width
 
-    pot = jnp.pad(potential, ((0, 0), (0, -coefficients % own_width)))
     own_base = (level * PAIR + pair) * slots
     pack_meta = jnp.stack([pair, box_counts[0], own_base]).astype(jnp.int32)
-    theirs, mine = pack(pack_meta, neighbours.reshape(slots, 6), levels, orbitals, pot)
+    theirs, mine = pack(pack_meta, neighbours, levels, orbitals, potential)
     active = orbitals
 
     far = {q: swap(active, "orb", q) for q in groups if q and q % 2 == 0}
@@ -712,10 +714,11 @@
         top, low = join(pieces[: level_count // 2]), join(pieces[level_count // 2 :])
         sent = [fock_blocks[0]] + [swap(fock_blocks[step], "lvl", step) for step in range(1, level_count)]
         got = [swap(top, "pair", 1), swap(low, "orb", 2)]
-        got, sent[:3] = lax.optimization_barrier((got, sent[:3]))
+        got, sent[:2] = lax.optimization_barrier((got, sent[:2]))
         tops, lows = [top, got[0]], [low, got[1]]
-        pieces = tops + [swap(piece, "orb", 2) for piece in tops] + lows + [swap(piece, "pair", 1) for piece in lows]
-        pieces, sent = lax.optimization_barrier((pieces, sent))
+        far_tops, far_lows = [swap(piece, "orb", 2) for piece in tops], [swap(piece, "pair", 1) for piece in lows]
+        far_tops, far_lows, sent = lax.optimization_barrier((far_tops, far_lows, sent))
+        pieces = tops + far_tops + lows + far_lows
         pieces += [swap(piece, "orb", 1) for piece in pieces]
         root_meta = jnp.stack([level, pair, orb]).astype(jnp.int32)
         inverse_root = root_of(root_meta, pieces, offset, all_width, level_count)

time: 190 us -> 186 us (0.979); the launches traced: 187 us -> 186 us
  waiting for transfers between devices: 60.1 us -> 52.5 us
  starting transfers between devices: 51.1 us -> 57.3 us
    ppermute x1, starting transfers between devices: 4.44 us -> 11 us  [body(): got = (swap(other, 'pair', 1), lax.ppermute(share, BOX + ('orb',), to))]
    ppermute x35, waiting for transfers between devices: 58.8 us -> 52.5 us  [swap(): return lax.ppermute(value, axis, [(i, i ^ bit) for i in range(count)])]
    unnamed x35 -> x37, local copies, waits for them, and re-layouts: 3.63 us -> 4.32 us
  transfers between devices with their start and end apart: 40 -> 40, of which waited for: 12 -> 7; matrix products, arithmetic and copies ran while one was open for 2% -> 2% of each run, Pallas kernels for 29% -> 30%
where the time goes in v7:
time: 186 us
  Pallas kernels  63.8 us (34%)
  starting transfers between devices  57.3 us (31%)
  waiting for transfers between devices  52.5 us (28%)
  local copies, waits for them, and re-layouts  8.71 us (5%)
  other arithmetic  2.1 us (1%)
    ppermute x35, waiting for transfers between devices, swap(): return lax.ppermute(value, axis, [(i, i ^ bit) for i in range(count)])  52.5 us
    ppermute x35, starting transfers between devices, swap(): return lax.ppermute(value, axis, [(i, i ^ bit) for i in range(count)])  38.1 us
    pallas_call x1, Pallas kernels, kinetic(): pl.pallas_call(functools.partial(kinetic_kernel, edge, slots, levels), ou...  23.5 us
    pallas_call x2, Pallas kernels, box_fock(): pl.pallas_call(functools.partial(fock_kernel, side, counts), out_shape=ou...  16.7 us
    ppermute x1, starting transfers between devices, body(): got = (swap(other, 'pair', 1), lax.ppermute(share, BOX + ('orb',), to))  11 us
    pallas_call x2, Pallas kernels, box_correlation(): pl.pallas_call(functools.partial(correlation_kernel, share, counts), out_...  9.16 us
    ppermute x4, starting transfers between devices, trade(): return lax.ppermute(value, axis, pairs + [(b, a) for a, b in pairs])  8.28 us
    pallas_call x1, Pallas kernels, root_of(): pl.pallas_call(functools.partial(root_kernel, levels), out_shape=jax.Shap...  6.38 us
  transfers between devices with their start and end apart: 40, of which 7 were waited for; matrix products, arithmetic and copies ran while one was open for 2% of the time, Pallas kernels for 30%

profile of v7, /device:TPU:2, one launch (start us, length us, event | category | flops | bytes accessed | tf_op | source)
XLA Modules:
  0.0 186.3 jit_solution(7936815878984400001)
XLA Ops:
  1.5 0.8 copy.20.neighbours
  2.3 0.7 copy-done.11
  3.7 3.2 %pack.1 = (bf16[2,528,384]{2,1,0:T(8,128)(2,1)S(1)}, bf16[2,528,384]{2,1,0:T(8,128)(2,1)}) custom-call(s32[3]{0:T(128)S(1)} %pad_add_fusion.1.meta, s32[2,3,2]{2,1,0:T(4,128)S(1)} %copy.20.neighbours, s32[2]{0:T(128)S(1)} %copy-done.12, bf16[2,1000,384]{2,1,0:T(8,128)(2,1)} %orbitals.1, f32[2,1000]{1,0:T(2,128)S(1)} %copy-done.11), custom_call_target="tpu_custom_call" | custom-call | tf_op jit(solution)/shard_map/pack/pallas_call | solution.py:78
  6.9 1.5 collective-permute-start.1
  8.4 1.5 collective-permute-start.4
  10.5 3.6 %collective-permute-start.2 = (bf16[2,528,384]{2,1,0:T(8,128)(2,1)}, bf16[2,528,384]{2,1,0:T(8,128)(2,1)}, u32[]{:S(2)}, u32[]{:S(2)}) collective-permute-start(bf16[2,528,384]{2,1,0:T(8,128)(2,1)} %get-tuple-element.89.refs_0_), channel_id=1, source_target_pairs={{0,8},{16,24},{8,0},{24,16},{1,9},{17,25},{9,1},{25,17},{2,10},{18... | collective-permute-start | bytes 2433032 | tf_op jit(solution)/shard_map/ppermute | solution.py:24
  14.1 12.7 %collective-permute-done.1.beside_in.refs_1_ = bf16[2,528,384]{2,1,0:T(8,128)(2,1)} collective-permute-done((bf16[2,528,384]{2,1,0:T(8,128)(2,1)S(1)}, bf16[2,528,384]{2,1,0:T(8,128)(2,1)}, u32[]{:S(2)}, u32[]{:S(2)}) %collective-permute-start.1) | collective-permute-done | bytes 811040 | tf_op jit(solution)/shard_map/ppermute | solution.py:19
  26.8 1.5 collective-permute-start.6
  28.3 1.6 collective-permute-start.3
  29.9 1.6 collective-permute-start.5
  32.3 1.0 matrices.1
  33.5 0.7 slice.22
  34.9 0.7 slice.28
  35.6 10.4 %collective-permute-done.6.rest_in = bf16[2,528,384]{2,1,0:T(8,128)(2,1)S(1)} collective-permute-done((bf16[2,528,384]{2,1,0:T(8,128)(2,1)}, bf16[2,528,384]{2,1,0:T(8,128)(2,1)S(1)}, u32[]{:S(2)}, u32[]{:S(2)}) %collective-permute-start.6) | collective-permute-done | bytes 811040 | tf_op jit(solution)/shard_map/ppermute | solution.py:19
  46.0 0.9 copy-done
  46.9 1.1 copy-done.1
  48.0 2.2 %unfold.1 = (bf16[2000,384]{1,0:T(8,128)(2,1)S(1)}, bf16[1008,384]{1,0:T(8,128)(2,1)S(1)}) custom-call(s32[3]{0:T(128)S(1)} %pad_add_fusion.1.meta, bf16[2,528,384]{2,1,0:T(8,128)(2,1)} %collective-permute-done.1.beside_in.refs_1_, bf16[2,528,384]{2,1,0:T(8,128)(2,1)S(1)} %copy-done.1), custom_call_target="tpu_custom_call" | custom-call | tf_op jit(solution)/shard_map/unfold/pallas_call | solution.py:113
  51.7 1.6 collective-permute-start.8
  54.4 23.5 %kinetic.1 = bf16[4,1000,576]{2,1,0:T(8,128)(2,1)} custom-call(s32[2]{0:T(128)S(1)} %pad_add_fusion.2.place_meta, s32[6,2,8]{2,1,0:T(2,128)S(1)} %pad_add_fusion.facts, bf16[2,528,384]{2,1,0:T(8,128)(2,1)} %get-tuple-element.89.refs_0_, bf16[2,528,384]{2,1,0:T(8,128)(2,1)} %collective-permute-done.1.beside_in.refs_1_, ...), custom_call_target="tpu_custom_call" | custom-call | flops 20000000000 | bytes 40000000 | tf_op jit(solution)/shard_map/kinetic/pallas_call | solution.py:554
  78.5 4.8 %correlation.2.refs_6_ = f32[4,192,384]{2,1,0:T(8,128)S(1)} custom-call(s32[3]{0:T(128)S(1)} %pad_add_fusion.3.meta, bf16[2000,384]{1,0:T(8,128)(2,1)} %bitcast.5.refs_0_, bf16[2000,384]{1,0:T(8,128)(2,1)} %bitcast.6.refs_1_, bf16[2000,384]{1,0:T(8,128)(2,1)S(1)} %bitcast.36, bf16[2000,384]{1,0:T(8,128)(2,1)} %bitcast.7.refs_3_), custom_call_target="tpu_custom_call" | custom-call | flops 1179648000 | bytes 6144000 | tf_op jit(solution)/shard_map/correlation/pallas_call | solution.py:182
  83.3 4.4 %correlation.3 = bf16[4,192,384]{2,1,0:T(8,128)(2,1)S(1)} custom-call(s32[3]{0:T(128)S(1)} %pad_add_fusion.3.meta, bf16[2000,384]{1,0:T(8,128)(2,1)S(1)} %get-tuple-element.99.refs_0_, bf16[2000,384]{1,0:T(8,128)(2,1)} %collective-permute-done.9.refs_1_, bf16[1008,384]{1,0:T(8,128)(2,1)} %collective-permute-done.7.refs_2_, ...), custom_call_target="tpu_custom_call" | custom-call | flops 1179648000 | bytes 6144000 | tf_op jit(solution)/shard_map/correlation/pallas_call | solution.py:182
  87.8 4.6 %collective-permute-start.14 = (bf16[192,384]{1,0:T(8,128)(2,1)S(1)}, bf16[192,384]{1,0:T(8,128)(2,1)S(1)}, u32[]{:S(2)}, u32[]{:S(2)}) collective-permute-start(bf16[192,384]{1,0:T(8,128)(2,1)S(1)} %get-tuple-element.147), channel_id=1, source_target_pairs={{0,8},{8,0},{16,24},{24,16},{1,9},{9,1},{17,25},{25,17},{2,10},{10... | collective-permute-start | bytes 442376 | tf_op jit(solution)/shard_map/ppermute | solution.py:19
  92.4 4.0 %collective-permute-start.15 = (bf16[192,384]{1,0:T(8,128)(2,1)S(1)}, bf16[192,384]{1,0:T(8,128)(2,1)S(1)}, u32[]{:S(2)}, u32[]{:S(2)}) collective-permute-start(bf16[192,384]{1,0:T(8,128)(2,1)S(1)} %get-tuple-element.146), channel_id=1, source_target_pairs={{0,16},{8,24},{16,0},{24,8},{1,17},{9,25},{17,1},{25,9},{2,18},{10... | collective-permute-start | bytes 442376 | tf_op jit(solution)/shard_map/ppermute | solution.py:19
  96.4 1.4 collective-permute-start.16
  97.8 8.2 %fock.2.refs_6_ = f32[4,576,384]{2,1,0:T(8,128)S(1)} custom-call(bf16[2,2000,576]{2,1,0:T(8,128)(2,1)} %bitcast.38, bf16[2000,384]{1,0:T(8,128)(2,1)} %bitcast.5.refs_0_, bf16[2000,384]{1,0:T(8,128)(2,1)} %bitcast.6.refs_1_, bf16[2000,384]{1,0:T(8,128)(2,1)S(1)} %bitcast.37, bf16[2000,384]{1,0:T(8,128)(2,1)} %bitcast.7.refs_3_), custom_call_target="tpu_custom_call" | custom-call | flops 3538944000 | bytes 6144000 | tf_op jit(solution)/shard_map/fock/pallas_call | solution.py:244
  105.9 2.0 %collective-permute-done.16.refs_3_ = bf16[192,384]{1,0:T(8,128)(2,1)S(1)} collective-permute-done((bf16[192,384]{1,0:T(8,128)(2,1)S(1)}, bf16[192,384]{1,0:T(8,128)(2,1)S(1)}, u32[]{:S(2)}, u32[]{:S(2)}) %collective-permute-start.16) | collective-permute-done | bytes 147488 | tf_op jit(solution)/shard_map/ppermute | solution.py:19
  108.0 0.8 level_sum.2
  108.8 2.7 %collective-permute-start.17 = (bf16[192,384]{1,0:T(8,128)(2,1)S(1)}, bf16[192,384]{1,0:T(8,128)(2,1)S(1)}, u32[]{:S(2)}, u32[]{:S(2)}) collective-permute-start(bf16[192,384]{1,0:T(8,128)(2,1)S(1)} %get-tuple-element.116), channel_id=1, source_target_pairs={{0,8},{8,0},{16,24},{24,16},{1,9},{9,1},{17,25},{25,17},{2,10},{10... | collective-permute-start | bytes 442376 | tf_op jit(solution)/shard_map/ppermute | solution.py:19
  111.5 2.0 %collective-permute-start.18 = (bf16[192,384]{1,0:T(8,128)(2,1)S(1)}, bf16[192,384]{1,0:T(8,128)(2,1)S(1)}, u32[]{:S(2)}, u32[]{:S(2)}) collective-permute-start(bf16[192,384]{1,0:T(8,128)(2,1)S(1)} %get-tuple-element.116), channel_id=1, source_target_pairs={{0,16},{8,24},{16,0},{24,8},{1,17},{9,25},{17,1},{25,9},{2,18},{10... | collective-permute-start | bytes 442376 | tf_op jit(solution)/shard_map/ppermute | solution.py:19
  113.5 1.4 collective-permute-start.19
  114.9 1.2 collective-permute-start.20
  116.1 8.5 %fock.3 = (bf16[3,192,384]{2,1,0:T(8,128)(2,1)S(1)}, bf16[3,192,384]{2,1,0:T(8,128)(2,1)S(1)}, bf16[3,192,384]{2,1,0:T(8,128)(2,1)S(1)}, bf16[3,192,384]{2,1,0:T(8,128)(2,1)S(1)}) custom-call(bf16[2,2000,576]{2,1,0:T(8,128)(2,1)} %bitcast.39, bf16[2000,384]{1,0:T(8,128)(2,1)S(1)} %get-tuple-element.99.refs_0_, ...), custom_call_target="tpu_custom_call" | custom-call | flops 3538944000 | bytes 6144000 | tf_op jit(solution)/shard_map/fock/pallas_call | solution.py:244
  124.7 0.9 convert_add_fusion
  125.6 1.6 collective-permute-start.23
  127.2 1.0 collective-permute-start.22
  128.2 2.7 %collective-permute-start.24 = (bf16[3,192,384]{2,1,0:T(8,128)(2,1)S(1)}, bf16[3,192,384]{2,1,0:T(8,128)(2,1)S(1)}, u32[]{:S(2)}, u32[]{:S(2)}) collective-permute-start(bf16[3,192,384]{2,1,0:T(8,128)(2,1)S(1)} %get-tuple-element.121), channel_id=1, source_target_pairs={{0,8},{8,0},{16,24},{24,16},{1,9},{9,1},{17,25},{25,17},{2,10},{10... | collective-permute-start | bytes 1327112 | tf_op jit(solution)/shard_map/ppermute | solution.py:19
  131.0 1.9 %collective-permute-start.28 = (bf16[3,192,384]{2,1,0:T(8,128)(2,1)S(1)}, bf16[3,192,384]{2,1,0:T(8,128)(2,1)S(1)}, u32[]{:S(2)}, u32[]{:S(2)}) collective-permute-start(bf16[3,192,384]{2,1,0:T(8,128)(2,1)S(1)} %get-tuple-element.126), channel_id=1, source_target_pairs={{0,16},{8,24},{16,0},{24,8},{1,17},{9,25},{17,1},{25,9},{2,18},{10... | collective-permute-start | bytes 1327112 | tf_op jit(solution)/shard_map/ppermute | solution.py:19
  132.8 1.5 collective-permute-start.29
  134.3 0.8 collective-permute-start.26
  135.1 1.0 collective-permute-start.21
  136.1 12.7 %collective-permute-done.24.refs_1_ = bf16[3,192,384]{2,1,0:T(8,128)(2,1)S(1)} collective-permute-done((bf16[3,192,384]{2,1,0:T(8,128)(2,1)S(1)}, bf16[3,192,384]{2,1,0:T(8,128)(2,1)S(1)}, u32[]{:S(2)}, u32[]{:S(2)}) %collective-permute-start.24) | collective-permute-done | bytes 442400 | tf_op jit(solution)/shard_map/ppermute | solution.py:19
  149.3 0.8 collective-permute-start.27
  150.2 13.8 %collective-permute-done.28.refs_2_ = bf16[3,192,384]{2,1,0:T(8,128)(2,1)S(1)} collective-permute-done((bf16[3,192,384]{2,1,0:T(8,128)(2,1)S(1)}, bf16[3,192,384]{2,1,0:T(8,128)(2,1)S(1)}, u32[]{:S(2)}, u32[]{:S(2)}) %collective-permute-start.28) | collective-permute-done | bytes 442400 | tf_op jit(solution)/shard_map/ppermute | solution.py:19
  166.1 0.9 level_sum.3
  167.1 0.9 collective-permute-start.38
  168.0 11.0 %collective-permute-start.39 = (bf16[192,384]{1,0:T(8,128)(2,1)S(1)}, bf16[192,384]{1,0:T(8,128)(2,1)S(1)}, u32[]{:S(2)}, u32[]{:S(2)}) collective-permute-start(bf16[192,384]{1,0:T(8,128)(2,1)S(1)} %get-tuple-element.139), channel_id=1, source_target_pairs={{0,0},{1,8},{2,16},{3,24},{4,4},{5,12},{6,20},{7,28},{8,1},{9,9},{... | collective-permute-start | bytes 442376 | tf_op jit(solution)/shard_map/ppermute | solution.py:732
  179.0 6.4 %root.1 = f32[192,384]{1,0:T(8,128)} custom-call(s32[3]{0:T(128)S(1)} %pad_add_fusion.4.meta, bf16[384,384]{1,0:T(8,128)(2,1)S(1)} %constant_dynamic-update-slice_fusion.refs_0_, bf16[384,384]{1,0:T(8,128)(2,1)S(1)} %collective-permute-done.22.refs_1_, bf16[384,384]{1,0:T(8,128)(2,1)S(1)} %collective-permute-done.21.refs_2_, ...), custom_call_target="tpu_custom_call" | custom-call | flops 14495514624 | bytes 9437184 | tf_op jit(solution)/shard_map/root/pallas_call | solution.py:319
  185.5 0.8 maximum_add_fusion
  (104 shorter events, 9.1 us)
Async XLA Ops:
  0.6 31.6 %copy-start.7 = (bf16[112,10]{1,0:T(8,128)(2,1)S(1)}, bf16[112,10]{1,0:T(8,128)(2,1)}, u32[]{:S(2)}) copy-start(bf16[112,10]{1,0:T(8,128)(2,1)} %constant.58.clone.refs_0_) | copy-start | bytes 6724
  0.6 31.6 %copy-start.9 = (bf16[30,336]{1,0:T(8,128)(2,1)S(1)}, bf16[30,336]{1,0:T(8,128)(2,1)}, u32[]{:S(2)}) copy-start(bf16[30,336]{1,0:T(8,128)(2,1)} %constant.59.clone.refs_1_) | copy-start | bytes 60484
  0.7 31.6 %copy-start.3 = (f32[112,112]{1,0:T(8,128)S(1)}, f32[112,112]{1,0:T(8,128)}, u32[]{:S(2)}) copy-start(f32[112,112]{1,0:T(8,128)} %constant.60.clone.refs_2_) | copy-start | bytes 150532
  0.7 31.6 %copy-start.8 = (bf16[112,10]{1,0:T(8,128)(2,1)S(1)}, bf16[112,10]{1,0:T(8,128)(2,1)}, u32[]{:S(2)}) copy-start(bf16[112,10]{1,0:T(8,128)(2,1)} %constant.61.clone.refs_3_) | copy-start | bytes 6724
  0.7 31.6 %copy-start.10 = (bf16[30,336]{1,0:T(8,128)(2,1)S(1)}, bf16[30,336]{1,0:T(8,128)(2,1)}, u32[]{:S(2)}) copy-start(bf16[30,336]{1,0:T(8,128)(2,1)} %constant.62.clone.refs_4_) | copy-start | bytes 60484
  0.7 31.6 %copy-start.4 = (f32[112,112]{1,0:T(8,128)S(1)}, f32[112,112]{1,0:T(8,128)}, u32[]{:S(2)}) copy-start(f32[112,112]{1,0:T(8,128)} %constant.63.clone.refs_5_) | copy-start | bytes 150532
  0.7 31.6 %copy-start.5 = (bf16[160,10]{1,0:T(8,128)(2,1)S(1)}, bf16[160,10]{1,0:T(8,128)(2,1)}, u32[]{:S(2)}) copy-start(bf16[160,10]{1,0:T(8,128)(2,1)} %constant.64.clone.refs_6_) | copy-start | bytes 9604
  0.7 31.6 %copy-start.6 = (bf16[30,480]{1,0:T(8,128)(2,1)S(1)}, bf16[30,480]{1,0:T(8,128)(2,1)}, u32[]{:S(2)}) copy-start(bf16[30,480]{1,0:T(8,128)(2,1)} %constant.65.clone.refs_7_) | copy-start | bytes 86404
  6.9 19.9 %collective-permute-start.1 = (bf16[2,528,384]{2,1,0:T(8,128)(2,1)S(1)}, bf16[2,528,384]{2,1,0:T(8,128)(2,1)}, u32[]{:S(2)}, u32[]{:S(2)}) collective-permute-start(bf16[2,528,384]{2,1,0:T(8,128)(2,1)S(1)} %get-tuple-element.74), channel_id=1, source_target_pairs={{0,4},{4,0},{1,5},{5,1},{2,6},{6,2},{3,7},{7,3},{8,12},{12,8},{9,1... | collective-permute-start | bytes 2433032 | tf_op jit(solution)/shard_map/ppermute | solution.py:19
  8.4 21.5 %collective-permute-start.4 = (bf16[2,528,384]{2,1,0:T(8,128)(2,1)}, bf16[2,528,384]{2,1,0:T(8,128)(2,1)}, u32[]{:S(2)}, u32[]{:S(2)}) collective-permute-start(bf16[2,528,384]{2,1,0:T(8,128)(2,1)} %get-tuple-element.89.refs_0_), channel_id=1, source_target_pairs={{8,16},{16,8},{9,17},{17,9},{10,18},{18,10},{11,19},{19,11},{12,20... | collective-permute-start | bytes 2433032 | tf_op jit(solution)/shard_map/ppermute | solution.py:24
  9.9 40.3 %collective-permute-start = (bf16[2,1000,384]{2,1,0:T(8,128)(2,1)}, bf16[2,1000,384]{2,1,0:T(8,128)(2,1)S(1)}, u32[]{:S(2)}, u32[]{:S(2)}) collective-permute-start(bf16[2,1000,384]{2,1,0:T(8,128)(2,1)} %orbitals.1), channel_id=1, source_target_pairs={{0,2},{1,3},{2,0},{3,1},{4,6},{5,7},{6,4},{7,5},{8,10},{9,11},{10,... | collective-permute-start | bytes 4608008 | tf_op jit(solution)/shard_map/ppermute | solution.py:19
  10.5 24.4 %collective-permute-start.2 = (bf16[2,528,384]{2,1,0:T(8,128)(2,1)}, bf16[2,528,384]{2,1,0:T(8,128)(2,1)}, u32[]{:S(2)}, u32[]{:S(2)}) collective-permute-start(bf16[2,528,384]{2,1,0:T(8,128)(2,1)} %get-tuple-element.89.refs_0_), channel_id=1, source_target_pairs={{0,8},{16,24},{8,0},{24,16},{1,9},{17,25},{9,1},{25,17},{2,10},{18... | collective-permute-start | bytes 2433032 | tf_op jit(solution)/shard_map/ppermute | solution.py:24
  26.8 19.1 %collective-permute-start.6 = (bf16[2,528,384]{2,1,0:T(8,128)(2,1)}, bf16[2,528,384]{2,1,0:T(8,128)(2,1)S(1)}, u32[]{:S(2)}, u32[]{:S(2)}) collective-permute-start(bf16[2,528,384]{2,1,0:T(8,128)(2,1)} %get-tuple-element.89.refs_0_), channel_id=1, source_target_pairs={{0,4},{4,0},{1,5},{5,1},{2,6},{6,2},{3,7},{7,3},{8,12},{12,8},{9,1... | collective-permute-start | bytes 2433032 | tf_op jit(solution)/shard_map/ppermute | solution.py:19
  28.3 21.9 %collective-permute-start.3 = (bf16[2,528,384]{2,1,0:T(8,128)(2,1)}, bf16[2,528,384]{2,1,0:T(8,128)(2,1)}, u32[]{:S(2)}, u32[]{:S(2)}) collective-permute-start(bf16[2,528,384]{2,1,0:T(8,128)(2,1)} %collective-permute-done.1.beside_in.refs_1_), channel_id=1, source_target_pairs={{0,8},{16,24},{8,0},{24,16},{1,9},{17,25},{9,1},{25,17},{2,10},{18... | collective-permute-start | bytes 2433032 | tf_op jit(solution)/shard_map/ppermute | solution.py:24
  29.9 20.3 %collective-permute-start.5 = (bf16[2,528,384]{2,1,0:T(8,128)(2,1)}, bf16[2,528,384]{2,1,0:T(8,128)(2,1)}, u32[]{:S(2)}, u32[]{:S(2)}) collective-permute-start(bf16[2,528,384]{2,1,0:T(8,128)(2,1)} %collective-permute-done.1.beside_in.refs_1_), channel_id=1, source_target_pairs={{8,16},{16,8},{9,17},{17,9},{10,18},{18,10},{11,19},{19,11},{12,20... | collective-permute-start | bytes 2433032 | tf_op jit(solution)/shard_map/ppermute | solution.py:24
  51.6 26.9 %collective-permute-start.13 = (bf16[2,1000,384]{2,1,0:T(8,128)(2,1)S(1)}, bf16[2,1000,384]{2,1,0:T(8,128)(2,1)}, u32[]{:S(2)}, u32[]{:S(2)}) collective-permute-start(bf16[2,1000,384]{2,1,0:T(8,128)(2,1)S(1)} %collective-permute-done), channel_id=1, source_target_pairs={{0,1},{1,0},{2,3},{3,2},{4,5},{5,4},{6,7},{7,6},{8,9},{9,8},{10,11... | collective-permute-start | bytes 4608008 | tf_op jit(solution)/shard_map/ppermute | solution.py:19
  51.7 26.2 %collective-permute-start.8 = (bf16[992,384]{1,0:T(8,128)(2,1)S(1)}, bf16[992,384]{1,0:T(8,128)(2,1)}, u32[]{:S(2)}, u32[]{:S(2)}) collective-permute-start(bf16[992,384]{1,0:T(8,128)(2,1)S(1)} %slice.30), channel_id=1, source_target_pairs={{0,4},{4,0},{1,5},{5,1},{2,6},{6,2},{3,7},{7,3},{8,12},{12,8},{9,1... | collective-permute-start | bytes 2285576 | tf_op jit(solution)/shard_map/ppermute | solution.py:19
  53.3 24.6 %collective-permute-start.7 = (bf16[1008,384]{1,0:T(8,128)(2,1)S(1)}, bf16[1008,384]{1,0:T(8,128)(2,1)}, u32[]{:S(2)}, u32[]{:S(2)}) collective-permute-start(bf16[1008,384]{1,0:T(8,128)(2,1)S(1)} %get-tuple-element.84), channel_id=1, source_target_pairs={{0,2},{1,3},{2,0},{3,1},{4,6},{5,7},{6,4},{7,5},{8,10},{9,11},{10,... | collective-permute-start | bytes 2322440 | tf_op jit(solution)/shard_map/ppermute | solution.py:19
  53.8 24.7 %collective-permute-start.12 = (bf16[2,1000,384]{2,1,0:T(8,128)(2,1)}, bf16[2,1000,384]{2,1,0:T(8,128)(2,1)}, u32[]{:S(2)}, u32[]{:S(2)}) collective-permute-start(bf16[2,1000,384]{2,1,0:T(8,128)(2,1)} %orbitals.1), channel_id=1, source_target_pairs={{0,1},{1,0},{2,3},{3,2},{4,5},{5,4},{6,7},{7,6},{8,9},{9,8},{10,11... | collective-permute-start | bytes 4608008 | tf_op jit(solution)/shard_map/ppermute | solution.py:19
  53.8 29.5 %collective-permute-start.9 = (bf16[2000,384]{1,0:T(8,128)(2,1)S(1)}, bf16[2000,384]{1,0:T(8,128)(2,1)}, u32[]{:S(2)}, u32[]{:S(2)}) collective-permute-start(bf16[2000,384]{1,0:T(8,128)(2,1)S(1)} %get-tuple-element.99.refs_0_), channel_id=1, source_target_pairs={{0,1},{1,0},{2,3},{3,2},{4,5},{5,4},{6,7},{7,6},{8,9},{9,8},{10,11... | collective-permute-start | bytes 4608008 | tf_op jit(solution)/shard_map/ppermute | solution.py:19
  77.9 5.4 %collective-permute-start.10 = (bf16[1008,384]{1,0:T(8,128)(2,1)}, bf16[1008,384]{1,0:T(8,128)(2,1)}, u32[]{:S(2)}, u32[]{:S(2)}) collective-permute-start(bf16[1008,384]{1,0:T(8,128)(2,1)} %collective-permute-done.7.refs_2_), channel_id=1, source_target_pairs={{0,1},{1,0},{2,3},{3,2},{4,5},{5,4},{6,7},{7,6},{8,9},{9,8},{10,11... | collective-permute-start | bytes 2322440 | tf_op jit(solution)/shard_map/ppermute | solution.py:19
  78.0 5.3 %collective-permute-start.11 = (bf16[992,384]{1,0:T(8,128)(2,1)}, bf16[992,384]{1,0:T(8,128)(2,1)}, u32[]{:S(2)}, u32[]{:S(2)}) collective-permute-start(bf16[992,384]{1,0:T(8,128)(2,1)} %collective-permute-done.8.refs_3_), channel_id=1, source_target_pairs={{0,1},{1,0},{2,3},{3,2},{4,5},{5,4},{6,7},{7,6},{8,9},{9,8},{10,11... | collective-permute-start | bytes 2285576 | tf_op jit(solution)/shard_map/ppermute | solution.py:19
  87.8 18.1 %collective-permute-start.14 = (bf16[192,384]{1,0:T(8,128)(2,1)S(1)}, bf16[192,384]{1,0:T(8,128)(2,1)S(1)}, u32[]{:S(2)}, u32[]{:S(2)}) collective-permute-start(bf16[192,384]{1,0:T(8,128)(2,1)S(1)} %get-tuple-element.147), channel_id=1, source_target_pairs={{0,8},{8,0},{16,24},{24,16},{1,9},{9,1},{17,25},{25,17},{2,10},{10... | collective-permute-start | bytes 442376 | tf_op jit(solution)/shard_map/ppermute | solution.py:19
  92.4 13.6 %collective-permute-start.15 = (bf16[192,384]{1,0:T(8,128)(2,1)S(1)}, bf16[192,384]{1,0:T(8,128)(2,1)S(1)}, u32[]{:S(2)}, u32[]{:S(2)}) collective-permute-start(bf16[192,384]{1,0:T(8,128)(2,1)S(1)} %get-tuple-element.146), channel_id=1, source_target_pairs={{0,16},{8,24},{16,0},{24,8},{1,17},{9,25},{17,1},{25,9},{2,18},{10... | collective-permute-start | bytes 442376 | tf_op jit(solution)/shard_map/ppermute | solution.py:19
  96.4 11.6 %collective-permute-start.16 = (bf16[192,384]{1,0:T(8,128)(2,1)S(1)}, bf16[192,384]{1,0:T(8,128)(2,1)S(1)}, u32[]{:S(2)}, u32[]{:S(2)}) collective-permute-start(bf16[192,384]{1,0:T(8,128)(2,1)S(1)} %get-tuple-element.145), channel_id=1, source_target_pairs={{0,24},{8,16},{16,8},{24,0},{1,25},{9,17},{17,9},{25,1},{2,26},{10... | collective-permute-start | bytes 442376 | tf_op jit(solution)/shard_map/ppermute | solution.py:19
  108.8 16.8 %collective-permute-start.17 = (bf16[192,384]{1,0:T(8,128)(2,1)S(1)}, bf16[192,384]{1,0:T(8,128)(2,1)S(1)}, u32[]{:S(2)}, u32[]{:S(2)}) collective-permute-start(bf16[192,384]{1,0:T(8,128)(2,1)S(1)} %get-tuple-element.116), channel_id=1, source_target_pairs={{0,8},{8,0},{16,24},{24,16},{1,9},{9,1},{17,25},{25,17},{2,10},{10... | collective-permute-start | bytes 442376 | tf_op jit(solution)/shard_map/ppermute | solution.py:19
  111.5 14.0 %collective-permute-start.18 = (bf16[192,384]{1,0:T(8,128)(2,1)S(1)}, bf16[192,384]{1,0:T(8,128)(2,1)S(1)}, u32[]{:S(2)}, u32[]{:S(2)}) collective-permute-start(bf16[192,384]{1,0:T(8,128)(2,1)S(1)} %get-tuple-element.116), channel_id=1, source_target_pairs={{0,16},{8,24},{16,0},{24,8},{1,17},{9,25},{17,1},{25,9},{2,18},{10... | collective-permute-start | bytes 442376 | tf_op jit(solution)/shard_map/ppermute | solution.py:19
  113.5 12.0 %collective-permute-start.19 = (bf16[192,384]{1,0:T(8,128)(2,1)S(1)}, bf16[192,384]{1,0:T(8,128)(2,1)S(1)}, u32[]{:S(2)}, u32[]{:S(2)}) collective-permute-start(bf16[192,384]{1,0:T(8,128)(2,1)S(1)} %get-tuple-element.116), channel_id=1, source_target_pairs={{0,24},{8,16},{16,8},{24,0},{1,25},{9,17},{17,9},{25,1},{2,26},{10... | collective-permute-start | bytes 442376 | tf_op jit(solution)/shard_map/ppermute | solution.py:19
  114.9 9.7 %collective-permute-start.20 = (f32[192,192]{1,0:T(8,128)S(1)}, f32[192,192]{1,0:T(8,128)S(1)}, u32[]{:S(2)}, u32[]{:S(2)}) collective-permute-start(f32[192,192]{1,0:T(8,128)S(1)} %get-tuple-element.115), channel_id=1, source_target_pairs={{0,4},{4,0},{1,5},{5,1},{2,6},{6,2},{3,7},{7,3},{8,12},{12,8},{9,1... | collective-permute-start | bytes 442376 | tf_op jit(solution)/shard_map/ppermute | solution.py:19
  125.6 8.7 %collective-permute-start.23 = (bf16[384,384]{1,0:T(8,128)(2,1)S(1)}, bf16[384,384]{1,0:T(8,128)(2,1)S(1)}, u32[]{:S(2)}, u32[]{:S(2)}) collective-permute-start(bf16[384,384]{1,0:T(8,128)(2,1)S(1)} %constant_dynamic-update-slice_fusion.2.refs_4_), channel_id=1, source_target_pairs={{0,2},{1,3},{2,0},{3,1},{4,6},{5,7},{6,4},{7,5},{8,10},{9,11},{10,... | collective-permute-start | bytes 884744 | tf_op jit(solution)/shard_map/ppermute | solution.py:19
  127.2 7.9 %collective-permute-start.22 = (bf16[384,384]{1,0:T(8,128)(2,1)S(1)}, bf16[384,384]{1,0:T(8,128)(2,1)S(1)}, u32[]{:S(2)}, u32[]{:S(2)}) collective-permute-start(bf16[384,384]{1,0:T(8,128)(2,1)S(1)} %constant_dynamic-update-slice_fusion.refs_0_), channel_id=1, source_target_pairs={{0,4},{4,0},{1,5},{5,1},{2,6},{6,2},{3,7},{7,3},{8,12},{12,8},{9,1... | collective-permute-start | bytes 884744 | tf_op jit(solution)/shard_map/ppermute | solution.py:19
  128.2 20.6 %collective-permute-start.24 = (bf16[3,192,384]{2,1,0:T(8,128)(2,1)S(1)}, bf16[3,192,384]{2,1,0:T(8,128)(2,1)S(1)}, u32[]{:S(2)}, u32[]{:S(2)}) collective-permute-start(bf16[3,192,384]{2,1,0:T(8,128)(2,1)S(1)} %get-tuple-element.121), channel_id=1, source_target_pairs={{0,8},{8,0},{16,24},{24,16},{1,9},{9,1},{17,25},{25,17},{2,10},{10... | collective-permute-start | bytes 1327112 | tf_op jit(solution)/shard_map/ppermute | solution.py:19
  131.0 33.0 %collective-permute-start.28 = (bf16[3,192,384]{2,1,0:T(8,128)(2,1)S(1)}, bf16[3,192,384]{2,1,0:T(8,128)(2,1)S(1)}, u32[]{:S(2)}, u32[]{:S(2)}) collective-permute-start(bf16[3,192,384]{2,1,0:T(8,128)(2,1)S(1)} %get-tuple-element.126), channel_id=1, source_target_pairs={{0,16},{8,24},{16,0},{24,8},{1,17},{9,25},{17,1},{25,9},{2,18},{10... | collective-permute-start | bytes 1327112 | tf_op jit(solution)/shard_map/ppermute | solution.py:19
  132.8 31.1 %collective-permute-start.29 = (bf16[3,192,384]{2,1,0:T(8,128)(2,1)S(1)}, bf16[3,192,384]{2,1,0:T(8,128)(2,1)S(1)}, u32[]{:S(2)}, u32[]{:S(2)}) collective-permute-start(bf16[3,192,384]{2,1,0:T(8,128)(2,1)S(1)} %get-tuple-element.127), channel_id=1, source_target_pairs={{0,24},{8,16},{16,8},{24,0},{1,25},{9,17},{17,9},{25,1},{2,26},{10... | collective-permute-start | bytes 1327112 | tf_op jit(solution)/shard_map/ppermute | solution.py:19
  134.3 15.0 %collective-permute-start.26 = (bf16[384,384]{1,0:T(8,128)(2,1)S(1)}, bf16[384,384]{1,0:T(8,128)(2,1)S(1)}, u32[]{:S(2)}, u32[]{:S(2)}) collective-permute-start(bf16[384,384]{1,0:T(8,128)(2,1)S(1)} %constant_dynamic-update-slice_fusion.2.refs_4_), channel_id=1, source_target_pairs={{0,4},{4,0},{1,5},{5,1},{2,6},{6,2},{3,7},{7,3},{8,12},{12,8},{9,1... | collective-permute-start | bytes 884744 | tf_op jit(solution)/shard_map/ppermute | solution.py:19
  135.1 15.0 %collective-permute-start.21 = (bf16[384,384]{1,0:T(8,128)(2,1)S(1)}, bf16[384,384]{1,0:T(8,128)(2,1)S(1)}, u32[]{:S(2)}, u32[]{:S(2)}) collective-permute-start(bf16[384,384]{1,0:T(8,128)(2,1)S(1)} %constant_dynamic-update-slice_fusion.refs_0_), channel_id=1, source_target_pairs={{0,2},{1,3},{2,0},{3,1},{4,6},{5,7},{6,4},{7,5},{8,10},{9,11},{10,... | collective-permute-start | bytes 884744 | tf_op jit(solution)/shard_map/ppermute | solution.py:19
  148.8 15.6 %collective-permute-start.25 = (bf16[384,384]{1,0:T(8,128)(2,1)S(1)}, bf16[384,384]{1,0:T(8,128)(2,1)S(1)}, u32[]{:S(2)}, u32[]{:S(2)}) collective-permute-start(bf16[384,384]{1,0:T(8,128)(2,1)S(1)} %collective-permute-done.22.refs_1_), channel_id=1, source_target_pairs={{0,2},{1,3},{2,0},{3,1},{4,6},{5,7},{6,4},{7,5},{8,10},{9,11},{10,... | collective-permute-start | bytes 884744 | tf_op jit(solution)/shard_map/ppermute | solution.py:19
  149.3 15.2 %collective-permute-start.27 = (bf16[384,384]{1,0:T(8,128)(2,1)S(1)}, bf16[384,384]{1,0:T(8,128)(2,1)S(1)}, u32[]{:S(2)}, u32[]{:S(2)}) collective-permute-start(bf16[384,384]{1,0:T(8,128)(2,1)S(1)} %collective-permute-done.23.refs_5_), channel_id=1, source_target_pairs={{0,4},{4,0},{1,5},{5,1},{2,6},{6,2},{3,7},{7,3},{8,12},{12,8},{9,1... | collective-permute-start | bytes 884744 | tf_op jit(solution)/shard_map/ppermute | solution.py:19
  150.1 14.8 %collective-permute-start.34 = (bf16[384,384]{1,0:T(8,128)(2,1)S(1)}, bf16[384,384]{1,0:T(8,128)(2,1)S(1)}, u32[]{:S(2)}, u32[]{:S(2)}) collective-permute-start(bf16[384,384]{1,0:T(8,128)(2,1)S(1)} %constant_dynamic-update-slice_fusion.2.refs_4_), channel_id=1, source_target_pairs={{0,1},{1,0},{2,3},{3,2},{4,5},{5,4},{6,7},{7,6},{8,9},{9,8},{10,11... | collective-permute-start | bytes 884744 | tf_op jit(solution)/shard_map/ppermute | solution.py:19
  163.9 1.6 collective-permute-start.30
  163.9 2.0 %collective-permute-start.31 = (bf16[384,384]{1,0:T(8,128)(2,1)S(1)}, bf16[384,384]{1,0:T(8,128)(2,1)S(1)}, u32[]{:S(2)}, u32[]{:S(2)}) collective-permute-start(bf16[384,384]{1,0:T(8,128)(2,1)S(1)} %collective-permute-done.22.refs_1_), channel_id=1, source_target_pairs={{0,1},{1,0},{2,3},{3,2},{4,5},{5,4},{6,7},{7,6},{8,9},{9,8},{10,11... | collective-permute-start | bytes 884744 | tf_op jit(solution)/shard_map/ppermute | solution.py:19
  164.4 2.6 %collective-permute-start.35 = (bf16[384,384]{1,0:T(8,128)(2,1)S(1)}, bf16[384,384]{1,0:T(8,128)(2,1)S(1)}, u32[]{:S(2)}, u32[]{:S(2)}) collective-permute-start(bf16[384,384]{1,0:T(8,128)(2,1)S(1)} %collective-permute-done.23.refs_5_), channel_id=1, source_target_pairs={{0,1},{1,0},{2,3},{3,2},{4,5},{5,4},{6,7},{7,6},{8,9},{9,8},{10,11... | collective-permute-start | bytes 884744 | tf_op jit(solution)/shard_map/ppermute | solution.py:19
  164.5 3.5 %collective-permute-start.32 = (bf16[384,384]{1,0:T(8,128)(2,1)S(1)}, bf16[384,384]{1,0:T(8,128)(2,1)S(1)}, u32[]{:S(2)}, u32[]{:S(2)}) collective-permute-start(bf16[384,384]{1,0:T(8,128)(2,1)S(1)} %collective-permute-done.21.refs_2_), channel_id=1, source_target_pairs={{0,1},{1,0},{2,3},{3,2},{4,5},{5,4},{6,7},{7,6},{8,9},{9,8},{10,11... | collective-permute-start | bytes 884744 | tf_op jit(solution)/shard_map/ppermute | solution.py:19
  165.0 14.0 %collective-permute-start.33 = (bf16[384,384]{1,0:T(8,128)(2,1)S(1)}, bf16[384,384]{1,0:T(8,128)(2,1)S(1)}, u32[]{:S(2)}, u32[]{:S(2)}) collective-permute-start(bf16[384,384]{1,0:T(8,128)(2,1)S(1)} %collective-permute-done.25.refs_3_), channel_id=1, source_target_pairs={{0,1},{1,0},{2,3},{3,2},{4,5},{5,4},{6,7},{7,6},{8,9},{9,8},{10,11... | collective-permute-start | bytes 884744 | tf_op jit(solution)/shard_map/ppermute | solution.py:19
  165.5 13.5 %collective-permute-start.36 = (bf16[384,384]{1,0:T(8,128)(2,1)S(1)}, bf16[384,384]{1,0:T(8,128)(2,1)S(1)}, u32[]{:S(2)}, u32[]{:S(2)}) collective-permute-start(bf16[384,384]{1,0:T(8,128)(2,1)S(1)} %collective-permute-done.26.refs_6_), channel_id=1, source_target_pairs={{0,1},{1,0},{2,3},{3,2},{4,5},{5,4},{6,7},{7,6},{8,9},{9,8},{10,11... | collective-permute-start | bytes 884744 | tf_op jit(solution)/shard_map/ppermute | solution.py:19
  165.9 13.1 %collective-permute-start.37 = (bf16[384,384]{1,0:T(8,128)(2,1)S(1)}, bf16[384,384]{1,0:T(8,128)(2,1)S(1)}, u32[]{:S(2)}, u32[]{:S(2)}) collective-permute-start(bf16[384,384]{1,0:T(8,128)(2,1)S(1)} %collective-permute-done.27.refs_7_), channel_id=1, source_target_pairs={{0,1},{1,0},{2,3},{3,2},{4,5},{5,4},{6,7},{7,6},{8,9},{9,8},{10,11... | collective-permute-start | bytes 884744 | tf_op jit(solution)/shard_map/ppermute | solution.py:19
  167.1 18.3 %collective-permute-start.38 = (f32[192,192]{1,0:T(8,128)S(1)}, f32[192,192]{1,0:T(8,128)S(1)}, u32[]{:S(2)}, u32[]{:S(2)}) collective-permute-start(f32[192,192]{1,0:T(8,128)S(1)} %get-tuple-element.138), channel_id=1, source_target_pairs={{0,4},{4,0},{1,5},{5,1},{2,6},{6,2},{3,7},{7,3},{8,12},{12,8},{9,1... | collective-permute-start | bytes 442376 | tf_op jit(solution)/shard_map/ppermute | solution.py:19
  168.0 17.4 %collective-permute-start.39 = (bf16[192,384]{1,0:T(8,128)(2,1)S(1)}, bf16[192,384]{1,0:T(8,128)(2,1)S(1)}, u32[]{:S(2)}, u32[]{:S(2)}) collective-permute-start(bf16[192,384]{1,0:T(8,128)(2,1)S(1)} %get-tuple-element.139), channel_id=1, source_target_pairs={{0,0},{1,8},{2,16},{3,24},{4,4},{5,12},{6,20},{7,28},{8,1},{9,9},{... | collective-permute-start | bytes 442376 | tf_op jit(solution)/shard_map/ppermute | solution.py:732
  (6 other events, 63.5 us)

commit v8 on v7

--- a/solution.py
+++ b/solution.py
@@ -53,8 +53,8 @@
             facts = jnp.where(place == c, jnp.where(target >= 0, target - own_id, 16 * slots), facts)
         facts = facts.astype(f32).astype(bf16)
         for packed in (theirs, mine):
-            packed[slot, fold : fold + 8, :] = facts
-        row = fold + 8
+            packed[slot, fold : fold + 1, :] = facts[:1]
+        row = fold + 1
         for start in range(0, pot.shape[1], width):
             stop = min(start + width, pot.shape[1])
             exact = pot[slot : slot + 1, start:stop]
@@ -73,7 +73,7 @@
 def pack(meta, neighbours, levels, orbitals, pot):
     slots, coefficients, width = orbitals.shape
     fold = coefficients // 2
-    padded = -(-(fold + 8 + 3 * -(-coefficients // width)) // ROWS) * ROWS
+    padded = -(-(fold + 1 + 3 * -(-coefficients // width)) // ROWS) * ROWS
     vmem, smem = pl.BlockSpec(memory_space=pltpu.VMEM), pl.BlockSpec(memory_space=pltpu.SMEM)
     return pl.pallas_call(
         pack_kernel,
@@ -261,14 +261,14 @@
     )(right, *[piece for pieces in lefts for piece in pieces], *extra)
 
 
-def root_kernel(levels, meta, *refs):
+def root_kernel(meta, *refs):
     pieces, (offset, root, whole, rows_f, cols_b, sems) = refs[:-6], refs[-6:]
     level, pair, orb = meta[0], meta[1], meta[2]
     coarse, width = offset.shape
     side = whole.shape[0]
     groups = side // width
     copies = []
-    for piece, (z, y, q) in zip(pieces, piece_places(levels)):
+    for piece, (z, y, q) in zip(pieces, piece_places()):
         for i in range(len(z)):
             start = ((orb ^ q) * PAIR + (pair ^ y)) * coarse
             rows = pl.ds(pl.multiple_of(start, coarse), coarse)
@@ -301,11 +301,11 @@
     root[...] = value + jnp.where(row_ids == col_ids, 1.0, 0.0)
 
 
-def piece_places(levels):
+def piece_places():
     places = []
     for core in (0, 1):
-        for half in range(2):
-            z = [half * levels // 2 + i for i in range(levels // 2)]
+        for half in (0, 1):
+            z = [half, half ^ 2]
             for second in (0, 1):
                 for inner in (0, 1):
                     y, far = (second, inner) if half else (inner, second)
@@ -313,11 +313,11 @@
     return places
 
 
-def root_of(meta, pieces, offset, side, levels):
+def root_of(meta, pieces, offset, side):
     coarse, width = offset.shape
     vmem, anywhere = pl.BlockSpec(memory_space=pltpu.VMEM), pl.BlockSpec(memory_space=pl.ANY)
     return pl.pallas_call(
-        functools.partial(root_kernel, levels),
+        root_kernel,
         out_shape=jax.ShapeDtypeStruct(offset.shape, f32),
         in_specs=[pl.BlockSpec(memory_space=pltpu.SMEM)] + [anywhere] * len(pieces) + [vmem],
         out_specs=vmem,
@@ -397,7 +397,7 @@
     lanes = raw.shape[3]
     for t in range(own):
         for start in range(0, lines.shape[1], lanes):
-            row = edge * square // 2 + 8 + 3 * (start // lanes)
+            row = edge * square // 2 + 1 + 3 * (start // lanes)
             high, middle, low = (
                 raw[t // slots, t % slots, row + i : row + i + 1, :].astype(f32) for i in range(3)
             )
@@ -708,20 +708,20 @@
     apart = (orb ^ level if square_grid else 0 * orb).reshape(1).astype(jnp.int32)
     fock_blocks = box_fock(1, lefts_beside, right, fock_part, apart)
     if square_grid:
-        pieces = [small] + [swap(small, "lvl", z) for z in range(1, level_count)]
-        pieces, fock_blocks, offset = lax.optimization_barrier((pieces, fock_blocks, offset))
-        join = functools.partial(jnp.concatenate, axis=0)
-        top, low = join(pieces[: level_count // 2]), join(pieces[level_count // 2 :])
+        over = swap(small, "lvl", 2)
+        over, fock_blocks, offset = lax.optimization_barrier((over, fock_blocks, offset))
+        top = jnp.concatenate([small, over])
+        low = swap(top, "lvl", 1)
         sent = [fock_blocks[0]] + [swap(fock_blocks[step], "lvl", step) for step in range(1, level_count)]
         got = [swap(top, "pair", 1), swap(low, "orb", 2)]
         got, sent[:2] = lax.optimization_barrier((got, sent[:2]))
         tops, lows = [top, got[0]], [low, got[1]]
         far_tops, far_lows = [swap(piece, "orb", 2) for piece in tops], [swap(piece, "pair", 1) for piece in lows]
-        far_tops, far_lows, sent = lax.optimization_barrier((far_tops, far_lows, sent))
+        far_lows[1], sent = lax.optimization_barrier((far_lows[1], sent))
         pieces = tops + far_tops + lows + far_lows
         pieces += [swap(piece, "orb", 1) for piece in pieces]
         root_meta = jnp.stack([level, pair, orb]).astype(jnp.int32)
-        inverse_root = root_of(root_meta, pieces, offset, all_width, level_count)
+        inverse_root = root_of(root_meta, pieces, offset, all_width)
         share, kept, other = level_sum(fock_sum_kernel, meta, sent)
         to = [
             ((z * PAIR + y) * orb_count + o, (o * PAIR + y) * orb_count + z)

time: 186 us -> 193 us (1.038)
  waiting for transfers between devices: 52.5 us -> 62.2 us
  starting transfers between devices: 57.3 us -> 53.8 us
    ppermute x35 -> x34, waiting for transfers between devices: 52.5 us -> 62.2 us  [swap(): return lax.ppermute(value, axis, [(i, i ^ bit) for i in range(count)])]
    ppermute x1, starting transfers between devices: 11 us -> 9.01 us  [body(): got = (swap(other, 'pair', 1), lax.ppermute(share, BOX + ('orb',), to))]
    ppermute x35 -> x34, starting transfers between devices: 38.1 us -> 36.5 us  [swap(): return lax.ppermute(value, axis, [(i, i ^ bit) for i in range(count)])]
    unnamed x37 -> x36, local copies, waits for them, and re-layouts: 4.32 us -> 4.3 us
  transfers between devices with their start and end apart: 40 -> 39, of which waited for: 7 -> 9; matrix products, arithmetic and copies ran while one was open for 2% -> 2% of each run, Pallas kernels for 30% -> 29%
where the time goes in v8:
time: 193 us
  Pallas kernels  64.2 us (33%)
  waiting for transfers between devices  62.2 us (32%)
  starting transfers between devices  53.8 us (28%)
  local copies, waits for them, and re-layouts  8.65 us (4%)
  other arithmetic  2.1 us (1%)
    ppermute x34, waiting for transfers between devices, swap(): return lax.ppermute(value, axis, [(i, i ^ bit) for i in range(count)])  62.2 us
    ppermute x34, starting transfers between devices, swap(): return lax.ppermute(value, axis, [(i, i ^ bit) for i in range(count)])  36.5 us
    pallas_call x1, Pallas kernels, kinetic(): pl.pallas_call(functools.partial(kinetic_kernel, edge, slots, levels), ou...  23.8 us
    pallas_call x2, Pallas kernels, box_fock(): pl.pallas_call(functools.partial(fock_kernel, side, counts), out_shape=ou...  16.7 us
    pallas_call x2, Pallas kernels, box_correlation(): pl.pallas_call(functools.partial(correlation_kernel, share, counts), out_...  9.17 us
    ppermute x1, starting transfers between devices, body(): got = (swap(other, 'pair', 1), lax.ppermute(share, BOX + ('orb',), to))  9.01 us
    ppermute x4, starting transfers between devices, trade(): return lax.ppermute(value, axis, pairs + [(b, a) for a, b in pairs])  8.26 us
    pallas_call x1, Pallas kernels, root_of(): pl.pallas_call(root_kernel, out_shape=jax.ShapeDtypeStruct(offset.shape,...  6.38 us
  transfers between devices with their start and end apart: 39, of which 9 were waited for; matrix products, arithmetic and copies ran while one was open for 2% of the time, Pallas kernels for 29%

profile of v8, /device:TPU:2, one launch (start us, length us, event | category | flops | bytes accessed | tf_op | source)
XLA Modules:
  0.0 192.7 jit_solution(17878371050156688635)
XLA Ops:
  1.5 0.8 copy.20.neighbours
  2.3 0.7 copy-done.11
  3.7 3.2 %pack.1 = (bf16[2,512,384]{2,1,0:T(8,128)(2,1)S(1)}, bf16[2,512,384]{2,1,0:T(8,128)(2,1)}) custom-call(s32[3]{0:T(128)S(1)} %pad_add_fusion.1.meta, s32[2,3,2]{2,1,0:T(4,128)S(1)} %copy.20.neighbours, s32[2]{0:T(128)S(1)} %copy-done.12, bf16[2,1000,384]{2,1,0:T(8,128)(2,1)} %orbitals.1, f32[2,1000]{1,0:T(2,128)S(1)} %copy-done.11), custom_call_target="tpu_custom_call" | custom-call | tf_op jit(solution)/shard_map/pack/pallas_call | solution.py:78
  6.9 1.5 collective-permute-start.1
  8.4 1.5 collective-permute-start.4
  10.5 3.6 %collective-permute-start.2 = (bf16[2,512,384]{2,1,0:T(8,128)(2,1)}, bf16[2,512,384]{2,1,0:T(8,128)(2,1)}, u32[]{:S(2)}, u32[]{:S(2)}) collective-permute-start(bf16[2,512,384]{2,1,0:T(8,128)(2,1)} %get-tuple-element.83.refs_0_), channel_id=1, source_target_pairs={{0,8},{16,24},{8,0},{24,16},{1,9},{17,25},{9,1},{25,17},{2,10},{18... | collective-permute-start | bytes 2359304 | tf_op jit(solution)/shard_map/ppermute | solution.py:24
  14.1 12.2 %collective-permute-done.1.beside_in.refs_1_ = bf16[2,512,384]{2,1,0:T(8,128)(2,1)} collective-permute-done((bf16[2,512,384]{2,1,0:T(8,128)(2,1)S(1)}, bf16[2,512,384]{2,1,0:T(8,128)(2,1)}, u32[]{:S(2)}, u32[]{:S(2)}) %collective-permute-start.1) | collective-permute-done | bytes 786464 | tf_op jit(solution)/shard_map/ppermute | solution.py:19
  26.3 1.5 collective-permute-start.6
  27.8 1.6 collective-permute-start.3
  29.4 1.6 collective-permute-start.5
  31.8 1.0 matrices.1
  33.0 0.7 slice.22
  34.3 0.7 slice.28
  35.0 9.9 %collective-permute-done.6.rest_in = bf16[2,512,384]{2,1,0:T(8,128)(2,1)S(1)} collective-permute-done((bf16[2,512,384]{2,1,0:T(8,128)(2,1)}, bf16[2,512,384]{2,1,0:T(8,128)(2,1)S(1)}, u32[]{:S(2)}, u32[]{:S(2)}) %collective-permute-start.6) | collective-permute-done | bytes 786464 | tf_op jit(solution)/shard_map/ppermute | solution.py:19
  44.9 0.9 copy-done
  45.8 1.1 copy-done.1
  47.0 2.2 %unfold.1 = (bf16[2000,384]{1,0:T(8,128)(2,1)S(1)}, bf16[1008,384]{1,0:T(8,128)(2,1)S(1)}) custom-call(s32[3]{0:T(128)S(1)} %pad_add_fusion.1.meta, bf16[2,512,384]{2,1,0:T(8,128)(2,1)} %collective-permute-done.1.beside_in.refs_1_, bf16[2,512,384]{2,1,0:T(8,128)(2,1)S(1)} %copy-done.1), custom_call_target="tpu_custom_call" | custom-call | tf_op jit(solution)/shard_map/unfold/pallas_call | solution.py:113
  49.2 0.7 slice.26
  50.7 1.6 collective-permute-start.8
  53.3 23.8 %kinetic.1 = bf16[4,1000,576]{2,1,0:T(8,128)(2,1)} custom-call(s32[2]{0:T(128)S(1)} %pad_add_fusion.2.place_meta, s32[6,2,8]{2,1,0:T(2,128)S(1)} %pad_add_fusion.facts, bf16[2,512,384]{2,1,0:T(8,128)(2,1)} %get-tuple-element.83.refs_0_, bf16[2,512,384]{2,1,0:T(8,128)(2,1)} %collective-permute-done.1.beside_in.refs_1_, ...), custom_call_target="tpu_custom_call" | custom-call | flops 20000000000 | bytes 40000000 | tf_op jit(solution)/shard_map/kinetic/pallas_call | solution.py:554
  77.8 4.8 %correlation.2.refs_6_ = f32[4,192,384]{2,1,0:T(8,128)S(1)} custom-call(s32[3]{0:T(128)S(1)} %pad_add_fusion.3.meta, bf16[2000,384]{1,0:T(8,128)(2,1)} %bitcast.5.refs_0_, bf16[2000,384]{1,0:T(8,128)(2,1)} %bitcast.6.refs_1_, bf16[2000,384]{1,0:T(8,128)(2,1)S(1)} %bitcast.36, bf16[2000,384]{1,0:T(8,128)(2,1)} %bitcast.7.refs_3_), custom_call_target="tpu_custom_call" | custom-call | flops 1179648000 | bytes 6144000 | tf_op jit(solution)/shard_map/correlation/pallas_call | solution.py:182
  82.6 4.4 %correlation.3 = bf16[4,192,384]{2,1,0:T(8,128)(2,1)S(1)} custom-call(s32[3]{0:T(128)S(1)} %pad_add_fusion.3.meta, bf16[2000,384]{1,0:T(8,128)(2,1)S(1)} %get-tuple-element.93.refs_0_, bf16[2000,384]{1,0:T(8,128)(2,1)} %collective-permute-done.9.refs_1_, bf16[1008,384]{1,0:T(8,128)(2,1)} %collective-permute-done.7.refs_2_, ...), custom_call_target="tpu_custom_call" | custom-call | flops 1179648000 | bytes 6144000 | tf_op jit(solution)/shard_map/correlation/pallas_call | solution.py:182
  87.1 7.1 %collective-permute-start.14 = (bf16[192,384]{1,0:T(8,128)(2,1)S(1)}, bf16[192,384]{1,0:T(8,128)(2,1)S(1)}, u32[]{:S(2)}, u32[]{:S(2)}) collective-permute-start(bf16[192,384]{1,0:T(8,128)(2,1)S(1)} %get-tuple-element.135), channel_id=1, source_target_pairs={{0,8},{8,0},{16,24},{24,16},{1,9},{9,1},{17,25},{25,17},{2,10},{10... | collective-permute-start | bytes 442376 | tf_op jit(solution)/shard_map/ppermute | solution.py:19
  94.2 2.4 %collective-permute-start.16 = (bf16[192,384]{1,0:T(8,128)(2,1)S(1)}, bf16[192,384]{1,0:T(8,128)(2,1)S(1)}, u32[]{:S(2)}, u32[]{:S(2)}) collective-permute-start(bf16[192,384]{1,0:T(8,128)(2,1)S(1)} %get-tuple-element.133), channel_id=1, source_target_pairs={{0,24},{8,16},{16,8},{24,0},{1,25},{9,17},{17,9},{25,1},{2,26},{10... | collective-permute-start | bytes 442376 | tf_op jit(solution)/shard_map/ppermute | solution.py:19
  96.6 8.2 %fock.2.refs_6_ = f32[4,576,384]{2,1,0:T(8,128)S(1)} custom-call(bf16[2,2000,576]{2,1,0:T(8,128)(2,1)} %bitcast.38, bf16[2000,384]{1,0:T(8,128)(2,1)} %bitcast.5.refs_0_, bf16[2000,384]{1,0:T(8,128)(2,1)} %bitcast.6.refs_1_, bf16[2000,384]{1,0:T(8,128)(2,1)S(1)} %bitcast.37, bf16[2000,384]{1,0:T(8,128)(2,1)} %bitcast.7.refs_3_), custom_call_target="tpu_custom_call" | custom-call | flops 3538944000 | bytes 6144000 | tf_op jit(solution)/shard_map/fock/pallas_call | solution.py:244
  104.8 2.7 %collective-permute-done.15.refs_2_ = bf16[192,384]{1,0:T(8,128)(2,1)S(1)} collective-permute-done((bf16[192,384]{1,0:T(8,128)(2,1)S(1)}, bf16[192,384]{1,0:T(8,128)(2,1)S(1)}, u32[]{:S(2)}, u32[]{:S(2)}) %collective-permute-start.15) | collective-permute-done | bytes 147488 | tf_op jit(solution)/shard_map/ppermute | solution.py:19
  107.5 0.8 level_sum.2
  108.3 1.3 collective-permute-start.18
  109.6 2.1 %collective-permute-start.17 = (bf16[192,384]{1,0:T(8,128)(2,1)S(1)}, bf16[192,384]{1,0:T(8,128)(2,1)S(1)}, u32[]{:S(2)}, u32[]{:S(2)}) collective-permute-start(bf16[192,384]{1,0:T(8,128)(2,1)S(1)} %get-tuple-element.102), channel_id=1, source_target_pairs={{0,16},{8,24},{16,0},{24,8},{1,17},{9,25},{17,1},{25,9},{2,18},{10... | collective-permute-start | bytes 442376 | tf_op jit(solution)/shard_map/ppermute | solution.py:19
  111.7 8.5 %fock.3 = (bf16[3,192,384]{2,1,0:T(8,128)(2,1)S(1)}, bf16[3,192,384]{2,1,0:T(8,128)(2,1)S(1)}, bf16[3,192,384]{2,1,0:T(8,128)(2,1)S(1)}, bf16[3,192,384]{2,1,0:T(8,128)(2,1)S(1)}) custom-call(bf16[2,2000,576]{2,1,0:T(8,128)(2,1)} %bitcast.39, bf16[2000,384]{1,0:T(8,128)(2,1)S(1)} %get-tuple-element.93.refs_0_, ...), custom_call_target="tpu_custom_call" | custom-call | flops 3538944000 | bytes 6144000 | tf_op jit(solution)/shard_map/fock/pallas_call | solution.py:244
  120.2 0.9 convert_add_fusion
  121.1 1.1 collective-permute-start.20
  122.2 1.0 collective-permute-start.22
  123.2 0.8 collective-permute-start.19
  124.0 7.1 %collective-permute-done.20.refs_4_ = bf16[384,384]{1,0:T(8,128)(2,1)S(1)} collective-permute-done((bf16[384,384]{1,0:T(8,128)(2,1)S(1)}, bf16[384,384]{1,0:T(8,128)(2,1)S(1)}, u32[]{:S(2)}, u32[]{:S(2)}) %collective-permute-start.20) | collective-permute-done | bytes 294944 | tf_op jit(solution)/shard_map/ppermute | solution.py:19
  131.2 6.2 %collective-permute-start.21 = (bf16[384,384]{1,0:T(8,128)(2,1)S(1)}, bf16[384,384]{1,0:T(8,128)(2,1)S(1)}, u32[]{:S(2)}, u32[]{:S(2)}) collective-permute-start(bf16[384,384]{1,0:T(8,128)(2,1)S(1)} %collective-permute-done.20.refs_4_), channel_id=1, source_target_pairs={{0,2},{1,3},{2,0},{3,1},{4,6},{5,7},{6,4},{7,5},{8,10},{9,11},{10,... | collective-permute-start | bytes 884744 | tf_op jit(solution)/shard_map/ppermute | solution.py:19
  137.4 3.4 %collective-permute-start.25 = (bf16[3,192,384]{2,1,0:T(8,128)(2,1)S(1)}, bf16[3,192,384]{2,1,0:T(8,128)(2,1)S(1)}, u32[]{:S(2)}, u32[]{:S(2)}) collective-permute-start(bf16[3,192,384]{2,1,0:T(8,128)(2,1)S(1)} %get-tuple-element.117), channel_id=1, source_target_pairs={{0,24},{8,16},{16,8},{24,0},{1,25},{9,17},{17,9},{25,1},{2,26},{10... | collective-permute-start | bytes 1327112 | tf_op jit(solution)/shard_map/ppermute | solution.py:19
  140.8 2.5 %collective-permute-done.22.refs_1_ = bf16[3,192,384]{2,1,0:T(8,128)(2,1)S(1)} collective-permute-done((bf16[3,192,384]{2,1,0:T(8,128)(2,1)S(1)}, bf16[3,192,384]{2,1,0:T(8,128)(2,1)S(1)}, u32[]{:S(2)}, u32[]{:S(2)}) %collective-permute-start.22) | collective-permute-done | bytes 442400 | tf_op jit(solution)/shard_map/ppermute | solution.py:19
  143.3 0.8 collective-permute-start.23
  144.1 3.4 %collective-permute-done.26.refs_2_ = bf16[384,384]{1,0:T(8,128)(2,1)S(1)} collective-permute-done((bf16[384,384]{1,0:T(8,128)(2,1)S(1)}, bf16[384,384]{1,0:T(8,128)(2,1)S(1)}, u32[]{:S(2)}, u32[]{:S(2)}) %collective-permute-start.26) | collective-permute-done | bytes 294944 | tf_op jit(solution)/shard_map/ppermute | solution.py:19
  147.5 0.8 collective-permute-start.28
  148.3 16.7 %collective-permute-done.24.refs_2_ = bf16[3,192,384]{2,1,0:T(8,128)(2,1)S(1)} collective-permute-done((bf16[3,192,384]{2,1,0:T(8,128)(2,1)S(1)}, bf16[3,192,384]{2,1,0:T(8,128)(2,1)S(1)}, u32[]{:S(2)}, u32[]{:S(2)}) %collective-permute-start.24) | collective-permute-done | bytes 442400 | tf_op jit(solution)/shard_map/ppermute | solution.py:19
  167.2 7.4 %collective-permute-done.27.refs_3_ = bf16[384,384]{1,0:T(8,128)(2,1)S(1)} collective-permute-done((bf16[384,384]{1,0:T(8,128)(2,1)S(1)}, bf16[384,384]{1,0:T(8,128)(2,1)S(1)}, u32[]{:S(2)}, u32[]{:S(2)}) %collective-permute-start.27) | collective-permute-done | bytes 294944 | tf_op jit(solution)/shard_map/ppermute | solution.py:19
  174.6 0.9 level_sum.3
  175.5 0.9 collective-permute-start.37
  176.4 9.0 %collective-permute-start.38 = (bf16[192,384]{1,0:T(8,128)(2,1)S(1)}, bf16[192,384]{1,0:T(8,128)(2,1)S(1)}, u32[]{:S(2)}, u32[]{:S(2)}) collective-permute-start(bf16[192,384]{1,0:T(8,128)(2,1)S(1)} %get-tuple-element.127), channel_id=1, source_target_pairs={{0,0},{1,8},{2,16},{3,24},{4,4},{5,12},{6,20},{7,28},{8,1},{9,9},{... | collective-permute-start | bytes 442376 | tf_op jit(solution)/shard_map/ppermute | solution.py:732
  185.5 6.4 %root.1 = f32[192,384]{1,0:T(8,128)} custom-call(s32[3]{0:T(128)S(1)} %pad_add_fusion.4.meta, bf16[384,384]{1,0:T(8,128)(2,1)S(1)} %constant_dynamic-update-slice_fusion.refs_0_, bf16[384,384]{1,0:T(8,128)(2,1)S(1)} %collective-permute-done.19.refs_1_, bf16[384,384]{1,0:T(8,128)(2,1)S(1)} %collective-permute-done.26.refs_2_, ...), custom_call_target="tpu_custom_call" | custom-call | flops 14495514624 | bytes 9437184 | tf_op jit(solution)/shard_map/root/pallas_call | solution.py:319
  191.9 0.8 maximum_add_fusion
  (100 shorter events, 7.8 us)
Async XLA Ops:
  0.6 31.1 %copy-start.7 = (bf16[112,10]{1,0:T(8,128)(2,1)S(1)}, bf16[112,10]{1,0:T(8,128)(2,1)}, u32[]{:S(2)}) copy-start(bf16[112,10]{1,0:T(8,128)(2,1)} %constant.58.clone.refs_0_) | copy-start | bytes 6724
  0.6 31.1 %copy-start.9 = (bf16[30,336]{1,0:T(8,128)(2,1)S(1)}, bf16[30,336]{1,0:T(8,128)(2,1)}, u32[]{:S(2)}) copy-start(bf16[30,336]{1,0:T(8,128)(2,1)} %constant.59.clone.refs_1_) | copy-start | bytes 60484
  0.7 31.1 %copy-start.3 = (f32[112,112]{1,0:T(8,128)S(1)}, f32[112,112]{1,0:T(8,128)}, u32[]{:S(2)}) copy-start(f32[112,112]{1,0:T(8,128)} %constant.60.clone.refs_2_) | copy-start | bytes 150532
  0.7 31.1 %copy-start.8 = (bf16[112,10]{1,0:T(8,128)(2,1)S(1)}, bf16[112,10]{1,0:T(8,128)(2,1)}, u32[]{:S(2)}) copy-start(bf16[112,10]{1,0:T(8,128)(2,1)} %constant.61.clone.refs_3_) | copy-start | bytes 6724
  0.7 31.1 %copy-start.10 = (bf16[30,336]{1,0:T(8,128)(2,1)S(1)}, bf16[30,336]{1,0:T(8,128)(2,1)}, u32[]{:S(2)}) copy-start(bf16[30,336]{1,0:T(8,128)(2,1)} %constant.62.clone.refs_4_) | copy-start | bytes 60484
  0.7 31.1 %copy-start.4 = (f32[112,112]{1,0:T(8,128)S(1)}, f32[112,112]{1,0:T(8,128)}, u32[]{:S(2)}) copy-start(f32[112,112]{1,0:T(8,128)} %constant.63.clone.refs_5_) | copy-start | bytes 150532
  0.7 31.1 %copy-start.5 = (bf16[160,10]{1,0:T(8,128)(2,1)S(1)}, bf16[160,10]{1,0:T(8,128)(2,1)}, u32[]{:S(2)}) copy-start(bf16[160,10]{1,0:T(8,128)(2,1)} %constant.64.clone.refs_6_) | copy-start | bytes 9604
  0.7 31.1 %copy-start.6 = (bf16[30,480]{1,0:T(8,128)(2,1)S(1)}, bf16[30,480]{1,0:T(8,128)(2,1)}, u32[]{:S(2)}) copy-start(bf16[30,480]{1,0:T(8,128)(2,1)} %constant.65.clone.refs_7_) | copy-start | bytes 86404
  0.7 31.1 %copy-start.2 = (f32[160,160]{1,0:T(8,128)S(1)}, f32[160,160]{1,0:T(8,128)}, u32[]{:S(2)}) copy-start(f32[160,160]{1,0:T(8,128)} %constant.66.clone.refs_8_) | copy-start | bytes 307204
  6.9 19.4 %collective-permute-start.1 = (bf16[2,512,384]{2,1,0:T(8,128)(2,1)S(1)}, bf16[2,512,384]{2,1,0:T(8,128)(2,1)}, u32[]{:S(2)}, u32[]{:S(2)}) collective-permute-start(bf16[2,512,384]{2,1,0:T(8,128)(2,1)S(1)} %get-tuple-element.68), channel_id=1, source_target_pairs={{0,4},{4,0},{1,5},{5,1},{2,6},{6,2},{3,7},{7,3},{8,12},{12,8},{9,1... | collective-permute-start | bytes 2359304 | tf_op jit(solution)/shard_map/ppermute | solution.py:19
  8.4 21.0 %collective-permute-start.4 = (bf16[2,512,384]{2,1,0:T(8,128)(2,1)}, bf16[2,512,384]{2,1,0:T(8,128)(2,1)}, u32[]{:S(2)}, u32[]{:S(2)}) collective-permute-start(bf16[2,512,384]{2,1,0:T(8,128)(2,1)} %get-tuple-element.83.refs_0_), channel_id=1, source_target_pairs={{8,16},{16,8},{9,17},{17,9},{10,18},{18,10},{11,19},{19,11},{12,20... | collective-permute-start | bytes 2359304 | tf_op jit(solution)/shard_map/ppermute | solution.py:24
  10.0 39.2 %collective-permute-start = (bf16[2,1000,384]{2,1,0:T(8,128)(2,1)}, bf16[2,1000,384]{2,1,0:T(8,128)(2,1)S(1)}, u32[]{:S(2)}, u32[]{:S(2)}) collective-permute-start(bf16[2,1000,384]{2,1,0:T(8,128)(2,1)} %orbitals.1), channel_id=1, source_target_pairs={{0,2},{1,3},{2,0},{3,1},{4,6},{5,7},{6,4},{7,5},{8,10},{9,11},{10,... | collective-permute-start | bytes 4608008 | tf_op jit(solution)/shard_map/ppermute | solution.py:19
  10.5 23.8 %collective-permute-start.2 = (bf16[2,512,384]{2,1,0:T(8,128)(2,1)}, bf16[2,512,384]{2,1,0:T(8,128)(2,1)}, u32[]{:S(2)}, u32[]{:S(2)}) collective-permute-start(bf16[2,512,384]{2,1,0:T(8,128)(2,1)} %get-tuple-element.83.refs_0_), channel_id=1, source_target_pairs={{0,8},{16,24},{8,0},{24,16},{1,9},{17,25},{9,1},{25,17},{2,10},{18... | collective-permute-start | bytes 2359304 | tf_op jit(solution)/shard_map/ppermute | solution.py:24
  26.3 18.6 %collective-permute-start.6 = (bf16[2,512,384]{2,1,0:T(8,128)(2,1)}, bf16[2,512,384]{2,1,0:T(8,128)(2,1)S(1)}, u32[]{:S(2)}, u32[]{:S(2)}) collective-permute-start(bf16[2,512,384]{2,1,0:T(8,128)(2,1)} %get-tuple-element.83.refs_0_), channel_id=1, source_target_pairs={{0,4},{4,0},{1,5},{5,1},{2,6},{6,2},{3,7},{7,3},{8,12},{12,8},{9,1... | collective-permute-start | bytes 2359304 | tf_op jit(solution)/shard_map/ppermute | solution.py:19
  27.8 21.4 %collective-permute-start.3 = (bf16[2,512,384]{2,1,0:T(8,128)(2,1)}, bf16[2,512,384]{2,1,0:T(8,128)(2,1)}, u32[]{:S(2)}, u32[]{:S(2)}) collective-permute-start(bf16[2,512,384]{2,1,0:T(8,128)(2,1)} %collective-permute-done.1.beside_in.refs_1_), channel_id=1, source_target_pairs={{0,8},{16,24},{8,0},{24,16},{1,9},{17,25},{9,1},{25,17},{2,10},{18... | collective-permute-start | bytes 2359304 | tf_op jit(solution)/shard_map/ppermute | solution.py:24
  29.4 19.8 %collective-permute-start.5 = (bf16[2,512,384]{2,1,0:T(8,128)(2,1)}, bf16[2,512,384]{2,1,0:T(8,128)(2,1)}, u32[]{:S(2)}, u32[]{:S(2)}) collective-permute-start(bf16[2,512,384]{2,1,0:T(8,128)(2,1)} %collective-permute-done.1.beside_in.refs_1_), channel_id=1, source_target_pairs={{8,16},{16,8},{9,17},{17,9},{10,18},{18,10},{11,19},{19,11},{12,20... | collective-permute-start | bytes 2359304 | tf_op jit(solution)/shard_map/ppermute | solution.py:24
  50.6 27.2 %collective-permute-start.13 = (bf16[2,1000,384]{2,1,0:T(8,128)(2,1)S(1)}, bf16[2,1000,384]{2,1,0:T(8,128)(2,1)}, u32[]{:S(2)}, u32[]{:S(2)}) collective-permute-start(bf16[2,1000,384]{2,1,0:T(8,128)(2,1)S(1)} %collective-permute-done), channel_id=1, source_target_pairs={{0,1},{1,0},{2,3},{3,2},{4,5},{5,4},{6,7},{7,6},{8,9},{9,8},{10,11... | collective-permute-start | bytes 4608008 | tf_op jit(solution)/shard_map/ppermute | solution.py:19
  50.7 26.5 %collective-permute-start.8 = (bf16[992,384]{1,0:T(8,128)(2,1)S(1)}, bf16[992,384]{1,0:T(8,128)(2,1)}, u32[]{:S(2)}, u32[]{:S(2)}) collective-permute-start(bf16[992,384]{1,0:T(8,128)(2,1)S(1)} %slice.30), channel_id=1, source_target_pairs={{0,4},{4,0},{1,5},{5,1},{2,6},{6,2},{3,7},{7,3},{8,12},{12,8},{9,1... | collective-permute-start | bytes 2285576 | tf_op jit(solution)/shard_map/ppermute | solution.py:19
  52.2 24.9 %collective-permute-start.7 = (bf16[1008,384]{1,0:T(8,128)(2,1)S(1)}, bf16[1008,384]{1,0:T(8,128)(2,1)}, u32[]{:S(2)}, u32[]{:S(2)}) collective-permute-start(bf16[1008,384]{1,0:T(8,128)(2,1)S(1)} %get-tuple-element.78), channel_id=1, source_target_pairs={{0,2},{1,3},{2,0},{3,1},{4,6},{5,7},{6,4},{7,5},{8,10},{9,11},{10,... | collective-permute-start | bytes 2322440 | tf_op jit(solution)/shard_map/ppermute | solution.py:19
  52.8 25.0 %collective-permute-start.12 = (bf16[2,1000,384]{2,1,0:T(8,128)(2,1)}, bf16[2,1000,384]{2,1,0:T(8,128)(2,1)}, u32[]{:S(2)}, u32[]{:S(2)}) collective-permute-start(bf16[2,1000,384]{2,1,0:T(8,128)(2,1)} %orbitals.1), channel_id=1, source_target_pairs={{0,1},{1,0},{2,3},{3,2},{4,5},{5,4},{6,7},{7,6},{8,9},{9,8},{10,11... | collective-permute-start | bytes 4608008 | tf_op jit(solution)/shard_map/ppermute | solution.py:19
  52.8 29.8 %collective-permute-start.9 = (bf16[2000,384]{1,0:T(8,128)(2,1)S(1)}, bf16[2000,384]{1,0:T(8,128)(2,1)}, u32[]{:S(2)}, u32[]{:S(2)}) collective-permute-start(bf16[2000,384]{1,0:T(8,128)(2,1)S(1)} %get-tuple-element.93.refs_0_), channel_id=1, source_target_pairs={{0,1},{1,0},{2,3},{3,2},{4,5},{5,4},{6,7},{7,6},{8,9},{9,8},{10,11... | collective-permute-start | bytes 4608008 | tf_op jit(solution)/shard_map/ppermute | solution.py:19
  77.2 5.4 %collective-permute-start.10 = (bf16[1008,384]{1,0:T(8,128)(2,1)}, bf16[1008,384]{1,0:T(8,128)(2,1)}, u32[]{:S(2)}, u32[]{:S(2)}) collective-permute-start(bf16[1008,384]{1,0:T(8,128)(2,1)} %collective-permute-done.7.refs_2_), channel_id=1, source_target_pairs={{0,1},{1,0},{2,3},{3,2},{4,5},{5,4},{6,7},{7,6},{8,9},{9,8},{10,11... | collective-permute-start | bytes 2322440 | tf_op jit(solution)/shard_map/ppermute | solution.py:19
  77.2 5.3 %collective-permute-start.11 = (bf16[992,384]{1,0:T(8,128)(2,1)}, bf16[992,384]{1,0:T(8,128)(2,1)}, u32[]{:S(2)}, u32[]{:S(2)}) collective-permute-start(bf16[992,384]{1,0:T(8,128)(2,1)} %collective-permute-done.8.refs_3_), channel_id=1, source_target_pairs={{0,1},{1,0},{2,3},{3,2},{4,5},{5,4},{6,7},{7,6},{8,9},{9,8},{10,11... | collective-permute-start | bytes 2285576 | tf_op jit(solution)/shard_map/ppermute | solution.py:19
  87.1 17.7 %collective-permute-start.14 = (bf16[192,384]{1,0:T(8,128)(2,1)S(1)}, bf16[192,384]{1,0:T(8,128)(2,1)S(1)}, u32[]{:S(2)}, u32[]{:S(2)}) collective-permute-start(bf16[192,384]{1,0:T(8,128)(2,1)S(1)} %get-tuple-element.135), channel_id=1, source_target_pairs={{0,8},{8,0},{16,24},{24,16},{1,9},{9,1},{17,25},{25,17},{2,10},{10... | collective-permute-start | bytes 442376 | tf_op jit(solution)/shard_map/ppermute | solution.py:19
  94.2 13.3 %collective-permute-start.15 = (bf16[192,384]{1,0:T(8,128)(2,1)S(1)}, bf16[192,384]{1,0:T(8,128)(2,1)S(1)}, u32[]{:S(2)}, u32[]{:S(2)}) collective-permute-start(bf16[192,384]{1,0:T(8,128)(2,1)S(1)} %get-tuple-element.134), channel_id=1, source_target_pairs={{0,16},{8,24},{16,0},{24,8},{1,17},{9,25},{17,1},{25,9},{2,18},{10... | collective-permute-start | bytes 442376 | tf_op jit(solution)/shard_map/ppermute | solution.py:19
  94.2 13.3 %collective-permute-start.16 = (bf16[192,384]{1,0:T(8,128)(2,1)S(1)}, bf16[192,384]{1,0:T(8,128)(2,1)S(1)}, u32[]{:S(2)}, u32[]{:S(2)}) collective-permute-start(bf16[192,384]{1,0:T(8,128)(2,1)S(1)} %get-tuple-element.133), channel_id=1, source_target_pairs={{0,24},{8,16},{16,8},{24,0},{1,25},{9,17},{17,9},{25,1},{2,26},{10... | collective-permute-start | bytes 442376 | tf_op jit(solution)/shard_map/ppermute | solution.py:19
  108.3 11.9 %collective-permute-start.18 = (f32[192,192]{1,0:T(8,128)S(1)}, f32[192,192]{1,0:T(8,128)S(1)}, u32[]{:S(2)}, u32[]{:S(2)}) collective-permute-start(f32[192,192]{1,0:T(8,128)S(1)} %get-tuple-element.109), channel_id=1, source_target_pairs={{0,4},{4,0},{1,5},{5,1},{2,6},{6,2},{3,7},{7,3},{8,12},{12,8},{9,1... | collective-permute-start | bytes 442376 | tf_op jit(solution)/shard_map/ppermute | solution.py:19
  109.6 11.5 %collective-permute-start.17 = (bf16[192,384]{1,0:T(8,128)(2,1)S(1)}, bf16[192,384]{1,0:T(8,128)(2,1)S(1)}, u32[]{:S(2)}, u32[]{:S(2)}) collective-permute-start(bf16[192,384]{1,0:T(8,128)(2,1)S(1)} %get-tuple-element.102), channel_id=1, source_target_pairs={{0,16},{8,24},{16,0},{24,8},{1,17},{9,25},{17,1},{25,9},{2,18},{10... | collective-permute-start | bytes 442376 | tf_op jit(solution)/shard_map/ppermute | solution.py:19
  121.1 10.0 %collective-permute-start.20 = (bf16[384,384]{1,0:T(8,128)(2,1)S(1)}, bf16[384,384]{1,0:T(8,128)(2,1)S(1)}, u32[]{:S(2)}, u32[]{:S(2)}) collective-permute-start(bf16[384,384]{1,0:T(8,128)(2,1)S(1)} %constant_dynamic-update-slice_fusion.refs_0_), channel_id=1, source_target_pairs={{0,8},{8,0},{16,24},{24,16},{1,9},{9,1},{17,25},{25,17},{2,10},{10... | collective-permute-start | bytes 884744 | tf_op jit(solution)/shard_map/ppermute | solution.py:19
  122.2 21.1 %collective-permute-start.22 = (bf16[3,192,384]{2,1,0:T(8,128)(2,1)S(1)}, bf16[3,192,384]{2,1,0:T(8,128)(2,1)S(1)}, u32[]{:S(2)}, u32[]{:S(2)}) collective-permute-start(bf16[3,192,384]{2,1,0:T(8,128)(2,1)S(1)} %get-tuple-element.112), channel_id=1, source_target_pairs={{0,8},{8,0},{16,24},{24,16},{1,9},{9,1},{17,25},{25,17},{2,10},{10... | collective-permute-start | bytes 1327112 | tf_op jit(solution)/shard_map/ppermute | solution.py:19
  123.2 17.5 %collective-permute-start.19 = (bf16[384,384]{1,0:T(8,128)(2,1)S(1)}, bf16[384,384]{1,0:T(8,128)(2,1)S(1)}, u32[]{:S(2)}, u32[]{:S(2)}) collective-permute-start(bf16[384,384]{1,0:T(8,128)(2,1)S(1)} %constant_dynamic-update-slice_fusion.refs_0_), channel_id=1, source_target_pairs={{0,4},{4,0},{1,5},{5,1},{2,6},{6,2},{3,7},{7,3},{8,12},{12,8},{9,1... | collective-permute-start | bytes 884744 | tf_op jit(solution)/shard_map/ppermute | solution.py:19
  131.2 12.2 %collective-permute-start.21 = (bf16[384,384]{1,0:T(8,128)(2,1)S(1)}, bf16[384,384]{1,0:T(8,128)(2,1)S(1)}, u32[]{:S(2)}, u32[]{:S(2)}) collective-permute-start(bf16[384,384]{1,0:T(8,128)(2,1)S(1)} %collective-permute-done.20.refs_4_), channel_id=1, source_target_pairs={{0,2},{1,3},{2,0},{3,1},{4,6},{5,7},{6,4},{7,5},{8,10},{9,11},{10,... | collective-permute-start | bytes 884744 | tf_op jit(solution)/shard_map/ppermute | solution.py:19
  137.4 27.6 %collective-permute-start.24 = (bf16[3,192,384]{2,1,0:T(8,128)(2,1)S(1)}, bf16[3,192,384]{2,1,0:T(8,128)(2,1)S(1)}, u32[]{:S(2)}, u32[]{:S(2)}) collective-permute-start(bf16[3,192,384]{2,1,0:T(8,128)(2,1)S(1)} %get-tuple-element.116), channel_id=1, source_target_pairs={{0,16},{8,24},{16,0},{24,8},{1,17},{9,25},{17,1},{25,9},{2,18},{10... | collective-permute-start | bytes 1327112 | tf_op jit(solution)/shard_map/ppermute | solution.py:19
  137.4 27.6 %collective-permute-start.25 = (bf16[3,192,384]{2,1,0:T(8,128)(2,1)S(1)}, bf16[3,192,384]{2,1,0:T(8,128)(2,1)S(1)}, u32[]{:S(2)}, u32[]{:S(2)}) collective-permute-start(bf16[3,192,384]{2,1,0:T(8,128)(2,1)S(1)} %get-tuple-element.117), channel_id=1, source_target_pairs={{0,24},{8,16},{16,8},{24,0},{1,25},{9,17},{17,9},{25,1},{2,26},{10... | collective-permute-start | bytes 1327112 | tf_op jit(solution)/shard_map/ppermute | solution.py:19
  140.8 6.7 %collective-permute-start.26 = (bf16[384,384]{1,0:T(8,128)(2,1)S(1)}, bf16[384,384]{1,0:T(8,128)(2,1)S(1)}, u32[]{:S(2)}, u32[]{:S(2)}) collective-permute-start(bf16[384,384]{1,0:T(8,128)(2,1)S(1)} %constant_dynamic-update-slice_fusion.refs_0_), channel_id=1, source_target_pairs={{0,2},{1,3},{2,0},{3,1},{4,6},{5,7},{6,4},{7,5},{8,10},{9,11},{10,... | collective-permute-start | bytes 884744 | tf_op jit(solution)/shard_map/ppermute | solution.py:19
  143.3 22.2 %collective-permute-start.23 = (bf16[384,384]{1,0:T(8,128)(2,1)S(1)}, bf16[384,384]{1,0:T(8,128)(2,1)S(1)}, u32[]{:S(2)}, u32[]{:S(2)}) collective-permute-start(bf16[384,384]{1,0:T(8,128)(2,1)S(1)} %collective-permute-done.21.refs_5_), channel_id=1, source_target_pairs={{0,4},{4,0},{1,5},{5,1},{2,6},{6,2},{3,7},{7,3},{8,12},{12,8},{9,1... | collective-permute-start | bytes 884744 | tf_op jit(solution)/shard_map/ppermute | solution.py:19
  144.1 21.9 %collective-permute-start.29 = (bf16[384,384]{1,0:T(8,128)(2,1)S(1)}, bf16[384,384]{1,0:T(8,128)(2,1)S(1)}, u32[]{:S(2)}, u32[]{:S(2)}) collective-permute-start(bf16[384,384]{1,0:T(8,128)(2,1)S(1)} %constant_dynamic-update-slice_fusion.refs_0_), channel_id=1, source_target_pairs={{0,1},{1,0},{2,3},{3,2},{4,5},{5,4},{6,7},{7,6},{8,9},{9,8},{10,11... | collective-permute-start | bytes 884744 | tf_op jit(solution)/shard_map/ppermute | solution.py:19
  147.5 18.6 %collective-permute-start.28 = (bf16[384,384]{1,0:T(8,128)(2,1)S(1)}, bf16[384,384]{1,0:T(8,128)(2,1)S(1)}, u32[]{:S(2)}, u32[]{:S(2)}) collective-permute-start(bf16[384,384]{1,0:T(8,128)(2,1)S(1)} %collective-permute-done.20.refs_4_), channel_id=1, source_target_pairs={{0,4},{4,0},{1,5},{5,1},{2,6},{6,2},{3,7},{7,3},{8,12},{12,8},{9,1... | collective-permute-start | bytes 884744 | tf_op jit(solution)/shard_map/ppermute | solution.py:19
  165.0 1.6 collective-permute-start.31
  165.0 2.0 %collective-permute-start.33 = (bf16[384,384]{1,0:T(8,128)(2,1)S(1)}, bf16[384,384]{1,0:T(8,128)(2,1)S(1)}, u32[]{:S(2)}, u32[]{:S(2)}) collective-permute-start(bf16[384,384]{1,0:T(8,128)(2,1)S(1)} %collective-permute-done.20.refs_4_), channel_id=1, source_target_pairs={{0,1},{1,0},{2,3},{3,2},{4,5},{5,4},{6,7},{7,6},{8,9},{9,8},{10,11... | collective-permute-start | bytes 884744 | tf_op jit(solution)/shard_map/ppermute | solution.py:19
  165.5 9.0 %collective-permute-start.27 = (bf16[384,384]{1,0:T(8,128)(2,1)S(1)}, bf16[384,384]{1,0:T(8,128)(2,1)S(1)}, u32[]{:S(2)}, u32[]{:S(2)}) collective-permute-start(bf16[384,384]{1,0:T(8,128)(2,1)S(1)} %collective-permute-done.19.refs_1_), channel_id=1, source_target_pairs={{0,2},{1,3},{2,0},{3,1},{4,6},{5,7},{6,4},{7,5},{8,10},{9,11},{10,... | collective-permute-start | bytes 884744 | tf_op jit(solution)/shard_map/ppermute | solution.py:19
  166.1 9.5 %collective-permute-start.30 = (bf16[384,384]{1,0:T(8,128)(2,1)S(1)}, bf16[384,384]{1,0:T(8,128)(2,1)S(1)}, u32[]{:S(2)}, u32[]{:S(2)}) collective-permute-start(bf16[384,384]{1,0:T(8,128)(2,1)S(1)} %collective-permute-done.19.refs_1_), channel_id=1, source_target_pairs={{0,1},{1,0},{2,3},{3,2},{4,5},{5,4},{6,7},{7,6},{8,9},{9,8},{10,11... | collective-permute-start | bytes 884744 | tf_op jit(solution)/shard_map/ppermute | solution.py:19
  166.1 10.3 %collective-permute-start.34 = (bf16[384,384]{1,0:T(8,128)(2,1)S(1)}, bf16[384,384]{1,0:T(8,128)(2,1)S(1)}, u32[]{:S(2)}, u32[]{:S(2)}) collective-permute-start(bf16[384,384]{1,0:T(8,128)(2,1)S(1)} %collective-permute-done.21.refs_5_), channel_id=1, source_target_pairs={{0,1},{1,0},{2,3},{3,2},{4,5},{5,4},{6,7},{7,6},{8,9},{9,8},{10,11... | collective-permute-start | bytes 884744 | tf_op jit(solution)/shard_map/ppermute | solution.py:19
  166.6 18.8 %collective-permute-start.35 = (bf16[384,384]{1,0:T(8,128)(2,1)S(1)}, bf16[384,384]{1,0:T(8,128)(2,1)S(1)}, u32[]{:S(2)}, u32[]{:S(2)}) collective-permute-start(bf16[384,384]{1,0:T(8,128)(2,1)S(1)} %collective-permute-done.28.refs_6_), channel_id=1, source_target_pairs={{0,1},{1,0},{2,3},{3,2},{4,5},{5,4},{6,7},{7,6},{8,9},{9,8},{10,11... | collective-permute-start | bytes 884744 | tf_op jit(solution)/shard_map/ppermute | solution.py:19
  167.0 18.4 %collective-permute-start.36 = (bf16[384,384]{1,0:T(8,128)(2,1)S(1)}, bf16[384,384]{1,0:T(8,128)(2,1)S(1)}, u32[]{:S(2)}, u32[]{:S(2)}) collective-permute-start(bf16[384,384]{1,0:T(8,128)(2,1)S(1)} %collective-permute-done.23.refs_7_), channel_id=1, source_target_pairs={{0,1},{1,0},{2,3},{3,2},{4,5},{5,4},{6,7},{7,6},{8,9},{9,8},{10,11... | collective-permute-start | bytes 884744 | tf_op jit(solution)/shard_map/ppermute | solution.py:19
  174.5 10.9 %collective-permute-start.32 = (bf16[384,384]{1,0:T(8,128)(2,1)S(1)}, bf16[384,384]{1,0:T(8,128)(2,1)S(1)}, u32[]{:S(2)}, u32[]{:S(2)}) collective-permute-start(bf16[384,384]{1,0:T(8,128)(2,1)S(1)} %collective-permute-done.27.refs_3_), channel_id=1, source_target_pairs={{0,1},{1,0},{2,3},{3,2},{4,5},{5,4},{6,7},{7,6},{8,9},{9,8},{10,11... | collective-permute-start | bytes 884744 | tf_op jit(solution)/shard_map/ppermute | solution.py:19
  175.5 16.3 %collective-permute-start.37 = (f32[192,192]{1,0:T(8,128)S(1)}, f32[192,192]{1,0:T(8,128)S(1)}, u32[]{:S(2)}, u32[]{:S(2)}) collective-permute-start(f32[192,192]{1,0:T(8,128)S(1)} %get-tuple-element.126), channel_id=1, source_target_pairs={{0,4},{4,0},{1,5},{5,1},{2,6},{6,2},{3,7},{7,3},{8,12},{12,8},{9,1... | collective-permute-start | bytes 442376 | tf_op jit(solution)/shard_map/ppermute | solution.py:19
  176.4 15.5 %collective-permute-start.38 = (bf16[192,384]{1,0:T(8,128)(2,1)S(1)}, bf16[192,384]{1,0:T(8,128)(2,1)S(1)}, u32[]{:S(2)}, u32[]{:S(2)}) collective-permute-start(bf16[192,384]{1,0:T(8,128)(2,1)S(1)} %get-tuple-element.127), channel_id=1, source_target_pairs={{0,0},{1,8},{2,16},{3,24},{4,4},{5,12},{6,20},{7,28},{8,1},{9,9},{... | collective-permute-start | bytes 442376 | tf_op jit(solution)/shard_map/ppermute | solution.py:732
  (5 other events, 31.4 us)
